TPU v7x, 32 devices: a whole 2x2x4 slice. The times are simulated.
32 devices in a mesh: dp: 4 (over x, core), row: 4 (over z), col: 2 (over y).
Axes of the slice: x: 2, y: 2, z: 4, core: 2. Of those that a mesh axis runs over, the one named last changes fastest.
Arguments:
- tokens: bfloat16 [768, 4096], P('row', ('dp', 'col')), may hold values from -6 to 6
- lengths: int32 [4], replicated, may hold values from 1024 to 1024, as said below
- w_query: bfloat16 [768, 768], P('row', 'col'), may hold values from -0.21875 to 0.21875
- w_key: bfloat16 [768, 768], P('row', 'col'), may hold values from -0.21875 to 0.21875
- w_value: bfloat16 [768, 768], P('row', 'col'), may hold values from -0.21875 to 0.21875
- w_out: bfloat16 [768, 768], P('col', 'row'), may hold values from -3.5 to 3.5
- gain_one: float32 [768], P('row'), may hold values from 0.5 to 1.5
- bias_one: float32 [768], P('row'), may hold values from -3 to 3
- w_up: bfloat16 [768, 3072], P('row', 'col'), may hold values from -0.21875 to 0.21875
- w_down: bfloat16 [3072, 768], P('col', 'row'), may hold values from -0.109375 to 0.109375
- gain_two: float32 [768], P('row'), may hold values from 0.5 to 1.5
- bias_two: float32 [768], P('row'), may hold values from -3 to 3
- cotangent: bfloat16 [768, 4096], P('row', ('dp', 'col')), may hold values from -6 to 6
Outputs:
- output: bfloat16 [768, 4096], P('row', ('dp', 'col'))
- input_grad: float32 [768, 4096], P('row', ('dp', 'col'))
- grad_query: float32 [768, 768], P('row', 'col')
- grad_key: float32 [768, 768], P('row', 'col')
- grad_value: float32 [768, 768], P('row', 'col')
- grad_out: float32 [768, 768], P('col', 'row')
- grad_gain_one: float32 [768], P('row')
- grad_bias_one: float32 [768], P('row')
- grad_up: float32 [768, 3072], P('row', 'col')
- grad_down: float32 [3072, 768], P('col', 'row')
- grad_gain_two: float32 [768], P('row')
- grad_bias_two: float32 [768], P('row')
Inputs may be any that keep to these rules, and one draw needn't show every extreme that they name: lengths counts the real tokens at the start of each sequence's 1024 slots; some sequence is full and some has 1024.
All inputs are finite; a program needn't handle non-finite values.
Results may differ from a plain program's by a relative error of at most 0.02.
Values may be sent and summed in bfloat16 or wider, within the bound.
No kernel may reach another device: no remote copies, remote signals or barrier semaphores. Data moves between devices by JAX's collectives and lax.ppermute only.
A program may use at most 192 MiB of HBM per device.

v0:
```python
from functools import partial
import math

import jax
import jax.numpy as jnp
from jax import lax
from jax.sharding import PartitionSpec as P

D = 768
H = 12
HD = 64
SEQ_MAX = 4096
TOK_DEV = 128


norm_eps = 1e-05
highest = lax.Precision.HIGHEST


def carried_in(shard, axis, join, neutral, backward):
    count = lax.axis_size(axis)
    place = lax.axis_index(axis)
    ahead = count - 1 - place if backward else place
    gathered = jax.tree.map(
        lambda a, kind: lax.all_gather(a.astype(kind), axis),
        shard,
        jax.tree.map(lambda a: jnp.bfloat16 if a.dtype == jnp.float32 else a.dtype, shard),
    )
    state = jax.tree.map(lambda a, e: jnp.zeros_like(a) + jnp.asarray(e, a.dtype), shard, neutral)

    def one(turn, state):
        source = count - 1 - turn if backward else turn
        return join(
            state,
            jax.tree.map(
                lambda a, own: lax.dynamic_index_in_dim(a, source, 0, False).astype(own.dtype),
                gathered,
                shard,
            ),
        )

    return lax.fori_loop(0, ahead, one, state)


def gather_cols(operand):
    return lax.all_gather(operand, "col", axis=0, tiled=True)


def gather_rows(operand):
    return lax.all_gather(operand, "row", axis=0, tiled=True)


def summed_over_rows(gathered, matrix):
    out_rows = gathered.shape[0] // lax.axis_size("row")

    def term_rows(first_row, row_count):
        sliced = lax.dynamic_slice_in_dim(gathered, first_row, row_count, 0)
        return jnp.dot(sliced, matrix, preferred_element_type=jnp.float32)

    return lax.psum_scatter(
        term_rows(jnp.int32(0), out_rows * lax.axis_size("row")),
        "row",
        scatter_dimension=0,
        tiled=True,
    )


def summed_over_cols(gathered, matrix):
    out_rows = gathered.shape[0] // lax.axis_size("col")

    def term_rows(first_row, row_count):
        sliced = lax.dynamic_slice_in_dim(gathered, first_row, row_count, 0)
        return jnp.dot(sliced, matrix, preferred_element_type=jnp.float32)

    return lax.psum_scatter(
        term_rows(jnp.int32(0), out_rows * lax.axis_size("col")).astype(jnp.bfloat16),
        "col",
        scatter_dimension=0,
        tiled=True,
    ).astype(jnp.float32)


def to_heads(stacked):
    return lax.all_to_all(stacked, "col", split_axis=1, concat_axis=2, tiled=True)


def to_tokens(stacked):
    return lax.all_to_all(stacked, "col", split_axis=2, concat_axis=1, tiled=True)


def row_totals(first_part, second_part):
    return lax.psum((first_part, second_part), "row")


def norm_forward(hidden, scale_vec, shift_vec):
    sum_one, sum_two = row_totals(jnp.sum(hidden, 1), jnp.sum(hidden * hidden, 1))
    row_mean = sum_one / D
    variance = sum_two / D - row_mean * row_mean
    inv_std = lax.rsqrt(variance + norm_eps)
    normed = (hidden - row_mean[:, None]) * inv_std[:, None]
    return (normed * scale_vec + shift_vec, normed, inv_std)


def norm_backward(grad_in, normed, inv_std, scale_vec):
    grad_normed = grad_in * scale_vec
    total_one, total_two = row_totals(jnp.sum(grad_normed, 1), jnp.sum(grad_normed * normed, 1))
    grad_hidden = inv_std[:, None] * (
        grad_normed - total_one[:, None] / D - normed * (total_two[:, None] / D)
    )
    return (grad_hidden, jnp.sum(grad_in * normed, 0), jnp.sum(grad_in, 0))


def seq_lengths(lengths, seq_ids):
    matches = seq_ids[:, None] == jnp.arange(lengths.shape[0], dtype=jnp.int32)[None, :]
    return jnp.sum(jnp.where(matches, lengths[None, :], 0), 1)


def reset_combine(earlier, later):
    keep_prior = 1.0 - later[4]
    joined = tuple(
        (
            keep_prior * prior_part + next_part
            for prior_part, next_part in zip(earlier[:4], later[:4])
        )
    )
    return joined + (jnp.maximum(earlier[4], later[4]),)


def empty_state():
    return (
        jnp.zeros((H, HD, HD), jnp.float32),
        jnp.zeros((H, HD, HD), jnp.float32),
        jnp.zeros((H, HD), jnp.float32),
        jnp.zeros((H, HD), jnp.float32),
        jnp.zeros((), jnp.float32),
    )


def attend_forward(queries, keys_in, values_in, present, cos_flat, sin_flat, opens_seq):
    block_rows = queries.shape[0]
    cos_pos = cos_flat[:, None, None]
    sin_pos = sin_flat[:, None, None]
    q_pos = jnp.maximum(queries, 0)
    k_pos = jnp.maximum(keys_in, 0) * present[:, None, None].astype(jnp.bfloat16)
    q_cos = q_pos.astype(jnp.float32) * cos_pos
    q_sin = q_pos.astype(jnp.float32) * sin_pos
    k_cos = k_pos.astype(jnp.float32) * cos_pos
    k_sin = k_pos.astype(jnp.float32) * sin_pos
    values_wide = values_in.astype(jnp.float32)
    local_state = (
        jnp.einsum("jhd,jhe->hde", k_cos, values_wide, precision=highest),
        jnp.einsum("jhd,jhe->hde", k_sin, values_wide, precision=highest),
        jnp.sum(k_cos, 0),
        jnp.sum(k_sin, 0),
    )
    arrived = carried_in(
        local_state + (opens_seq,), ("row", "col"), reset_combine, empty_state(), False
    )
    s_cos, s_sin, z_cos, z_sin = tuple(
        (state_part * (1.0 - opens_seq) for state_part in arrived[:4])
    )
    row_ids = jnp.arange(block_rows, dtype=jnp.int32)
    causal = (row_ids[:, None] >= row_ids[None, :]).astype(jnp.float32)
    reweight = (
        cos_flat[:, None] * cos_flat[None, :] + sin_flat[:, None] * sin_flat[None, :]
    ) * causal
    scores = jnp.einsum("ihd,jhd->hij", q_pos, k_pos, preferred_element_type=jnp.float32)
    weights = scores * reweight[None]
    weights_low = weights.astype(jnp.bfloat16)
    numerator = jnp.einsum(
        "hij,jhe->ihe", weights_low, values_in, preferred_element_type=jnp.float32
    )
    numerator = numerator + jnp.einsum("ihd,hde->ihe", q_cos, s_cos, precision=highest)
    numerator = numerator + jnp.einsum("ihd,hde->ihe", q_sin, s_sin, precision=highest)
    denominator = 1.0 + jnp.sum(weights, 2).T
    denominator = denominator + jnp.einsum("ihd,hd->ih", q_cos, z_cos, precision=highest)
    denominator = denominator + jnp.einsum("ihd,hd->ih", q_sin, z_sin, precision=highest)
    mixed = (numerator / denominator[:, :, None]).astype(jnp.bfloat16).reshape(block_rows, D)
    kept = (
        queries,
        keys_in,
        values_in,
        q_pos,
        k_pos,
        q_cos,
        q_sin,
        k_cos,
        k_sin,
        values_wide,
        reweight,
        weights_low,
        numerator,
        denominator,
        s_cos,
        s_sin,
        z_cos,
        z_sin,
        present,
        cos_pos,
        sin_pos,
    )
    return (mixed, kept)


def attend_backward(grad_heads, kept, closes_seq):
    (
        queries,
        keys_in,
        values_in,
        q_pos,
        k_pos,
        q_cos,
        q_sin,
        k_cos,
        k_sin,
        values_wide,
        reweight,
        weights_low,
        numerator,
        denominator,
        s_cos,
        s_sin,
        z_cos,
        z_sin,
        present,
        cos_pos,
        sin_pos,
    ) = kept
    block_rows = queries.shape[0]
    grad_attn = grad_heads.astype(jnp.float32).reshape(block_rows, H, HD)
    grad_num_low = (grad_attn / denominator[:, :, None]).astype(jnp.bfloat16)
    grad_num = grad_num_low.astype(jnp.float32)
    grad_den = -jnp.sum(grad_attn * numerator, 2) / (denominator * denominator)
    grad_weights = jnp.einsum(
        "ihe,jhe->hij", grad_num_low, values_in, preferred_element_type=jnp.float32
    )
    grad_weights = grad_weights + grad_den.T[:, :, None]
    grad_scores = (grad_weights * reweight[None]).astype(jnp.bfloat16)
    local_grad = (
        jnp.einsum("ihd,ihe->hde", q_cos, grad_num, precision=highest),
        jnp.einsum("ihd,ihe->hde", q_sin, grad_num, precision=highest),
        jnp.einsum("ihd,ih->hd", q_cos, grad_den, precision=highest),
        jnp.einsum("ihd,ih->hd", q_sin, grad_den, precision=highest),
    )
    later_sum = carried_in(
        local_grad + (closes_seq,), ("row", "col"), reset_combine, empty_state(), True
    )
    g_cos, g_sin, gz_cos, gz_sin = tuple(
        (state_part * (1.0 - closes_seq) for state_part in later_sum[:4])
    )
    grad_qpos = jnp.einsum("hij,jhd->ihd", grad_scores, k_pos, preferred_element_type=jnp.float32)
    grad_qpos = grad_qpos + cos_pos * (
        jnp.einsum("ihe,hde->ihd", grad_num, s_cos, precision=highest)
        + grad_den[:, :, None] * z_cos[None]
    )
    grad_qpos = grad_qpos + sin_pos * (
        jnp.einsum("ihe,hde->ihd", grad_num, s_sin, precision=highest)
        + grad_den[:, :, None] * z_sin[None]
    )
    grad_kpos = jnp.einsum("hij,ihd->jhd", grad_scores, q_pos, preferred_element_type=jnp.float32)
    grad_kpos = grad_kpos + cos_pos * (
        jnp.einsum("jhe,hde->jhd", values_wide, g_cos, precision=highest) + gz_cos[None]
    )
    grad_kpos = grad_kpos + sin_pos * (
        jnp.einsum("jhe,hde->jhd", values_wide, g_sin, precision=highest) + gz_sin[None]
    )
    grad_values = jnp.einsum(
        "hij,ihe->jhe", weights_low, grad_num_low, preferred_element_type=jnp.float32
    )
    grad_values = grad_values + jnp.einsum("jhd,hde->jhe", k_cos, g_cos, precision=highest)
    grad_values = grad_values + jnp.einsum("jhd,hde->jhe", k_sin, g_sin, precision=highest)
    grad_q = (grad_qpos * (queries > 0).astype(jnp.float32)).astype(jnp.bfloat16)
    grad_k = (grad_kpos * (keys_in > 0).astype(jnp.float32) * present[:, None, None]).astype(
        jnp.bfloat16
    )
    grad_v = grad_values.astype(jnp.bfloat16)
    return (
        grad_q.reshape(block_rows, D),
        grad_k.reshape(block_rows, D),
        grad_v.reshape(block_rows, D),
    )


def on_device(
    tokens,
    lengths,
    w_query,
    w_key,
    w_value,
    w_out,
    gain_one,
    bias_one,
    w_up,
    w_down,
    gain_two,
    bias_two,
    cotangent,
):
    row_count = lax.axis_size("row")
    col_count = lax.axis_size("col")
    seq_len = min(SEQ_MAX, TOK_DEV * row_count * col_count)
    data_idx = lax.axis_index("dp")
    row_idx = lax.axis_index("row")
    col_idx = lax.axis_index("col")
    feat_rows = tokens.shape[0]
    group_idx = row_idx * col_count + col_idx
    global_idx = (data_idx * row_count * col_count + group_idx) * TOK_DEV + jnp.arange(
        TOK_DEV, dtype=jnp.int32
    )
    positions = global_idx % seq_len
    present = (positions < seq_lengths(lengths, global_idx // seq_len)).astype(jnp.float32)
    angles = math.pi * positions.astype(jnp.float32) / (2.0 * seq_len)
    cos_flat = jnp.cos(angles)
    sin_flat = jnp.sin(angles)
    opens_seq = (group_idx * TOK_DEV % seq_len == 0).astype(jnp.float32)
    closes_seq = ((group_idx + 1) * TOK_DEV % seq_len == 0).astype(jnp.float32)
    token_rows = tokens.T
    width_col = w_query.shape[1]
    w_cat = jnp.concatenate([w_query, w_key, w_value], 1)
    x_gathered = gather_cols(token_rows)
    qkv = summed_over_rows(x_gathered, w_cat).astype(jnp.bfloat16)
    stacked = jnp.stack(
        [qkv[:, :width_col], qkv[:, width_col : 2 * width_col], qkv[:, 2 * width_col :]], 0
    )
    head_rows = to_heads(stacked)
    mixed, kept = attend_forward(
        head_rows[0].reshape(TOK_DEV, H, HD),
        head_rows[1].reshape(TOK_DEV, H, HD),
        head_rows[2].reshape(TOK_DEV, H, HD),
        present,
        cos_flat,
        sin_flat,
        opens_seq,
    )
    mixed_two = to_tokens(mixed[None])[0]
    mixed_gathered = gather_rows(mixed_two)
    branch = summed_over_cols(mixed_gathered, w_out)
    first, normed_one, inv_one = norm_forward(
        token_rows.astype(jnp.float32) + branch, gain_one, bias_one
    )
    first_low = first.astype(jnp.bfloat16)
    first_gathered = gather_cols(first_low)
    pre = summed_over_rows(first_gathered, w_up)
    act, gelu_pull = jax.vjp(partial(jax.nn.gelu, approximate=False), pre)
    act_low = act.astype(jnp.bfloat16)
    act_gathered = gather_rows(act_low)
    ffn = summed_over_cols(act_gathered, w_down)
    result, normed_two, inv_two = norm_forward(first + ffn, gain_two, bias_two)
    rows_one = token_rows.shape[0]
    global_one = (data_idx * col_count + col_idx) * rows_one + jnp.arange(rows_one, dtype=jnp.int32)
    present_one = (global_one % seq_len < seq_lengths(lengths, global_one // seq_len)).astype(
        jnp.float32
    )
    grad_result = cotangent.T.astype(jnp.float32) * present_one[:, None]
    grad_second, grad_gain_two, grad_bias_two = norm_backward(
        grad_result, normed_two, inv_two, gain_two
    )
    grad_ffn_gathered = gather_cols(grad_second.astype(jnp.bfloat16))
    act_again = gather_rows(act_low)
    grad_down = jnp.einsum(
        "tf,td->fd", act_again, grad_ffn_gathered, preferred_element_type=jnp.float32
    )
    grad_act = summed_over_rows(grad_ffn_gathered, w_down.T)
    grad_pre = gelu_pull(grad_act)[0].astype(jnp.bfloat16)
    grad_pre_gathered = gather_rows(grad_pre)
    first_again = gather_cols(first_low)
    grad_up = jnp.einsum(
        "td,tf->df", first_again, grad_pre_gathered, preferred_element_type=jnp.float32
    )
    grad_first = summed_over_cols(grad_pre_gathered, w_up.T) + grad_second
    grad_hidden, grad_gain_one, grad_bias_one = norm_backward(
        grad_first, normed_one, inv_one, gain_one
    )
    branch_grad_gathered = gather_cols(grad_hidden.astype(jnp.bfloat16))
    mixed_again = gather_rows(mixed_two)
    grad_out = jnp.einsum(
        "tc,tr->cr", mixed_again, branch_grad_gathered, preferred_element_type=jnp.float32
    )
    grad_mixed = summed_over_rows(branch_grad_gathered, w_out.T).astype(jnp.bfloat16)
    grad_heads = to_heads(grad_mixed[None])[0]
    grad_q, grad_k, grad_v = attend_backward(grad_heads, kept, closes_seq)
    grad_rows = to_tokens(jnp.stack([grad_q, grad_k, grad_v], 0))
    grad_cat = jnp.concatenate([grad_rows[0], grad_rows[1], grad_rows[2]], 1)
    grad_cat_gathered = gather_rows(grad_cat)
    x_again = gather_cols(token_rows)
    grad_cat_w = jnp.einsum(
        "tr,tc->rc", x_again, grad_cat_gathered, preferred_element_type=jnp.float32
    )
    input_rows = summed_over_cols(grad_cat_gathered, w_cat.T) + grad_hidden
    gain_parts = jnp.stack([grad_gain_one, grad_bias_one, grad_gain_two, grad_bias_two], 0)
    gain_sums = lax.psum(gain_parts.reshape(4 * feat_rows), "col")
    grad_query = grad_cat_w[:, :width_col]
    grad_key = grad_cat_w[:, width_col : 2 * width_col]
    grad_value = grad_cat_w[:, 2 * width_col :]
    output = result.astype(jnp.bfloat16).T
    input_grad = input_rows.T
    sums = (
        lax.psum(grad_query.astype(jnp.bfloat16), "dp").astype(jnp.float32),
        lax.psum(grad_key.astype(jnp.bfloat16), "dp").astype(jnp.float32),
        lax.psum(grad_value.astype(jnp.bfloat16), "dp").astype(jnp.float32),
        lax.psum(grad_out.astype(jnp.bfloat16), "dp").astype(jnp.float32),
        lax.psum(grad_up.astype(jnp.bfloat16), "dp").astype(jnp.float32),
        lax.psum(grad_down.astype(jnp.bfloat16), "dp").astype(jnp.float32),
        lax.psum(gain_sums.astype(jnp.bfloat16), "dp").astype(jnp.float32),
    )
    gain_total = sums[6].reshape(4, feat_rows)
    return (
        output,
        input_grad,
        sums[0],
        sums[1],
        sums[2],
        sums[3],
        gain_total[0],
        gain_total[1],
        sums[4],
        sums[5],
        gain_total[2],
        gain_total[3],
    )


def solution(mesh):
    placed = (
        P("row", ("dp", "col")),
        P(),
        P("row", "col"),
        P("row", "col"),
        P("row", "col"),
        P("col", "row"),
        P("row"),
        P("row"),
        P("row", "col"),
        P("col", "row"),
        P("row"),
        P("row"),
        P("row", ("dp", "col")),
    )
    return jax.shard_map(
        on_device,
        mesh=mesh,
        in_specs=placed,
        out_specs=(
            P("row", ("dp", "col")),
            P("row", ("dp", "col")),
            P("row", "col"),
            P("row", "col"),
            P("row", "col"),
            P("col", "row"),
            P("row"),
            P("row"),
            P("row", "col"),
            P("col", "row"),
            P("row"),
            P("row"),
        ),
        check_vma=False,
    )
```

profile of v0, /device:TPU:0, one launch (start us, length us, event | category | flops | bytes accessed | tf_op | source)
XLA Modules:
  0.0 1174.7 jit_solution(3939567655958172333)
XLA Ops:
  7.2 8.9 all_gather.84
  24.9 22.9 %all-reduce.6 = (bf16[8]{0:T(256)(128)(2,1)S(1)}, bf16[8]{0:T(256)(128)(2,1)}) all-reduce(bf16[8]{0:T(256)(128)(2,1)S(1)} %dynamic-update-slice, bf16[8]{0:T(256)(128)(2,1)S(1)} %dynamic-update-slice.1), channel_id=1, replica_groups=mesh['dp'=4,'row'=4,'col'=2] {'row','col'}, use_global_device_ids=true, to_apply=%add | all-reduce | flops 16 | bytes 64
  48.5 60.6 %reduce-scatter.9.cloned.1.call-done = f32[256,1152]{0,1:T(8,128)} async-done(((f32[1024,1152]{0,1:T(8,128)}), f32[256,1152]{0,1:T(8,128)}) %reduce-scatter.9.cloned.1.call-update) | async-done | bytes 1179664 | tf_op jit(solution)/shard_map/reduce_scatter | solution.py:60
  115.6 10.9 all-to-all-done
  130.3 30.4 %all_gather.92 = bf16[8,12,64]{2,1,0:T(8,128)(2,1)S(1)} all-gather(bf16[1,12,64]{2,1,0:T(8,128)(2,1)S(1)} %convert_element_type.346), channel_id=1, replica_groups=mesh['dp'=4,'row'=4,'col'=2] {'row','col'}, dimensions={0}, use_global_device_ids=true | all-gather | bytes 13824 | tf_op jit(solution)/shard_map/all_gather | solution.py:25
  160.7 30.4 %all_gather.91 = bf16[8,12,64]{2,1,0:T(8,128)(2,1)S(1)} all-gather(bf16[1,12,64]{2,1,0:T(8,128)(2,1)S(1)} %convert_element_type.344), channel_id=1, replica_groups=mesh['dp'=4,'row'=4,'col'=2] {'row','col'}, dimensions={0}, use_global_device_ids=true | all-gather | bytes 13824 | tf_op jit(solution)/shard_map/all_gather | solution.py:25
  191.1 38.0 %all-gather = bf16[96,64,64]{2,1,0:T(8,128)(2,1)} all-gather(bf16[12,64,64]{2,1,0:T(8,128)(2,1)S(1)} %convolution_convert_fusion.10), channel_id=2, replica_groups=mesh['dp'=4,'row'=4,'col'=2] {'row','col'}, dimensions={0}, use_global_device_ids=true | all-gather | bytes 884736 | tf_op jit(solution)/shard_map/all_gather | solution.py:25
  229.2 35.5 %all-gather.1 = bf16[96,64,64]{2,1,0:T(8,128)(2,1)} all-gather(bf16[12,64,64]{2,1,0:T(8,128)(2,1)S(1)} %convolution_convert_fusion.9), channel_id=3, replica_groups=mesh['dp'=4,'row'=4,'col'=2] {'row','col'}, dimensions={0}, use_global_device_ids=true | all-gather | bytes 884736 | tf_op jit(solution)/shard_map/all_gather | solution.py:25
  271.5 7.7 all_to_all.54
  279.7 30.6 %all_gather.93 = bf16[1024,384]{1,0:T(8,128)(2,1)S(1)} all-gather(bf16[256,384]{1,0:T(8,128)(2,1)S(1)} %bitcast.276), channel_id=1, replica_groups=mesh['dp'=4,'row'=4,'col'=2] {'row'}, dimensions={0}, use_global_device_ids=true | all-gather | bytes 983040 | tf_op jit(solution)/shard_map/all_gather | solution.py:50
  311.6 14.0 %reduce-scatter.11.cloned.1.call-done = bf16[512,192]{0,1:T(8,128)(2,1)} async-done(((bf16[1024,192]{0,1:T(8,128)(2,1)}), bf16[512,192]{0,1:T(8,128)(2,1)}) %reduce-scatter.11.cloned.1.call-update) | async-done | bytes 196624 | tf_op jit(solution)/shard_map/reduce_scatter | solution.py:75
  326.6 11.7 all-reduce.5
  339.4 6.5 all_gather.94
  351.5 108.1 %reduce-scatter.13.cloned.1.call-done = f32[256,1536]{1,0:T(8,128)} async-done(((f32[1024,1536]{1,0:T(8,128)}), f32[256,1536]{1,0:T(8,128)}) %reduce-scatter.13.cloned.1.call-update) | async-done | bytes 1572880 | tf_op jit(solution)/shard_map/reduce_scatter | solution.py:60
  465.1 64.1 %all-gather.12.cloned.1.call-done = bf16[1024,1536]{1,0:T(8,128)(2,1)} async-done(((bf16[256,1536]{1,0:T(8,128)(2,1)}), bf16[1024,1536]{1,0:T(8,128)(2,1)}) %all-gather.12.cloned.1.call-update) | async-done | bytes 3145744 | tf_op jit(solution)/shard_map/all_gather | solution.py:50
  533.9 11.2 reduce-scatter.15.cloned.1.call-done
  546.7 12.4 %all-reduce.4 = (f32[512]{0:T(512)}, f32[512]{0:T(512)}) all-reduce(f32[512]{0:T(512)} %get-tuple-element.289, f32[512]{0:T(512)} %get-tuple-element.288), channel_id=1, replica_groups=mesh['dp'=4,'row'=4,'col'=2] {'row'}, use_global_device_ids=true, to_apply=%region_17.18 | all-reduce | flops 1024 | bytes 8192 | tf_op jit(solution)/shard_map/psum | solution.py:92
  562.1 9.0 all-reduce.3
  573.6 6.3 all_gather.96
  584.4 109.6 %reduce-scatter.17.cloned.1.call-done = f32[256,1536]{1,0:T(8,128)} async-done(((f32[1024,1536]{1,0:T(8,128)}), f32[256,1536]{1,0:T(8,128)}) %reduce-scatter.17.cloned.1.call-update) | async-done | bytes 1572880 | tf_op jit(solution)/shard_map/reduce_scatter | solution.py:60
  698.0 64.1 %all-gather.14.cloned.1.call-done = bf16[1024,1536]{1,0:T(8,128)(2,1)} async-done(((bf16[256,1536]{1,0:T(8,128)(2,1)}), bf16[1024,1536]{1,0:T(8,128)(2,1)}) %all-gather.14.cloned.1.call-update) | async-done | bytes 3145744 | tf_op jit(solution)/shard_map/all_gather | solution.py:50
  766.1 11.9 %reduce-scatter.19.cloned.1.call-done = bf16[512,192]{0,1:T(8,128)(2,1)} async-done(((bf16[1024,192]{0,1:T(8,128)(2,1)}), bf16[512,192]{0,1:T(8,128)(2,1)}) %reduce-scatter.19.cloned.1.call-update) | async-done | bytes 196624 | tf_op jit(solution)/shard_map/reduce_scatter | solution.py:75
  780.6 11.8 %all-reduce.2 = (f32[512]{0:T(512)S(1)}, f32[512]{0:T(512)S(1)}) all-reduce(f32[512]{0:T(512)} %get-tuple-element.281, f32[512]{0:T(512)} %get-tuple-element.286), channel_id=1, replica_groups=mesh['dp'=4,'row'=4,'col'=2] {'row'}, use_global_device_ids=true, to_apply=%region_28.29 | all-reduce | flops 1024 | bytes 8192 | tf_op jit(solution)/shard_map/psum | solution.py:92
  802.7 32.6 %reduce-scatter.21.cloned.1.call-done = f32[256,384]{1,0:T(8,128)} async-done(((f32[1024,384]{1,0:T(8,128)}), f32[256,384]{1,0:T(8,128)}) %reduce-scatter.21.cloned.1.call-update) | async-done | bytes 393232 | tf_op jit(solution)/shard_map/reduce_scatter | solution.py:60
  858.4 32.0 %all-gather.6 = bf16[8,12,64]{2,1,0:T(8,128)(2,1)} all-gather(bf16[1,12,64]{2,1,0:T(8,128)(2,1)S(1)} %bitcast.288), channel_id=6, replica_groups=mesh['dp'=4,'row'=4,'col'=2] {'row','col'}, dimensions={0}, use_global_device_ids=true | all-gather | bytes 13824 | tf_op jit(solution)/shard_map/all_gather | solution.py:25
  890.4 32.3 %all-gather.7 = bf16[8,12,64]{2,1,0:T(8,128)(2,1)} all-gather(bf16[1,12,64]{2,1,0:T(8,128)(2,1)S(1)} %bitcast.287), channel_id=7, replica_groups=mesh['dp'=4,'row'=4,'col'=2] {'row','col'}, dimensions={0}, use_global_device_ids=true | all-gather | bytes 13824 | tf_op jit(solution)/shard_map/all_gather | solution.py:25
  924.7 38.9 %all-gather.2 = bf16[96,64,64]{2,1,0:T(8,128)(2,1)} all-gather(bf16[12,64,64]{2,1,0:T(8,128)(2,1)S(1)} %convolution_convert_fusion.8), channel_id=4, replica_groups=mesh['dp'=4,'row'=4,'col'=2] {'row','col'}, dimensions={0}, use_global_device_ids=true | all-gather | bytes 884736 | tf_op jit(solution)/shard_map/all_gather | solution.py:25
  963.6 35.3 %all-gather.3 = bf16[96,64,64]{2,1,0:T(8,128)(2,1)} all-gather(bf16[12,64,64]{2,1,0:T(8,128)(2,1)S(1)} %convolution_convert_fusion.7), channel_id=5, replica_groups=mesh['dp'=4,'row'=4,'col'=2] {'row','col'}, dimensions={0}, use_global_device_ids=true | all-gather | bytes 884736 | tf_op jit(solution)/shard_map/all_gather | solution.py:25
  999.0 26.7 %while.39 = (s32[]{:T(128)}, f32[12,64,64]{2,1,0:T(8,128)S(1)}, f32[12,64,64]{2,1,0:T(8,128)S(1)}, f32[12,64]{1,0:T(8,128)S(1)}, f32[12,64]{1,0:T(8,128)S(1)}, /...) while((s32[]{:T(128)}, f32[12,64,64]{2,1,0:T(8,128)S(1)}, ...), condition=%wide.region_32.33_spmd, body=%wide.region_31.32_spmd.sunk | while | flops 299527 | bytes 998637 | solution.py:42
  1032.3 10.4 all_to_all.55
  1049.9 42.7 %all-gather.16.cloned.1.call-done = bf16[1024,1152]{1,0:T(8,128)(2,1)} async-done(((bf16[256,1152]{1,0:T(8,128)(2,1)}), bf16[1024,1152]{1,0:T(8,128)(2,1)}) %all-gather.16.cloned.1.call-update) | async-done | bytes 2359312 | tf_op jit(solution)/shard_map/all_gather | solution.py:50
  1113.8 45.1 %all-reduce.10.cloned.1.call-done = (bf16[192,384]{1,0:T(8,128)(2,1)}, bf16[192,384]{1,0:T(8,128)(2,1)}, bf16[192,384]{1,0:T(8,128)(2,1)}, bf16[384,192]{0,1:T(8...) async-done(((bf16[192,384]{1,0:T(8,128)(2,1)}, bf16[192,384]{1,0:T(8,128)(2,1)}, bf16[192,384]{1,0:T(8,128)(2,1)}, bf16[384,192]{0,1:T(8,128)(2,1)}, ...) | async-done | bytes 1769488 | tf_op jit(solution)/shard_map/psum | solution.py:398
  (312 shorter events, 168.7 us)
Async XLA Ops:
  7.2 522.1 %copy-start = (bf16[1536,192]{0,1:T(8,128)(2,1)S(1)}, bf16[1536,192]{0,1:T(8,128)(2,1)}, u32[]{:S(2)}) copy-start(bf16[1536,192]{0,1:T(8,128)(2,1)} %param.26) | copy-start | bytes 1769476
  7.2 101.9 %reduce-scatter.9.cloned.1.call-start = ((), (), s32[]{:S(2)}) async-start(), calls=%async_computation.12 | async-start | bytes 5898240 | tf_op jit(solution)/shard_map/reduce_scatter | solution.py:60
  47.8 218.3 %copy-start.34 = (f32[128]{0:T(128)}, f32[128]{0:T(128)S(1)}, u32[]{:S(2)}) copy-start(f32[128]{0:T(128)S(1)} %fusion.87) | copy-start | bytes 1540
  48.5 216.3 %copy-start.39 = (bf16[128]{0:T(256)(128)(2,1)}, bf16[128]{0:T(256)(128)(2,1)S(1)}, u32[]{:S(2)}) copy-start(bf16[128]{0:T(256)(128)(2,1)S(1)} %get-tuple-element.357) | copy-start | bytes 772
  111.9 14.7 %all-to-all-start = ((bf16[3,256,384]{2,0,1:T(4,128)(2,1)}), bf16[3,256,384]{2,0,1:T(4,128)(2,1)S(1)}, u32[]{:S(2)}, u32[]{:S(2)}) async-start(bf16[3,256,384]{2,0,1:T(4,128)(2,1)} %copy.159), calls=%async_computation.1 | async-start | bytes 1572864 | tf_op jit(solution)/shard_map/all_to_all | solution.py:84
  115.4 210.2 %reduce-scatter.11.cloned.1.call-start = ((), (), s32[]{:S(2)}) async-start(), calls=%async_computation.13 | async-start | bytes 589824 | tf_op jit(solution)/shard_map/reduce_scatter | solution.py:75
  115.5 151.4 %copy-start.36 = (f32[128]{0:T(128)}, f32[128]{0:T(128)S(1)}, u32[]{:S(2)}) copy-start(f32[128]{0:T(128)S(1)} %fusion.86) | copy-start | bytes 1540
  115.6 149.2 %copy-start.25 = (f32[128,128]{0,1:T(8,128)}, f32[128,128]{0,1:T(8,128)S(1)}, u32[]{:S(2)}) copy-start(f32[128,128]{0,1:T(8,128)S(1)} %add_select_fusion) | copy-start | bytes 196612
  279.5 46.1 %copy-start.2 = (bf16[192,512]{1,0:T(8,128)(2,1)S(1)}, bf16[192,512]{1,0:T(8,128)(2,1)}, u32[]{:S(2)}) copy-start(bf16[192,512]{1,0:T(8,128)(2,1)} %param.17) | copy-start | bytes 589828
  279.7 58.7 %copy-start.47 = (f32[192]{0:T(256)S(1)}, f32[192]{0:T(256)}, u32[]{:S(2)}) copy-start(f32[192]{0:T(256)} %param.23) | copy-start | bytes 2308
  279.7 58.7 %copy-start.58 = (f32[192]{0:T(256)S(1)}, f32[192]{0:T(256)}, u32[]{:S(2)}) copy-start(f32[192]{0:T(256)} %param.24) | copy-start | bytes 2308
  311.6 148.0 %reduce-scatter.13.cloned.1.call-start = ((), (), s32[]{:S(2)}) async-start(), calls=%async_computation.14 | async-start | bytes 7864320 | tf_op jit(solution)/shard_map/reduce_scatter | solution.py:60
  338.3 454.0 %copy-start.29 = (f32[512]{0:T(512)}, f32[512]{0:T(512)S(1)}, u32[]{:S(2)}) copy-start(f32[512]{0:T(512)S(1)} %get-tuple-element.390) | copy-start | bytes 6148
  338.3 454.1 %copy-start.31 = (f32[512]{0:T(512)}, f32[512]{0:T(512)S(1)}, u32[]{:S(2)}) copy-start(f32[512]{0:T(512)S(1)} %get-tuple-element.391) | copy-start | bytes 6148
  351.5 177.8 %all-gather.12.cloned.1.call-start = ((), (), s32[]{:S(2)}) async-start(), calls=%async_computation.15 | async-start | bytes 3932160 | tf_op jit(solution)/shard_map/all_gather | solution.py:50
  465.1 79.9 %copy-start.3 = (bf16[512,192]{0,1:T(8,128)(2,1)S(1)}, bf16[512,192]{0,1:T(8,128)(2,1)}, u32[]{:S(2)}) copy-start(bf16[512,192]{0,1:T(8,128)(2,1)} %reduce-scatter.11.cloned.1.call-done) | copy-start | bytes 589828
  465.1 79.9 %reduce-scatter.15.cloned.1.call-start = ((), (), s32[]{:S(2)}) async-start(), calls=%async_computation.16 | async-start | bytes 589824 | tf_op jit(solution)/shard_map/reduce_scatter | solution.py:75
  533.1 160.9 %reduce-scatter.17.cloned.1.call-start = ((), (), s32[]{:S(2)}) async-start(), calls=%async_computation.17 | async-start | bytes 7864320 | tf_op jit(solution)/shard_map/reduce_scatter | solution.py:60
  584.4 177.7 %all-gather.14.cloned.1.call-start = ((), (), s32[]{:S(2)}) async-start(), calls=%async_computation.18 | async-start | bytes 3932160 | tf_op jit(solution)/shard_map/all_gather | solution.py:50
  697.9 80.0 %copy-start.17 = (bf16[192,512]{1,0:T(8,128)(2,1)S(1)}, bf16[192,512]{1,0:T(8,128)(2,1)}, u32[]{:S(2)}) copy-start(bf16[192,512]{1,0:T(8,128)(2,1)} %param.29) | copy-start | bytes 589828
  697.9 80.0 %reduce-scatter.19.cloned.1.call-start = ((), (), s32[]{:S(2)}) async-start(), calls=%async_computation.19 | async-start | bytes 589824 | tf_op jit(solution)/shard_map/reduce_scatter | solution.py:75
  766.0 69.4 %reduce-scatter.21.cloned.1.call-start = ((), (), s32[]{:S(2)}) async-start(), calls=%async_computation.20 | async-start | bytes 1966080 | tf_op jit(solution)/shard_map/reduce_scatter | solution.py:60
  802.7 44.2 %copy-start.5 = (bf16[3,2,128,384]{2,1,3,0:T(2,128)(2,1)S(1)}, bf16[3,2,128,384]{2,1,3,0:T(2,128)(2,1)}, u32[]{:S(2)}) copy-start(bf16[3,2,128,384]{2,1,3,0:T(2,128)(2,1)} %copy-done.4) | copy-start | bytes 1769476
  842.6 9.0 all-to-all-start.2
  846.6 245.9 %all-gather.16.cloned.1.call-start = ((), (), s32[]{:S(2)}) async-start(), calls=%async_computation.21 | async-start | bytes 2949120 | tf_op jit(solution)/shard_map/all_gather | solution.py:50
  854.9 67.8 %copy-start.26 = (f32[128,128]{0,1:T(8,128)S(1)}, f32[128,128]{0,1:T(8,128)}, u32[]{:S(2)}) copy-start(f32[128,128]{0,1:T(8,128)} %copy-done.25) | copy-start | bytes 196612
  856.4 66.6 %copy-start.40 = (bf16[128]{0:T(256)(128)(2,1)S(1)}, bf16[128]{0:T(256)(128)(2,1)}, u32[]{:S(2)}) copy-start(bf16[128]{0:T(256)(128)(2,1)} %copy-done.39) | copy-start | bytes 772
  857.9 65.3 %copy-start.28 = (pred[1,128,2,384]{1,3,2,0:T(32,128)(4,1)S(1)}, pred[1,128,2,384]{1,3,2,0:T(32,128)(4,1)}, u32[]{:S(2)}) copy-start(pred[1,128,2,384]{1,3,2,0:T(32,128)(4,1)} %copy.171) | copy-start | bytes 294916
  857.9 65.3 %copy-start.43 = (f32[12,64]{1,0:T(8,128)S(1)}, f32[12,64]{1,0:T(8,128)}, u32[]{:S(2)}) copy-start(f32[12,64]{1,0:T(8,128)} %copy-done.42) | copy-start | bytes 9220
  1044.3 67.6 %reduce-scatter.23.cloned.1.call-start = ((), (), s32[]{:S(2)}) async-start(), calls=%async_computation.22 | async-start | bytes 589824 | tf_op jit(solution)/shard_map/reduce_scatter | solution.py:75
  1048.3 44.3 %copy-start.20 = (bf16[192,1152]{1,0:T(8,128)(2,1)S(1)}, bf16[192,1152]{1,0:T(8,128)(2,1)}, u32[]{:S(2)}) copy-start(bf16[192,1152]{1,0:T(8,128)(2,1)} %copy-done.19) | copy-start | bytes 1327108
  1095.9 63.0 %all-reduce.10.cloned.1.call-start = ((), (), s32[]{:S(2)}) async-start(), calls=%async_computation.23 | async-start | bytes 3538944 | tf_op jit(solution)/shard_map/psum | solution.py:398
  (44 other events, 246.0 us)
Sparse Core Ops, SparseCore 0:
  22.3 86.8 reduce-scatter.8
  311.7 13.8 reduce-scatter.10
  351.6 107.9 reduce-scatter.12
  465.2 64.0 all-gather.11
  533.2 11.7 reduce-scatter.14
  584.5 109.4 reduce-scatter.16
  698.0 63.9 all-gather.13
  766.1 11.7 reduce-scatter.18
  802.8 32.4 reduce-scatter.20
  1044.4 48.0 all-gather.15
  1096.0 11.9 reduce-scatter.22
  1111.9 46.9 all-reduce.9
where the time goes:
time: 1180 us; the launch traced here: 1170 us
  waiting for transfers between devices  578 us (49%)
  blocking collectives  428 us (36%)
  other arithmetic  60.8 us (5%)
  matrix products  48.3 us (4%)
  local copies, waits for them, and re-layouts  31 us (3%)
  between operations  15.4 us (1%)
    reduce_scatter x4, waiting for transfers between devices, summed_over_rows(): lax.psum_scatter(term_rows(jnp.int32(0), out_rows * lax.axis_size('row'))...  311 us
    all_gather x8, blocking collectives, carried_in(): lax.all_gather(a.astype(kind), axis)  273 us
    all_gather x3, waiting for transfers between devices, gather_rows(): return lax.all_gather(operand, 'row', axis=0, tiled=True)  171 us
    psum x1, waiting for transfers between devices, on_device(): lax.psum(grad_query.astype(jnp.bfloat16), 'dp').astype(jnp.float32)  45.1 us
    psum x4, blocking collectives, row_totals(): return lax.psum((first_part, second_part), 'row')  44.9 us
    reduce_scatter x4, waiting for transfers between devices, summed_over_cols(): lax.psum_scatter(term_rows(jnp.int32(0), out_rows * lax.axis_size('col'))...  37 us
    all_gather x1, blocking collectives, gather_rows(): return lax.all_gather(operand, 'row', axis=0, tiled=True)  30.6 us
    all_gather x4, blocking collectives, gather_cols(): return lax.all_gather(operand, 'col', axis=0, tiled=True)  28.1 us
  transfers between devices with their start and end apart: 14, of which 13 were waited for; matrix products, arithmetic and copies ran while one was open for 2% of the time, Pallas kernels for 0%

commit v1 on v0

--- a/solution.py
+++ b/solution.py
@@ -420,6 +420,366 @@
     )
 
 
+def paired_layout(mesh):
+    rows, cols, dps = mesh.shape["row"], mesh.shape["col"], mesh.shape["dp"]
+    return cols == 2 and dps == 4 and H % (2 * cols) == 0 and TOK_DEV * rows * cols <= SEQ_MAX
+
+
+def swap_cols(operand):
+    return lax.ppermute(operand, "col", [(0, 1), (1, 0)])
+
+
+def swap_pair(operand):
+    return lax.ppermute(operand, "dp", [(i, i ^ 1) for i in range(lax.axis_size("dp"))])
+
+
+def swap_copies(operand):
+    return lax.ppermute(operand, "dp", [(i, i ^ 2) for i in range(lax.axis_size("dp"))])
+
+
+def shift_rows(operand, step):
+    count = lax.axis_size("row")
+    pairs = [(i, i + step) for i in range(count) if 0 <= i + step < count]
+    return lax.ppermute(operand, "row", pairs)
+
+
+def rotate_rows(operand, step):
+    count = lax.axis_size("row")
+    return lax.ppermute(operand, "row", [(i, (i + step) % count) for i in range(count)])
+
+
+def by_col(own, other):
+    first_col = lax.axis_index("col") == 0
+    return (jnp.where(first_col, own, other), jnp.where(first_col, other, own))
+
+
+def col_part(operand, axis, other=False):
+    part = operand.shape[axis] // 2
+    place = lax.axis_index("col")
+    place = 1 - place if other else place
+    return lax.dynamic_slice_in_dim(operand, place * part, part, axis)
+
+
+def spread_tokens(block):
+    rows = lax.axis_size("row")
+    own = col_part(block, 0)
+    other = swap_cols(col_part(block, 0, True))
+    wide = jnp.concatenate(by_col(own, other), 1)
+    some = lax.all_to_all(wide, "row", split_axis=1, concat_axis=0, tiled=True)
+    part = own.shape[0]
+    count = some.shape[1]
+    rest = swap_cols(some)
+    pair = by_col(some.reshape(rows, 1, part, count), rest.reshape(rows, 1, part, count))
+    return jnp.concatenate(pair, 1).reshape(rows * 2 * part, count)
+
+
+def gather_tokens(some):
+    wide = lax.all_to_all(some, "row", split_axis=0, concat_axis=1, tiled=True)
+    own = col_part(wide, 1)
+    other = swap_cols(col_part(wide, 1, True))
+    return jnp.concatenate(by_col(own, other), 0)
+
+
+def half_features(full):
+    rows = lax.axis_size("row")
+    feats, count = full.shape
+    cut = full.reshape(rows, 2, feats // rows // 2, count)
+    first_col = lax.axis_index("col") == 0
+    own = jnp.where(first_col, cut[:, 0], cut[:, 1]).reshape(feats // 2, count)
+    other = jnp.where(first_col, cut[:, 1], cut[:, 0]).reshape(feats // 2, count)
+    return own, other
+
+
+def with_pair(own):
+    return jnp.concatenate([own, swap_pair(own)], 1)
+
+
+def pair_sum(partial_sum):
+    count = partial_sum.shape[1] // 2
+    return partial_sum[:, :count] + swap_pair(
+        partial_sum[:, count:].astype(jnp.bfloat16)
+    ).astype(jnp.float32)
+
+
+def full_sum(partial_sum):
+    half = pair_sum(partial_sum)
+    return half + swap_cols(half.astype(jnp.bfloat16)).astype(jnp.float32)
+
+
+def dot_tn(left, right):
+    return lax.dot_general(
+        left, right, (((0,), (0,)), ((), ())), preferred_element_type=jnp.float32
+    )
+
+
+def dot_nt(left, right):
+    return lax.dot_general(
+        left, right, (((1,), (1,)), ((), ())), preferred_element_type=jnp.float32
+    )
+
+
+def dot_nn(left, right):
+    return jnp.dot(left, right, preferred_element_type=jnp.float32)
+
+
+def norm_columns(hidden, scale_vec, shift_vec):
+    mean = jnp.mean(hidden, 0, keepdims=True)
+    centered = hidden - mean
+    variance = jnp.mean(centered * centered, 0, keepdims=True)
+    inv_std = lax.rsqrt(variance + norm_eps)
+    normed = centered * inv_std
+    return (normed * scale_vec[:, None] + shift_vec[:, None], normed, inv_std)
+
+
+def norm_columns_back(grad_in, normed, inv_std, scale_vec):
+    grad_normed = grad_in * scale_vec[:, None]
+    mean_one = jnp.mean(grad_normed, 0, keepdims=True)
+    mean_two = jnp.mean(grad_normed * normed, 0, keepdims=True)
+    grad_hidden = inv_std * (grad_normed - mean_one - normed * mean_two)
+    return grad_hidden
+
+
+def batch_dot(spec, left, right):
+    return jnp.einsum(spec, left, right, preferred_element_type=jnp.float32)
+
+
+def reduce_copies(own):
+    total = own.astype(jnp.float32) + swap_copies(own).astype(jnp.float32)
+    low = total.astype(jnp.bfloat16)
+    return low, swap_pair(low)
+
+
+def in_pair_order(own, other, axis):
+    first = lax.axis_index("dp") % 2 == 0
+    return jnp.concatenate([jnp.where(first, own, other), jnp.where(first, other, own)], axis)
+
+
+def on_device_paired(
+    tokens,
+    lengths,
+    w_query,
+    w_key,
+    w_value,
+    w_out,
+    gain_one,
+    bias_one,
+    w_up,
+    w_down,
+    gain_two,
+    bias_two,
+    cotangent,
+):
+    rows = lax.axis_size("row")
+    low = jnp.bfloat16
+    seq_len = TOK_DEV * rows * 2
+    span = TOK_DEV * 2
+    heads = H // 4
+    sets = 2 * heads
+    row_idx = lax.axis_index("row")
+    dp_idx = lax.axis_index("dp")
+    core = dp_idx % 2
+    feat_rows = tokens.shape[0]
+
+    positions = row_idx * span + jnp.arange(span, dtype=jnp.int32)
+    seq_pair = jnp.stack([dp_idx, dp_idx + 1 - 2 * core])
+    present = (positions[None, :] < seq_lengths(lengths, seq_pair)[:, None]).astype(jnp.float32)
+    angles = math.pi * positions.astype(jnp.float32) / (2.0 * seq_len)
+    cos = jnp.cos(angles)
+    sin = jnp.sin(angles)
+
+    def core_part(operand, axis):
+        part = operand.shape[axis] // 2
+        return lax.dynamic_slice_in_dim(operand, core * part, part, axis)
+
+    first_block = jnp.concatenate(
+        [core_part(w_query, 1), core_part(w_key, 1), core_part(w_value, 1), core_part(w_out, 0).T],
+        1,
+    )
+    width = H * HD // 4
+    first_all = gather_rows(first_block)
+    w_qkv = first_all[:, : 3 * width]
+    w_out_t = first_all[:, 3 * width :]
+    up_all = gather_rows(core_part(w_up, 1))
+    down_t = gather_rows(core_part(w_down, 0).T)
+    norm_vecs = jnp.stack([gain_one, bias_one, gain_two, bias_two], 0)
+    vec_parts = [norm_vecs] + [rotate_rows(norm_vecs, step) for step in range(1, rows)]
+    vec_stack = jnp.stack(vec_parts, 0)
+    order = (row_idx - jnp.arange(rows)) % rows
+    vecs = vec_stack[order].transpose(1, 0, 2).reshape(4, D)
+    gain_1, bias_1, gain_2, bias_2 = (vecs[i] for i in range(4))
+
+    x_own = spread_tokens(tokens)
+    x_pair = with_pair(x_own)
+    qkv = dot_tn(w_qkv, x_pair).astype(low)
+
+    def by_set(flat):
+        parts = flat.reshape(heads, HD, 2, span)
+        return parts.transpose(2, 0, 1, 3).reshape(sets, HD, span)
+
+    def from_set(parts):
+        return parts.reshape(2, heads, HD, span).transpose(1, 2, 0, 3).reshape(width, 2 * span)
+
+    q = by_set(qkv[:width])
+    k = by_set(qkv[width : 2 * width])
+    v = by_set(qkv[2 * width :])
+    present_set = jnp.repeat(present, heads, 0)[:, None, :]
+    q_pos = jnp.maximum(q, 0)
+    k_pos = jnp.maximum(k, 0) * present_set.astype(low)
+    turn = jnp.stack([cos, sin], 0)[None, :, None, :]
+
+    def turned(parts):
+        wide = parts.astype(jnp.float32)[:, None] * turn
+        return wide.astype(low).reshape(sets, 2 * HD, span)
+
+    q_turn = turned(q_pos)
+    k_turn = turned(k_pos)
+    ones = jnp.ones((sets, 1, span), low)
+    zeros = jnp.zeros((sets, 15, span), low)
+    v_ext = jnp.concatenate([v, ones, zeros], 1)
+    state = batch_dot("bej,bdj->bed", v_ext, k_turn)
+    state_low = state.astype(low)
+    arrived = [shift_rows(state_low, step).astype(jnp.float32) for step in range(1, rows)]
+    prior = sum(arrived[1:], arrived[0])
+    prior_low = prior.astype(low)
+
+    ids = jnp.arange(span, dtype=jnp.int32)
+    causal = (ids[:, None] <= ids[None, :]).astype(jnp.float32)
+    reweight = (cos[:, None] * cos[None, :] + sin[:, None] * sin[None, :]) * causal
+    scores = batch_dot("bdj,bdi->bji", k_pos, q_pos)
+    weights = scores * reweight[None]
+    weights_low = weights.astype(low)
+    numer = batch_dot("bej,bji->bei", v, weights_low) + batch_dot(
+        "bed,bdi->bei", prior_low[:, :HD], q_turn
+    )
+    denom = (
+        1.0
+        + jnp.sum(weights, 1, keepdims=True)
+        + batch_dot("bed,bdi->bei", prior_low[:, HD : HD + 1], q_turn)
+    )
+    attn_set = (numer / denom).astype(low)
+    attn = from_set(attn_set)
+
+    branch = full_sum(dot_nn(w_out_t, attn))
+    first, normed_one, inv_one = norm_columns(x_own.astype(jnp.float32) + branch, gain_1, bias_1)
+    first_pair = with_pair(first.astype(low))
+    pre = dot_tn(up_all, first_pair)
+    act, gelu_pull = jax.vjp(partial(jax.nn.gelu, approximate=False), pre)
+    act_low = act.astype(low)
+    ffn = full_sum(dot_nn(down_t, act_low))
+    result, normed_two, inv_two = norm_columns(first + ffn, gain_2, bias_2)
+
+    cot = spread_tokens(cotangent)
+    grad_result = cot.astype(jnp.float32) * present[0][None, :]
+    grad_second = norm_columns_back(grad_result, normed_two, inv_two, gain_2)
+    grad_ffn = with_pair(grad_second.astype(low))
+    grad_down_t = dot_nt(grad_ffn, act_low).astype(low)
+    grad_act = dot_tn(down_t, grad_ffn)
+    grad_pre = gelu_pull(grad_act)[0].astype(low)
+    grad_up = dot_nt(first_pair, grad_pre).astype(low)
+    grad_first = full_sum(dot_nn(up_all, grad_pre)) + grad_second
+    grad_hidden = norm_columns_back(grad_first, normed_one, inv_one, gain_1)
+    grad_branch = with_pair(grad_hidden.astype(low))
+    grad_out_t = dot_nt(grad_branch, attn).astype(low)
+    grad_attn = by_set(dot_tn(w_out_t, grad_branch).astype(low)).astype(jnp.float32)
+
+    grad_num = (grad_attn / denom).astype(low)
+    grad_den = -jnp.sum(grad_attn * numer, 1, keepdims=True) / (denom * denom)
+    grad_ext = jnp.concatenate([grad_num, grad_den.astype(low), zeros], 1)
+    grad_state = batch_dot("bei,bdi->bed", grad_ext, q_turn)
+    grad_state_low = grad_state.astype(low)
+    later = [shift_rows(grad_state_low, -step).astype(jnp.float32) for step in range(1, rows)]
+    after = sum(later[1:], later[0])
+    after_low = after.astype(low)
+
+    grad_scores = (
+        (batch_dot("bej,bei->bji", v, grad_num) + grad_den) * reweight[None]
+    ).astype(low)
+
+    def unturned(parts):
+        wide = parts.reshape(sets, 2, HD, span)
+        return jnp.sum(wide * turn, 1)
+
+    grad_qp = batch_dot("bdj,bji->bdi", k_pos, grad_scores) + unturned(
+        batch_dot("bed,bei->bdi", prior_low, grad_ext)
+    )
+    grad_kp = batch_dot("bdi,bji->bdj", q_pos, grad_scores) + unturned(
+        batch_dot("bed,bej->bdj", after_low, v_ext)
+    )
+    grad_v = batch_dot("bei,bji->bej", grad_num, weights_low) + batch_dot(
+        "bed,bdj->bej", after_low[:, :HD], k_turn
+    )
+    grad_q = (grad_qp * (q > 0).astype(jnp.float32)).astype(low)
+    grad_k = (grad_kp * (k > 0).astype(jnp.float32) * present_set).astype(low)
+    grad_qkv = jnp.concatenate(
+        [from_set(grad_q), from_set(grad_k), from_set(grad_v.astype(low))], 0
+    )
+    grad_w_qkv = dot_nt(x_pair, grad_qkv).astype(low)
+    grad_x = pair_sum(dot_nn(w_qkv, grad_qkv))
+    own_x, other_x = half_features(grad_x)
+    own_h, _ = half_features(grad_hidden)
+    own_x = own_x + swap_cols(other_x.astype(low)).astype(jnp.float32) + own_h
+    input_grad = gather_tokens(own_x.astype(low)).astype(jnp.float32)
+
+    out_half, _ = half_features(result.astype(low))
+    output = gather_tokens(out_half)
+
+    half_span = span // 2
+    col = lax.axis_index("col")
+    mine = (ids // half_span == col).astype(jnp.float32)[None, :]
+    vec_sums = jnp.stack(
+        [
+            jnp.sum(grad_first * normed_one * mine, 1),
+            jnp.sum(grad_first * mine, 1),
+            jnp.sum(grad_result * normed_two * mine, 1),
+            jnp.sum(grad_result * mine, 1),
+        ],
+        0,
+    )
+    vec_sums = vec_sums + swap_pair(vec_sums)
+    vec_sums = vec_sums + swap_cols(vec_sums)
+    vec_sums = vec_sums + swap_copies(vec_sums)
+    vec_rows = vec_sums.reshape(4, rows, feat_rows)
+
+    def vec_part(place):
+        return lax.dynamic_index_in_dim(vec_rows, place % rows, 1, False)
+
+    vec_total = vec_part(row_idx)
+    for step in range(1, rows):
+        vec_total = vec_total + rotate_rows(vec_part(row_idx + step), step)
+
+    def scatter_rows(partial_grad):
+        return lax.psum_scatter(partial_grad, "row", scatter_dimension=0, tiled=True)
+
+    down_own, down_other = reduce_copies(scatter_rows(grad_down_t))
+    up_own, up_other = reduce_copies(scatter_rows(grad_up))
+    last_own, last_other = reduce_copies(
+        scatter_rows(jnp.concatenate([grad_w_qkv, grad_out_t], 1))
+    )
+    down_grad = in_pair_order(down_own, down_other, 1).T.astype(jnp.float32)
+    up_grad = in_pair_order(up_own, up_other, 1).astype(jnp.float32)
+
+    def piece(index):
+        cut = slice(index * width, (index + 1) * width)
+        return in_pair_order(last_own[:, cut], last_other[:, cut], 1)
+
+    query_grad, key_grad, value_grad = (piece(i).astype(jnp.float32) for i in range(3))
+    out_grad = piece(3).T.astype(jnp.float32)
+    return (
+        output,
+        input_grad,
+        query_grad,
+        key_grad,
+        value_grad,
+        out_grad,
+        vec_total[0],
+        vec_total[1],
+        up_grad,
+        down_grad,
+        vec_total[2],
+        vec_total[3],
+    )
+
+
 def solution(mesh):
     placed = (
         P("row", ("dp", "col")),
@@ -437,7 +797,7 @@
         P("row", ("dp", "col")),
     )
     return jax.shard_map(
-        on_device,
+        on_device_paired if paired_layout(mesh) else on_device,
         mesh=mesh,
         in_specs=placed,
         out_specs=(

time: 1180 us -> 304 us (0.26)
  waiting for transfers between devices: 578 us -> 110 us
  blocking collectives: 428 us -> 0 us
  starting transfers between devices: 8.58 us -> 73 us
  other arithmetic: 60.8 us -> 31.1 us
  matrix products: 48.3 us -> 31.4 us
    reduce_scatter x8 -> x2, waiting for transfers between devices: 348 us -> 0.02 us  [scatter_rows(): lax.psum_scatter(partial_grad, 'row', scatter_dimension=0, tiled=True)]
    all_gather x13 -> x0, blocking collectives: 332 us -> none  [the longest x8 273 us: carried_in(): lax.all_gather(a.astype(kind), axis)]
    all_gather x3, waiting for transfers between devices: 171 us -> 10.5 us  [gather_rows(): return lax.all_gather(operand, 'row', axis=0, tiled=True)]
    ppermute x0 -> x39, waiting for transfers between devices: none -> 69.7 us  [the longest x11 27.3 us: swap_cols(): return lax.ppermute(operand, 'col', [(0, 1), (1, 0)])]
    psum x6 -> x0, blocking collectives: 55.6 us -> none  [the longest x4 44.9 us: row_totals(): return lax.psum((first_part, second_part), 'row')]
    ppermute x0 -> x39, starting transfers between devices: none -> 55.1 us  [the longest x6 22.3 us: rotate_rows(): lax.ppermute(operand, 'row', [(i, (i + step) % count) for i in range(coun...]
    psum x1 -> x0, waiting for transfers between devices: 45.1 us -> none  [on_device(): lax.psum(grad_query.astype(jnp.bfloat16), 'dp').astype(jnp.float32)]
    unnamed x1 -> x0, blocking collectives: 22.9 us -> none
  transfers between devices with their start and end apart: 14 -> 49, of which waited for: 13 -> 29; matrix products, arithmetic and copies ran while one was open for 2% -> 27% of each run, Pallas kernels for 0% -> 0%
where the time goes in v1:
time: 304 us; the launch traced here: 302 us
  waiting for transfers between devices  110 us (36%)
  starting transfers between devices  73 us (24%)
  local copies, waits for them, and re-layouts  40.9 us (13%)
  matrix products  31.4 us (10%)
  other arithmetic  31.1 us (10%)
  between operations  15.8 us (5%)
    ppermute x11, waiting for transfers between devices, swap_cols(): return lax.ppermute(operand, 'col', [(0, 1), (1, 0)])  27.3 us
    ppermute x6, starting transfers between devices, rotate_rows(): lax.ppermute(operand, 'row', [(i, (i + step) % count) for i in range(coun...  22.3 us
    ppermute x6, waiting for transfers between devices, shift_rows(): return lax.ppermute(operand, 'row', pairs)  18.1 us
    all_to_all x2, waiting for transfers between devices, spread_tokens(): some = lax.all_to_all(wide, 'row', split_axis=1, concat_axis=0, tiled=True)  17.4 us
    ppermute x4, waiting for transfers between devices, swap_copies(): lax.ppermute(operand, 'dp', [(i, i ^ 2) for i in range(lax.axis_size('dp'...  16.4 us
    ppermute x11, starting transfers between devices, swap_cols(): return lax.ppermute(operand, 'col', [(0, 1), (1, 0)])  15.1 us
    all_to_all x2, waiting for transfers between devices, gather_tokens(): wide = lax.all_to_all(some, 'row', split_axis=0, concat_axis=1, tiled=True)  12 us
    dot_general x4, matrix products, dot_tn(): lax.dot_general(left, right, (((0,), (0,)), ((), ())), preferred_element_...  11.6 us
  transfers between devices with their start and end apart: 49, of which 29 were waited for; matrix products, arithmetic and copies ran while one was open for 27% of the time, Pallas kernels for 0%

profile of v1, /device:TPU:0, one launch (start us, length us, event | category | flops | bytes accessed | tf_op | source)
XLA Modules:
  0.0 301.9 jit_solution(5403417472015354628)
XLA Ops:
  11.5 3.0 %collective-permute-start.15 = (bf16[96,512]{1,0:T(8,128)(2,1)S(1)}, bf16[96,512]{1,0:T(8,128)(2,1)S(1)}, u32[]{:S(2)}, u32[]{:S(2)}) collective-permute-start(bf16[96,512]{1,0:T(8,128)(2,1)S(1)} %constant_dynamic-slice_fusion.5), channel_id=1, source_target_pairs={{0,1},{1,0},{2,3},{3,2},{4,5},{5,4},{6,7},{7,6},{8,9},{9,8},{10,11... | collective-permute-start | bytes 294920 | tf_op jit(solution)/shard_map/ppermute | solution.py:429
  15.4 2.4 collective-permute-done.15
  20.8 5.2 %all-to-all-start = ((bf16[96,4,256]{2,0,1:T(8,128)(2,1)}), bf16[96,4,256]{2,0,1:T(8,128)(2,1)S(1)}, u32[]{:S(2)}, u32[]{:S(2)}) async-start(bf16[96,4,256]{2,0,1:T(8,128)(2,1)} %bitcast.208), calls=%async_computation | async-start | bytes 393216 | tf_op jit(solution)/shard_map/all_to_all | solution.py:468
  26.4 12.4 %all-to-all-done = bf16[96,4,256]{2,0,1:T(8,128)(2,1)S(1)} async-done(((bf16[96,4,256]{2,0,1:T(8,128)(2,1)}), bf16[96,4,256]{2,0,1:T(8,128)(2,1)S(1)}, u32[]{:S(2)}, u32[]{:S(2)}) %all-to-all-start) | async-done | bytes 196640 | tf_op jit(solution)/shard_map/all_to_all | solution.py:468
  40.3 4.2 %collective-permute-done.1 = bf16[384,256]{1,0:T(8,128)(2,1)S(1)} collective-permute-done((bf16[384,256]{1,0:T(8,128)(2,1)S(1)}, bf16[384,256]{1,0:T(8,128)(2,1)S(1)}, u32[]{:S(2)}, u32[]{:S(2)}) %collective-permute-start.1) | collective-permute-done | bytes 196640 | tf_op jit(solution)/shard_map/ppermute | solution.py:429
  46.4 2.7 all-gather.4.cloned.1.call-done
  52.8 2.9 collective-permute-start.5
  57.1 2.5 collective-permute-start.3
  60.7 5.3 %collective-permute-done.4 = bf16[6,80,128]{2,1,0:T(8,128)(2,1)S(1)} collective-permute-done((bf16[6,80,128]{2,1,0:T(8,128)(2,1)S(1)}, bf16[6,80,128]{2,1,0:T(8,128)(2,1)S(1)}, u32[]{:S(2)}, u32[]{:S(2)}) %collective-permute-start.4) | collective-permute-done | bytes 122912 | tf_op jit(solution)/shard_map/ppermute | solution.py:443
  65.9 4.4 %collective-permute-done.3 = bf16[6,80,128]{2,1,0:T(8,128)(2,1)S(1)} collective-permute-done((bf16[6,80,128]{2,1,0:T(8,128)(2,1)S(1)}, bf16[6,80,128]{2,1,0:T(8,128)(2,1)S(1)}, u32[]{:S(2)}, u32[]{:S(2)}) %collective-permute-start.3) | collective-permute-done | bytes 122912 | tf_op jit(solution)/shard_map/ppermute | solution.py:443
  74.1 12.7 %collective-permute-start.9 = (f32[4,192]{1,0:T(4,128)}, f32[4,192]{1,0:T(4,128)}, u32[]{:S(2)}, u32[]{:S(2)}) collective-permute-start(f32[4,192]{1,0:T(4,128)} %get-tuple-element.142), channel_id=1, source_target_pairs={{0,4},{2,6},{4,0},{6,2},{1,5},{3,7},{5,1},{7,3},{8,12},{10,14},{12... | collective-permute-start | bytes 9224 | tf_op jit(solution)/shard_map/ppermute | solution.py:448
  86.8 3.8 %collective-permute-start.10 = (f32[4,192]{1,0:T(4,128)}, f32[4,192]{1,0:T(4,128)}, u32[]{:S(2)}, u32[]{:S(2)}) collective-permute-start(f32[4,192]{1,0:T(4,128)} %get-tuple-element.142), channel_id=1, source_target_pairs={{0,6},{2,0},{4,2},{6,4},{1,7},{3,1},{5,3},{7,5},{8,14},{10,8},{12,... | collective-permute-start | bytes 9224 | tf_op jit(solution)/shard_map/ppermute | solution.py:448
  98.9 3.4 %collective-permute-done.7 = bf16[768,256]{1,0:T(8,128)(2,1)} collective-permute-done((bf16[768,256]{1,0:T(8,128)(2,1)S(1)}, bf16[768,256]{1,0:T(8,128)(2,1)}, u32[]{:S(2)}, u32[]{:S(2)}) %collective-permute-start.7) | collective-permute-done | bytes 393248 | tf_op jit(solution)/shard_map/ppermute | solution.py:429
  106.1 6.7 %multiply_convert_fusion.1 = (bf16[768,512]{1,0:T(8,128)(2,1)}, f32[768,512]{1,0:T(8,128)}, f32[768,512]{1,0:T(8,128)}) fusion(bf16[768,768]{1,0:T(8,128)(2,1)} %all-gather.8.cloned.1.call-done, bf16[768,256]{1,0:T(8,128)(2,1)S(1)} %collective-permute-done.11, bf16[768,256]{1,0:T(8,128)(2,1)S(1)} %fusion.19), kind=kOutput, calls=%fused_computation.5 | convolution fusion | flops 631111680 | bytes 5898240 | tf_op jit(solution)/shard_map/dot_general | solution.py:510
  112.8 7.8 %all-gather.6.cloned.1.call-done = bf16[768,768]{1,0:T(8,128)(2,1)} async-done(((bf16[192,768]{1,0:T(8,128)(2,1)}), bf16[768,768]{1,0:T(8,128)(2,1)}) %all-gather.6.cloned.1.call-update) | async-done | bytes 1179664 | tf_op jit(solution)/shard_map/all_gather | solution.py:50
  120.6 2.3 fusion.82
  124.5 4.0 %all-to-all-start.2 = ((bf16[96,4,256]{2,0,1:T(8,128)(2,1)}), bf16[96,4,256]{2,0,1:T(8,128)(2,1)}, u32[]{:S(2)}, u32[]{:S(2)}) async-start(bf16[96,4,256]{2,0,1:T(8,128)(2,1)} %bitcast.237), calls=%async_computation.2 | async-start | bytes 393216 | tf_op jit(solution)/shard_map/all_to_all | solution.py:468
  132.0 5.0 %all-to-all-done.2 = bf16[96,4,256]{2,0,1:T(8,128)(2,1)} async-done(((bf16[96,4,256]{2,0,1:T(8,128)(2,1)}), bf16[96,4,256]{2,0,1:T(8,128)(2,1)}, u32[]{:S(2)}, u32[]{:S(2)}) %all-to-all-start.2) | async-done | bytes 196640 | tf_op jit(solution)/shard_map/all_to_all | solution.py:468
  140.3 4.7 %collective-permute-done.16 = bf16[384,256]{1,0:T(8,128)(2,1)S(1)} collective-permute-done((bf16[384,256]{1,0:T(8,128)(2,1)}, bf16[384,256]{1,0:T(8,128)(2,1)S(1)}, u32[]{:S(2)}, u32[]{:S(2)}) %collective-permute-start.16) | collective-permute-done | bytes 196640 | tf_op jit(solution)/shard_map/ppermute | solution.py:429
  147.0 4.4 %collective-permute-done.13 = bf16[768,256]{1,0:T(8,128)(2,1)S(1)} collective-permute-done((bf16[768,256]{1,0:T(8,128)(2,1)S(1)}, bf16[768,256]{1,0:T(8,128)(2,1)S(1)}, u32[]{:S(2)}, u32[]{:S(2)}) %collective-permute-start.13) | collective-permute-done | bytes 393248 | tf_op jit(solution)/shard_map/ppermute | solution.py:429
  160.5 3.4 %fusion.83 = f32[768,512]{1,0:T(8,128)} fusion(bf16[768,768]{1,0:T(8,128)(2,1)} %all-gather.8.cloned.1.call-done, bf16[768,512]{1,0:T(8,128)(2,1)} %copy-done.75), kind=kOutput, calls=%fused_computation.266 | convolution fusion | flops 603979776 | bytes 3538944 | tf_op jit(solution)/shard_map/dot_general | solution.py:522
  180.8 3.2 %convolution_convert_fusion = bf16[768,768]{1,0:T(8,128)(2,1)} fusion(bf16[768,512]{1,0:T(8,128)(2,1)} %get-tuple-element.93, bf16[768,256]{1,0:T(8,128)(2,1)} %copy-done.69, bf16[768,256]{1,0:T(8,128)(2,1)} %copy-done.30), kind=kOutput, calls=%fused_computation.19 | convolution fusion | flops 606142464 | bytes 2752512 | tf_op jit(solution)/shard_map/dot_general | solution.py:516
  184.1 2.9 multiply_reduce_fusion.3
  189.5 4.0 %all-to-all-start.1 = ((bf16[4,96,256]{2,1,0:T(8,128)(2,1)}), bf16[4,96,256]{2,1,0:T(8,128)(2,1)}, u32[]{:S(2)}, u32[]{:S(2)}) async-start(bf16[4,96,256]{2,1,0:T(8,128)(2,1)} %fusion.35), calls=%async_computation.1 | async-start | bytes 393216 | tf_op jit(solution)/shard_map/all_to_all | solution.py:477
  200.1 2.4 collective-permute-start.33
  220.6 3.6 %collective-permute-done.23 = bf16[6,80,128]{2,1,0:T(8,128)(2,1)S(1)} collective-permute-done((bf16[6,80,128]{2,1,0:T(8,128)(2,1)S(1)}, bf16[6,80,128]{2,1,0:T(8,128)(2,1)S(1)}, u32[]{:S(2)}, u32[]{:S(2)}) %collective-permute-start.23) | collective-permute-done | bytes 122912 | tf_op jit(solution)/shard_map/ppermute | solution.py:443
  224.2 4.4 %collective-permute-done.22 = bf16[6,80,128]{2,1,0:T(8,128)(2,1)S(1)} collective-permute-done((bf16[6,80,128]{2,1,0:T(8,128)(2,1)S(1)}, bf16[6,80,128]{2,1,0:T(8,128)(2,1)S(1)}, u32[]{:S(2)}, u32[]{:S(2)}) %collective-permute-start.22) | collective-permute-done | bytes 122912 | tf_op jit(solution)/shard_map/ppermute | solution.py:443
  237.2 5.5 %collective-permute-done.25 = bf16[384,256]{1,0:T(8,128)(2,1)S(1)} collective-permute-done((bf16[384,256]{1,0:T(8,128)(2,1)S(1)}, bf16[384,256]{1,0:T(8,128)(2,1)S(1)}, u32[]{:S(2)}, u32[]{:S(2)}) %collective-permute-start.25) | collective-permute-done | bytes 196640 | tf_op jit(solution)/shard_map/ppermute | solution.py:429
  243.5 4.3 %all-to-all-start.3 = ((bf16[4,96,256]{2,1,0:T(8,128)(2,1)}), bf16[4,96,256]{2,1,0:T(8,128)(2,1)S(1)}, u32[]{:S(2)}, u32[]{:S(2)}) async-start(bf16[4,96,256]{2,1,0:T(8,128)(2,1)} %bitcast.65), calls=%async_computation.3 | async-start | bytes 393216 | tf_op jit(solution)/shard_map/all_to_all | solution.py:477
  249.3 12.0 %all-to-all-done.3 = bf16[4,96,256]{2,1,0:T(8,128)(2,1)S(1)} async-done(((bf16[4,96,256]{2,1,0:T(8,128)(2,1)}), bf16[4,96,256]{2,1,0:T(8,128)(2,1)S(1)}, u32[]{:S(2)}, u32[]{:S(2)}) %all-to-all-start.3) | async-done | bytes 196640 | tf_op jit(solution)/shard_map/all_to_all | solution.py:477
  267.7 5.4 %collective-permute-done.35 = bf16[192,768]{1,0:T(8,128)(2,1)S(1)} collective-permute-done((bf16[192,768]{1,0:T(8,128)(2,1)}, bf16[192,768]{1,0:T(8,128)(2,1)S(1)}, u32[]{:S(2)}, u32[]{:S(2)}) %collective-permute-start.35) | collective-permute-done | bytes 294944 | tf_op jit(solution)/shard_map/ppermute | solution.py:437
  280.7 8.8 %collective-permute-done.27 = bf16[192,768]{0,1:T(8,128)(2,1)S(1)} collective-permute-done((bf16[192,768]{0,1:T(8,128)(2,1)S(1)}, bf16[192,768]{0,1:T(8,128)(2,1)S(1)}, u32[]{:S(2)}, u32[]{:S(2)}) %collective-permute-start.27) | collective-permute-done | bytes 294944 | tf_op jit(solution)/shard_map/ppermute | solution.py:437
  (406 shorter events, 126.3 us)
Async XLA Ops:
  7.2 41.9 %all-gather.4.cloned.1.call-start = ((), (), s32[]{:S(2)}) async-start(), calls=%async_computation.7 | async-start | bytes 1474560 | tf_op jit(solution)/shard_map/all_gather | solution.py:50
  11.4 93.0 %all-gather.8.cloned.1.call-start = ((), (), s32[]{:S(2)}) async-start(), calls=%async_computation.9 | async-start | bytes 1474560 | tf_op jit(solution)/shard_map/all_gather | solution.py:50
  20.8 18.0 %all-to-all-start = ((bf16[96,4,256]{2,0,1:T(8,128)(2,1)}), bf16[96,4,256]{2,0,1:T(8,128)(2,1)S(1)}, u32[]{:S(2)}, u32[]{:S(2)}) async-start(bf16[96,4,256]{2,0,1:T(8,128)(2,1)} %bitcast.208), calls=%async_computation | async-start | bytes 393216 | tf_op jit(solution)/shard_map/all_to_all | solution.py:468
  26.1 94.5 %all-gather.6.cloned.1.call-start = ((), (), s32[]{:S(2)}) async-start(), calls=%async_computation.8 | async-start | bytes 1474560 | tf_op jit(solution)/shard_map/all_gather | solution.py:50
  52.8 7.8 %collective-permute-start.5 = (bf16[6,80,128]{2,1,0:T(8,128)(2,1)S(1)}, bf16[6,80,128]{2,1,0:T(8,128)(2,1)S(1)}, u32[]{:S(2)}, u32[]{:S(2)}) collective-permute-start(bf16[6,80,128]{2,1,0:T(8,128)(2,1)S(1)} %convolution_convert_fusion.7), channel_id=1, source_target_pairs={{0,6},{1,7},{8,14},{9,15},{16,22},{17,23},{24,30},{25,31}} | collective-permute-start | bytes 368648 | tf_op jit(solution)/shard_map/ppermute | solution.py:443
  55.8 10.2 %collective-permute-start.4 = (bf16[6,80,128]{2,1,0:T(8,128)(2,1)S(1)}, bf16[6,80,128]{2,1,0:T(8,128)(2,1)S(1)}, u32[]{:S(2)}, u32[]{:S(2)}) collective-permute-start(bf16[6,80,128]{2,1,0:T(8,128)(2,1)S(1)} %convolution_convert_fusion.7), channel_id=1, source_target_pairs={{0,4},{2,6},{1,5},{3,7},{8,12},{10,14},{9,13},{11,15},{16,20},{18,... | collective-permute-start | bytes 368648 | tf_op jit(solution)/shard_map/ppermute | solution.py:443
  57.1 13.2 %collective-permute-start.3 = (bf16[6,80,128]{2,1,0:T(8,128)(2,1)S(1)}, bf16[6,80,128]{2,1,0:T(8,128)(2,1)S(1)}, u32[]{:S(2)}, u32[]{:S(2)}) collective-permute-start(bf16[6,80,128]{2,1,0:T(8,128)(2,1)S(1)} %convolution_convert_fusion.7), channel_id=1, source_target_pairs={{0,2},{2,4},{4,6},{1,3},{3,5},{5,7},{8,10},{10,12},{12,14},{9,11},... | collective-permute-start | bytes 368648 | tf_op jit(solution)/shard_map/ppermute | solution.py:443
  73.4 18.0 %collective-permute-start.6 = (bf16[768,256]{1,0:T(8,128)(2,1)S(1)}, bf16[768,256]{1,0:T(8,128)(2,1)S(1)}, u32[]{:S(2)}, u32[]{:S(2)}) collective-permute-start(bf16[768,256]{1,0:T(8,128)(2,1)S(1)} %slice.278), channel_id=1, source_target_pairs={{0,8},{8,0},{16,24},{24,16},{1,9},{9,1},{17,25},{25,17},{2,10},{10... | collective-permute-start | bytes 1179656 | tf_op jit(solution)/shard_map/ppermute | solution.py:433
  74.1 19.2 %collective-permute-start.9 = (f32[4,192]{1,0:T(4,128)}, f32[4,192]{1,0:T(4,128)}, u32[]{:S(2)}, u32[]{:S(2)}) collective-permute-start(f32[4,192]{1,0:T(4,128)} %get-tuple-element.142), channel_id=1, source_target_pairs={{0,4},{2,6},{4,0},{6,2},{1,5},{3,7},{5,1},{7,3},{8,12},{10,14},{12... | collective-permute-start | bytes 9224 | tf_op jit(solution)/shard_map/ppermute | solution.py:448
  86.8 6.6 %collective-permute-start.10 = (f32[4,192]{1,0:T(4,128)}, f32[4,192]{1,0:T(4,128)}, u32[]{:S(2)}, u32[]{:S(2)}) collective-permute-start(f32[4,192]{1,0:T(4,128)} %get-tuple-element.142), channel_id=1, source_target_pairs={{0,6},{2,0},{4,2},{6,4},{1,7},{3,1},{5,3},{7,5},{8,14},{10,8},{12,... | collective-permute-start | bytes 9224 | tf_op jit(solution)/shard_map/ppermute | solution.py:448
  91.6 10.8 %collective-permute-start.7 = (bf16[768,256]{1,0:T(8,128)(2,1)S(1)}, bf16[768,256]{1,0:T(8,128)(2,1)}, u32[]{:S(2)}, u32[]{:S(2)}) collective-permute-start(bf16[768,256]{1,0:T(8,128)(2,1)S(1)} %fusion.22), channel_id=1, source_target_pairs={{0,1},{1,0},{2,3},{3,2},{4,5},{5,4},{6,7},{7,6},{8,9},{9,8},{10,11... | collective-permute-start | bytes 1179656 | tf_op jit(solution)/shard_map/ppermute | solution.py:429
  123.8 14.8 %collective-permute-start.12 = (bf16[768,256]{1,0:T(8,128)(2,1)}, bf16[768,256]{1,0:T(8,128)(2,1)}, u32[]{:S(2)}, u32[]{:S(2)}) collective-permute-start(bf16[768,256]{1,0:T(8,128)(2,1)} %slice.277), channel_id=1, source_target_pairs={{0,8},{8,0},{16,24},{24,16},{1,9},{9,1},{17,25},{25,17},{2,10},{10... | collective-permute-start | bytes 1179656 | tf_op jit(solution)/shard_map/ppermute | solution.py:433
  124.5 12.5 %all-to-all-start.2 = ((bf16[96,4,256]{2,0,1:T(8,128)(2,1)}), bf16[96,4,256]{2,0,1:T(8,128)(2,1)}, u32[]{:S(2)}, u32[]{:S(2)}) async-start(bf16[96,4,256]{2,0,1:T(8,128)(2,1)} %bitcast.237), calls=%async_computation.2 | async-start | bytes 393216 | tf_op jit(solution)/shard_map/all_to_all | solution.py:468
  128.5 134.4 %reduce-scatter.6.cloned.1.call-start = ((), (), s32[]{:S(2)}) async-start(), calls=%async_computation.10 | async-start | bytes 1474560 | tf_op jit(solution)/shard_map/reduce_scatter | solution.py:751
  137.0 8.0 %collective-permute-start.16 = (bf16[384,256]{1,0:T(8,128)(2,1)}, bf16[384,256]{1,0:T(8,128)(2,1)S(1)}, u32[]{:S(2)}, u32[]{:S(2)}) collective-permute-start(bf16[384,256]{1,0:T(8,128)(2,1)} %bitcast.39), channel_id=1, source_target_pairs={{0,1},{1,0},{2,3},{3,2},{4,5},{5,4},{6,7},{7,6},{8,9},{9,8},{10,11... | collective-permute-start | bytes 589832 | tf_op jit(solution)/shard_map/ppermute | solution.py:429
  139.7 11.7 %collective-permute-start.13 = (bf16[768,256]{1,0:T(8,128)(2,1)S(1)}, bf16[768,256]{1,0:T(8,128)(2,1)S(1)}, u32[]{:S(2)}, u32[]{:S(2)}) collective-permute-start(bf16[768,256]{1,0:T(8,128)(2,1)S(1)} %fusion.23), channel_id=1, source_target_pairs={{0,1},{1,0},{2,3},{3,2},{4,5},{5,4},{6,7},{7,6},{8,9},{9,8},{10,11... | collective-permute-start | bytes 1179656 | tf_op jit(solution)/shard_map/ppermute | solution.py:429
  160.4 105.7 %reduce-scatter.8.cloned.1.call-start = ((), (), s32[]{:S(2)}) async-start(), calls=%async_computation.11 | async-start | bytes 1474560 | tf_op jit(solution)/shard_map/reduce_scatter | solution.py:751
  170.7 13.4 %collective-permute-start.19 = (bf16[768,256]{1,0:T(8,128)(2,1)}, bf16[768,256]{1,0:T(8,128)(2,1)}, u32[]{:S(2)}, u32[]{:S(2)}) collective-permute-start(bf16[768,256]{1,0:T(8,128)(2,1)} %fusion.24), channel_id=1, source_target_pairs={{0,1},{1,0},{2,3},{3,2},{4,5},{5,4},{6,7},{7,6},{8,9},{9,8},{10,11... | collective-permute-start | bytes 1179656 | tf_op jit(solution)/shard_map/ppermute | solution.py:429
  189.5 17.7 %all-to-all-start.1 = ((bf16[4,96,256]{2,1,0:T(8,128)(2,1)}), bf16[4,96,256]{2,1,0:T(8,128)(2,1)}, u32[]{:S(2)}, u32[]{:S(2)}) async-start(bf16[4,96,256]{2,1,0:T(8,128)(2,1)} %fusion.35), calls=%async_computation.1 | async-start | bytes 393216 | tf_op jit(solution)/shard_map/all_to_all | solution.py:477
  193.5 83.3 %reduce-scatter.10.cloned.1.call-start = ((), (), s32[]{:S(2)}) async-start(), calls=%async_computation.12 | async-start | bytes 1474560
  197.5 13.4 %collective-permute-start.20 = (bf16[768,256]{1,0:T(8,128)(2,1)}, bf16[768,256]{1,0:T(8,128)(2,1)S(1)}, u32[]{:S(2)}, u32[]{:S(2)}) collective-permute-start(bf16[768,256]{1,0:T(8,128)(2,1)} %get-tuple-element.88), channel_id=1, source_target_pairs={{0,8},{8,0},{16,24},{24,16},{1,9},{9,1},{17,25},{25,17},{2,10},{10... | collective-permute-start | bytes 1179656 | tf_op jit(solution)/shard_map/ppermute | solution.py:433
  198.2 6.6 %collective-permute-start.32 = (f32[4,192]{1,0:T(4,128)S(1)}, f32[4,192]{1,0:T(4,128)S(1)}, u32[]{:S(2)}, u32[]{:S(2)}) collective-permute-start(f32[4,192]{1,0:T(4,128)S(1)} %bitcast.267), channel_id=1, source_target_pairs={{0,2},{2,4},{4,6},{6,0},{1,3},{3,5},{5,7},{7,1},{8,10},{10,12},{12... | collective-permute-start | bytes 9224 | tf_op jit(solution)/shard_map/ppermute | solution.py:448
  209.4 38.9 %collective-permute-start.14 = (bf16[96,512]{1,0:T(8,128)(2,1)}, bf16[96,512]{1,0:T(8,128)(2,1)}, u32[]{:S(2)}, u32[]{:S(2)}) collective-permute-start(bf16[96,512]{1,0:T(8,128)(2,1)} %constant_dynamic-slice_fusion.6), channel_id=1, source_target_pairs={{0,1},{1,0},{2,3},{3,2},{4,5},{5,4},{6,7},{7,6},{8,9},{9,8},{10,11... | collective-permute-start | bytes 294920 | tf_op jit(solution)/shard_map/ppermute | solution.py:429
  214.3 10.0 %collective-permute-start.23 = (bf16[6,80,128]{2,1,0:T(8,128)(2,1)S(1)}, bf16[6,80,128]{2,1,0:T(8,128)(2,1)S(1)}, u32[]{:S(2)}, u32[]{:S(2)}) collective-permute-start(bf16[6,80,128]{2,1,0:T(8,128)(2,1)S(1)} %convolution_convert_fusion.6), channel_id=1, source_target_pairs={{6,0},{7,1},{14,8},{15,9},{22,16},{23,17},{30,24},{31,25}} | collective-permute-start | bytes 368648 | tf_op jit(solution)/shard_map/ppermute | solution.py:443
  215.6 13.1 %collective-permute-start.22 = (bf16[6,80,128]{2,1,0:T(8,128)(2,1)S(1)}, bf16[6,80,128]{2,1,0:T(8,128)(2,1)S(1)}, u32[]{:S(2)}, u32[]{:S(2)}) collective-permute-start(bf16[6,80,128]{2,1,0:T(8,128)(2,1)S(1)} %convolution_convert_fusion.6), channel_id=1, source_target_pairs={{4,0},{6,2},{5,1},{7,3},{12,8},{14,10},{13,9},{15,11},{20,16},{22,... | collective-permute-start | bytes 368648 | tf_op jit(solution)/shard_map/ppermute | solution.py:443
  216.9 11.8 %collective-permute-start.21 = (bf16[6,80,128]{2,1,0:T(8,128)(2,1)S(1)}, bf16[6,80,128]{2,1,0:T(8,128)(2,1)S(1)}, u32[]{:S(2)}, u32[]{:S(2)}) collective-permute-start(bf16[6,80,128]{2,1,0:T(8,128)(2,1)S(1)} %convolution_convert_fusion.6), channel_id=1, source_target_pairs={{2,0},{4,2},{6,4},{3,1},{5,3},{7,5},{10,8},{12,10},{14,12},{11,9},... | collective-permute-start | bytes 368648 | tf_op jit(solution)/shard_map/ppermute | solution.py:443
  235.6 7.2 %collective-permute-start.25 = (bf16[384,256]{1,0:T(8,128)(2,1)S(1)}, bf16[384,256]{1,0:T(8,128)(2,1)S(1)}, u32[]{:S(2)}, u32[]{:S(2)}) collective-permute-start(bf16[384,256]{1,0:T(8,128)(2,1)S(1)} %bitcast.259), channel_id=1, source_target_pairs={{0,1},{1,0},{2,3},{3,2},{4,5},{5,4},{6,7},{7,6},{8,9},{9,8},{10,11... | collective-permute-start | bytes 589832 | tf_op jit(solution)/shard_map/ppermute | solution.py:429
  243.5 17.8 %all-to-all-start.3 = ((bf16[4,96,256]{2,1,0:T(8,128)(2,1)}), bf16[4,96,256]{2,1,0:T(8,128)(2,1)S(1)}, u32[]{:S(2)}, u32[]{:S(2)}) async-start(bf16[4,96,256]{2,1,0:T(8,128)(2,1)} %bitcast.65), calls=%async_computation.3 | async-start | bytes 393216 | tf_op jit(solution)/shard_map/all_to_all | solution.py:477
  262.9 10.2 %collective-permute-start.35 = (bf16[192,768]{1,0:T(8,128)(2,1)}, bf16[192,768]{1,0:T(8,128)(2,1)S(1)}, u32[]{:S(2)}, u32[]{:S(2)}) collective-permute-start(bf16[192,768]{1,0:T(8,128)(2,1)} %reduce-scatter.6.cloned.1.call-done), channel_id=1, source_target_pairs={{0,16},{8,24},{16,0},{24,8},{1,17},{9,25},{17,1},{25,9},{2,18},{10... | collective-permute-start | bytes 884744 | tf_op jit(solution)/shard_map/ppermute | solution.py:437
  266.1 10.5 %collective-permute-start.37 = (bf16[192,768]{1,0:T(8,128)(2,1)}, bf16[192,768]{1,0:T(8,128)(2,1)S(1)}, u32[]{:S(2)}, u32[]{:S(2)}) collective-permute-start(bf16[192,768]{1,0:T(8,128)(2,1)} %reduce-scatter.8.cloned.1.call-done), channel_id=1, source_target_pairs={{0,16},{8,24},{16,0},{24,8},{1,17},{9,25},{17,1},{25,9},{2,18},{10... | collective-permute-start | bytes 884744 | tf_op jit(solution)/shard_map/ppermute | solution.py:437
  276.7 13.0 %collective-permute-start.38 = (bf16[192,768]{1,0:T(8,128)(2,1)S(1)}, bf16[192,768]{1,0:T(8,128)(2,1)S(1)}, u32[]{:S(2)}, u32[]{:S(2)}) collective-permute-start(bf16[192,768]{1,0:T(8,128)(2,1)S(1)} %add_convert_fusion.3), channel_id=1, source_target_pairs={{0,8},{8,0},{16,24},{24,16},{1,9},{9,1},{17,25},{25,17},{2,10},{10... | collective-permute-start | bytes 884744 | tf_op jit(solution)/shard_map/ppermute | solution.py:433
  278.0 11.6 %collective-permute-start.27 = (bf16[192,768]{0,1:T(8,128)(2,1)S(1)}, bf16[192,768]{0,1:T(8,128)(2,1)S(1)}, u32[]{:S(2)}, u32[]{:S(2)}) collective-permute-start(bf16[192,768]{0,1:T(8,128)(2,1)S(1)} %copy.126), channel_id=1, source_target_pairs={{0,16},{8,24},{16,0},{24,8},{1,17},{9,25},{17,1},{25,9},{2,18},{10... | collective-permute-start | bytes 884744 | tf_op jit(solution)/shard_map/ppermute | solution.py:437
  (95 other events, 513.2 us)
Sparse Core Ops, SparseCore 0:
  11.5 37.5 all-gather.3
  51.3 31.6 all-gather.7
  91.5 29.0 all-gather.5
  160.5 29.1 reduce-scatter.5
  191.9 29.0 reduce-scatter.7
  235.5 32.8 reduce-scatter.9

commit v2 on v0

--- a/solution.py
+++ b/solution.py
@@ -4,6 +4,8 @@
 import jax
 import jax.numpy as jnp
 from jax import lax
+from jax.experimental import pallas as pl
+from jax.experimental.pallas import tpu as pltpu
 from jax.sharding import PartitionSpec as P
 
 D = 768
@@ -420,6 +422,856 @@
     )
 
 
+def paired_layout(mesh):
+    rows, cols, dps = mesh.shape["row"], mesh.shape["col"], mesh.shape["dp"]
+    return cols == 2 and dps == 4 and H % (2 * cols) == 0 and TOK_DEV * rows * cols <= SEQ_MAX
+
+
+low = jnp.bfloat16
+wide = jnp.float32
+SPAN = 2 * TOK_DEV
+HEADS = H // 4
+WIDTH = HEADS * HD
+STATE_ROWS = 2 * HEADS * HD
+SUM_ROWS = 16
+SUM_LANES = 64
+
+
+def swap_cols(operand):
+    return lax.ppermute(operand, "col", [(0, 1), (1, 0)])
+
+
+def swap_pair(operand):
+    return lax.ppermute(operand, "dp", [(i, i ^ 1) for i in range(lax.axis_size("dp"))])
+
+
+def swap_copies(operand):
+    return lax.ppermute(operand, "dp", [(i, i ^ 2) for i in range(lax.axis_size("dp"))])
+
+
+def shift_rows(operand, step):
+    count = lax.axis_size("row")
+    pairs = [(i, i + step) for i in range(count) if 0 <= i + step < count]
+    return lax.ppermute(operand, "row", pairs)
+
+
+def rotate_rows(operand, step):
+    count = lax.axis_size("row")
+    return lax.ppermute(operand, "row", [(i, (i + step) % count) for i in range(count)])
+
+
+def by_col(own, other):
+    first_col = lax.axis_index("col") == 0
+    return (jnp.where(first_col, own, other), jnp.where(first_col, other, own))
+
+
+def col_halves(operand, axis):
+    part = operand.shape[axis] // 2
+    return by_col(
+        lax.slice_in_dim(operand, 0, part, axis=axis),
+        lax.slice_in_dim(operand, part, 2 * part, axis=axis),
+    )
+
+
+def spread_tokens(blocks, extra):
+    rows = lax.axis_size("row")
+    row_idx = lax.axis_index("row")
+    count, feats, _ = blocks.shape
+    own, other = col_halves(blocks, 1)
+    whole = jnp.concatenate(by_col(own, swap_cols(other)), 2)
+    part = feats // 2
+
+    def piece(place):
+        cut = lax.dynamic_slice_in_dim(whole, place % rows * SPAN, SPAN, 2)
+        return jnp.concatenate([cut.reshape(count * part, SPAN), extra], 0)
+
+    total = count * part + extra.shape[0]
+    buf = jnp.zeros((rows, total, SPAN), low)
+    for step in range(rows):
+        sent = piece(row_idx + step)
+        got = rotate_rows(sent, step) if step else sent
+        buf = lax.dynamic_update_slice_in_dim(buf, got[None], (row_idx - step) % rows, 0)
+    halves = [buf[:, i * part : (i + 1) * part] for i in range(count)]
+    return halves, buf[:, count * part :]
+
+
+def join_halves(half):
+    pair = by_col(half, swap_cols(half))
+    return jnp.stack(pair, 1).reshape(-1, half.shape[2])
+
+
+def gather_tokens(halves):
+    rows = lax.axis_size("row")
+    row_idx = lax.axis_index("row")
+    pieces = jnp.stack(halves, 1)
+    _, count, part, _ = pieces.shape
+    buf = jnp.zeros((count, part, rows * SPAN), low)
+    for step in range(rows):
+        sent = lax.dynamic_index_in_dim(pieces, (row_idx + step) % rows, 0, False)
+        got = rotate_rows(sent, step) if step else sent
+        buf = lax.dynamic_update_slice_in_dim(buf, got, (row_idx - step) % rows * SPAN, 2)
+    own, other = col_halves(buf, 2)
+    return jnp.concatenate(by_col(own, swap_cols(other)), 1)
+
+
+def feature_halves(full):
+    rows = lax.axis_size("row")
+    feats, count = full.shape
+    cut = full.reshape(rows, 2, feats // rows // 2, count)
+    return by_col(cut[:, 0], cut[:, 1])
+
+
+def column_parts(own_part, other_part):
+    half = (own_part + swap_pair(other_part).astype(wide)).astype(low)
+    return half, swap_cols(half)
+
+
+def dot_tn(left, right):
+    return lax.dot_general(left, right, (((0,), (0,)), ((), ())), preferred_element_type=wide)
+
+
+def dot_nt(left, right):
+    return lax.dot_general(left, right, (((1,), (1,)), ((), ())), preferred_element_type=wide)
+
+
+def dot_nn(left, right):
+    return jnp.dot(left, right, preferred_element_type=wide)
+
+
+def norm_columns(hidden, scale, shift):
+    mean = jnp.mean(hidden, 0, keepdims=True)
+    centered = hidden - mean
+    variance = jnp.mean(centered * centered, 0, keepdims=True)
+    inv_std = lax.rsqrt(variance + norm_eps)
+    normed = centered * inv_std
+    return (normed * scale + shift, normed, inv_std)
+
+
+def norm_columns_back(grad_in, normed, inv_std, scale):
+    grad_normed = grad_in * scale
+    mean_one = jnp.mean(grad_normed, 0, keepdims=True)
+    mean_two = jnp.mean(grad_normed * normed, 0, keepdims=True)
+    return inv_std * (grad_normed - mean_one - normed * mean_two)
+
+
+def local_call(body, outs, name, *operands, scratch=()):
+    return pl.pallas_call(
+        body,
+        out_shape=[jax.ShapeDtypeStruct(shape, kind) for shape, kind in outs],
+        in_specs=[
+            pl.BlockSpec(memory_space=pltpu.SMEM if operand.dtype == jnp.int32 else pltpu.VMEM)
+            for operand in operands
+        ],
+        out_specs=[pl.BlockSpec(memory_space=pltpu.VMEM)] * len(outs),
+        scratch_shapes=[pltpu.VMEM(shape, kind) for shape, kind in scratch],
+        compiler_params=pltpu.CompilerParams(vmem_limit_bytes=24 * 2**20),
+        name=name,
+    )(*operands)
+
+
+def head_sets():
+    return [(seq, head, seq * HEADS + head) for seq in range(2) for head in range(HEADS)]
+
+
+def set_row(place):
+    ids = lax.broadcasted_iota(jnp.int32, (SUM_ROWS, SPAN), 0)
+    return (ids == place).astype(wide)
+
+
+def turned(parts, trig_ref):
+    part_wide = parts.astype(wide)
+    return jnp.concatenate(
+        [(part_wide * trig_ref[0:1, :]).astype(low), (part_wide * trig_ref[1:2, :]).astype(low)], 0
+    )
+
+
+def unturned(pair, trig_ref):
+    return pair[:HD] * trig_ref[0:1, :] + pair[HD:] * trig_ref[1:2, :]
+
+
+def query_part(qkv_ref, seq, head):
+    return qkv_ref[seq, head * HD : (head + 1) * HD, :]
+
+
+def key_part(qkv_ref, seq, head):
+    return qkv_ref[seq, WIDTH + head * HD : WIDTH + (head + 1) * HD, :]
+
+
+def value_part(qkv_ref, seq, head):
+    return qkv_ref[seq, 2 * WIDTH + head * HD : 2 * WIDTH + (head + 1) * HD, :]
+
+
+def kept_keys(qkv_ref, trig_ref, seq, head):
+    keys = jnp.maximum(key_part(qkv_ref, seq, head), 0)
+    return (keys.astype(wide) * trig_ref[2 + seq : 3 + seq, :]).astype(low)
+
+
+def state_slice(state, place):
+    return state[place * HD : (place + 1) * HD]
+
+
+def pack_first_body(flags_ref, query_ref, key_ref, value_ref, out_ref, packed_ref):
+    first_core = flags_ref[0] == 0
+    first_copy = flags_ref[1] == 0
+    for place, (left_ref, right_ref) in enumerate(((query_ref, value_ref), (key_ref, out_ref))):
+        left = jnp.where(first_core, left_ref[:, :WIDTH], left_ref[:, WIDTH:])
+        right = jnp.where(first_core, right_ref[:, :WIDTH], right_ref[:, WIDTH:])
+        packed_ref[:, place * WIDTH : (place + 1) * WIDTH] = jnp.where(first_copy, left, right)
+
+
+def pack_hidden_body(flags_ref, up_ref, down_ref, packed_ref):
+    part = packed_ref.shape[1] // 2
+    start = pl.multiple_of((flags_ref[0] * 2 + flags_ref[1]) * part, 128)
+    packed_ref[:, :part] = up_ref[:, pl.ds(start, part)]
+    packed_ref[:, part:] = down_ref[:, pl.ds(start, part)]
+
+
+def project_body(
+    flags_ref, mine_ref, copy_ref, own_ref, other_ref, trig_ref, weight_ref, qkv_ref, state_ref
+):
+    first_copy = flags_ref[1] == 0
+    part = mine_ref.shape[1]
+    weight_ref[:, :part] = jnp.where(first_copy, mine_ref[...], copy_ref[...])
+    weight_ref[:, part:] = jnp.where(first_copy, copy_ref[...], mine_ref[...])
+    matrix = weight_ref[:, : 3 * WIDTH]
+    for seq, x_ref in enumerate((own_ref, other_ref)):
+        qkv_ref[seq] = dot_tn(matrix, x_ref[...]).astype(low)
+    sums = jnp.zeros((SUM_ROWS, 2 * HD), wide)
+    for seq, head, place in head_sets():
+        turned_keys = turned(kept_keys(qkv_ref, trig_ref, seq, head), trig_ref)
+        values = value_part(qkv_ref, seq, head)
+        state_ref[place * HD : (place + 1) * HD, :] = dot_nt(values, turned_keys).astype(low)
+        sums = sums + dot_nt(set_row(place).astype(low), turned_keys)
+    state_ref[STATE_ROWS:, :] = sums.astype(low)
+
+
+def block_body(qkv_ref, trig_ref, reweight_ref, weights_ref, numer_ref, denom_ref):
+    denoms = jnp.zeros((SUM_ROWS, SPAN), wide)
+    for seq, head, place in head_sets():
+        queries = jnp.maximum(query_part(qkv_ref, seq, head), 0)
+        keys = kept_keys(qkv_ref, trig_ref, seq, head)
+        weights = dot_tn(keys, queries) * reweight_ref[...]
+        weights_low = weights.astype(low)
+        weights_ref[place] = weights_low
+        numer_ref[place] = dot_nn(value_part(qkv_ref, seq, head), weights_low)
+        denoms = denoms + set_row(place) * jnp.sum(weights, 0, keepdims=True)
+    denom_ref[...] = denoms
+
+
+def attend_body(
+    qkv_ref,
+    trig_ref,
+    numer_ref,
+    denom_ref,
+    weight_ref,
+    *refs,
+):
+    arrived = refs[:-6]
+    prior_ref, attn_ref, attn_wide_ref, inverse_ref, own_ref, other_ref = refs[-6:]
+    total = arrived[0][...].astype(wide)
+    for ref in arrived[1:]:
+        total = total + ref[...].astype(wide)
+    prior_ref[...] = total.astype(low)
+    matrix = weight_ref[:, 3 * WIDTH : 4 * WIDTH]
+    prior_sums = prior_ref[STATE_ROWS:, :]
+    inverses = jnp.zeros((SUM_ROWS, SPAN), wide)
+    for seq, head, place in head_sets():
+        queries = turned(jnp.maximum(query_part(qkv_ref, seq, head), 0), trig_ref)
+        prior = prior_ref[place * HD : (place + 1) * HD, :]
+        numer = numer_ref[place] + dot_nn(prior, queries)
+        denoms = dot_nn(prior_sums, queries) + denom_ref[...]
+        denom = 1.0 + jnp.sum(denoms * set_row(place), 0, keepdims=True)
+        inverse = 1.0 / denom
+        inverses = inverses + set_row(place) * inverse
+        attended = numer * inverse
+        attn_wide_ref[place] = attended
+        attn_ref[seq, head * HD : (head + 1) * HD, :] = attended.astype(low)
+    inverse_ref[...] = inverses
+    own_ref[...] = dot_nn(matrix, attn_ref[0])
+    other_ref[...] = dot_nn(matrix, attn_ref[1]).astype(low)
+
+
+def grad_attend_body(
+    own_ref,
+    other_ref,
+    weight_ref,
+    attn_wide_ref,
+    inverse_ref,
+    qkv_ref,
+    trig_ref,
+    grad_num_ref,
+    grad_den_ref,
+    state_ref,
+):
+    matrix = weight_ref[:, 3 * WIDTH : 4 * WIDTH]
+    sums = jnp.zeros((SUM_ROWS, 2 * HD), wide)
+    dens = jnp.zeros((SUM_ROWS, SPAN), wide)
+    for seq, grad_ref in enumerate((own_ref, other_ref)):
+        grads = dot_tn(matrix, grad_ref[...]).astype(low).astype(wide)
+        for head in range(HEADS):
+            place = seq * HEADS + head
+            inverse = jnp.sum(inverse_ref[...] * set_row(place), 0, keepdims=True)
+            scaled = grads[head * HD : (head + 1) * HD] * inverse
+            grad_num = scaled.astype(low)
+            grad_num_ref[place] = grad_num
+            grad_den = -jnp.sum(scaled * attn_wide_ref[place], 0, keepdims=True)
+            den_row = set_row(place) * grad_den
+            dens = dens + den_row
+            queries = turned(jnp.maximum(query_part(qkv_ref, seq, head), 0), trig_ref)
+            state_ref[place * HD : (place + 1) * HD, :] = dot_nt(grad_num, queries).astype(low)
+            sums = sums + dot_nt(den_row.astype(low), queries)
+    state_ref[STATE_ROWS:, :] = sums.astype(low)
+    grad_den_ref[...] = dens
+
+
+def grad_block_body(
+    grad_num_ref,
+    grad_den_ref,
+    qkv_ref,
+    trig_ref,
+    reweight_ref,
+    weights_ref,
+    prior_ref,
+    own_ref,
+    other_ref,
+    attn_ref,
+    grad_query_ref,
+    grad_key_ref,
+    grad_value_ref,
+    grad_out_ref,
+):
+    prior_sums = prior_ref[STATE_ROWS:, :]
+    for seq, head, place in head_sets():
+        query = query_part(qkv_ref, seq, head)
+        queries = jnp.maximum(query, 0)
+        keys = kept_keys(qkv_ref, trig_ref, seq, head)
+        grad_num = grad_num_ref[place]
+        den_rows = grad_den_ref[...] * set_row(place)
+        grad_den = jnp.sum(den_rows, 0, keepdims=True)
+        grad_scores = (
+            (dot_tn(value_part(qkv_ref, seq, head), grad_num) + grad_den) * reweight_ref[...]
+        ).astype(low)
+        prior = jnp.concatenate([prior_ref[place * HD : (place + 1) * HD, :], prior_sums], 0)
+        grads = jnp.concatenate([grad_num, den_rows.astype(low)], 0)
+        grad_query = dot_nn(keys, grad_scores) + unturned(dot_tn(prior, grads), trig_ref)
+        grad_query_ref[seq, head * HD : (head + 1) * HD, :] = jnp.where(
+            query.astype(wide) > 0, grad_query, 0.0
+        ).astype(low)
+        grad_key_ref[place] = dot_nt(queries, grad_scores)
+        grad_value_ref[place] = dot_nt(grad_num, weights_ref[place])
+    grad_out_ref[...] = (
+        dot_nt(own_ref[...], attn_ref[0]) + dot_nt(other_ref[...], attn_ref[1])
+    ).astype(low)
+
+
+def grad_project_body(
+    grad_query_ref,
+    grad_key_ref,
+    grad_value_ref,
+    qkv_ref,
+    trig_ref,
+    x_own_ref,
+    x_other_ref,
+    weight_ref,
+    vec_ref,
+    flags_ref,
+    *refs,
+):
+    arrived = refs[:-6]
+    kept_ref, sent_ref, own_ref, other_ref, after_ref, grad_ref = refs[-6:]
+    total = arrived[0][...].astype(wide)
+    for ref in arrived[1:]:
+        total = total + ref[...].astype(wide)
+    after_ref[...] = total.astype(low)
+    after_sums = after_ref[STATE_ROWS:, :]
+    for seq, head, place in head_sets():
+        key = key_part(qkv_ref, seq, head)
+        keys = turned(kept_keys(qkv_ref, trig_ref, seq, head), trig_ref)
+        values = value_part(qkv_ref, seq, head)
+        after = after_ref[place * HD : (place + 1) * HD, :]
+        left = jnp.concatenate([after, after_sums], 0)
+        right = jnp.concatenate([values, set_row(place).astype(low)], 0)
+        grad_key = grad_key_ref[place] + unturned(dot_tn(left, right), trig_ref)
+        grad_key = jnp.where(key.astype(wide) > 0, grad_key, 0.0) * trig_ref[2 + seq : 3 + seq, :]
+        grad_value = grad_value_ref[place] + dot_nn(after, keys)
+        rows = slice(head * HD, (head + 1) * HD)
+        grad_ref[seq, rows, :] = grad_query_ref[seq, rows, :]
+        rows = slice(WIDTH + head * HD, WIDTH + (head + 1) * HD)
+        grad_ref[seq, rows, :] = grad_key.astype(low)
+        rows = slice(2 * WIDTH + head * HD, 2 * WIDTH + (head + 1) * HD)
+        grad_ref[seq, rows, :] = grad_value.astype(low)
+    matrix = weight_ref[:, : 3 * WIDTH]
+    grad_w = (
+        dot_nt(x_own_ref[...], grad_ref[0]) + dot_nt(x_other_ref[...], grad_ref[1])
+    ).astype(low)
+    rows, part, _ = kept_ref.shape
+    first_copy = flags_ref[1] == 0
+    for row in range(rows):
+        start = row * 2 * part
+        whole = jnp.concatenate(
+            [grad_w[start : start + 2 * part], vec_ref[start : start + 2 * part, : 2 * SUM_LANES]],
+            1,
+        )[:, : 3 * WIDTH + SUM_LANES]
+        first, second = whole[:part], whole[part:]
+        kept_ref[row] = jnp.where(first_copy, first, second)
+        sent_ref[row] = jnp.where(first_copy, second, first)
+    own_ref[...] = dot_nn(matrix, grad_ref[0])
+    other_ref[...] = dot_nn(matrix, grad_ref[1]).astype(low)
+
+
+def norm_body(x_ref, half_ref, recv_ref, vec_ref, first_ref, low_ref, normed_ref, inv_ref):
+    hidden = x_ref[...].astype(wide) + (half_ref[...].astype(wide) + recv_ref[...].astype(wide))
+    first, normed, inv_std = norm_columns(hidden, vec_ref[:, 0:1], vec_ref[:, 1:2])
+    first_ref[...] = first
+    low_ref[...] = first.astype(low)
+    normed_ref[...] = normed
+    inv_ref[...] = jnp.broadcast_to(inv_std, inv_ref.shape)
+
+
+def lane_sums(columns, place):
+    lanes = lax.broadcasted_iota(jnp.int32, (columns[0].shape[0], 2 * SUM_LANES), 1)
+    total = jnp.zeros(lanes.shape, wide)
+    for shift, column in enumerate(columns):
+        total = jnp.where(lanes == place + shift, jnp.sum(column, 1, keepdims=True), total)
+    return total
+
+
+def second_norm_body(
+    first_ref, half_ref, recv_ref, vec_ref, cot_ref, trig_ref, result_ref, grad_ref, low_ref, sum_ref
+):
+    hidden = first_ref[...] + (half_ref[...].astype(wide) + recv_ref[...].astype(wide))
+    scale = vec_ref[:, 2:3]
+    result, normed, inv_std = norm_columns(hidden, scale, vec_ref[:, 3:4])
+    result_ref[...] = result.astype(low)
+    grad_in = cot_ref[...].astype(wide) * trig_ref[2:3, :]
+    grad = norm_columns_back(grad_in, normed, inv_std, scale)
+    grad_ref[...] = grad
+    low_ref[...] = grad.astype(low)
+    sum_ref[...] = lane_sums((grad_in * normed, grad_in), 2)
+
+
+def norm_back_body(
+    grad_ref, half_ref, recv_ref, normed_ref, inv_ref, vec_ref, part_ref, hidden_ref, low_ref, sum_ref
+):
+    grad_in = grad_ref[...] + (half_ref[...].astype(wide) + recv_ref[...].astype(wide))
+    normed = normed_ref[...]
+    grad = norm_columns_back(grad_in, normed, inv_ref[0:1, :], vec_ref[:, 0:1])
+    hidden_ref[...] = grad
+    low_ref[...] = grad.astype(low)
+    sum_ref[...] = (lane_sums((grad_in * normed, grad_in), 0) + part_ref[...]).astype(low)
+
+
+def hidden_body(weight_ref, own_ref, other_ref, *refs):
+    act_ref, slope_ref, part_own_ref, part_other_ref = refs[-4:]
+    earlier = refs[:-4]
+    part = act_ref.shape[0]
+    up = weight_ref[:, :part]
+    down = weight_ref[:, part:]
+    for seq, (x_ref, part_ref) in enumerate(
+        ((own_ref, part_own_ref), (other_ref, part_other_ref))
+    ):
+        cols = slice(seq * SPAN, (seq + 1) * SPAN)
+        act, slope = gelu_and_slope(dot_tn(up, x_ref[...]))
+        act_ref[:, cols] = act
+        slope_ref[:, cols] = slope
+        total = dot_nn(down, act)
+        if earlier:
+            total = total + earlier[seq][...]
+        part_ref[...] = total.astype(part_ref.dtype)
+
+
+def hidden_back_body(
+    own_ref,
+    other_ref,
+    mine_ref,
+    copy_ref,
+    slope_mine_ref,
+    slope_copy_ref,
+    pre_mine_ref,
+    pre_copy_ref,
+    part_own_ref,
+    part_other_ref,
+):
+    part = slope_mine_ref.shape[0]
+    for seq, (x_ref, part_ref) in enumerate(
+        ((own_ref, part_own_ref), (other_ref, part_other_ref))
+    ):
+        cols = slice(seq * SPAN, (seq + 1) * SPAN)
+        total = None
+        for weight_ref, slope_ref, pre_ref in (
+            (mine_ref, slope_mine_ref, pre_mine_ref),
+            (copy_ref, slope_copy_ref, pre_copy_ref),
+        ):
+            grad_pre = (dot_tn(weight_ref[:, part:], x_ref[...]) * slope_ref[:, cols]).astype(low)
+            pre_ref[:, cols] = grad_pre
+            term = dot_nn(weight_ref[:, :part], grad_pre)
+            total = term if total is None else total + term
+        part_ref[...] = total.astype(part_ref.dtype)
+
+
+def pair_grad_body(own_ref, other_ref, mine_ref, copy_ref, kept_ref, sent_ref):
+    for hidden_ref, out_ref in ((copy_ref, sent_ref), (mine_ref, kept_ref)):
+        out_ref[...] = (
+            dot_nt(own_ref[...], hidden_ref[:, :SPAN]) + dot_nt(other_ref[...], hidden_ref[:, SPAN:])
+        ).astype(low)
+
+
+def place_hidden(flags_ref, refs, out_ref):
+    part = out_ref.shape[1] // 4
+    core, copy = flags_ref[0], flags_ref[1]
+    for ref, other_core, other_copy in zip(refs, (0, 0, 1, 1), (0, 1, 0, 1)):
+        core_place = 1 - core if other_core else core
+        copy_place = 1 - copy if other_copy else copy
+        start = pl.multiple_of((core_place * 2 + copy_place) * part, 128)
+        out_ref[:, pl.ds(start, part)] = ref[:, :part].astype(wide)
+
+
+def place_down_body(flags_ref, *refs):
+    place_hidden(flags_ref, refs[:4], refs[4])
+
+
+def place_up_body(flags_ref, *refs):
+    up_ref, out_ref = refs[4:]
+    place_hidden(flags_ref, refs[:4], up_ref)
+    part = up_ref.shape[1] // 4
+    sums = [ref[:, part : part + WIDTH].astype(wide) for ref in refs[:4]]
+    own, other = sums[0] + sums[1], sums[2] + sums[3]
+    first_core = flags_ref[0] == 0
+    out_ref[:, :WIDTH] = jnp.where(first_core, own, other)
+    out_ref[:, WIDTH:] = jnp.where(first_core, other, own)
+
+
+def place_last_body(flags_ref, *refs):
+    outs, vec_ref = refs[4:7], refs[7]
+    first_core = flags_ref[0] == 0
+    part = refs[0].shape[0]
+    for own_ref, other_ref, other_copy in ((refs[0], refs[2], 0), (refs[1], refs[3], 1)):
+        copy = 1 - flags_ref[1] if other_copy else flags_ref[1]
+        rows = pl.ds(pl.multiple_of(copy * part, 8), part)
+        own, other = own_ref[...].astype(wide), other_ref[...].astype(wide)
+        for place, out_ref in enumerate(outs):
+            cols = slice(place * WIDTH, (place + 1) * WIDTH)
+            out_ref[rows, :WIDTH] = jnp.where(first_core, own[:, cols], other[:, cols])
+            out_ref[rows, WIDTH:] = jnp.where(first_core, other[:, cols], own[:, cols])
+        vec_ref[rows, :] = own[:, 3 * WIDTH :] + other[:, 3 * WIDTH :]
+
+
+def gelu_and_slope(pre):
+    cdf = 0.5 * (1.0 + lax.erf(pre * math.sqrt(0.5)))
+    density = jnp.exp(-0.5 * pre * pre) * (1.0 / math.sqrt(2.0 * math.pi))
+    return (pre * cdf).astype(low), (cdf + pre * density)
+
+
+def all_quarters(own):
+    copied = swap_copies(own)
+    return own, copied, swap_pair(own), swap_pair(copied)
+
+
+def on_device_paired(
+    tokens,
+    lengths,
+    w_query,
+    w_key,
+    w_value,
+    w_out,
+    gain_one,
+    bias_one,
+    w_up,
+    w_down,
+    gain_two,
+    bias_two,
+    cotangent,
+):
+    rows = lax.axis_size("row")
+    seq_len = SPAN * rows
+    row_idx = lax.axis_index("row")
+    dp_idx = lax.axis_index("dp")
+    core = dp_idx % 2
+    feat_rows = tokens.shape[0]
+
+    positions = row_idx * SPAN + jnp.arange(SPAN, dtype=jnp.int32)
+    seq_pair = jnp.stack([dp_idx, dp_idx + 1 - 2 * core])
+    present = (positions[None, :] < seq_lengths(lengths, seq_pair)[:, None]).astype(wide)
+    angles = math.pi * positions.astype(wide) / (2.0 * seq_len)
+    cos = jnp.cos(angles)
+    sin = jnp.sin(angles)
+    ids = jnp.arange(SPAN, dtype=jnp.int32)
+    causal = (ids[:, None] <= ids[None, :]).astype(wide)
+    reweight = (cos[:, None] * cos[None, :] + sin[:, None] * sin[None, :]) * causal
+    trig = jnp.concatenate([jnp.stack([cos, sin], 0), present, jnp.zeros((4, SPAN), wide)], 0)
+
+    flags = jnp.stack([core, dp_idx // 2])
+
+    part = w_up.shape[1] // 4
+    (first_packed,) = local_call(
+        pack_first_body,
+        [((feat_rows, 2 * WIDTH), low)],
+        "pack_first",
+        flags,
+        w_query,
+        w_key,
+        w_value,
+        w_out.T,
+    )
+    (hidden_packed,) = local_call(
+        pack_hidden_body, [((feat_rows, 2 * part), low)], "pack_hidden", flags, w_up, w_down.T
+    )
+    first_mine = gather_rows(first_packed)
+    hidden_mine = gather_rows(hidden_packed)
+    first_copy = swap_copies(first_mine)
+    hidden_copy = swap_copies(hidden_mine)
+
+    vecs = jnp.stack([gain_one, bias_one, gain_two, bias_two], 0)
+    vecs_high = vecs.astype(low)
+    vecs_rest = (vecs - vecs_high.astype(wide)).astype(low)
+    vec_rows = 8 * feat_rows // SPAN
+    extra = jnp.concatenate(
+        [
+            jnp.stack([vecs_high, vecs_rest], 0).reshape(vec_rows, SPAN),
+            jnp.zeros((-vec_rows % 16, SPAN), low),
+        ],
+        0,
+    )
+    (x_half, cot_half), got_vecs = spread_tokens(jnp.stack([tokens, cotangent], 0), extra)
+    x_own = join_halves(x_half)
+    x_other = swap_pair(x_own)
+    cot = join_halves(cot_half)
+    got_vecs = got_vecs[:, :vec_rows].reshape(rows, 2, 4, feat_rows).astype(wide)
+    norm_vecs = (got_vecs[:, 0] + got_vecs[:, 1]).transpose(0, 2, 1).reshape(D, 4)
+
+    state_shape = ((STATE_ROWS + SUM_ROWS, 2 * HD), low)
+    sets = 2 * HEADS
+    block_low = ((D, SPAN), low)
+    block_wide = ((D, SPAN), wide)
+    weight, qkv, state = local_call(
+        project_body,
+        [((D, 4 * WIDTH), low), ((2, 3 * WIDTH, SPAN), low), state_shape],
+        "project",
+        flags,
+        first_mine,
+        first_copy,
+        x_own,
+        x_other,
+        trig,
+    )
+    arrived = [shift_rows(state, step) for step in range(1, rows)]
+    weights, numer, denom = local_call(
+        block_body,
+        [((sets, SPAN, SPAN), low), ((sets, HD, SPAN), wide), ((SUM_ROWS, SPAN), wide)],
+        "block",
+        qkv,
+        trig,
+        reweight,
+    )
+    prior, attn, attn_wide, inverse, branch_own, branch_other = local_call(
+        attend_body,
+        [
+            state_shape,
+            ((2, WIDTH, SPAN), low),
+            ((sets, HD, SPAN), wide),
+            ((SUM_ROWS, SPAN), wide),
+            block_wide,
+            block_low,
+        ],
+        "attend",
+        qkv,
+        trig,
+        numer,
+        denom,
+        weight,
+        *arrived,
+    )
+    branch = column_parts(branch_own, branch_other)
+    first, first_low, normed, inv_std = local_call(
+        norm_body,
+        [block_wide, block_low, block_wide, ((8, SPAN), wide)],
+        "norm",
+        x_own,
+        *branch,
+        norm_vecs,
+    )
+    first_other = swap_pair(first_low)
+    half_hidden = [((part, 2 * SPAN), low), ((part, 2 * SPAN), wide)]
+    act_mine, slope_mine, ffn_own, ffn_other = local_call(
+        hidden_body,
+        half_hidden + [block_wide, block_wide],
+        "hidden_mine",
+        hidden_mine,
+        first_low,
+        first_other,
+    )
+    act_copy, slope_copy, ffn_own, ffn_other = local_call(
+        hidden_body,
+        half_hidden + [block_wide, block_low],
+        "hidden_copy",
+        hidden_copy,
+        first_low,
+        first_other,
+        ffn_own,
+        ffn_other,
+    )
+    ffn = column_parts(ffn_own, ffn_other)
+    result, grad_second, grad_ffn, sums_two = local_call(
+        second_norm_body,
+        [block_low, block_wide, block_low, ((D, 2 * SUM_LANES), wide)],
+        "second_norm",
+        first,
+        *ffn,
+        norm_vecs,
+        cot,
+        trig,
+    )
+    grad_ffn_other = swap_pair(grad_ffn)
+    hidden_low = ((part, 2 * SPAN), low)
+    pre_mine, pre_copy, first_own_part, first_other_part = local_call(
+        hidden_back_body,
+        [hidden_low, hidden_low, block_wide, block_low],
+        "hidden_back",
+        grad_ffn,
+        grad_ffn_other,
+        hidden_mine,
+        hidden_copy,
+        slope_mine,
+        slope_copy,
+    )
+    first_sum = column_parts(first_own_part, first_other_part)
+
+    def hidden_grad(own, other, mine, copied, name):
+        kept, sent = local_call(
+            pair_grad_body,
+            [((D, part), low), ((D, part), low)],
+            name,
+            own,
+            other,
+            mine,
+            copied,
+        )
+        return (kept.astype(wide) + swap_copies(sent).astype(wide)).astype(low)
+
+    def scatter_rows(partial_grad):
+        return lax.psum_scatter(partial_grad, "row", scatter_dimension=0, tiled=True)
+
+    down_rows = scatter_rows(
+        hidden_grad(grad_ffn, grad_ffn_other, act_mine, act_copy, "grad_down")
+    )
+    up_part = hidden_grad(first_low, first_other, pre_mine, pre_copy, "grad_up")
+    grad_hidden, branch_grad, vec_sums = local_call(
+        norm_back_body,
+        [block_wide, block_low, ((D, 2 * SUM_LANES), low)],
+        "norm_back",
+        grad_second,
+        *first_sum,
+        normed,
+        inv_std,
+        norm_vecs,
+        sums_two,
+    )
+    branch_grad_other = swap_pair(branch_grad)
+    grad_num, grad_den, grad_state = local_call(
+        grad_attend_body,
+        [((sets, HD, SPAN), low), ((SUM_ROWS, SPAN), wide), state_shape],
+        "grad_attend",
+        branch_grad,
+        branch_grad_other,
+        weight,
+        attn_wide,
+        inverse,
+        qkv,
+        trig,
+    )
+    later = [shift_rows(grad_state, -step) for step in range(1, rows)]
+    grad_query, grad_key, grad_value, grad_out = local_call(
+        grad_block_body,
+        [
+            ((2, WIDTH, SPAN), low),
+            ((sets, HD, SPAN), wide),
+            ((sets, HD, SPAN), wide),
+            ((D, WIDTH), low),
+        ],
+        "grad_block",
+        grad_num,
+        grad_den,
+        qkv,
+        trig,
+        reweight,
+        weights,
+        prior,
+        branch_grad,
+        branch_grad_other,
+        attn,
+    )
+    up_part, grad_out, down_rows = lax.optimization_barrier((up_part, grad_out, down_rows))
+    up_rows = scatter_rows(jnp.concatenate([up_part, grad_out], 1))
+    half_rows = ((rows, feat_rows // 2, 3 * WIDTH + SUM_LANES), low)
+    kept_w, sent_w, x_grad_own, x_grad_other = local_call(
+        grad_project_body,
+        [half_rows, half_rows, block_wide, block_low],
+        "grad_project",
+        grad_query,
+        grad_key,
+        grad_value,
+        qkv,
+        trig,
+        x_own,
+        x_other,
+        weight,
+        vec_sums,
+        flags,
+        *later,
+        scratch=[state_shape, ((2, 3 * WIDTH, SPAN), low)],
+    )
+    half_w = (kept_w.astype(wide) + swap_copies(sent_w).astype(wide)).astype(low)
+
+    own_x, other_x = feature_halves(x_grad_own + swap_pair(x_grad_other).astype(wide))
+    own_h, _ = feature_halves(grad_hidden)
+    own_x = own_x + swap_cols(other_x.astype(low)).astype(wide) + own_h
+    out_half, _ = feature_halves(result)
+    placed_back = gather_tokens([own_x.astype(low), out_half])
+    input_grad = placed_back[0].astype(wide)
+    output = placed_back[1]
+
+    last_rows = lax.dynamic_index_in_dim(half_w, row_idx, 0, False).astype(wide)
+    for step in range(1, rows):
+        sent = lax.dynamic_index_in_dim(half_w, (row_idx + step) % rows, 0, False)
+        last_rows = last_rows + rotate_rows(sent, step).astype(wide)
+
+    (down_t,) = local_call(
+        place_down_body,
+        [((feat_rows, 4 * part), wide)],
+        "place_down",
+        flags,
+        *all_quarters(down_rows),
+    )
+    up_grad, out_t = local_call(
+        place_up_body,
+        [((feat_rows, 4 * part), wide), ((feat_rows, 2 * WIDTH), wide)],
+        "place_up",
+        flags,
+        *all_quarters(up_rows),
+    )
+    query_grad, key_grad, value_grad, vec_total = local_call(
+        place_last_body,
+        [((feat_rows, 2 * WIDTH), wide)] * 3 + [((feat_rows, SUM_LANES), wide)],
+        "place_last",
+        flags,
+        *all_quarters(last_rows.astype(low)),
+    )
+    return (
+        output,
+        input_grad,
+        query_grad,
+        key_grad,
+        value_grad,
+        out_t.T,
+        vec_total[:, 0],
+        vec_total[:, 1],
+        up_grad,
+        down_t.T,
+        vec_total[:, 2],
+        vec_total[:, 3],
+    )
+
+
 def solution(mesh):
     placed = (
         P("row", ("dp", "col")),
@@ -437,7 +1289,7 @@
         P("row", ("dp", "col")),
     )
     return jax.shard_map(
-        on_device,
+        on_device_paired if paired_layout(mesh) else on_device,
         mesh=mesh,
         in_specs=placed,
         out_specs=(

time: 1180 us -> 248 us (0.21)
  waiting for transfers between devices: 578 us -> 105 us
  blocking collectives: 428 us -> 16.6 us
  other arithmetic: 60.8 us -> 12.2 us
  matrix products: 48.3 us -> 0 us
  Pallas kernels: 0 us -> 33.6 us
  starting transfers between devices: 8.58 us -> 40.9 us
    reduce_scatter x8 -> x2, waiting for transfers between devices: 348 us -> 0.01 us  [scatter_rows(): lax.psum_scatter(partial_grad, 'row', scatter_dimension=0, tiled=True)]
    all_gather x12 -> x0, blocking collectives: 301 us -> none  [the longest x8 273 us: carried_in(): lax.all_gather(a.astype(kind), axis)]
    all_gather x3 -> x1, waiting for transfers between devices: 171 us -> 0.01 us  [gather_rows(): return lax.all_gather(operand, 'row', axis=0, tiled=True)]
    ppermute x0 -> x45, waiting for transfers between devices: none -> 105 us  [the longest x8 31.8 us: swap_copies(): lax.ppermute(operand, 'dp', [(i, i ^ 2) for i in range(lax.axis_size('dp'...]
    psum x6 -> x0, blocking collectives: 55.6 us -> none  [the longest x4 44.9 us: row_totals(): return lax.psum((first_part, second_part), 'row')]
    dot_general x34 -> x0, matrix products: 48.3 us -> none  [the longest x8 26.2 us: term_rows(): return jnp.dot(sliced, matrix, preferred_element_type=jnp.float32)]
    psum x1 -> x0, waiting for transfers between devices: 45.1 us -> none  [on_device(): lax.psum(grad_query.astype(jnp.bfloat16), 'dp').astype(jnp.float32)]
    ppermute x0 -> x45, starting transfers between devices: none -> 40.8 us  [the longest x9 13.7 us: rotate_rows(): lax.ppermute(operand, 'row', [(i, (i + step) % count) for i in range(coun...]
  transfers between devices with their start and end apart: 14 -> 48, of which waited for: 13 -> 25; matrix products, arithmetic and copies ran while one was open for 2% -> 5% of each run, Pallas kernels for 0% -> 10%
where the time goes in v2:
time: 248 us; the launch traced here: 247 us
  waiting for transfers between devices  105 us (42%)
  starting transfers between devices  40.9 us (16%)
  Pallas kernels  33.6 us (14%)
  local copies, waits for them, and re-layouts  24.9 us (10%)
  blocking collectives  16.6 us (7%)
  between operations  14.7 us (6%)
  other arithmetic  12.2 us (5%)
    pallas_call x19, Pallas kernels, local_call(): pl.pallas_call(body, out_shape=[jax.ShapeDtypeStruct(shape, kind) for sha...  33.6 us
    ppermute x8, waiting for transfers between devices, swap_copies(): lax.ppermute(operand, 'dp', [(i, i ^ 2) for i in range(lax.axis_size('dp'...  31.8 us
    ppermute x8, waiting for transfers between devices, swap_cols(): return lax.ppermute(operand, 'col', [(0, 1), (1, 0)])  30.5 us
    ppermute x9, waiting for transfers between devices, rotate_rows(): lax.ppermute(operand, 'row', [(i, (i + step) % count) for i in range(coun...  25.6 us
    unnamed x114, local copies, waits for them, and re-layouts  22.5 us
    all_gather x1, blocking collectives, gather_rows(): return lax.all_gather(operand, 'row', axis=0, tiled=True)  16.6 us
    ppermute x9, starting transfers between devices, rotate_rows(): lax.ppermute(operand, 'row', [(i, (i + step) % count) for i in range(coun...  13.7 us
    ppermute x6, starting transfers between devices, shift_rows(): return lax.ppermute(operand, 'row', pairs)  10.4 us
  transfers between devices with their start and end apart: 48, of which 25 were waited for; matrix products, arithmetic and copies ran while one was open for 5% of the time, Pallas kernels for 10%

profile of v2, /device:TPU:0, one launch (start us, length us, event | category | flops | bytes accessed | tf_op | source)
XLA Modules:
  0.0 247.4 jit_solution(5865701799904265469)
XLA Ops:
  8.4 3.0 %collective-permute-start = (bf16[2,96,512]{2,1,0:T(8,128)(2,1)S(1)}, bf16[2,96,512]{2,1,0:T(8,128)(2,1)S(1)}, u32[]{:S(2)}, u32[]{:S(2)}) collective-permute-start(bf16[2,96,512]{2,1,0:T(8,128)(2,1)S(1)} %broadcast_select_fusion.6), channel_id=1, source_target_pairs={{0,1},{1,0},{2,3},{3,2},{4,5},{5,4},{6,7},{7,6},{8,9},{9,8},{10,11... | collective-permute-start | bytes 589832 | tf_op jit(solution)/shard_map/ppermute | solution.py:441
  16.0 16.6 %all_gather.6.mine_ref = bf16[768,384]{1,0:T(8,128)(2,1)S(1)} all-gather(bf16[192,384]{1,0:T(8,128)(2,1)S(1)} %pack_first.1), channel_id=1, replica_groups=mesh['dp'=4,'row'=4,'col'=2] {'row'}, dimensions={0}, use_global_device_ids=true | all-gather | bytes 737280 | tf_op jit(solution)/shard_map/all_gather | solution.py:52
  36.4 1.9 collective-permute-start.1
  38.4 2.6 %collective-permute-start.2 = (bf16[208,256]{1,0:T(8,128)(2,1)S(1)}, bf16[208,256]{1,0:T(8,128)(2,1)S(1)}, u32[]{:S(2)}, u32[]{:S(2)}) collective-permute-start(bf16[208,256]{1,0:T(8,128)(2,1)S(1)} %get-tuple-element.157), channel_id=1, source_target_pairs={{0,4},{2,6},{4,0},{6,2},{1,5},{3,7},{5,1},{7,3},{8,12},{10,14},{12... | collective-permute-start | bytes 319496 | tf_op jit(solution)/shard_map/ppermute | solution.py:460
  41.1 2.0 collective-permute-done.1
  43.1 2.3 collective-permute-done.2
  45.4 5.4 %collective-permute-done.3 = bf16[208,256]{1,0:T(8,128)(2,1)S(1)} collective-permute-done((bf16[208,256]{1,0:T(8,128)(2,1)S(1)}, bf16[208,256]{1,0:T(8,128)(2,1)S(1)}, u32[]{:S(2)}, u32[]{:S(2)}) %collective-permute-start.3) | collective-permute-done | bytes 106528 | tf_op jit(solution)/shard_map/ppermute | solution.py:460
  51.0 5.6 %collective-permute-done.16 = bf16[4,96,256]{2,1,0:T(8,128)(2,1)S(1)} collective-permute-done((bf16[4,96,256]{2,1,0:T(8,128)(2,1)S(1)}, bf16[4,96,256]{2,1,0:T(8,128)(2,1)S(1)}, u32[]{:S(2)}, u32[]{:S(2)}) %collective-permute-start.16) | collective-permute-done | bytes 196640 | tf_op jit(solution)/shard_map/ppermute | solution.py:441
  57.6 5.4 %collective-permute-done.4 = bf16[4,96,256]{2,1,0:T(8,128)(2,1)S(1)} collective-permute-done((bf16[4,96,256]{2,1,0:T(8,128)(2,1)S(1)}, bf16[4,96,256]{2,1,0:T(8,128)(2,1)S(1)}, u32[]{:S(2)}, u32[]{:S(2)}) %collective-permute-start.4) | collective-permute-done | bytes 196640 | tf_op jit(solution)/shard_map/ppermute | solution.py:441
  67.8 3.6 %collective-permute-start.8 = (bf16[400,128]{1,0:T(8,128)(2,1)S(1)}, bf16[400,128]{1,0:T(8,128)(2,1)S(1)}, u32[]{:S(2)}, u32[]{:S(2)}) collective-permute-start(bf16[400,128]{1,0:T(8,128)(2,1)S(1)} %get-tuple-element.75), channel_id=1, source_target_pairs={{0,4},{2,6},{1,5},{3,7},{8,12},{10,14},{9,13},{11,15},{16,20},{18,... | collective-permute-start | bytes 307208 | tf_op jit(solution)/shard_map/ppermute | solution.py:455
  79.8 2.1 collective-permute-done.10
  85.9 8.3 %collective-permute-done.11.recv_ref = bf16[768,256]{1,0:T(8,128)(2,1)S(1)} collective-permute-done((bf16[768,256]{1,0:T(8,128)(2,1)S(1)}, bf16[768,256]{1,0:T(8,128)(2,1)S(1)}, u32[]{:S(2)}, u32[]{:S(2)}) %collective-permute-start.11) | collective-permute-done | bytes 393248 | tf_op jit(solution)/shard_map/ppermute | solution.py:441
  97.5 1.7 collective-permute-done.13.other_ref
  100.8 7.7 %collective-permute-done.12.weight_ref.copy_ref = bf16[768,768]{1,0:T(8,128)(2,1)} collective-permute-done((bf16[768,768]{1,0:T(8,128)(2,1)}, bf16[768,768]{1,0:T(8,128)(2,1)}, u32[]{:S(2)}, u32[]{:S(2)}) %collective-permute-start.12) | collective-permute-done | bytes 1179680 | tf_op jit(solution)/shard_map/ppermute | solution.py:449
  108.5 2.9 %hidden_copy.1 = (bf16[384,512]{1,0:T(8,128)(2,1)S(1)}, f32[384,512]{1,0:T(8,128)S(1)}, f32[768,256]{1,0:T(8,128)S(1)}, bf16[768,256]{1,0:T(8,128)(2,1)S(1)}) custom-call(bf16[768,768]{1,0:T(8,128)(2,1)} %collective-permute-done.12.weight_ref.copy_ref, bf16[768,256]{1,0:T(8,128)(2,1)S(1)} %get-tuple-element.79.own_ref, ...), custom_call_target="tpu_custom_call" | custom-call | tf_op jit(solution)/shard_map/hidden_copy/pallas_call | solution.py:558
  113.9 10.6 %collective-permute-done.15.recv_ref = bf16[768,256]{1,0:T(8,128)(2,1)S(1)} collective-permute-done((bf16[768,256]{1,0:T(8,128)(2,1)S(1)}, bf16[768,256]{1,0:T(8,128)(2,1)S(1)}, u32[]{:S(2)}, u32[]{:S(2)}) %collective-permute-start.15) | collective-permute-done | bytes 393248 | tf_op jit(solution)/shard_map/ppermute | solution.py:441
  129.9 3.1 %hidden_back.1 = (bf16[384,512]{1,0:T(8,128)(2,1)S(1)}, bf16[384,512]{1,0:T(8,128)(2,1)S(1)}, f32[768,256]{1,0:T(8,128)S(1)}, bf16[768,256]{1,0:T(8,128)(2,1)S(1)}) custom-call(bf16[768,256]{1,0:T(8,128)(2,1)S(1)} %get-tuple-element.85.own_ref, bf16[768,256]{1,0:T(8,128)(2,1)S(1)} %collective-permute-done.17.other_ref, bf16[768,768]{1,0:T(8,128)(2,1)S(1)} %copy-done, ...), custom_call_target="tpu_custom_call" | custom-call | tf_op jit(solution)/shard_map/hidden_back/pallas_call | solution.py:558
  137.5 13.7 %collective-permute-done.38 = bf16[768,384]{1,0:T(8,128)(2,1)S(1)} collective-permute-done((bf16[768,384]{1,0:T(8,128)(2,1)S(1)}, bf16[768,384]{1,0:T(8,128)(2,1)S(1)}, u32[]{:S(2)}, u32[]{:S(2)}) %collective-permute-start.38) | collective-permute-done | bytes 589856 | tf_op jit(solution)/shard_map/ppermute | solution.py:449
  156.3 2.5 %norm_back.1 = (f32[768,256]{1,0:T(8,128)S(1)}, bf16[768,256]{1,0:T(8,128)(2,1)}, bf16[768,128]{1,0:T(8,128)(2,1)S(1)}) custom-call(f32[768,256]{1,0:T(8,128)S(1)} %copy-done.12, bf16[768,256]{1,0:T(8,128)(2,1)} %add_convert_fusion.3.half_ref, bf16[768,256]{1,0:T(8,128)(2,1)} %collective-permute-done.19.recv_ref, f32[768,256]{1,0:T(8,128)S(1)} %copy-done.10, ...), custom_call_target="tpu_custom_call" | custom-call | tf_op jit(solution)/shard_map/norm_back/pallas_call | solution.py:558
  163.9 2.0 grad_attend.1
  170.8 2.8 %grad_block.1 = (bf16[2,192,256]{2,1,0:T(8,128)(2,1)S(1)}, f32[6,64,256]{2,1,0:T(8,128)S(1)}, f32[6,64,256]{2,1,0:T(8,128)S(1)}, bf16[768,192]{1,0:T(8,128)(2,1)S(1)}) custom-call(bf16[6,64,256]{2,1,0:T(8,128)(2,1)S(1)} %get-tuple-element.96.grad_num_ref, f32[16,256]{1,0:T(8,128)S(1)} %get-tuple-element.97.grad_den_ref, ...), custom_call_target="tpu_custom_call" | custom-call | tf_op jit(solution)/shard_map/grad_block/pallas_call | solution.py:558
  174.4 6.9 %collective-permute-done.22.refs_1_ = bf16[400,128]{1,0:T(8,128)(2,1)S(1)} collective-permute-done((bf16[400,128]{1,0:T(8,128)(2,1)S(1)}, bf16[400,128]{1,0:T(8,128)(2,1)S(1)}, u32[]{:S(2)}, u32[]{:S(2)}) %collective-permute-start.22) | collective-permute-done | bytes 102432 | tf_op jit(solution)/shard_map/ppermute | solution.py:455
  181.4 3.1 %grad_project.1 = (bf16[4,96,640]{2,1,0:T(8,128)(2,1)S(1)}, bf16[4,96,640]{2,1,0:T(8,128)(2,1)}, f32[768,256]{1,0:T(8,128)S(1)}, bf16[768,256]{1,0:T(8,128)(2,1)}) custom-call(bf16[2,192,256]{2,1,0:T(8,128)(2,1)S(1)} %get-tuple-element.101.grad_query_ref, f32[6,64,256]{2,1,0:T(8,128)S(1)} %get-tuple-element.102.grad_key_ref, ...), custom_call_target="tpu_custom_call" | custom-call | tf_op jit(solution)/shard_map/grad_project/pallas_call | solution.py:558
  185.9 1.7 collective-permute-start.30
  190.5 9.8 %collective-permute-done.30 = bf16[4,96,640]{2,1,0:T(8,128)(2,1)S(1)} collective-permute-done((bf16[4,96,640]{2,1,0:T(8,128)(2,1)}, bf16[4,96,640]{2,1,0:T(8,128)(2,1)S(1)}, u32[]{:S(2)}, u32[]{:S(2)}) %collective-permute-start.30) | collective-permute-done | bytes 491552 | tf_op jit(solution)/shard_map/ppermute | solution.py:449
  200.6 3.7 %collective-permute-start.33 = (bf16[96,640]{1,0:T(8,128)(2,1)S(1)}, bf16[96,640]{1,0:T(8,128)(2,1)S(1)}, u32[]{:S(2)}, u32[]{:S(2)}) collective-permute-start(bf16[96,640]{1,0:T(8,128)(2,1)S(1)} %get-tuple-element.143), channel_id=1, source_target_pairs={{0,6},{2,0},{4,2},{6,4},{1,7},{3,1},{5,3},{7,5},{8,14},{10,8},{12,... | collective-permute-start | bytes 368648 | tf_op jit(solution)/shard_map/ppermute | solution.py:460
  205.3 6.0 %collective-permute-done.31 = bf16[96,640]{1,0:T(8,128)(2,1)S(1)} collective-permute-done((bf16[96,640]{1,0:T(8,128)(2,1)S(1)}, bf16[96,640]{1,0:T(8,128)(2,1)S(1)}, u32[]{:S(2)}, u32[]{:S(2)}) %collective-permute-start.31) | collective-permute-done | bytes 122912 | tf_op jit(solution)/shard_map/ppermute | solution.py:460
  211.3 7.0 %collective-permute-done.32 = bf16[96,640]{1,0:T(8,128)(2,1)S(1)} collective-permute-done((bf16[96,640]{1,0:T(8,128)(2,1)S(1)}, bf16[96,640]{1,0:T(8,128)(2,1)S(1)}, u32[]{:S(2)}, u32[]{:S(2)}) %collective-permute-start.32) | collective-permute-done | bytes 122912 | tf_op jit(solution)/shard_map/ppermute | solution.py:460
  218.3 5.3 %collective-permute-start.28 = (bf16[2,96,256]{2,1,0:T(8,128)(2,1)S(1)}, bf16[2,96,256]{2,1,0:T(8,128)(2,1)S(1)}, u32[]{:S(2)}, u32[]{:S(2)}) collective-permute-start(bf16[2,96,256]{2,1,0:T(8,128)(2,1)S(1)} %get-tuple-element.148), channel_id=1, source_target_pairs={{0,6},{2,0},{4,2},{6,4},{1,7},{3,1},{5,3},{7,5},{8,14},{10,8},{12,... | collective-permute-start | bytes 294920 | tf_op jit(solution)/shard_map/ppermute | solution.py:460
  225.3 2.1 collective-permute-done.27
  230.2 2.8 %collective-permute-start.29 = (bf16[2,96,512]{2,1,0:T(8,128)(2,1)S(1)}, bf16[2,96,512]{2,1,0:T(8,128)(2,1)S(1)}, u32[]{:S(2)}, u32[]{:S(2)}) collective-permute-start(bf16[2,96,512]{2,1,0:T(8,128)(2,1)S(1)} %broadcast_select_fusion.2), channel_id=1, source_target_pairs={{0,1},{1,0},{2,3},{3,2},{4,5},{5,4},{6,7},{7,6},{8,9},{9,8},{10,11... | collective-permute-start | bytes 589832 | tf_op jit(solution)/shard_map/ppermute | solution.py:441
  239.1 1.8 place_up.1
  (261 shorter events, 76.7 us)
Async XLA Ops:
  7.2 72.6 %all-gather.2.cloned.1.call-start = ((), (), s32[]{:S(2)}) async-start(), calls=%async_computation.2 | async-start | bytes 1474560 | tf_op jit(solution)/shard_map/all_gather | solution.py:52
  8.4 27.5 %collective-permute-start = (bf16[2,96,512]{2,1,0:T(8,128)(2,1)S(1)}, bf16[2,96,512]{2,1,0:T(8,128)(2,1)S(1)}, u32[]{:S(2)}, u32[]{:S(2)}) collective-permute-start(bf16[2,96,512]{2,1,0:T(8,128)(2,1)S(1)} %broadcast_select_fusion.6), channel_id=1, source_target_pairs={{0,1},{1,0},{2,3},{3,2},{4,5},{5,4},{6,7},{7,6},{8,9},{9,8},{10,11... | collective-permute-start | bytes 589832 | tf_op jit(solution)/shard_map/ppermute | solution.py:441
  32.6 30.8 %collective-permute-start.5 = (bf16[768,384]{1,0:T(8,128)(2,1)S(1)}, bf16[768,384]{1,0:T(8,128)(2,1)S(1)}, u32[]{:S(2)}, u32[]{:S(2)}) collective-permute-start(bf16[768,384]{1,0:T(8,128)(2,1)S(1)} %all_gather.6.mine_ref), channel_id=1, source_target_pairs={{0,16},{8,24},{16,0},{24,8},{1,17},{9,25},{17,1},{25,9},{2,18},{10... | collective-permute-start | bytes 1769480 | tf_op jit(solution)/shard_map/ppermute | solution.py:449
  35.4 152.3 %reduce-scatter.3.cloned.1.call-start = ((), (), s32[]{:S(2)}) async-start(), calls=%async_computation.3 | async-start | bytes 737280 | tf_op jit(solution)/shard_map/reduce_scatter | solution.py:1152
  36.4 6.7 %collective-permute-start.1 = (bf16[208,256]{1,0:T(8,128)(2,1)S(1)}, bf16[208,256]{1,0:T(8,128)(2,1)S(1)}, u32[]{:S(2)}, u32[]{:S(2)}) collective-permute-start(bf16[208,256]{1,0:T(8,128)(2,1)S(1)} %get-tuple-element.156), channel_id=1, source_target_pairs={{0,2},{2,4},{4,6},{6,0},{1,3},{3,5},{5,7},{7,1},{8,10},{10,12},{12... | collective-permute-start | bytes 319496 | tf_op jit(solution)/shard_map/ppermute | solution.py:460
  38.4 7.1 %collective-permute-start.2 = (bf16[208,256]{1,0:T(8,128)(2,1)S(1)}, bf16[208,256]{1,0:T(8,128)(2,1)S(1)}, u32[]{:S(2)}, u32[]{:S(2)}) collective-permute-start(bf16[208,256]{1,0:T(8,128)(2,1)S(1)} %get-tuple-element.157), channel_id=1, source_target_pairs={{0,4},{2,6},{4,0},{6,2},{1,5},{3,7},{5,1},{7,3},{8,12},{10,14},{12... | collective-permute-start | bytes 319496 | tf_op jit(solution)/shard_map/ppermute | solution.py:460
  40.9 9.9 %collective-permute-start.3 = (bf16[208,256]{1,0:T(8,128)(2,1)S(1)}, bf16[208,256]{1,0:T(8,128)(2,1)S(1)}, u32[]{:S(2)}, u32[]{:S(2)}) collective-permute-start(bf16[208,256]{1,0:T(8,128)(2,1)S(1)} %get-tuple-element.155), channel_id=1, source_target_pairs={{0,6},{2,0},{4,2},{6,4},{1,7},{3,1},{5,3},{7,5},{8,14},{10,8},{12,... | collective-permute-start | bytes 319496 | tf_op jit(solution)/shard_map/ppermute | solution.py:460
  66.5 8.6 %collective-permute-start.7 = (bf16[400,128]{1,0:T(8,128)(2,1)S(1)}, bf16[400,128]{1,0:T(8,128)(2,1)S(1)}, u32[]{:S(2)}, u32[]{:S(2)}) collective-permute-start(bf16[400,128]{1,0:T(8,128)(2,1)S(1)} %get-tuple-element.75), channel_id=1, source_target_pairs={{0,2},{2,4},{4,6},{1,3},{3,5},{5,7},{8,10},{10,12},{12,14},{9,11},... | collective-permute-start | bytes 307208 | tf_op jit(solution)/shard_map/ppermute | solution.py:455
  67.8 7.3 %collective-permute-start.8 = (bf16[400,128]{1,0:T(8,128)(2,1)S(1)}, bf16[400,128]{1,0:T(8,128)(2,1)S(1)}, u32[]{:S(2)}, u32[]{:S(2)}) collective-permute-start(bf16[400,128]{1,0:T(8,128)(2,1)S(1)} %get-tuple-element.75), channel_id=1, source_target_pairs={{0,4},{2,6},{1,5},{3,7},{8,12},{10,14},{9,13},{11,15},{16,20},{18,... | collective-permute-start | bytes 307208 | tf_op jit(solution)/shard_map/ppermute | solution.py:455
  79.8 28.7 %collective-permute-start.12 = (bf16[768,768]{1,0:T(8,128)(2,1)}, bf16[768,768]{1,0:T(8,128)(2,1)}, u32[]{:S(2)}, u32[]{:S(2)}) collective-permute-start(bf16[768,768]{1,0:T(8,128)(2,1)} %all-gather.2.cloned.1.call-done.weight_ref.mine_ref), channel_id=1, source_target_pairs={{0,16},{8,24},{16,0},{24,8},{1,17},{9,25},{17,1},{25,9},{2,18},{10... | collective-permute-start | bytes 3538952 | tf_op jit(solution)/shard_map/ppermute | solution.py:449
  83.0 11.2 %collective-permute-start.11 = (bf16[768,256]{1,0:T(8,128)(2,1)S(1)}, bf16[768,256]{1,0:T(8,128)(2,1)S(1)}, u32[]{:S(2)}, u32[]{:S(2)}) collective-permute-start(bf16[768,256]{1,0:T(8,128)(2,1)S(1)} %add_convert_fusion.5.half_ref), channel_id=1, source_target_pairs={{0,1},{1,0},{2,3},{3,2},{4,5},{5,4},{6,7},{7,6},{8,9},{9,8},{10,11... | collective-permute-start | bytes 1179656 | tf_op jit(solution)/shard_map/ppermute | solution.py:441
  113.3 11.2 %collective-permute-start.15 = (bf16[768,256]{1,0:T(8,128)(2,1)S(1)}, bf16[768,256]{1,0:T(8,128)(2,1)S(1)}, u32[]{:S(2)}, u32[]{:S(2)}) collective-permute-start(bf16[768,256]{1,0:T(8,128)(2,1)S(1)} %add_convert_fusion.4.half_ref), channel_id=1, source_target_pairs={{0,1},{1,0},{2,3},{3,2},{4,5},{5,4},{6,7},{7,6},{8,9},{9,8},{10,11... | collective-permute-start | bytes 1179656 | tf_op jit(solution)/shard_map/ppermute | solution.py:441
  135.6 15.7 %collective-permute-start.38 = (bf16[768,384]{1,0:T(8,128)(2,1)S(1)}, bf16[768,384]{1,0:T(8,128)(2,1)S(1)}, u32[]{:S(2)}, u32[]{:S(2)}) collective-permute-start(bf16[768,384]{1,0:T(8,128)(2,1)S(1)} %get-tuple-element.123), channel_id=1, source_target_pairs={{0,16},{8,24},{16,0},{24,8},{1,17},{9,25},{17,1},{25,9},{2,18},{10... | collective-permute-start | bytes 1769480 | tf_op jit(solution)/shard_map/ppermute | solution.py:449
  137.0 15.3 %collective-permute-start.19 = (bf16[768,256]{1,0:T(8,128)(2,1)}, bf16[768,256]{1,0:T(8,128)(2,1)}, u32[]{:S(2)}, u32[]{:S(2)}) collective-permute-start(bf16[768,256]{1,0:T(8,128)(2,1)} %add_convert_fusion.3.half_ref), channel_id=1, source_target_pairs={{0,1},{1,0},{2,3},{3,2},{4,5},{5,4},{6,7},{7,6},{8,9},{9,8},{10,11... | collective-permute-start | bytes 1179656 | tf_op jit(solution)/shard_map/ppermute | solution.py:441
  152.2 76.4 %reduce-scatter.5.cloned.1.call-start = ((), (), s32[]{:S(2)}) async-start(), calls=%async_computation.4 | async-start | bytes 1228800 | tf_op jit(solution)/shard_map/reduce_scatter | solution.py:1152
  161.9 22.6 %collective-permute-start.37 = (bf16[768,384]{1,0:T(8,128)(2,1)}, bf16[768,384]{1,0:T(8,128)(2,1)}, u32[]{:S(2)}, u32[]{:S(2)}) collective-permute-start(bf16[768,384]{1,0:T(8,128)(2,1)} %get-tuple-element.118), channel_id=1, source_target_pairs={{0,16},{8,24},{16,0},{24,8},{1,17},{9,25},{17,1},{25,9},{2,18},{10... | collective-permute-start | bytes 1769480 | tf_op jit(solution)/shard_map/ppermute | solution.py:449
  166.0 8.4 %collective-permute-start.21 = (bf16[400,128]{1,0:T(8,128)(2,1)S(1)}, bf16[400,128]{1,0:T(8,128)(2,1)S(1)}, u32[]{:S(2)}, u32[]{:S(2)}) collective-permute-start(bf16[400,128]{1,0:T(8,128)(2,1)S(1)} %get-tuple-element.105), channel_id=1, source_target_pairs={{2,0},{4,2},{6,4},{3,1},{5,3},{7,5},{10,8},{12,10},{14,12},{11,9},... | collective-permute-start | bytes 307208 | tf_op jit(solution)/shard_map/ppermute | solution.py:455
  167.3 14.1 %collective-permute-start.22 = (bf16[400,128]{1,0:T(8,128)(2,1)S(1)}, bf16[400,128]{1,0:T(8,128)(2,1)S(1)}, u32[]{:S(2)}, u32[]{:S(2)}) collective-permute-start(bf16[400,128]{1,0:T(8,128)(2,1)S(1)} %get-tuple-element.105), channel_id=1, source_target_pairs={{4,0},{6,2},{5,1},{7,3},{12,8},{14,10},{13,9},{15,11},{20,16},{22,... | collective-permute-start | bytes 307208 | tf_op jit(solution)/shard_map/ppermute | solution.py:455
  168.6 12.8 %collective-permute-start.23 = (bf16[400,128]{1,0:T(8,128)(2,1)S(1)}, bf16[400,128]{1,0:T(8,128)(2,1)S(1)}, u32[]{:S(2)}, u32[]{:S(2)}) collective-permute-start(bf16[400,128]{1,0:T(8,128)(2,1)S(1)} %get-tuple-element.105), channel_id=1, source_target_pairs={{6,0},{7,1},{14,8},{15,9},{22,16},{23,17},{30,24},{31,25}} | collective-permute-start | bytes 307208 | tf_op jit(solution)/shard_map/ppermute | solution.py:455
  185.9 14.3 %collective-permute-start.30 = (bf16[4,96,640]{2,1,0:T(8,128)(2,1)}, bf16[4,96,640]{2,1,0:T(8,128)(2,1)S(1)}, u32[]{:S(2)}, u32[]{:S(2)}) collective-permute-start(bf16[4,96,640]{2,1,0:T(8,128)(2,1)} %get-tuple-element.111), channel_id=1, source_target_pairs={{0,16},{8,24},{16,0},{24,8},{1,17},{9,25},{17,1},{25,9},{2,18},{10... | collective-permute-start | bytes 1474568 | tf_op jit(solution)/shard_map/ppermute | solution.py:449
  188.9 11.7 %collective-permute-start.25 = (bf16[4,96,256]{2,1,0:T(8,128)(2,1)S(1)}, bf16[4,96,256]{2,1,0:T(8,128)(2,1)S(1)}, u32[]{:S(2)}, u32[]{:S(2)}) collective-permute-start(bf16[4,96,256]{2,1,0:T(8,128)(2,1)S(1)} %fusion.9), channel_id=1, source_target_pairs={{0,1},{1,0},{2,3},{3,2},{4,5},{5,4},{6,7},{7,6},{8,9},{9,8},{10,11... | collective-permute-start | bytes 589832 | tf_op jit(solution)/shard_map/ppermute | solution.py:441
  190.0 35.3 %collective-permute-start.42 = (bf16[192,384]{1,0:T(8,128)(2,1)S(1)}, bf16[192,384]{1,0:T(8,128)(2,1)S(1)}, u32[]{:S(2)}, u32[]{:S(2)}) collective-permute-start(bf16[192,384]{1,0:T(8,128)(2,1)S(1)} %copy-done.40), channel_id=1, source_target_pairs={{0,16},{8,24},{16,0},{24,8},{1,17},{9,25},{17,1},{25,9},{2,18},{10... | collective-permute-start | bytes 442376 | tf_op jit(solution)/shard_map/ppermute | solution.py:449
  190.5 39.7 %collective-permute-start.43 = (bf16[192,384]{1,0:T(8,128)(2,1)S(1)}, bf16[192,384]{1,0:T(8,128)(2,1)S(1)}, u32[]{:S(2)}, u32[]{:S(2)}) collective-permute-start(bf16[192,384]{1,0:T(8,128)(2,1)S(1)} %copy-done.40), channel_id=1, source_target_pairs={{0,8},{8,0},{16,24},{24,16},{1,9},{9,1},{17,25},{25,17},{2,10},{10... | collective-permute-start | bytes 442376 | tf_op jit(solution)/shard_map/ppermute | solution.py:445
  200.5 10.9 %collective-permute-start.31 = (bf16[96,640]{1,0:T(8,128)(2,1)S(1)}, bf16[96,640]{1,0:T(8,128)(2,1)S(1)}, u32[]{:S(2)}, u32[]{:S(2)}) collective-permute-start(bf16[96,640]{1,0:T(8,128)(2,1)S(1)} %get-tuple-element.142), channel_id=1, source_target_pairs={{0,2},{2,4},{4,6},{6,0},{1,3},{3,5},{5,7},{7,1},{8,10},{10,12},{12... | collective-permute-start | bytes 368648 | tf_op jit(solution)/shard_map/ppermute | solution.py:460
  200.5 17.8 %collective-permute-start.32 = (bf16[96,640]{1,0:T(8,128)(2,1)S(1)}, bf16[96,640]{1,0:T(8,128)(2,1)S(1)}, u32[]{:S(2)}, u32[]{:S(2)}) collective-permute-start(bf16[96,640]{1,0:T(8,128)(2,1)S(1)} %get-tuple-element.144), channel_id=1, source_target_pairs={{0,4},{2,6},{4,0},{6,2},{1,5},{3,7},{5,1},{7,3},{8,12},{10,14},{12... | collective-permute-start | bytes 368648 | tf_op jit(solution)/shard_map/ppermute | solution.py:460
  200.6 17.7 %collective-permute-start.33 = (bf16[96,640]{1,0:T(8,128)(2,1)S(1)}, bf16[96,640]{1,0:T(8,128)(2,1)S(1)}, u32[]{:S(2)}, u32[]{:S(2)}) collective-permute-start(bf16[96,640]{1,0:T(8,128)(2,1)S(1)} %get-tuple-element.143), channel_id=1, source_target_pairs={{0,6},{2,0},{4,2},{6,4},{1,7},{3,1},{5,3},{7,5},{8,14},{10,8},{12,... | collective-permute-start | bytes 368648 | tf_op jit(solution)/shard_map/ppermute | solution.py:460
  211.3 12.4 %collective-permute-start.26 = (bf16[2,96,256]{2,1,0:T(8,128)(2,1)S(1)}, bf16[2,96,256]{2,1,0:T(8,128)(2,1)S(1)}, u32[]{:S(2)}, u32[]{:S(2)}) collective-permute-start(bf16[2,96,256]{2,1,0:T(8,128)(2,1)S(1)} %get-tuple-element.149), channel_id=1, source_target_pairs={{0,2},{2,4},{4,6},{6,0},{1,3},{3,5},{5,7},{7,1},{8,10},{10,12},{12... | collective-permute-start | bytes 294920 | tf_op jit(solution)/shard_map/ppermute | solution.py:460
  218.3 9.1 %collective-permute-start.27 = (bf16[2,96,256]{2,1,0:T(8,128)(2,1)S(1)}, bf16[2,96,256]{2,1,0:T(8,128)(2,1)S(1)}, u32[]{:S(2)}, u32[]{:S(2)}) collective-permute-start(bf16[2,96,256]{2,1,0:T(8,128)(2,1)S(1)} %get-tuple-element.150), channel_id=1, source_target_pairs={{0,4},{2,6},{4,0},{6,2},{1,5},{3,7},{5,1},{7,3},{8,12},{10,14},{12... | collective-permute-start | bytes 294920 | tf_op jit(solution)/shard_map/ppermute | solution.py:460
  218.3 9.9 %collective-permute-start.28 = (bf16[2,96,256]{2,1,0:T(8,128)(2,1)S(1)}, bf16[2,96,256]{2,1,0:T(8,128)(2,1)S(1)}, u32[]{:S(2)}, u32[]{:S(2)}) collective-permute-start(bf16[2,96,256]{2,1,0:T(8,128)(2,1)S(1)} %get-tuple-element.148), channel_id=1, source_target_pairs={{0,6},{2,0},{4,2},{6,4},{1,7},{3,1},{5,3},{7,5},{8,14},{10,8},{12,... | collective-permute-start | bytes 294920 | tf_op jit(solution)/shard_map/ppermute | solution.py:460
  225.3 9.3 %collective-permute-start.35 = (bf16[96,640]{1,0:T(8,128)(2,1)S(1)}, bf16[96,640]{1,0:T(8,128)(2,1)S(1)}, u32[]{:S(2)}, u32[]{:S(2)}) collective-permute-start(bf16[96,640]{1,0:T(8,128)(2,1)S(1)} %fusion.8.refs_0_), channel_id=1, source_target_pairs={{0,8},{8,0},{16,24},{24,16},{1,9},{9,1},{17,25},{25,17},{2,10},{10... | collective-permute-start | bytes 368648 | tf_op jit(solution)/shard_map/ppermute | solution.py:445
  228.7 8.6 %collective-permute-start.39 = (bf16[192,576]{1,0:T(8,128)(2,1)}, bf16[192,576]{1,0:T(8,128)(2,1)S(1)}, u32[]{:S(2)}, u32[]{:S(2)}) collective-permute-start(bf16[192,576]{1,0:T(8,128)(2,1)} %reduce-scatter.5.cloned.1.call-done.refs_0_), channel_id=1, source_target_pairs={{0,16},{8,24},{16,0},{24,8},{1,17},{9,25},{17,1},{25,9},{2,18},{10... | collective-permute-start | bytes 663560 | tf_op jit(solution)/shard_map/ppermute | solution.py:449
  230.2 8.1 %collective-permute-start.29 = (bf16[2,96,512]{2,1,0:T(8,128)(2,1)S(1)}, bf16[2,96,512]{2,1,0:T(8,128)(2,1)S(1)}, u32[]{:S(2)}, u32[]{:S(2)}) collective-permute-start(bf16[2,96,512]{2,1,0:T(8,128)(2,1)S(1)} %broadcast_select_fusion.2), channel_id=1, source_target_pairs={{0,1},{1,0},{2,3},{3,2},{4,5},{5,4},{6,7},{7,6},{8,9},{9,8},{10,11... | collective-permute-start | bytes 589832 | tf_op jit(solution)/shard_map/ppermute | solution.py:441
  (73 other events, 377.3 us)
Sparse Core Ops, SparseCore 0:
  35.5 30.2 all-gather.1
  152.3 22.9 reduce-scatter.2
  188.9 28.9 reduce-scatter.4

commit v3 on v2

--- a/solution.py
+++ b/solution.py
@@ -424,7 +424,7 @@
 
 def paired_layout(mesh):
     rows, cols, dps = mesh.shape["row"], mesh.shape["col"], mesh.shape["dp"]
-    return cols == 2 and dps == 4 and H % (2 * cols) == 0 and TOK_DEV * rows * cols <= SEQ_MAX
+    return rows == 4 and cols == 2 and dps == 4 and H % 4 == 0 and 8 * TOK_DEV <= SEQ_MAX
 
 
 low = jnp.bfloat16
@@ -455,75 +455,13 @@
     return lax.ppermute(operand, "row", pairs)
 
 
+def swap_rows(operand, mask):
+    return lax.ppermute(operand, "row", [(i, i ^ mask) for i in range(4)])
+
+
 def rotate_rows(operand, step):
     count = lax.axis_size("row")
     return lax.ppermute(operand, "row", [(i, (i + step) % count) for i in range(count)])
-
-
-def by_col(own, other):
-    first_col = lax.axis_index("col") == 0
-    return (jnp.where(first_col, own, other), jnp.where(first_col, other, own))
-
-
-def col_halves(operand, axis):
-    part = operand.shape[axis] // 2
-    return by_col(
-        lax.slice_in_dim(operand, 0, part, axis=axis),
-        lax.slice_in_dim(operand, part, 2 * part, axis=axis),
-    )
-
-
-def spread_tokens(blocks, extra):
-    rows = lax.axis_size("row")
-    row_idx = lax.axis_index("row")
-    count, feats, _ = blocks.shape
-    own, other = col_halves(blocks, 1)
-    whole = jnp.concatenate(by_col(own, swap_cols(other)), 2)
-    part = feats // 2
-
-    def piece(place):
-        cut = lax.dynamic_slice_in_dim(whole, place % rows * SPAN, SPAN, 2)
-        return jnp.concatenate([cut.reshape(count * part, SPAN), extra], 0)
-
-    total = count * part + extra.shape[0]
-    buf = jnp.zeros((rows, total, SPAN), low)
-    for step in range(rows):
-        sent = piece(row_idx + step)
-        got = rotate_rows(sent, step) if step else sent
-        buf = lax.dynamic_update_slice_in_dim(buf, got[None], (row_idx - step) % rows, 0)
-    halves = [buf[:, i * part : (i + 1) * part] for i in range(count)]
-    return halves, buf[:, count * part :]
-
-
-def join_halves(half):
-    pair = by_col(half, swap_cols(half))
-    return jnp.stack(pair, 1).reshape(-1, half.shape[2])
-
-
-def gather_tokens(halves):
-    rows = lax.axis_size("row")
-    row_idx = lax.axis_index("row")
-    pieces = jnp.stack(halves, 1)
-    _, count, part, _ = pieces.shape
-    buf = jnp.zeros((count, part, rows * SPAN), low)
-    for step in range(rows):
-        sent = lax.dynamic_index_in_dim(pieces, (row_idx + step) % rows, 0, False)
-        got = rotate_rows(sent, step) if step else sent
-        buf = lax.dynamic_update_slice_in_dim(buf, got, (row_idx - step) % rows * SPAN, 2)
-    own, other = col_halves(buf, 2)
-    return jnp.concatenate(by_col(own, swap_cols(other)), 1)
-
-
-def feature_halves(full):
-    rows = lax.axis_size("row")
-    feats, count = full.shape
-    cut = full.reshape(rows, 2, feats // rows // 2, count)
-    return by_col(cut[:, 0], cut[:, 1])
-
-
-def column_parts(own_part, other_part):
-    half = (own_part + swap_pair(other_part).astype(wide)).astype(low)
-    return half, swap_cols(half)
 
 
 def dot_tn(left, right):
@@ -554,19 +492,230 @@
     return inv_std * (grad_normed - mean_one - normed * mean_two)
 
 
-def local_call(body, outs, name, *operands, scratch=()):
+def local_call(body, outs, name, *operands, scratch=(), space=None):
+    shapes = [jax.ShapeDtypeStruct(shape, kind) for shape, kind in outs]
     return pl.pallas_call(
         body,
-        out_shape=[jax.ShapeDtypeStruct(shape, kind) for shape, kind in outs],
+        out_shape=shapes,
         in_specs=[
-            pl.BlockSpec(memory_space=pltpu.SMEM if operand.dtype == jnp.int32 else pltpu.VMEM)
+            pl.BlockSpec(
+                memory_space=pltpu.SMEM
+                if operand.dtype == jnp.int32
+                else space or pltpu.VMEM
+            )
             for operand in operands
         ],
         out_specs=[pl.BlockSpec(memory_space=pltpu.VMEM)] * len(outs),
-        scratch_shapes=[pltpu.VMEM(shape, kind) for shape, kind in scratch],
+        scratch_shapes=[
+            pltpu.VMEM(*kind) if isinstance(kind, tuple) else kind for kind in scratch
+        ],
         compiler_params=pltpu.CompilerParams(vmem_limit_bytes=24 * 2**20),
         name=name,
     )(*operands)
+
+
+CORE, COPY, ROW, COL, SEQ = range(5)
+
+
+def low_outs(count, *shape):
+    return [(shape, low)] * count
+
+
+def turn_body(flags_ref, lengths_ref, trig_ref, reweight_ref, *, seq_len):
+    start = flags_ref[ROW] * SPAN
+    positions = start + lax.broadcasted_iota(jnp.int32, (8, SPAN), 1)
+    lines = lax.broadcasted_iota(jnp.int32, (8, SPAN), 0)
+    angles = math.pi * positions.astype(wide) / (2.0 * seq_len)
+    turns = jnp.where(lines == 0, jnp.cos(angles), jnp.where(lines == 1, jnp.sin(angles), 0.0))
+    own = lengths_ref[flags_ref[SEQ]]
+    other = lengths_ref[flags_ref[SEQ] + 1 - 2 * flags_ref[CORE]]
+    limits = jnp.where(lines == 2, own, other)
+    present = jnp.where(positions < limits, 1.0, 0.0)
+    trig_ref[...] = turns + jnp.where(lines == 2, present, jnp.where(lines == 3, present, 0.0))
+    rows = lax.broadcasted_iota(jnp.int32, (SPAN, SPAN), 0)
+    cols = lax.broadcasted_iota(jnp.int32, (SPAN, SPAN), 1)
+    both = lax.dot_general(
+        turns, turns, (((0,), (0,)), ((), ())), precision=highest, preferred_element_type=wide
+    )
+    reweight_ref[...] = jnp.where(rows <= cols, both, 0.0)
+
+
+def token_piece(flags_ref, own_ref, recv_ref, step, rows):
+    place = lax.rem(flags_ref[ROW] + step, rows)
+    half = lax.div(place, rows // 2)
+    cols = pl.ds(pl.multiple_of(lax.rem(place, rows // 2) * SPAN, SPAN), SPAN)
+    return jnp.where(half == flags_ref[COL], own_ref[:, cols], recv_ref[:, cols])
+
+
+def pieces_body(flags_ref, own_ref, cot_ref, recv_ref, *refs, rows):
+    vec_ref, piece_refs = refs[0], refs[1:]
+    part = own_ref.shape[0]
+    lines = []
+    for line in range(4):
+        vec = vec_ref[line : line + 1, :]
+        vec = jnp.concatenate([vec, jnp.zeros((1, SPAN - vec.shape[1]), wide)], 1)
+        high = vec.astype(low).astype(wide)
+        lines = lines + [high, vec - high]
+    for step, ref in enumerate(piece_refs):
+        ref[:part] = token_piece(flags_ref, own_ref, recv_ref.at[:part], step, rows)
+        ref[part : 2 * part] = token_piece(flags_ref, cot_ref, recv_ref.at[part:], step, rows)
+        ref[2 * part :] = jnp.concatenate(lines + [jnp.zeros((8, SPAN), wide)], 0).astype(low)
+
+
+def came_from(flags_ref, step, rows):
+    return lax.rem(flags_ref[ROW] + rows - step, rows)
+
+
+def place_tokens_body(flags_ref, *refs, rows, part):
+    pieces, (half_ref, cot_ref, vec_ref) = refs[:rows], refs[rows:]
+    for step, ref in enumerate(pieces):
+        row = came_from(flags_ref, step, rows)
+        half_ref[pl.ds(pl.multiple_of(row * part, 16), part), :] = ref[:part]
+        cot_ref[pl.ds(pl.multiple_of(row * part, 16), part), :] = ref[part : 2 * part]
+        extra = ref[2 * part :].astype(wide)
+        sums = [extra[2 * i : 2 * i + 1] + extra[2 * i + 1 : 2 * i + 2] for i in range(4)]
+        columns = jnp.concatenate(sums + [jnp.zeros((4, SPAN), wide)], 0).T
+        vec_ref[pl.ds(pl.multiple_of(row * 2 * part, 8), 2 * part), :] = columns[: 2 * part]
+
+
+def join_halves_body(flags_ref, half_ref, recv_ref, full_ref, *, rows):
+    part = half_ref.shape[0] // rows
+    first_col = flags_ref[COL] == 0
+    for row in range(rows):
+        own = half_ref[row * part : (row + 1) * part]
+        other = recv_ref[row * part : (row + 1) * part]
+        full_ref[2 * row * part : (2 * row + 1) * part] = jnp.where(first_col, own, other)
+        full_ref[(2 * row + 1) * part : (2 * row + 2) * part] = jnp.where(first_col, other, own)
+
+
+def add_body(own_ref, recv_ref, half_ref):
+    half_ref[...] = (own_ref[...] + recv_ref[...].astype(wide)).astype(low)
+
+
+def feature_piece(flags_ref, source, step, rows):
+    part = source.shape[0] // (2 * rows)
+    start = (lax.rem(flags_ref[ROW] + step, rows) * 2 + flags_ref[COL]) * part
+    return source[pl.ds(pl.multiple_of(start, 16), part), :]
+
+
+def place_back(flags_ref, pieces, rows, own_ref, other_ref):
+    half = len(pieces) // 2
+    for row, piece in zip(rows, pieces):
+        cols = pl.ds(pl.multiple_of(lax.rem(row, half) * SPAN, SPAN), SPAN)
+        mine = lax.div(row, half) == flags_ref[COL]
+
+        @pl.when(mine)
+        def _(piece=piece, cols=cols):
+            own_ref[:, cols] = piece[...]
+
+        @pl.when(jnp.logical_not(mine))
+        def _(piece=piece, cols=cols):
+            other_ref[:, cols] = piece[...]
+
+
+def sum_of(refs):
+    total = refs[0][...].astype(wide)
+    for ref in refs[1:]:
+        total = total + ref[...].astype(wide)
+    return total
+
+
+def join_back_body(flags_ref, own_ref, recv_ref, out_ref):
+    part = own_ref.shape[0]
+    first_col = flags_ref[COL] == 0
+    out_ref[:part] = jnp.where(first_col, own_ref[...], recv_ref[...]).astype(out_ref.dtype)
+    out_ref[part:] = jnp.where(first_col, recv_ref[...], own_ref[...]).astype(out_ref.dtype)
+
+
+def input_halves_body(flags_ref, own_ref, recv_ref, half_ref, sent_ref, sum_ref, *, rows):
+    part = own_ref.shape[0] // (2 * rows)
+    sum_ref[...] = own_ref[...] + recv_ref[...].astype(wide)
+    for row in range(rows):
+        rows_out = slice(row * part, (row + 1) * part)
+        mine = pl.multiple_of((2 * row + flags_ref[COL]) * part, 16)
+        theirs = pl.multiple_of((2 * row + 1 - flags_ref[COL]) * part, 16)
+        half_ref[rows_out] = sum_ref[pl.ds(mine, part), :]
+        sent_ref[rows_out] = sum_ref[pl.ds(theirs, part), :].astype(low)
+
+
+def last_pieces_body(
+    flags_ref, kept_ref, got_ref, half_ref, recv_ref, hidden_ref, held_ref, sent_ref
+):
+    rows = kept_ref.shape[0]
+    part = half_ref.shape[0] // rows
+    lanes = kept_ref.shape[2]
+    for mask in range(rows):
+        ref = sent_ref if mask % 2 else held_ref
+        out = slice(mask // 2 * part, (mask // 2 + 1) * part)
+        place = partner(flags_ref[ROW], mask)
+        ref[out, :lanes] = (kept_ref[place].astype(wide) + got_ref[place].astype(wide)).astype(low)
+        rows_in = pl.ds(pl.multiple_of(place * part, 16), part)
+        total = half_ref[rows_in, :] + recv_ref[rows_in, :].astype(wide)
+        start = pl.multiple_of((place * 2 + flags_ref[COL]) * part, 16)
+        ref[out, lanes:] = (total + hidden_ref[pl.ds(start, part), :]).astype(low)
+
+
+def last_pairs_body(held_ref, got_ref, sum_ref, sent_ref):
+    part, lanes = sum_ref.shape
+    sum_ref[...] = held_ref[:part, :lanes].astype(wide) + got_ref[:part, :lanes].astype(wide)
+    pair = held_ref[part:, :lanes].astype(wide) + got_ref[part:, :lanes].astype(wide)
+    sent_ref[:, :lanes] = pair.astype(low)
+    sent_ref[:, lanes : lanes + SPAN] = held_ref[part:, lanes:]
+    sent_ref[:, lanes + SPAN :] = got_ref[part:, lanes:]
+
+
+def last_sums_body(
+    flags_ref, part_ref, held_ref, got_ref, far_ref, sum_ref, own_ref, other_ref
+):
+    part, lanes = part_ref.shape
+    sum_ref[...] = (part_ref[...] + far_ref[:, :lanes].astype(wide)).astype(low)
+    pieces = (
+        held_ref.at[:part, lanes:],
+        got_ref.at[:part, lanes:],
+        far_ref.at[:, lanes : lanes + SPAN],
+        far_ref.at[:, lanes + SPAN :],
+    )
+    rows = [partner(flags_ref[ROW], mask) for mask in range(4)]
+    place_back(flags_ref, pieces, rows, own_ref, other_ref)
+
+
+def pair_pieces_body(flags_ref, kept_ref, got_ref, *refs):
+    extras, (held_ref, sent_ref) = refs[:-2], refs[-2:]
+    rows = 4
+    feats, part = kept_ref.shape[0] // rows, kept_ref.shape[1]
+    for mask in range(rows):
+        ref = sent_ref if mask % 2 else held_ref
+        out = slice(mask // 2 * feats, (mask // 2 + 1) * feats)
+        place = partner(flags_ref[ROW], mask)
+        rows_in = pl.ds(pl.multiple_of(place * feats, 16), feats)
+        ref[out, :part] = (
+            kept_ref[rows_in, :].astype(wide) + got_ref[rows_in, :].astype(wide)
+        ).astype(low)
+        for extra in extras:
+            ref[out, part:] = extra[rows_in, :]
+
+
+def pair_sums_body(held_ref, got_ref, sum_ref, sent_ref):
+    feats = sum_ref.shape[0]
+    sum_ref[...] = held_ref[:feats].astype(wide) + got_ref[:feats].astype(wide)
+    sent_ref[...] = (held_ref[feats:].astype(wide) + got_ref[feats:].astype(wide)).astype(low)
+
+
+def hidden_sums_body(down_ref, down_far_ref, up_ref, up_far_ref, sum_ref):
+    part = down_ref.shape[1]
+    sum_ref[:, :part] = (down_ref[...] + down_far_ref[...].astype(wide)).astype(low)
+    sum_ref[:, part:] = (up_ref[...] + up_far_ref[...].astype(wide)).astype(low)
+
+
+def out_pieces_body(flags_ref, result_ref, *refs):
+    for step, ref in enumerate(refs):
+        ref[...] = feature_piece(flags_ref, result_ref, step, len(refs))
+
+
+def out_place_body(flags_ref, *refs):
+    pieces = refs[:-2]
+    rows = [came_from(flags_ref, step, len(pieces)) for step in range(len(pieces))]
+    place_back(flags_ref, pieces, rows, *refs[-2:])
 
 
 def head_sets():
@@ -610,29 +759,54 @@
     return state[place * HD : (place + 1) * HD]
 
 
-def pack_first_body(flags_ref, query_ref, key_ref, value_ref, out_ref, packed_ref):
-    first_core = flags_ref[0] == 0
-    first_copy = flags_ref[1] == 0
-    for place, (left_ref, right_ref) in enumerate(((query_ref, value_ref), (key_ref, out_ref))):
-        left = jnp.where(first_core, left_ref[:, :WIDTH], left_ref[:, WIDTH:])
-        right = jnp.where(first_core, right_ref[:, :WIDTH], right_ref[:, WIDTH:])
-        packed_ref[:, place * WIDTH : (place + 1) * WIDTH] = jnp.where(first_copy, left, right)
-
-
-def pack_hidden_body(flags_ref, up_ref, down_ref, packed_ref):
+def pack_hidden_body(flags_ref, up_ref, down_ref, mine_ref, copy_ref, sems):
+    part = mine_ref.shape[1] // 2
+    copies = []
+    for half, packed_ref in enumerate((mine_ref, copy_ref)):
+        copy = 1 - flags_ref[COPY] if half else flags_ref[COPY]
+        start = pl.multiple_of((flags_ref[CORE] * 2 + copy) * part, 128)
+        for place, ref in enumerate((up_ref, down_ref)):
+            copies.append(
+                pltpu.make_async_copy(
+                    ref.at[:, pl.ds(start, part)],
+                    packed_ref.at[:, pl.ds(place * part, part)],
+                    sems.at[2 * half + place],
+                )
+            )
+    for copy in copies:
+        copy.start()
+    for copy in copies:
+        copy.wait()
+
+
+def partner(row, mask):
+    if mask == 0:
+        return row
+    if mask == 1:
+        return row + 1 - 2 * lax.rem(row, 2)
+    return lax.rem(row + 2, 4) if mask == 2 else 3 - row
+
+
+def row_block(flags_ref, mask, feats):
+    return pl.ds(pl.multiple_of(partner(flags_ref[ROW], mask) * feats, 16), feats)
+
+
+def project_body(flags_ref, own_ref, other_ref, trig_ref, packed_ref, *refs):
+    weight_ref, qkv_ref, state_ref = refs[-3:]
+    blocks = refs[:-3]
+    count = len(blocks) // 2
+    first_copy = flags_ref[COPY] == 0
+    feats = packed_ref.shape[0]
     part = packed_ref.shape[1] // 2
-    start = pl.multiple_of((flags_ref[0] * 2 + flags_ref[1]) * part, 128)
-    packed_ref[:, :part] = up_ref[:, pl.ds(start, part)]
-    packed_ref[:, part:] = down_ref[:, pl.ds(start, part)]
-
-
-def project_body(
-    flags_ref, mine_ref, copy_ref, own_ref, other_ref, trig_ref, weight_ref, qkv_ref, state_ref
-):
-    first_copy = flags_ref[1] == 0
-    part = mine_ref.shape[1]
-    weight_ref[:, :part] = jnp.where(first_copy, mine_ref[...], copy_ref[...])
-    weight_ref[:, part:] = jnp.where(first_copy, copy_ref[...], mine_ref[...])
+
+    def rows_of(mask):
+        return row_block(flags_ref, mask, feats)
+
+    weight_ref[rows_of(0), :] = packed_ref[...]
+    for step in range(1, count + 1):
+        mine, copied = blocks[step - 1][...], blocks[count + step - 1][...]
+        weight_ref[rows_of(step), :part] = jnp.where(first_copy, mine, copied)
+        weight_ref[rows_of(step), part:] = jnp.where(first_copy, copied, mine)
     matrix = weight_ref[:, : 3 * WIDTH]
     for seq, x_ref in enumerate((own_ref, other_ref)):
         qkv_ref[seq] = dot_tn(matrix, x_ref[...]).astype(low)
@@ -666,8 +840,8 @@
     weight_ref,
     *refs,
 ):
-    arrived = refs[:-6]
-    prior_ref, attn_ref, attn_wide_ref, inverse_ref, own_ref, other_ref = refs[-6:]
+    arrived = refs[:-5]
+    prior_ref, attn_wide_ref, own_ref, other_ref, attn_ref = refs[-5:]
     total = arrived[0][...].astype(wide)
     for ref in arrived[1:]:
         total = total + ref[...].astype(wide)
@@ -684,9 +858,9 @@
         inverse = 1.0 / denom
         inverses = inverses + set_row(place) * inverse
         attended = numer * inverse
-        attn_wide_ref[place] = attended
+        attn_wide_ref[place * HD : (place + 1) * HD, :] = attended
         attn_ref[seq, head * HD : (head + 1) * HD, :] = attended.astype(low)
-    inverse_ref[...] = inverses
+    attn_wide_ref[STATE_ROWS:, :] = inverses
     own_ref[...] = dot_nn(matrix, attn_ref[0])
     other_ref[...] = dot_nn(matrix, attn_ref[1]).astype(low)
 
@@ -696,7 +870,6 @@
     other_ref,
     weight_ref,
     attn_wide_ref,
-    inverse_ref,
     qkv_ref,
     trig_ref,
     grad_num_ref,
@@ -710,11 +883,11 @@
         grads = dot_tn(matrix, grad_ref[...]).astype(low).astype(wide)
         for head in range(HEADS):
             place = seq * HEADS + head
-            inverse = jnp.sum(inverse_ref[...] * set_row(place), 0, keepdims=True)
+            inverse = jnp.sum(attn_wide_ref[STATE_ROWS:, :] * set_row(place), 0, keepdims=True)
             scaled = grads[head * HD : (head + 1) * HD] * inverse
             grad_num = scaled.astype(low)
             grad_num_ref[place] = grad_num
-            grad_den = -jnp.sum(scaled * attn_wide_ref[place], 0, keepdims=True)
+            grad_den = -jnp.sum(scaled * attn_wide_ref[place * HD : (place + 1) * HD, :], 0, keepdims=True)
             den_row = set_row(place) * grad_den
             dens = dens + den_row
             queries = turned(jnp.maximum(query_part(qkv_ref, seq, head), 0), trig_ref)
@@ -732,13 +905,9 @@
     reweight_ref,
     weights_ref,
     prior_ref,
-    own_ref,
-    other_ref,
-    attn_ref,
     grad_query_ref,
     grad_key_ref,
     grad_value_ref,
-    grad_out_ref,
 ):
     prior_sums = prior_ref[STATE_ROWS:, :]
     for seq, head, place in head_sets():
@@ -759,9 +928,6 @@
         ).astype(low)
         grad_key_ref[place] = dot_nt(queries, grad_scores)
         grad_value_ref[place] = dot_nt(grad_num, weights_ref[place])
-    grad_out_ref[...] = (
-        dot_nt(own_ref[...], attn_ref[0]) + dot_nt(other_ref[...], attn_ref[1])
-    ).astype(low)
 
 
 def grad_project_body(
@@ -805,7 +971,7 @@
         dot_nt(x_own_ref[...], grad_ref[0]) + dot_nt(x_other_ref[...], grad_ref[1])
     ).astype(low)
     rows, part, _ = kept_ref.shape
-    first_copy = flags_ref[1] == 0
+    first_copy = flags_ref[COPY] == 0
     for row in range(rows):
         start = row * 2 * part
         whole = jnp.concatenate(
@@ -819,13 +985,13 @@
     other_ref[...] = dot_nn(matrix, grad_ref[1]).astype(low)
 
 
-def norm_body(x_ref, half_ref, recv_ref, vec_ref, first_ref, low_ref, normed_ref, inv_ref):
+def norm_body(x_ref, half_ref, recv_ref, vec_ref, first_ref, low_ref, normed_ref):
     hidden = x_ref[...].astype(wide) + (half_ref[...].astype(wide) + recv_ref[...].astype(wide))
     first, normed, inv_std = norm_columns(hidden, vec_ref[:, 0:1], vec_ref[:, 1:2])
     first_ref[...] = first
     low_ref[...] = first.astype(low)
-    normed_ref[...] = normed
-    inv_ref[...] = jnp.broadcast_to(inv_std, inv_ref.shape)
+    normed_ref[:D, :] = normed
+    normed_ref[D:, :] = jnp.broadcast_to(inv_std, (8, SPAN))
 
 
 def lane_sums(columns, place):
@@ -837,7 +1003,7 @@
 
 
 def second_norm_body(
-    first_ref, half_ref, recv_ref, vec_ref, cot_ref, trig_ref, result_ref, grad_ref, low_ref, sum_ref
+    first_ref, half_ref, recv_ref, vec_ref, cot_ref, trig_ref, result_ref, grad_ref, low_ref
 ):
     hidden = first_ref[...] + (half_ref[...].astype(wide) + recv_ref[...].astype(wide))
     scale = vec_ref[:, 2:3]
@@ -845,26 +1011,28 @@
     result_ref[...] = result.astype(low)
     grad_in = cot_ref[...].astype(wide) * trig_ref[2:3, :]
     grad = norm_columns_back(grad_in, normed, inv_std, scale)
-    grad_ref[...] = grad
+    grad_ref[:, :SPAN] = grad
     low_ref[...] = grad.astype(low)
-    sum_ref[...] = lane_sums((grad_in * normed, grad_in), 2)
+    grad_ref[:, SPAN:] = lane_sums((grad_in * normed, grad_in), 2)
 
 
 def norm_back_body(
-    grad_ref, half_ref, recv_ref, normed_ref, inv_ref, vec_ref, part_ref, hidden_ref, low_ref, sum_ref
+    grad_ref, half_ref, recv_ref, normed_ref, vec_ref, hidden_ref, low_ref, sum_ref
 ):
-    grad_in = grad_ref[...] + (half_ref[...].astype(wide) + recv_ref[...].astype(wide))
-    normed = normed_ref[...]
-    grad = norm_columns_back(grad_in, normed, inv_ref[0:1, :], vec_ref[:, 0:1])
+    grad_in = grad_ref[:, :SPAN] + (half_ref[...].astype(wide) + recv_ref[...].astype(wide))
+    normed = normed_ref[:D, :]
+    grad = norm_columns_back(grad_in, normed, normed_ref[D : D + 1, :], vec_ref[:, 0:1])
     hidden_ref[...] = grad
     low_ref[...] = grad.astype(low)
-    sum_ref[...] = (lane_sums((grad_in * normed, grad_in), 0) + part_ref[...]).astype(low)
-
-
-def hidden_body(weight_ref, own_ref, other_ref, *refs):
-    act_ref, slope_ref, part_own_ref, part_other_ref = refs[-4:]
-    earlier = refs[:-4]
+    sum_ref[...] = (lane_sums((grad_in * normed, grad_in), 0) + grad_ref[:, SPAN:]).astype(low)
+
+
+def hidden_body(flags_ref, own_ref, other_ref, *refs):
+    weight_ref, act_ref, slope_ref, part_own_ref, part_other_ref = refs[-5:]
+    blocks, earlier = refs[:4], refs[4:-5]
     part = act_ref.shape[0]
+    for mask, ref in enumerate(blocks):
+        weight_ref[row_block(flags_ref, mask, ref.shape[0]), :] = ref[...]
     up = weight_ref[:, :part]
     down = weight_ref[:, part:]
     for seq, (x_ref, part_ref) in enumerate(
@@ -909,44 +1077,48 @@
         part_ref[...] = total.astype(part_ref.dtype)
 
 
-def pair_grad_body(own_ref, other_ref, mine_ref, copy_ref, kept_ref, sent_ref):
-    for hidden_ref, out_ref in ((copy_ref, sent_ref), (mine_ref, kept_ref)):
+def half_grads_body(own_ref, other_ref, mine_ref, copy_ref, kept_ref, sent_ref):
+    for pre_ref, out_ref in ((copy_ref, sent_ref), (mine_ref, kept_ref)):
         out_ref[...] = (
-            dot_nt(own_ref[...], hidden_ref[:, :SPAN]) + dot_nt(other_ref[...], hidden_ref[:, SPAN:])
+            dot_nt(own_ref[...], pre_ref[:, :SPAN]) + dot_nt(other_ref[...], pre_ref[:, SPAN:])
         ).astype(low)
 
 
-def place_hidden(flags_ref, refs, out_ref):
-    part = out_ref.shape[1] // 4
-    core, copy = flags_ref[0], flags_ref[1]
+def out_grad_body(own_ref, other_ref, attn_wide_ref, out_ref):
+    out_ref[...] = (
+        dot_nt(own_ref[...], attn_wide_ref[:WIDTH, :].astype(low))
+        + dot_nt(other_ref[...], attn_wide_ref[WIDTH : 2 * WIDTH, :].astype(low))
+    ).astype(low)
+
+
+def quarters(flags_ref, refs):
+    core, copy = flags_ref[CORE], flags_ref[COPY]
     for ref, other_core, other_copy in zip(refs, (0, 0, 1, 1), (0, 1, 0, 1)):
         core_place = 1 - core if other_core else core
         copy_place = 1 - copy if other_copy else copy
-        start = pl.multiple_of((core_place * 2 + copy_place) * part, 128)
-        out_ref[:, pl.ds(start, part)] = ref[:, :part].astype(wide)
-
-
-def place_down_body(flags_ref, *refs):
-    place_hidden(flags_ref, refs[:4], refs[4])
-
-
-def place_up_body(flags_ref, *refs):
-    up_ref, out_ref = refs[4:]
-    place_hidden(flags_ref, refs[:4], up_ref)
+        yield core_place * 2 + copy_place, ref
+
+
+def place_hidden_body(flags_ref, *refs):
+    down_ref, up_ref, out_ref = refs[4:]
     part = up_ref.shape[1] // 4
-    sums = [ref[:, part : part + WIDTH].astype(wide) for ref in refs[:4]]
+    for place, ref in quarters(flags_ref, refs[:4]):
+        cols = pl.ds(pl.multiple_of(place * part, 128), part)
+        down_ref[:, cols] = ref[:, :part].astype(wide)
+        up_ref[:, cols] = ref[:, part : 2 * part].astype(wide)
+    sums = [ref[:, 2 * part :].astype(wide) for ref in refs[:4]]
     own, other = sums[0] + sums[1], sums[2] + sums[3]
-    first_core = flags_ref[0] == 0
+    first_core = flags_ref[CORE] == 0
     out_ref[:, :WIDTH] = jnp.where(first_core, own, other)
     out_ref[:, WIDTH:] = jnp.where(first_core, other, own)
 
 
 def place_last_body(flags_ref, *refs):
     outs, vec_ref = refs[4:7], refs[7]
-    first_core = flags_ref[0] == 0
+    first_core = flags_ref[CORE] == 0
     part = refs[0].shape[0]
     for own_ref, other_ref, other_copy in ((refs[0], refs[2], 0), (refs[1], refs[3], 1)):
-        copy = 1 - flags_ref[1] if other_copy else flags_ref[1]
+        copy = 1 - flags_ref[COPY] if other_copy else flags_ref[COPY]
         rows = pl.ds(pl.multiple_of(copy * part, 8), part)
         own, other = own_ref[...].astype(wide), other_ref[...].astype(wide)
         for place, out_ref in enumerate(outs):
@@ -984,61 +1156,117 @@
 ):
     rows = lax.axis_size("row")
     seq_len = SPAN * rows
-    row_idx = lax.axis_index("row")
     dp_idx = lax.axis_index("dp")
-    core = dp_idx % 2
     feat_rows = tokens.shape[0]
-
-    positions = row_idx * SPAN + jnp.arange(SPAN, dtype=jnp.int32)
-    seq_pair = jnp.stack([dp_idx, dp_idx + 1 - 2 * core])
-    present = (positions[None, :] < seq_lengths(lengths, seq_pair)[:, None]).astype(wide)
-    angles = math.pi * positions.astype(wide) / (2.0 * seq_len)
-    cos = jnp.cos(angles)
-    sin = jnp.sin(angles)
-    ids = jnp.arange(SPAN, dtype=jnp.int32)
-    causal = (ids[:, None] <= ids[None, :]).astype(wide)
-    reweight = (cos[:, None] * cos[None, :] + sin[:, None] * sin[None, :]) * causal
-    trig = jnp.concatenate([jnp.stack([cos, sin], 0), present, jnp.zeros((4, SPAN), wide)], 0)
-
-    flags = jnp.stack([core, dp_idx // 2])
+    half_feats = feat_rows // 2
+    flags = jnp.stack(
+        [dp_idx % 2, dp_idx // 2, lax.axis_index("row"), lax.axis_index("col"), dp_idx]
+    )
+    trig, reweight = local_call(
+        partial(turn_body, seq_len=seq_len),
+        [((8, SPAN), wide), ((SPAN, SPAN), wide)],
+        "turn",
+        flags,
+        lengths,
+    )
+
+    def passed_on(pieces):
+        return [pieces[0]] + [
+            rotate_rows(piece, step) for step, piece in enumerate(pieces) if step
+        ]
+
+    def joined_halves(half, name):
+        return local_call(
+            partial(join_halves_body, rows=rows),
+            [((D, SPAN), low)],
+            name,
+            flags,
+            half,
+            swap_cols(half),
+        )[0]
+
+    def cols_back(own, other, kind, name):
+        return local_call(
+            join_back_body,
+            [((feat_rows, SPAN * rows // 2), kind)],
+            name,
+            flags,
+            own,
+            swap_cols(other),
+        )[0]
+
+    def column_parts(own_part, other_part, name):
+        (half,) = local_call(add_body, low_outs(1, D, SPAN), name, own_part, swap_pair(other_part))
+        return half, swap_cols(half)
+
+    first_col = lax.axis_index("col") == 0
+
+    def halved(block):
+        top, bottom = block[:half_feats], block[half_feats:]
+        return jnp.where(first_col, top, bottom), jnp.where(first_col, bottom, top)
+
+    (token_own, token_sent), (cot_own, cot_sent) = halved(tokens), halved(cotangent)
+    got = swap_cols(jnp.concatenate([token_sent, cot_sent], 0))
 
     part = w_up.shape[1] // 4
-    (first_packed,) = local_call(
-        pack_first_body,
-        [((feat_rows, 2 * WIDTH), low)],
-        "pack_first",
+    first_core = dp_idx % 2 == 0
+
+    def core_part(operand):
+        return jnp.where(first_core, operand[:, :WIDTH], operand[:, WIDTH:])
+
+    parts = [core_part(operand) for operand in (w_query, w_key, w_value, w_out.T)]
+    first_packed = jnp.concatenate(parts, 1)
+    first_mine = jnp.where(
+        dp_idx < 2, jnp.concatenate(parts[:2], 1), jnp.concatenate(parts[2:], 1)
+    )
+
+    def row_blocks(block):
+        return swap_rows(block, 1), swap_rows(block, 2)
+
+    first_one, first_two = row_blocks(first_mine)
+    first_one, got = lax.optimization_barrier((first_one, got))
+    first_blocks = [first_one, first_two, swap_rows(first_two, 1)]
+    first_blocks = first_blocks + [swap_copies(block) for block in first_blocks]
+    hidden_packed = local_call(
+        pack_hidden_body,
+        low_outs(2, feat_rows, 2 * part),
+        "pack_hidden",
         flags,
-        w_query,
-        w_key,
-        w_value,
-        w_out.T,
-    )
-    (hidden_packed,) = local_call(
-        pack_hidden_body, [((feat_rows, 2 * part), low)], "pack_hidden", flags, w_up, w_down.T
-    )
-    first_mine = gather_rows(first_packed)
-    hidden_mine = gather_rows(hidden_packed)
-    first_copy = swap_copies(first_mine)
-    hidden_copy = swap_copies(hidden_mine)
-
+        w_up,
+        w_down.T,
+        scratch=[pltpu.SemaphoreType.DMA((4,))],
+        space=pltpu.HBM,
+    )
     vecs = jnp.stack([gain_one, bias_one, gain_two, bias_two], 0)
-    vecs_high = vecs.astype(low)
-    vecs_rest = (vecs - vecs_high.astype(wide)).astype(low)
-    vec_rows = 8 * feat_rows // SPAN
-    extra = jnp.concatenate(
-        [
-            jnp.stack([vecs_high, vecs_rest], 0).reshape(vec_rows, SPAN),
-            jnp.zeros((-vec_rows % 16, SPAN), low),
-        ],
-        0,
-    )
-    (x_half, cot_half), got_vecs = spread_tokens(jnp.stack([tokens, cotangent], 0), extra)
-    x_own = join_halves(x_half)
+    token_pieces = local_call(
+        partial(pieces_body, rows=rows),
+        low_outs(rows, feat_rows + 16, SPAN),
+        "token_pieces",
+        flags,
+        token_own,
+        cot_own,
+        got,
+        vecs,
+    )
+    x_half, cot_half, norm_vecs = local_call(
+        partial(place_tokens_body, rows=rows, part=half_feats),
+        low_outs(2, D // 2, SPAN) + [((D, 8), wide)],
+        "token_place",
+        flags,
+        *passed_on(token_pieces),
+    )
+    x_half, trig, reweight, hidden_packed = lax.optimization_barrier(
+        (x_half, trig, reweight, hidden_packed)
+    )
+    hidden_one, hidden_two = row_blocks(hidden_packed[0])
+    x_own = joined_halves(x_half, "token_join")
+    cot = joined_halves(cot_half, "cot_join")
+    x_own, first_blocks, hidden_one, hidden_two, cot = lax.optimization_barrier(
+        (x_own, first_blocks, hidden_one, hidden_two, cot)
+    )
     x_other = swap_pair(x_own)
-    cot = join_halves(cot_half)
-    got_vecs = got_vecs[:, :vec_rows].reshape(rows, 2, 4, feat_rows).astype(wide)
-    norm_vecs = (got_vecs[:, 0] + got_vecs[:, 1]).transpose(0, 2, 1).reshape(D, 4)
-
+    hidden_three = swap_rows(hidden_two, 1)
+    copy_two = swap_copies(hidden_two)
     state_shape = ((STATE_ROWS + SUM_ROWS, 2 * HD), low)
     sets = 2 * HEADS
     block_low = ((D, SPAN), low)
@@ -1048,13 +1276,16 @@
         [((D, 4 * WIDTH), low), ((2, 3 * WIDTH, SPAN), low), state_shape],
         "project",
         flags,
-        first_mine,
-        first_copy,
         x_own,
         x_other,
         trig,
+        first_packed,
+        *first_blocks,
     )
     arrived = [shift_rows(state, step) for step in range(1, rows)]
+    arrived, hidden_three, copy_two = lax.optimization_barrier(
+        (arrived, hidden_three, copy_two)
+    )
     weights, numer, denom = local_call(
         block_body,
         [((sets, SPAN, SPAN), low), ((sets, HD, SPAN), wide), ((SUM_ROWS, SPAN), wide)],
@@ -1063,13 +1294,11 @@
         trig,
         reweight,
     )
-    prior, attn, attn_wide, inverse, branch_own, branch_other = local_call(
+    prior, attn_wide, branch_own, branch_other = local_call(
         attend_body,
         [
             state_shape,
-            ((2, WIDTH, SPAN), low),
-            ((sets, HD, SPAN), wide),
-            ((SUM_ROWS, SPAN), wide),
+            ((STATE_ROWS + SUM_ROWS, SPAN), wide),
             block_wide,
             block_low,
         ],
@@ -1080,11 +1309,16 @@
         denom,
         weight,
         *arrived,
-    )
-    branch = column_parts(branch_own, branch_other)
-    first, first_low, normed, inv_std = local_call(
+        scratch=[((2, WIDTH, SPAN), low)],
+    )
+    branch = column_parts(branch_own, branch_other, "branch_half")
+    copy_one, copy_three = swap_copies(hidden_one), swap_copies(hidden_three)
+    branch, copy_one, copy_three = lax.optimization_barrier((branch, copy_one, copy_three))
+    hidden_mine = [hidden_packed[0], hidden_one, hidden_two, hidden_three]
+    hidden_copy = [hidden_packed[1], copy_one, copy_two, copy_three]
+    first, first_low, normed = local_call(
         norm_body,
-        [block_wide, block_low, block_wide, ((8, SPAN), wide)],
+        [block_wide, block_low, ((D + 8, SPAN), wide)],
         "norm",
         x_own,
         *branch,
@@ -1092,28 +1326,31 @@
     )
     first_other = swap_pair(first_low)
     half_hidden = [((part, 2 * SPAN), low), ((part, 2 * SPAN), wide)]
-    act_mine, slope_mine, ffn_own, ffn_other = local_call(
+    hidden_weight = [((D, 2 * part), low)]
+    hidden_mine, act_mine, slope_mine, ffn_own, ffn_other = local_call(
         hidden_body,
-        half_hidden + [block_wide, block_wide],
+        hidden_weight + half_hidden + [block_wide, block_wide],
         "hidden_mine",
-        hidden_mine,
+        flags,
         first_low,
         first_other,
-    )
-    act_copy, slope_copy, ffn_own, ffn_other = local_call(
+        *hidden_mine,
+    )
+    hidden_copy, act_copy, slope_copy, ffn_own, ffn_other = local_call(
         hidden_body,
-        half_hidden + [block_wide, block_low],
+        hidden_weight + half_hidden + [block_wide, block_low],
         "hidden_copy",
-        hidden_copy,
+        flags,
         first_low,
         first_other,
+        *hidden_copy,
         ffn_own,
         ffn_other,
     )
-    ffn = column_parts(ffn_own, ffn_other)
-    result, grad_second, grad_ffn, sums_two = local_call(
+    ffn = column_parts(ffn_own, ffn_other, "ffn_half")
+    result, grad_second, grad_ffn = local_call(
         second_norm_body,
-        [block_low, block_wide, block_low, ((D, 2 * SUM_LANES), wide)],
+        [block_low, ((D, SPAN + 2 * SUM_LANES), wide), block_low],
         "second_norm",
         first,
         *ffn,
@@ -1122,6 +1359,20 @@
         trig,
     )
     grad_ffn_other = swap_pair(grad_ffn)
+    pair_low = ((D, part), low)
+    kept_down, sent_down = local_call(
+        half_grads_body,
+        [pair_low, pair_low],
+        "down_grad",
+        grad_ffn,
+        grad_ffn_other,
+        act_mine,
+        act_copy,
+    )
+    got_down = swap_copies(sent_down)
+    grad_ffn, grad_ffn_other, kept_down = lax.optimization_barrier(
+        (grad_ffn, grad_ffn_other, kept_down)
+    )
     hidden_low = ((part, 2 * SPAN), low)
     pre_mine, pre_copy, first_own_part, first_other_part = local_call(
         hidden_back_body,
@@ -1134,27 +1385,30 @@
         slope_mine,
         slope_copy,
     )
-    first_sum = column_parts(first_own_part, first_other_part)
-
-    def hidden_grad(own, other, mine, copied, name):
-        kept, sent = local_call(
-            pair_grad_body,
-            [((D, part), low), ((D, part), low)],
-            name,
-            own,
-            other,
-            mine,
-            copied,
-        )
-        return (kept.astype(wide) + swap_copies(sent).astype(wide)).astype(low)
-
-    def scatter_rows(partial_grad):
-        return lax.psum_scatter(partial_grad, "row", scatter_dimension=0, tiled=True)
-
-    down_rows = scatter_rows(
-        hidden_grad(grad_ffn, grad_ffn_other, act_mine, act_copy, "grad_down")
-    )
-    up_part = hidden_grad(first_low, first_other, pre_mine, pre_copy, "grad_up")
+    first_sum = column_parts(first_own_part, first_other_part, "first_half")
+
+    kept_up, sent_up = local_call(
+        half_grads_body,
+        [pair_low, pair_low],
+        "up_grad",
+        first_low,
+        first_other,
+        pre_mine,
+        pre_copy,
+    )
+    got_up = swap_copies(sent_up)
+    out_pieces = local_call(
+        out_pieces_body, low_outs(rows, half_feats, SPAN), "out_pieces", flags, result
+    )
+    out_wide = local_call(
+        out_place_body,
+        low_outs(2, half_feats, SPAN * rows // 2),
+        "out_place",
+        flags,
+        *passed_on(out_pieces),
+    )
+    first_sum, kept_up, out_wide = lax.optimization_barrier((first_sum, kept_up, out_wide))
+    output = cols_back(*out_wide, low, "out_join")
     grad_hidden, branch_grad, vec_sums = local_call(
         norm_back_body,
         [block_wide, block_low, ((D, 2 * SUM_LANES), low)],
@@ -1162,11 +1416,17 @@
         grad_second,
         *first_sum,
         normed,
-        inv_std,
         norm_vecs,
-        sums_two,
     )
     branch_grad_other = swap_pair(branch_grad)
+    (grad_out,) = local_call(
+        out_grad_body,
+        [((D, WIDTH), low)],
+        "out_grad",
+        branch_grad,
+        branch_grad_other,
+        attn_wide,
+    )
     grad_num, grad_den, grad_state = local_call(
         grad_attend_body,
         [((sets, HD, SPAN), low), ((SUM_ROWS, SPAN), wide), state_shape],
@@ -1175,18 +1435,16 @@
         branch_grad_other,
         weight,
         attn_wide,
-        inverse,
         qkv,
         trig,
     )
     later = [shift_rows(grad_state, -step) for step in range(1, rows)]
-    grad_query, grad_key, grad_value, grad_out = local_call(
+    grad_query, grad_key, grad_value = local_call(
         grad_block_body,
         [
             ((2, WIDTH, SPAN), low),
             ((sets, HD, SPAN), wide),
             ((sets, HD, SPAN), wide),
-            ((D, WIDTH), low),
         ],
         "grad_block",
         grad_num,
@@ -1196,12 +1454,41 @@
         reweight,
         weights,
         prior,
-        branch_grad,
-        branch_grad_other,
-        attn,
-    )
-    up_part, grad_out, down_rows = lax.optimization_barrier((up_part, grad_out, down_rows))
-    up_rows = scatter_rows(jnp.concatenate([up_part, grad_out], 1))
+    )
+    down_held, down_sent = local_call(
+        pair_pieces_body,
+        low_outs(2, 2 * feat_rows, part),
+        "down_pieces",
+        flags,
+        kept_down,
+        got_down,
+    )
+    down_got = swap_rows(down_sent, 1)
+    later, got_up, down_got = lax.optimization_barrier((later, got_up, down_got))
+
+    def pair_sums(held, got, name):
+        shape = (feat_rows, held.shape[1])
+        mine, sent = local_call(pair_sums_body, [(shape, wide), (shape, low)], name, held, got)
+        return mine, swap_rows(sent, 2)
+
+    down_sums = pair_sums(down_held, down_got, "down_sums")
+    up_held, up_sent = local_call(
+        pair_pieces_body,
+        low_outs(2, 2 * feat_rows, part + WIDTH),
+        "up_pieces",
+        flags,
+        kept_up,
+        got_up,
+        grad_out,
+    )
+    up_sums = pair_sums(up_held, swap_rows(up_sent, 1), "up_sums")
+    (hidden_sum,) = local_call(
+        hidden_sums_body,
+        low_outs(1, feat_rows, 2 * part + WIDTH),
+        "hidden_sums",
+        *down_sums,
+        *up_sums,
+    )
     half_rows = ((rows, feat_rows // 2, 3 * WIDTH + SUM_LANES), low)
     kept_w, sent_w, x_grad_own, x_grad_other = local_call(
         grad_project_body,
@@ -1220,41 +1507,62 @@
         *later,
         scratch=[state_shape, ((2, 3 * WIDTH, SPAN), low)],
     )
-    half_w = (kept_w.astype(wide) + swap_copies(sent_w).astype(wide)).astype(low)
-
-    own_x, other_x = feature_halves(x_grad_own + swap_pair(x_grad_other).astype(wide))
-    own_h, _ = feature_halves(grad_hidden)
-    own_x = own_x + swap_cols(other_x.astype(low)).astype(wide) + own_h
-    out_half, _ = feature_halves(result)
-    placed_back = gather_tokens([own_x.astype(low), out_half])
-    input_grad = placed_back[0].astype(wide)
-    output = placed_back[1]
-
-    last_rows = lax.dynamic_index_in_dim(half_w, row_idx, 0, False).astype(wide)
-    for step in range(1, rows):
-        sent = lax.dynamic_index_in_dim(half_w, (row_idx + step) % rows, 0, False)
-        last_rows = last_rows + rotate_rows(sent, step).astype(wide)
-
-    (down_t,) = local_call(
-        place_down_body,
-        [((feat_rows, 4 * part), wide)],
-        "place_down",
+    got_w = swap_copies(sent_w)
+    got_x = swap_pair(x_grad_other)
+    x_grad_own, got_x, got_w = lax.optimization_barrier((x_grad_own, got_x, got_w))
+    x_half_grad, x_half_sent = local_call(
+        partial(input_halves_body, rows=rows),
+        [((D // 2, SPAN), wide), ((D // 2, SPAN), low)],
+        "input_halves",
         flags,
-        *all_quarters(down_rows),
-    )
-    up_grad, out_t = local_call(
-        place_up_body,
-        [((feat_rows, 4 * part), wide), ((feat_rows, 2 * WIDTH), wide)],
-        "place_up",
+        x_grad_own,
+        got_x,
+        scratch=[block_wide],
+    )
+    last_lanes = 3 * WIDTH + SUM_LANES
+    last_held, last_sent = local_call(
+        last_pieces_body,
+        low_outs(2, 2 * half_feats, last_lanes + SPAN),
+        "last_pieces",
         flags,
-        *all_quarters(up_rows),
+        kept_w,
+        got_w,
+        x_half_grad,
+        swap_cols(x_half_sent),
+        grad_hidden,
+    )
+    last_got = swap_rows(last_sent, 1)
+    last_part, last_far = local_call(
+        last_pairs_body,
+        [((half_feats, last_lanes), wide), ((half_feats, last_lanes + 2 * SPAN), low)],
+        "last_pairs",
+        last_held,
+        last_got,
+    )
+    last_sum, *input_wide = local_call(
+        last_sums_body,
+        low_outs(1, half_feats, last_lanes) + low_outs(2, half_feats, SPAN * rows // 2),
+        "last_sums",
+        flags,
+        last_part,
+        last_held,
+        last_got,
+        swap_rows(last_far, 2),
+    )
+    input_grad = cols_back(*input_wide, wide, "input_join")
+    down_t, up_grad, out_t = local_call(
+        place_hidden_body,
+        [((feat_rows, 4 * part), wide)] * 2 + [((feat_rows, 2 * WIDTH), wide)],
+        "place_hidden",
+        flags,
+        *all_quarters(hidden_sum),
     )
     query_grad, key_grad, value_grad, vec_total = local_call(
         place_last_body,
         [((feat_rows, 2 * WIDTH), wide)] * 3 + [((feat_rows, SUM_LANES), wide)],
         "place_last",
         flags,
-        *all_quarters(last_rows.astype(low)),
+        *all_quarters(last_sum),
     )
     return (
         output,

time: 248 us -> 213 us (0.86)
  local copies, waits for them, and re-layouts: 24.9 us -> 1.05 us
  starting transfers between devices: 40.9 us -> 63.7 us
  blocking collectives: 16.6 us -> 0 us
  between operations: 14.7 us -> 1.19 us
  other arithmetic: 12.2 us -> 1.67 us
  waiting for transfers between devices: 105 us -> 109 us
    ppermute x0 -> x12, waiting for transfers between devices: none -> 35.8 us  [swap_rows(): return lax.ppermute(operand, 'row', [(i, i ^ mask) for i in range(4)])]
    unnamed x114 -> x22, local copies, waits for them, and re-layouts: 22.5 us -> 0.06 us
    ppermute x9 -> x6, waiting for transfers between devices: 25.6 us -> 6.04 us  [rotate_rows(): lax.ppermute(operand, 'row', [(i, (i + step) % count) for i in range(coun...]
    ppermute x8 -> x9, waiting for transfers between devices: 30.5 us -> 13.3 us  [swap_cols(): return lax.ppermute(operand, 'col', [(0, 1), (1, 0)])]
    all_gather x1 -> x0, blocking collectives: 16.6 us -> none  [gather_rows(): return lax.all_gather(operand, 'row', axis=0, tiled=True)]
    ppermute x0 -> x12, starting transfers between devices: none -> 14.8 us  [swap_rows(): return lax.ppermute(operand, 'row', [(i, i ^ mask) for i in range(4)])]
    ppermute x8 -> x11, waiting for transfers between devices: 31.8 us -> 38.8 us  [swap_copies(): lax.ppermute(operand, 'dp', [(i, i ^ 2) for i in range(lax.axis_size('dp'...]
    convert_element_type x13 -> x0, other arithmetic: 6.34 us -> none  [the longest x2 2.39 us: hidden_grad(): return (kept.astype(wide) + swap_copies(sent).astype(wide)).astype(low)]
  transfers between devices with their start and end apart: 48 -> 56, of which waited for: 25 -> 30; matrix products, arithmetic and copies ran while one was open for 5% -> 0% of each run, Pallas kernels for 10% -> 10%
where the time goes in v3:
time: 213 us; the launch traced here: 212 us
  waiting for transfers between devices  109 us (51%)
  starting transfers between devices  63.7 us (30%)
  Pallas kernels  35.3 us (17%)
    ppermute x11, waiting for transfers between devices, swap_copies(): lax.ppermute(operand, 'dp', [(i, i ^ 2) for i in range(lax.axis_size('dp'...  38.8 us
    ppermute x12, waiting for transfers between devices, swap_rows(): return lax.ppermute(operand, 'row', [(i, i ^ mask) for i in range(4)])  35.8 us
    pallas_call x39, Pallas kernels, local_call(): pl.pallas_call(body, out_shape=shapes, in_specs=[pl.BlockSpec(memory_spac...  35.3 us
    ppermute x12, starting transfers between devices, swap_rows(): return lax.ppermute(operand, 'row', [(i, i ^ mask) for i in range(4)])  14.8 us
    ppermute x9, waiting for transfers between devices, swap_cols(): return lax.ppermute(operand, 'col', [(0, 1), (1, 0)])  13.3 us
    ppermute x6, starting transfers between devices, rotate_rows(): lax.ppermute(operand, 'row', [(i, (i + step) % count) for i in range(coun...  12.9 us
    ppermute x11, starting transfers between devices, swap_copies(): lax.ppermute(operand, 'dp', [(i, i ^ 2) for i in range(lax.axis_size('dp'...  12 us
    ppermute x9, starting transfers between devices, swap_cols(): return lax.ppermute(operand, 'col', [(0, 1), (1, 0)])  11.7 us
  transfers between devices with their start and end apart: 56, of which 30 were waited for; matrix products, arithmetic and copies ran while one was open for 0% of the time, Pallas kernels for 10%

profile of v3, /device:TPU:0, one launch (start us, length us, event | category | flops | bytes accessed | tf_op | source)
XLA Modules:
  0.0 212.4 jit_solution(1853272953089854327)
XLA Ops:
  1.9 3.0 %collective-permute-start.1 = (bf16[192,512]{1,0:T(8,128)(2,1)S(1)}, bf16[192,512]{1,0:T(8,128)(2,1)S(1)}, u32[]{:S(2)}, u32[]{:S(2)}) collective-permute-start(bf16[192,512]{1,0:T(8,128)(2,1)S(1)} %pad_maximum_fusion.1), channel_id=1, source_target_pairs={{0,1},{1,0},{2,3},{3,2},{4,5},{5,4},{6,7},{7,6},{8,9},{9,8},{10,11... | collective-permute-start | bytes 589832 | tf_op jit(solution)/shard_map/ppermute | solution.py:441
  7.2 3.6 %collective-permute-done.refs_0_ = bf16[192,384]{1,0:T(8,128)(2,1)S(1)} collective-permute-done((bf16[192,384]{1,0:T(8,128)(2,1)S(1)}, bf16[192,384]{1,0:T(8,128)(2,1)S(1)}, u32[]{:S(2)}, u32[]{:S(2)}) %collective-permute-start) | collective-permute-done | bytes 147488 | tf_op jit(solution)/shard_map/ppermute | solution.py:459
  13.0 2.6 %collective-permute-start.3 = (bf16[208,256]{1,0:T(8,128)(2,1)S(1)}, bf16[208,256]{1,0:T(8,128)(2,1)S(1)}, u32[]{:S(2)}, u32[]{:S(2)}) collective-permute-start(bf16[208,256]{1,0:T(8,128)(2,1)S(1)} %get-tuple-element.145), channel_id=1, source_target_pairs={{0,4},{2,6},{4,0},{6,2},{1,5},{3,7},{5,1},{7,3},{8,12},{10,14},{12... | collective-permute-start | bytes 319496 | tf_op jit(solution)/shard_map/ppermute | solution.py:464
  19.1 4.2 %collective-permute-done.3.refs_2_ = bf16[208,256]{1,0:T(8,128)(2,1)S(1)} collective-permute-done((bf16[208,256]{1,0:T(8,128)(2,1)S(1)}, bf16[208,256]{1,0:T(8,128)(2,1)S(1)}, u32[]{:S(2)}, u32[]{:S(2)}) %collective-permute-start.3) | collective-permute-done | bytes 106528 | tf_op jit(solution)/shard_map/ppermute | solution.py:464
  26.1 3.9 %collective-permute-done.6.refs_1_ = bf16[192,384]{1,0:T(8,128)(2,1)S(1)} collective-permute-done((bf16[192,384]{1,0:T(8,128)(2,1)S(1)}, bf16[192,384]{1,0:T(8,128)(2,1)S(1)}, u32[]{:S(2)}, u32[]{:S(2)}) %collective-permute-start.6) | collective-permute-done | bytes 147488 | tf_op jit(solution)/shard_map/ppermute | solution.py:459
  30.5 3.0 %collective-permute-start.12 = (bf16[192,768]{1,0:T(8,128)(2,1)S(1)}, bf16[192,768]{1,0:T(8,128)(2,1)S(1)}, u32[]{:S(2)}, u32[]{:S(2)}) collective-permute-start(bf16[192,768]{1,0:T(8,128)(2,1)S(1)} %get-tuple-element.154.refs_0_), channel_id=1, source_target_pairs={{0,4},{2,6},{4,0},{6,2},{1,5},{3,7},{5,1},{7,3},{8,12},{10,14},{12... | collective-permute-start | bytes 884744 | tf_op jit(solution)/shard_map/ppermute | solution.py:459
  33.5 5.9 %collective-permute-done.7.refs_2_ = bf16[192,384]{1,0:T(8,128)(2,1)S(1)} collective-permute-done((bf16[192,384]{1,0:T(8,128)(2,1)S(1)}, bf16[192,384]{1,0:T(8,128)(2,1)S(1)}, u32[]{:S(2)}, u32[]{:S(2)}) %collective-permute-start.7) | collective-permute-done | bytes 147488 | tf_op jit(solution)/shard_map/ppermute | solution.py:459
  52.3 3.5 %collective-permute-start.17 = (bf16[400,128]{1,0:T(8,128)(2,1)S(1)}, bf16[400,128]{1,0:T(8,128)(2,1)S(1)}, u32[]{:S(2)}, u32[]{:S(2)}) collective-permute-start(bf16[400,128]{1,0:T(8,128)(2,1)S(1)} %get-tuple-element.169), channel_id=1, source_target_pairs={{0,6},{1,7},{8,14},{9,15},{16,22},{17,23},{24,30},{25,31}} | collective-permute-start | bytes 307208 | tf_op jit(solution)/shard_map/ppermute | solution.py:455
  57.2 2.7 %collective-permute-start.15 = (bf16[400,128]{1,0:T(8,128)(2,1)S(1)}, bf16[400,128]{1,0:T(8,128)(2,1)S(1)}, u32[]{:S(2)}, u32[]{:S(2)}) collective-permute-start(bf16[400,128]{1,0:T(8,128)(2,1)S(1)} %get-tuple-element.169), channel_id=1, source_target_pairs={{0,2},{2,4},{4,6},{1,3},{3,5},{5,7},{8,10},{10,12},{12,14},{9,11},... | collective-permute-start | bytes 307208 | tf_op jit(solution)/shard_map/ppermute | solution.py:455
  70.0 7.9 %collective-permute-done.22.refs_1_ = bf16[192,768]{1,0:T(8,128)(2,1)S(1)} collective-permute-done((bf16[192,768]{1,0:T(8,128)(2,1)S(1)}, bf16[192,768]{1,0:T(8,128)(2,1)S(1)}, u32[]{:S(2)}, u32[]{:S(2)}) %collective-permute-start.22) | collective-permute-done | bytes 294944 | tf_op jit(solution)/shard_map/ppermute | solution.py:449
  77.9 5.2 %collective-permute-done.23.refs_3_ = bf16[192,768]{1,0:T(8,128)(2,1)S(1)} collective-permute-done((bf16[192,768]{1,0:T(8,128)(2,1)S(1)}, bf16[192,768]{1,0:T(8,128)(2,1)S(1)}, u32[]{:S(2)}, u32[]{:S(2)}) %collective-permute-start.23) | collective-permute-done | bytes 294944 | tf_op jit(solution)/shard_map/ppermute | solution.py:449
  85.5 2.2 %hidden_mine.1 = (bf16[768,768]{1,0:T(8,128)(2,1)S(1)}, bf16[384,512]{1,0:T(8,128)(2,1)S(1)}, f32[384,512]{1,0:T(8,128)S(1)}, f32[768,256]{1,0:T(8,128)S(1)}, f32[768,256]{1,0:T(8,128)S(1)}) custom-call(s32[5]{0:T(128)S(1)} %stack.38.flags_ref, bf16[768,256]{1,0:T(8,128)(2,1)S(1)} %get-tuple-element.182.own_ref, ...), custom_call_target="tpu_custom_call" | custom-call | tf_op jit(solution)/shard_map/hidden_mine/pallas_call | solution.py:497
  87.7 2.2 %hidden_copy.1 = (bf16[768,768]{1,0:T(8,128)(2,1)S(1)}, bf16[384,512]{1,0:T(8,128)(2,1)S(1)}, f32[384,512]{1,0:T(8,128)S(1)}, f32[768,256]{1,0:T(8,128)S(1)}, bf16[768,256]{1,0:T(8,128)(2,1)S(1)}) custom-call(s32[5]{0:T(128)S(1)} %stack.38.flags_ref, bf16[768,256]{1,0:T(8,128)(2,1)S(1)} %get-tuple-element.182.own_ref, ...), custom_call_target="tpu_custom_call" | custom-call | tf_op jit(solution)/shard_map/hidden_copy/pallas_call | solution.py:497
  92.6 10.4 %collective-permute-done.26.recv_ref = bf16[768,256]{1,0:T(8,128)(2,1)S(1)} collective-permute-done((bf16[768,256]{1,0:T(8,128)(2,1)S(1)}, bf16[768,256]{1,0:T(8,128)(2,1)S(1)}, u32[]{:S(2)}, u32[]{:S(2)}) %collective-permute-start.26) | collective-permute-done | bytes 393248 | tf_op jit(solution)/shard_map/ppermute | solution.py:441
  107.1 1.8 hidden_back.1
  112.7 2.5 %collective-permute-start.30 = (bf16[96,256]{1,0:T(8,128)(2,1)S(1)}, bf16[96,256]{1,0:T(8,128)(2,1)S(1)}, u32[]{:S(2)}, u32[]{:S(2)}) collective-permute-start(bf16[96,256]{1,0:T(8,128)(2,1)S(1)} %get-tuple-element.209), channel_id=1, source_target_pairs={{0,2},{2,4},{4,6},{6,0},{1,3},{3,5},{5,7},{7,1},{8,10},{10,12},{12... | collective-permute-start | bytes 147464 | tf_op jit(solution)/shard_map/ppermute | solution.py:464
  117.8 2.0 collective-permute-start.31
  119.8 2.8 %collective-permute-start.32 = (bf16[96,256]{1,0:T(8,128)(2,1)S(1)}, bf16[96,256]{1,0:T(8,128)(2,1)S(1)}, u32[]{:S(2)}, u32[]{:S(2)}) collective-permute-start(bf16[96,256]{1,0:T(8,128)(2,1)S(1)} %get-tuple-element.211), channel_id=1, source_target_pairs={{0,6},{2,0},{4,2},{6,4},{1,7},{3,1},{5,3},{7,5},{8,14},{10,8},{12,... | collective-permute-start | bytes 147464 | tf_op jit(solution)/shard_map/ppermute | solution.py:464
  125.9 1.9 collective-permute-done.39.got_ref
  128.5 2.5 %collective-permute-start.40 = (bf16[384,384]{1,0:T(8,128)(2,1)S(1)}, bf16[384,384]{1,0:T(8,128)(2,1)S(1)}, u32[]{:S(2)}, u32[]{:S(2)}) collective-permute-start(bf16[384,384]{1,0:T(8,128)(2,1)S(1)} %get-tuple-element.234), channel_id=1, source_target_pairs={{0,2},{2,0},{4,6},{6,4},{1,3},{3,1},{5,7},{7,5},{8,10},{10,8},{12,... | collective-permute-start | bytes 884744 | tf_op jit(solution)/shard_map/ppermute | solution.py:459
  139.3 4.4 %collective-permute-done.37.refs_2_ = bf16[400,128]{1,0:T(8,128)(2,1)S(1)} collective-permute-done((bf16[400,128]{1,0:T(8,128)(2,1)S(1)}, bf16[400,128]{1,0:T(8,128)(2,1)S(1)}, u32[]{:S(2)}, u32[]{:S(2)}) %collective-permute-start.37) | collective-permute-done | bytes 102432 | tf_op jit(solution)/shard_map/ppermute | solution.py:455
  143.7 2.3 %grad_project.1 = (bf16[4,96,640]{2,1,0:T(8,128)(2,1)S(1)}, bf16[4,96,640]{2,1,0:T(8,128)(2,1)S(1)}, f32[768,256]{1,0:T(8,128)S(1)}, bf16[768,256]{1,0:T(8,128)(2,1)S(1)}) custom-call(bf16[2,192,256]{2,1,0:T(8,128)(2,1)S(1)} %get-tuple-element.226.grad_query_ref, f32[6,64,256]{2,1,0:T(8,128)S(1)} %get-tuple-element.227.grad_key_ref, ...), custom_call_target="tpu_custom_call" | custom-call | tf_op jit(solution)/shard_map/grad_project/pallas_call | solution.py:497
  147.7 1.9 collective-permute-start.51
  149.6 5.4 %collective-permute-done.42.got_ref = bf16[4,96,640]{2,1,0:T(8,128)(2,1)S(1)} collective-permute-done((bf16[4,96,640]{2,1,0:T(8,128)(2,1)S(1)}, bf16[4,96,640]{2,1,0:T(8,128)(2,1)S(1)}, u32[]{:S(2)}, u32[]{:S(2)}) %collective-permute-start.42) | collective-permute-done | bytes 491552 | tf_op jit(solution)/shard_map/ppermute | solution.py:449
  157.0 4.5 %collective-permute-done.51.got_ref = bf16[384,576]{1,0:T(8,128)(2,1)S(1)} collective-permute-done((bf16[384,576]{1,0:T(8,128)(2,1)S(1)}, bf16[384,576]{1,0:T(8,128)(2,1)S(1)}, u32[]{:S(2)}, u32[]{:S(2)}) %collective-permute-start.51) | collective-permute-done | bytes 442400 | tf_op jit(solution)/shard_map/ppermute | solution.py:459
  161.6 2.7 %collective-permute-start.52 = (bf16[192,576]{1,0:T(8,128)(2,1)S(1)}, bf16[192,576]{1,0:T(8,128)(2,1)S(1)}, u32[]{:S(2)}, u32[]{:S(2)}) collective-permute-start(bf16[192,576]{1,0:T(8,128)(2,1)S(1)} %get-tuple-element.267), channel_id=1, source_target_pairs={{0,4},{2,6},{4,0},{6,2},{1,5},{3,7},{5,1},{7,3},{8,12},{10,14},{12... | collective-permute-start | bytes 663560 | tf_op jit(solution)/shard_map/ppermute | solution.py:459
  167.2 14.7 %collective-permute-done.50.down_far_ref = bf16[192,384]{1,0:T(8,128)(2,1)S(1)} collective-permute-done((bf16[192,384]{1,0:T(8,128)(2,1)S(1)}, bf16[192,384]{1,0:T(8,128)(2,1)S(1)}, u32[]{:S(2)}, u32[]{:S(2)}) %collective-permute-start.50) | collective-permute-done | bytes 147488 | tf_op jit(solution)/shard_map/ppermute | solution.py:459
  183.8 8.2 %collective-permute-done.53.refs_1_ = bf16[192,960]{1,0:T(8,128)(2,1)S(1)} collective-permute-done((bf16[192,960]{1,0:T(8,128)(2,1)S(1)}, bf16[192,960]{1,0:T(8,128)(2,1)S(1)}, u32[]{:S(2)}, u32[]{:S(2)}) %collective-permute-start.53) | collective-permute-done | bytes 368672 | tf_op jit(solution)/shard_map/ppermute | solution.py:449
  192.0 3.3 %collective-permute-done.45.far_ref = bf16[96,1152]{1,0:T(8,128)(2,1)S(1)} collective-permute-done((bf16[96,1152]{1,0:T(8,128)(2,1)S(1)}, bf16[96,1152]{1,0:T(8,128)(2,1)S(1)}, u32[]{:S(2)}, u32[]{:S(2)}) %collective-permute-start.45) | collective-permute-done | bytes 221216 | tf_op jit(solution)/shard_map/ppermute | solution.py:459
  197.6 3.6 %collective-permute-done.47.refs_1_ = bf16[96,640]{1,0:T(8,128)(2,1)S(1)} collective-permute-done((bf16[96,640]{1,0:T(8,128)(2,1)S(1)}, bf16[96,640]{1,0:T(8,128)(2,1)S(1)}, u32[]{:S(2)}, u32[]{:S(2)}) %collective-permute-start.47) | collective-permute-done | bytes 122912 | tf_op jit(solution)/shard_map/ppermute | solution.py:449
  203.5 2.8 %collective-permute-done.46.recv_ref = bf16[96,512]{1,0:T(8,128)(2,1)S(1)} collective-permute-done((bf16[96,512]{1,0:T(8,128)(2,1)S(1)}, bf16[96,512]{1,0:T(8,128)(2,1)S(1)}, u32[]{:S(2)}, u32[]{:S(2)}) %collective-permute-start.46) | collective-permute-done | bytes 98336 | tf_op jit(solution)/shard_map/ppermute | solution.py:441
  207.7 2.2 %place_hidden.1 = (f32[192,1536]{1,0:T(8,128)}, f32[192,1536]{1,0:T(8,128)}, f32[192,384]{1,0:T(8,128)}) custom-call(s32[5]{0:T(128)S(1)} %stack.38.flags_ref, bf16[192,960]{1,0:T(8,128)(2,1)S(1)} %hidden_sums.1.refs_0_, bf16[192,960]{1,0:T(8,128)(2,1)S(1)} %collective-permute-done.53.refs_1_, bf16[192,960]{1,0:T(8,128)(2,1)S(1)} %collective-permute-done.54.refs_2_, ...), custom_call_target="tpu_custom_call" | custom-call | tf_op jit(solution)/shard_map/place_hidden/pallas_call | solution.py:497
  (150 shorter events, 81.5 us)
Async XLA Ops:
  13.0 10.3 %collective-permute-start.3 = (bf16[208,256]{1,0:T(8,128)(2,1)S(1)}, bf16[208,256]{1,0:T(8,128)(2,1)S(1)}, u32[]{:S(2)}, u32[]{:S(2)}) collective-permute-start(bf16[208,256]{1,0:T(8,128)(2,1)S(1)} %get-tuple-element.145), channel_id=1, source_target_pairs={{0,4},{2,6},{4,0},{6,2},{1,5},{3,7},{5,1},{7,3},{8,12},{10,14},{12... | collective-permute-start | bytes 319496 | tf_op jit(solution)/shard_map/ppermute | solution.py:464
  16.9 13.0 %collective-permute-start.6 = (bf16[192,384]{1,0:T(8,128)(2,1)S(1)}, bf16[192,384]{1,0:T(8,128)(2,1)S(1)}, u32[]{:S(2)}, u32[]{:S(2)}) collective-permute-start(bf16[192,384]{1,0:T(8,128)(2,1)S(1)} %maximum_select_fusion), channel_id=1, source_target_pairs={{0,4},{2,6},{4,0},{6,2},{1,5},{3,7},{5,1},{7,3},{8,12},{10,14},{12... | collective-permute-start | bytes 442376 | tf_op jit(solution)/shard_map/ppermute | solution.py:459
  24.0 16.8 %collective-permute-start.13 = (bf16[384,256]{1,0:T(8,128)(2,1)S(1)}, bf16[384,256]{1,0:T(8,128)(2,1)S(1)}, u32[]{:S(2)}, u32[]{:S(2)}) collective-permute-start(bf16[384,256]{1,0:T(8,128)(2,1)S(1)} %get-tuple-element.155.half_ref), channel_id=1, source_target_pairs={{0,1},{1,0},{2,3},{3,2},{4,5},{5,4},{6,7},{7,6},{8,9},{9,8},{10,11... | collective-permute-start | bytes 589832 | tf_op jit(solution)/shard_map/ppermute | solution.py:441
  25.1 16.3 %collective-permute-start.5 = (bf16[384,256]{1,0:T(8,128)(2,1)S(1)}, bf16[384,256]{1,0:T(8,128)(2,1)S(1)}, u32[]{:S(2)}, u32[]{:S(2)}) collective-permute-start(bf16[384,256]{1,0:T(8,128)(2,1)S(1)} %get-tuple-element.152.half_ref), channel_id=1, source_target_pairs={{0,1},{1,0},{2,3},{3,2},{4,5},{5,4},{6,7},{7,6},{8,9},{9,8},{10,11... | collective-permute-start | bytes 589832 | tf_op jit(solution)/shard_map/ppermute | solution.py:441
  30.0 9.4 %collective-permute-start.7 = (bf16[192,384]{1,0:T(8,128)(2,1)S(1)}, bf16[192,384]{1,0:T(8,128)(2,1)S(1)}, u32[]{:S(2)}, u32[]{:S(2)}) collective-permute-start(bf16[192,384]{1,0:T(8,128)(2,1)S(1)} %collective-permute-done.6.refs_1_), channel_id=1, source_target_pairs={{0,2},{2,0},{4,6},{6,4},{1,3},{3,1},{5,7},{7,5},{8,10},{10,8},{12,... | collective-permute-start | bytes 442376 | tf_op jit(solution)/shard_map/ppermute | solution.py:459
  30.5 18.5 %collective-permute-start.12 = (bf16[192,768]{1,0:T(8,128)(2,1)S(1)}, bf16[192,768]{1,0:T(8,128)(2,1)S(1)}, u32[]{:S(2)}, u32[]{:S(2)}) collective-permute-start(bf16[192,768]{1,0:T(8,128)(2,1)S(1)} %get-tuple-element.154.refs_0_), channel_id=1, source_target_pairs={{0,4},{2,6},{4,0},{6,2},{1,5},{3,7},{5,1},{7,3},{8,12},{10,14},{12... | collective-permute-start | bytes 884744 | tf_op jit(solution)/shard_map/ppermute | solution.py:459
  33.5 15.6 %collective-permute-start.11 = (bf16[192,768]{1,0:T(8,128)(2,1)S(1)}, bf16[192,768]{1,0:T(8,128)(2,1)S(1)}, u32[]{:S(2)}, u32[]{:S(2)}) collective-permute-start(bf16[192,768]{1,0:T(8,128)(2,1)S(1)} %get-tuple-element.154.refs_0_), channel_id=1, source_target_pairs={{0,2},{2,0},{4,6},{6,4},{1,3},{3,1},{5,7},{7,5},{8,10},{10,8},{12,... | collective-permute-start | bytes 884744 | tf_op jit(solution)/shard_map/ppermute | solution.py:459
  49.0 12.2 %collective-permute-start.19 = (bf16[192,768]{1,0:T(8,128)(2,1)S(1)}, bf16[192,768]{1,0:T(8,128)(2,1)S(1)}, u32[]{:S(2)}, u32[]{:S(2)}) collective-permute-start(bf16[192,768]{1,0:T(8,128)(2,1)S(1)} %collective-permute-done.12.refs_2_), channel_id=1, source_target_pairs={{0,16},{8,24},{16,0},{24,8},{1,17},{9,25},{17,1},{25,9},{2,18},{10... | collective-permute-start | bytes 884744 | tf_op jit(solution)/shard_map/ppermute | solution.py:449
  50.6 10.7 %collective-permute-start.18 = (bf16[192,768]{1,0:T(8,128)(2,1)S(1)}, bf16[192,768]{1,0:T(8,128)(2,1)S(1)}, u32[]{:S(2)}, u32[]{:S(2)}) collective-permute-start(bf16[192,768]{1,0:T(8,128)(2,1)S(1)} %collective-permute-done.12.refs_2_), channel_id=1, source_target_pairs={{0,2},{2,0},{4,6},{6,4},{1,3},{3,1},{5,7},{7,5},{8,10},{10,8},{12,... | collective-permute-start | bytes 884744 | tf_op jit(solution)/shard_map/ppermute | solution.py:459
  52.3 8.9 %collective-permute-start.17 = (bf16[400,128]{1,0:T(8,128)(2,1)S(1)}, bf16[400,128]{1,0:T(8,128)(2,1)S(1)}, u32[]{:S(2)}, u32[]{:S(2)}) collective-permute-start(bf16[400,128]{1,0:T(8,128)(2,1)S(1)} %get-tuple-element.169), channel_id=1, source_target_pairs={{0,6},{1,7},{8,14},{9,15},{16,22},{17,23},{24,30},{25,31}} | collective-permute-start | bytes 307208 | tf_op jit(solution)/shard_map/ppermute | solution.py:455
  66.6 16.5 %collective-permute-start.21 = (bf16[768,256]{1,0:T(8,128)(2,1)S(1)}, bf16[768,256]{1,0:T(8,128)(2,1)S(1)}, u32[]{:S(2)}, u32[]{:S(2)}) collective-permute-start(bf16[768,256]{1,0:T(8,128)(2,1)S(1)} %branch_half.1.half_ref), channel_id=1, source_target_pairs={{0,1},{1,0},{2,3},{3,2},{4,5},{5,4},{6,7},{7,6},{8,9},{9,8},{10,11... | collective-permute-start | bytes 1179656 | tf_op jit(solution)/shard_map/ppermute | solution.py:441
  68.0 9.9 %collective-permute-start.22 = (bf16[192,768]{1,0:T(8,128)(2,1)S(1)}, bf16[192,768]{1,0:T(8,128)(2,1)S(1)}, u32[]{:S(2)}, u32[]{:S(2)}) collective-permute-start(bf16[192,768]{1,0:T(8,128)(2,1)S(1)} %collective-permute-done.11.refs_1_), channel_id=1, source_target_pairs={{0,16},{8,24},{16,0},{24,8},{1,17},{9,25},{17,1},{25,9},{2,18},{10... | collective-permute-start | bytes 884744 | tf_op jit(solution)/shard_map/ppermute | solution.py:449
  68.5 14.6 %collective-permute-start.23 = (bf16[192,768]{1,0:T(8,128)(2,1)S(1)}, bf16[192,768]{1,0:T(8,128)(2,1)S(1)}, u32[]{:S(2)}, u32[]{:S(2)}) collective-permute-start(bf16[192,768]{1,0:T(8,128)(2,1)S(1)} %collective-permute-done.18.refs_3_), channel_id=1, source_target_pairs={{0,16},{8,24},{16,0},{24,8},{1,17},{9,25},{17,1},{25,9},{2,18},{10... | collective-permute-start | bytes 884744 | tf_op jit(solution)/shard_map/ppermute | solution.py:449
  91.9 11.2 %collective-permute-start.26 = (bf16[768,256]{1,0:T(8,128)(2,1)S(1)}, bf16[768,256]{1,0:T(8,128)(2,1)S(1)}, u32[]{:S(2)}, u32[]{:S(2)}) collective-permute-start(bf16[768,256]{1,0:T(8,128)(2,1)S(1)} %ffn_half.1.half_ref), channel_id=1, source_target_pairs={{0,1},{1,0},{2,3},{3,2},{4,5},{5,4},{6,7},{7,6},{8,9},{9,8},{10,11... | collective-permute-start | bytes 1179656 | tf_op jit(solution)/shard_map/ppermute | solution.py:441
  110.8 14.2 %collective-permute-start.29 = (bf16[768,256]{1,0:T(8,128)(2,1)S(1)}, bf16[768,256]{1,0:T(8,128)(2,1)S(1)}, u32[]{:S(2)}, u32[]{:S(2)}) collective-permute-start(bf16[768,256]{1,0:T(8,128)(2,1)S(1)} %first_half.1.half_ref), channel_id=1, source_target_pairs={{0,1},{1,0},{2,3},{3,2},{4,5},{5,4},{6,7},{7,6},{8,9},{9,8},{10,11... | collective-permute-start | bytes 1179656 | tf_op jit(solution)/shard_map/ppermute | solution.py:441
  111.6 16.2 %collective-permute-start.39 = (bf16[768,384]{1,0:T(8,128)(2,1)S(1)}, bf16[768,384]{1,0:T(8,128)(2,1)S(1)}, u32[]{:S(2)}, u32[]{:S(2)}) collective-permute-start(bf16[768,384]{1,0:T(8,128)(2,1)S(1)} %get-tuple-element.233), channel_id=1, source_target_pairs={{0,16},{8,24},{16,0},{24,8},{1,17},{9,25},{17,1},{25,9},{2,18},{10... | collective-permute-start | bytes 1769480 | tf_op jit(solution)/shard_map/ppermute | solution.py:449
  116.2 23.1 %collective-permute-start.38 = (bf16[768,384]{1,0:T(8,128)(2,1)S(1)}, bf16[768,384]{1,0:T(8,128)(2,1)S(1)}, u32[]{:S(2)}, u32[]{:S(2)}) collective-permute-start(bf16[768,384]{1,0:T(8,128)(2,1)S(1)} %get-tuple-element.231), channel_id=1, source_target_pairs={{0,16},{8,24},{16,0},{24,8},{1,17},{9,25},{17,1},{25,9},{2,18},{10... | collective-permute-start | bytes 1769480 | tf_op jit(solution)/shard_map/ppermute | solution.py:449
  128.5 10.8 %collective-permute-start.40 = (bf16[384,384]{1,0:T(8,128)(2,1)S(1)}, bf16[384,384]{1,0:T(8,128)(2,1)S(1)}, u32[]{:S(2)}, u32[]{:S(2)}) collective-permute-start(bf16[384,384]{1,0:T(8,128)(2,1)S(1)} %get-tuple-element.234), channel_id=1, source_target_pairs={{0,2},{2,0},{4,6},{6,4},{1,3},{3,1},{5,7},{7,5},{8,10},{10,8},{12,... | collective-permute-start | bytes 884744 | tf_op jit(solution)/shard_map/ppermute | solution.py:459
  132.0 11.7 %collective-permute-start.37 = (bf16[400,128]{1,0:T(8,128)(2,1)S(1)}, bf16[400,128]{1,0:T(8,128)(2,1)S(1)}, u32[]{:S(2)}, u32[]{:S(2)}) collective-permute-start(bf16[400,128]{1,0:T(8,128)(2,1)S(1)} %get-tuple-element.230), channel_id=1, source_target_pairs={{6,0},{7,1},{14,8},{15,9},{22,16},{23,17},{30,24},{31,25}} | collective-permute-start | bytes 307208 | tf_op jit(solution)/shard_map/ppermute | solution.py:455
  133.3 10.4 %collective-permute-start.36 = (bf16[400,128]{1,0:T(8,128)(2,1)S(1)}, bf16[400,128]{1,0:T(8,128)(2,1)S(1)}, u32[]{:S(2)}, u32[]{:S(2)}) collective-permute-start(bf16[400,128]{1,0:T(8,128)(2,1)S(1)} %get-tuple-element.230), channel_id=1, source_target_pairs={{4,0},{6,2},{5,1},{7,3},{12,8},{14,10},{13,9},{15,11},{20,16},{22,... | collective-permute-start | bytes 307208 | tf_op jit(solution)/shard_map/ppermute | solution.py:455
  134.6 9.1 %collective-permute-start.35 = (bf16[400,128]{1,0:T(8,128)(2,1)S(1)}, bf16[400,128]{1,0:T(8,128)(2,1)S(1)}, u32[]{:S(2)}, u32[]{:S(2)}) collective-permute-start(bf16[400,128]{1,0:T(8,128)(2,1)S(1)} %get-tuple-element.230), channel_id=1, source_target_pairs={{2,0},{4,2},{6,4},{3,1},{5,3},{7,5},{10,8},{12,10},{14,12},{11,9},... | collective-permute-start | bytes 307208 | tf_op jit(solution)/shard_map/ppermute | solution.py:455
  146.0 8.9 %collective-permute-start.42 = (bf16[4,96,640]{2,1,0:T(8,128)(2,1)S(1)}, bf16[4,96,640]{2,1,0:T(8,128)(2,1)S(1)}, u32[]{:S(2)}, u32[]{:S(2)}) collective-permute-start(bf16[4,96,640]{2,1,0:T(8,128)(2,1)S(1)} %get-tuple-element.241), channel_id=1, source_target_pairs={{0,16},{8,24},{16,0},{24,8},{1,17},{9,25},{17,1},{25,9},{2,18},{10... | collective-permute-start | bytes 1474568 | tf_op jit(solution)/shard_map/ppermute | solution.py:449
  147.7 13.8 %collective-permute-start.51 = (bf16[384,576]{1,0:T(8,128)(2,1)S(1)}, bf16[384,576]{1,0:T(8,128)(2,1)S(1)}, u32[]{:S(2)}, u32[]{:S(2)}) collective-permute-start(bf16[384,576]{1,0:T(8,128)(2,1)S(1)} %get-tuple-element.265), channel_id=1, source_target_pairs={{0,2},{2,0},{4,6},{6,4},{1,3},{3,1},{5,7},{7,5},{8,10},{10,8},{12,... | collective-permute-start | bytes 1327112 | tf_op jit(solution)/shard_map/ppermute | solution.py:459
  155.7 9.1 %collective-permute-start.43 = (bf16[384,256]{1,0:T(8,128)(2,1)S(1)}, bf16[384,256]{1,0:T(8,128)(2,1)S(1)}, u32[]{:S(2)}, u32[]{:S(2)}) collective-permute-start(bf16[384,256]{1,0:T(8,128)(2,1)S(1)} %get-tuple-element.246), channel_id=1, source_target_pairs={{0,1},{1,0},{2,3},{3,2},{4,5},{5,4},{6,7},{7,6},{8,9},{9,8},{10,11... | collective-permute-start | bytes 589832 | tf_op jit(solution)/shard_map/ppermute | solution.py:441
  161.6 20.3 %collective-permute-start.52 = (bf16[192,576]{1,0:T(8,128)(2,1)S(1)}, bf16[192,576]{1,0:T(8,128)(2,1)S(1)}, u32[]{:S(2)}, u32[]{:S(2)}) collective-permute-start(bf16[192,576]{1,0:T(8,128)(2,1)S(1)} %get-tuple-element.267), channel_id=1, source_target_pairs={{0,4},{2,6},{4,0},{6,2},{1,5},{3,7},{5,1},{7,3},{8,12},{10,14},{12... | collective-permute-start | bytes 663560 | tf_op jit(solution)/shard_map/ppermute | solution.py:459
  164.4 17.6 %collective-permute-start.50 = (bf16[192,384]{1,0:T(8,128)(2,1)S(1)}, bf16[192,384]{1,0:T(8,128)(2,1)S(1)}, u32[]{:S(2)}, u32[]{:S(2)}) collective-permute-start(bf16[192,384]{1,0:T(8,128)(2,1)S(1)} %get-tuple-element.261), channel_id=1, source_target_pairs={{0,4},{2,6},{4,0},{6,2},{1,5},{3,7},{5,1},{7,3},{8,12},{10,14},{12... | collective-permute-start | bytes 442376 | tf_op jit(solution)/shard_map/ppermute | solution.py:459
  165.4 18.1 %collective-permute-start.44 = (bf16[192,896]{1,0:T(8,128)(2,1)S(1)}, bf16[192,896]{1,0:T(8,128)(2,1)S(1)}, u32[]{:S(2)}, u32[]{:S(2)}) collective-permute-start(bf16[192,896]{1,0:T(8,128)(2,1)S(1)} %get-tuple-element.249), channel_id=1, source_target_pairs={{0,2},{2,0},{4,6},{6,4},{1,3},{3,1},{5,7},{7,5},{8,10},{10,8},{12,... | collective-permute-start | bytes 1032200 | tf_op jit(solution)/shard_map/ppermute | solution.py:459
  182.0 10.0 %collective-permute-start.53 = (bf16[192,960]{1,0:T(8,128)(2,1)S(1)}, bf16[192,960]{1,0:T(8,128)(2,1)S(1)}, u32[]{:S(2)}, u32[]{:S(2)}) collective-permute-start(bf16[192,960]{1,0:T(8,128)(2,1)S(1)} %hidden_sums.1.refs_0_), channel_id=1, source_target_pairs={{0,16},{8,24},{16,0},{24,8},{1,17},{9,25},{17,1},{25,9},{2,18},{10... | collective-permute-start | bytes 1105928 | tf_op jit(solution)/shard_map/ppermute | solution.py:449
  183.6 11.6 %collective-permute-start.45 = (bf16[96,1152]{1,0:T(8,128)(2,1)S(1)}, bf16[96,1152]{1,0:T(8,128)(2,1)S(1)}, u32[]{:S(2)}, u32[]{:S(2)}) collective-permute-start(bf16[96,1152]{1,0:T(8,128)(2,1)S(1)} %get-tuple-element.251), channel_id=1, source_target_pairs={{0,4},{2,6},{4,0},{6,2},{1,5},{3,7},{5,1},{7,3},{8,12},{10,14},{12... | collective-permute-start | bytes 663560 | tf_op jit(solution)/shard_map/ppermute | solution.py:459
  183.7 24.0 %collective-permute-start.54 = (bf16[192,960]{1,0:T(8,128)(2,1)S(1)}, bf16[192,960]{1,0:T(8,128)(2,1)S(1)}, u32[]{:S(2)}, u32[]{:S(2)}) collective-permute-start(bf16[192,960]{1,0:T(8,128)(2,1)S(1)} %hidden_sums.1.refs_0_), channel_id=1, source_target_pairs={{0,8},{8,0},{16,24},{24,16},{1,9},{9,1},{17,25},{25,17},{2,10},{10... | collective-permute-start | bytes 1105928 | tf_op jit(solution)/shard_map/ppermute | solution.py:445
  192.0 15.7 %collective-permute-start.55 = (bf16[192,960]{1,0:T(8,128)(2,1)S(1)}, bf16[192,960]{1,0:T(8,128)(2,1)S(1)}, u32[]{:S(2)}, u32[]{:S(2)}) collective-permute-start(bf16[192,960]{1,0:T(8,128)(2,1)S(1)} %collective-permute-done.53.refs_1_), channel_id=1, source_target_pairs={{0,8},{8,0},{16,24},{24,16},{1,9},{9,1},{17,25},{25,17},{2,10},{10... | collective-permute-start | bytes 1105928 | tf_op jit(solution)/shard_map/ppermute | solution.py:445
  197.6 12.3 %collective-permute-start.48 = (bf16[96,640]{1,0:T(8,128)(2,1)S(1)}, bf16[96,640]{1,0:T(8,128)(2,1)S(1)}, u32[]{:S(2)}, u32[]{:S(2)}) collective-permute-start(bf16[96,640]{1,0:T(8,128)(2,1)S(1)} %get-tuple-element.254.refs_0_), channel_id=1, source_target_pairs={{0,8},{8,0},{16,24},{24,16},{1,9},{9,1},{17,25},{25,17},{2,10},{10... | collective-permute-start | bytes 368648 | tf_op jit(solution)/shard_map/ppermute | solution.py:445
  (35 other events, 210.6 us)

commit v4 on v3

--- a/solution.py
+++ b/solution.py
@@ -691,8 +691,11 @@
         ref[out, :part] = (
             kept_ref[rows_in, :].astype(wide) + got_ref[rows_in, :].astype(wide)
         ).astype(low)
+        lane = part
         for extra in extras:
-            ref[out, part:] = extra[rows_in, :]
+            width = min(extra.shape[1], ref.shape[1] - lane)
+            ref[out, lane : lane + width] = extra[rows_in, :width]
+            lane = lane + width
 
 
 def pair_sums_body(held_ref, got_ref, sum_ref, sent_ref):
@@ -701,21 +704,55 @@
     sent_ref[...] = (held_ref[feats:].astype(wide) + got_ref[feats:].astype(wide)).astype(low)
 
 
-def hidden_sums_body(down_ref, down_far_ref, up_ref, up_far_ref, sum_ref):
+def hidden_sums_body(down_ref, up_ref, up_far_ref, sum_ref):
     part = down_ref.shape[1]
-    sum_ref[:, :part] = (down_ref[...] + down_far_ref[...].astype(wide)).astype(low)
+    sum_ref[:, :part] = down_ref[...]
     sum_ref[:, part:] = (up_ref[...] + up_far_ref[...].astype(wide)).astype(low)
 
 
-def out_pieces_body(flags_ref, result_ref, *refs):
-    for step, ref in enumerate(refs):
-        ref[...] = feature_piece(flags_ref, result_ref, step, len(refs))
-
-
-def out_place_body(flags_ref, *refs):
-    pieces = refs[:-2]
-    rows = [came_from(flags_ref, step, len(pieces)) for step in range(len(pieces))]
-    place_back(flags_ref, pieces, rows, *refs[-2:])
+def down_pieces_body(flags_ref, kept_ref, got_ref, result_ref, held_ref, sent_ref):
+    feats, part = kept_ref.shape[0] // 4, kept_ref.shape[1]
+    half = feats // 2
+    for mask in range(4):
+        ref = sent_ref if mask % 2 else held_ref
+        start = mask // 2 * feats
+        place = partner(flags_ref[ROW], mask)
+        rows_in = pl.ds(pl.multiple_of(place * feats, 16), feats)
+        ref[start : start + feats, :part] = (
+            kept_ref[rows_in, :].astype(wide) + got_ref[rows_in, :].astype(wide)
+        ).astype(low)
+        rows_in = pl.ds(pl.multiple_of((place * 2 + flags_ref[COL]) * half, 16), half)
+        ref[start : start + half, part:] = result_ref[rows_in, : SPAN // 2]
+        ref[start + half : start + feats, part:] = result_ref[rows_in, SPAN // 2 :]
+
+
+def down_pairs_body(held_ref, got_ref, sum_ref, sent_ref):
+    feats, part = sum_ref.shape
+    lanes = SPAN // 2
+    sum_ref[...] = held_ref[:feats, :part].astype(wide) + got_ref[:feats, :part].astype(wide)
+    pair = held_ref[feats:, :part].astype(wide) + got_ref[feats:, :part].astype(wide)
+    sent_ref[:, :part] = pair.astype(low)
+    sent_ref[:, part : part + lanes] = held_ref[feats:, part:]
+    sent_ref[:, part + lanes :] = got_ref[feats:, part:]
+
+
+def down_sums_body(
+    flags_ref, part_ref, held_ref, got_ref, far_ref, sum_ref, own_ref, other_ref, piece_ref
+):
+    feats, part = part_ref.shape
+    lanes = SPAN // 2
+    sum_ref[...] = (part_ref[...] + far_ref[:, :part].astype(wide)).astype(low)
+    pieces = (
+        held_ref[:feats, part:],
+        got_ref[:feats, part:],
+        far_ref[:, part : part + lanes],
+        far_ref[:, part + lanes :],
+    )
+    for place, piece in enumerate(pieces):
+        piece_ref[place, :, :lanes] = piece[: feats // 2]
+        piece_ref[place, :, lanes:] = piece[feats // 2 :]
+    rows = [partner(flags_ref[ROW], mask) for mask in range(4)]
+    place_back(flags_ref, [piece_ref.at[i] for i in range(4)], rows, own_ref, other_ref)
 
 
 def head_sets():
@@ -939,7 +976,6 @@
     x_own_ref,
     x_other_ref,
     weight_ref,
-    vec_ref,
     flags_ref,
     *refs,
 ):
@@ -974,11 +1010,7 @@
     first_copy = flags_ref[COPY] == 0
     for row in range(rows):
         start = row * 2 * part
-        whole = jnp.concatenate(
-            [grad_w[start : start + 2 * part], vec_ref[start : start + 2 * part, : 2 * SUM_LANES]],
-            1,
-        )[:, : 3 * WIDTH + SUM_LANES]
-        first, second = whole[:part], whole[part:]
+        first, second = grad_w[start : start + part], grad_w[start + part : start + 2 * part]
         kept_ref[row] = jnp.where(first_copy, first, second)
         sent_ref[row] = jnp.where(first_copy, second, first)
     own_ref[...] = dot_nn(matrix, grad_ref[0])
@@ -1100,7 +1132,7 @@
 
 
 def place_hidden_body(flags_ref, *refs):
-    down_ref, up_ref, out_ref = refs[4:]
+    down_ref, up_ref, out_ref, vec_ref = refs[4:]
     part = up_ref.shape[1] // 4
     for place, ref in quarters(flags_ref, refs[:4]):
         cols = pl.ds(pl.multiple_of(place * part, 128), part)
@@ -1108,13 +1140,15 @@
         up_ref[:, cols] = ref[:, part : 2 * part].astype(wide)
     sums = [ref[:, 2 * part :].astype(wide) for ref in refs[:4]]
     own, other = sums[0] + sums[1], sums[2] + sums[3]
+    vec_ref[...] = own[:, WIDTH:] + other[:, WIDTH:]
+    own, other = own[:, :WIDTH], other[:, :WIDTH]
     first_core = flags_ref[CORE] == 0
     out_ref[:, :WIDTH] = jnp.where(first_core, own, other)
     out_ref[:, WIDTH:] = jnp.where(first_core, other, own)
 
 
 def place_last_body(flags_ref, *refs):
-    outs, vec_ref = refs[4:7], refs[7]
+    outs = refs[4:]
     first_core = flags_ref[CORE] == 0
     part = refs[0].shape[0]
     for own_ref, other_ref, other_copy in ((refs[0], refs[2], 0), (refs[1], refs[3], 1)):
@@ -1125,7 +1159,6 @@
             cols = slice(place * WIDTH, (place + 1) * WIDTH)
             out_ref[rows, :WIDTH] = jnp.where(first_core, own[:, cols], other[:, cols])
             out_ref[rows, WIDTH:] = jnp.where(first_core, other[:, cols], own[:, cols])
-        vec_ref[rows, :] = own[:, 3 * WIDTH :] + other[:, 3 * WIDTH :]
 
 
 def gelu_and_slope(pre):
@@ -1134,8 +1167,11 @@
     return (pre * cdf).astype(low), (cdf + pre * density)
 
 
-def all_quarters(own):
+def all_quarters(own, direct=False):
     copied = swap_copies(own)
+    if direct:
+        pairs = [(i, i ^ 3) for i in range(lax.axis_size("dp"))]
+        return own, copied, swap_pair(own), lax.ppermute(own, "dp", pairs)
     return own, copied, swap_pair(own), swap_pair(copied)
 
 
@@ -1175,14 +1211,9 @@
             rotate_rows(piece, step) for step, piece in enumerate(pieces) if step
         ]
 
-    def joined_halves(half, name):
+    def joined_halves(half, got, name):
         return local_call(
-            partial(join_halves_body, rows=rows),
-            [((D, SPAN), low)],
-            name,
-            flags,
-            half,
-            swap_cols(half),
+            partial(join_halves_body, rows=rows), [((D, SPAN), low)], name, flags, half, got
         )[0]
 
     def cols_back(own, other, kind, name):
@@ -1225,8 +1256,6 @@
 
     first_one, first_two = row_blocks(first_mine)
     first_one, got = lax.optimization_barrier((first_one, got))
-    first_blocks = [first_one, first_two, swap_rows(first_two, 1)]
-    first_blocks = first_blocks + [swap_copies(block) for block in first_blocks]
     hidden_packed = local_call(
         pack_hidden_body,
         low_outs(2, feat_rows, 2 * part),
@@ -1248,22 +1277,35 @@
         got,
         vecs,
     )
+    def after(value, *others):
+        return lax.optimization_barrier((value, others))[0]
+
+    first_three = swap_rows(after(first_two, token_pieces[0]), 1)
+    first_copies = [
+        swap_copies(after(first_one, token_pieces[0])),
+        swap_copies(first_two),
+        swap_copies(first_three),
+    ]
+    token_pieces = passed_on(token_pieces)
+    token_pieces, first_three, first_copies[0] = lax.optimization_barrier(
+        (token_pieces, first_three, first_copies[0])
+    )
+    first_blocks = [first_one, first_two, first_three, *first_copies]
     x_half, cot_half, norm_vecs = local_call(
         partial(place_tokens_body, rows=rows, part=half_feats),
         low_outs(2, D // 2, SPAN) + [((D, 8), wide)],
         "token_place",
         flags,
-        *passed_on(token_pieces),
+        *token_pieces,
     )
     x_half, trig, reweight, hidden_packed = lax.optimization_barrier(
         (x_half, trig, reweight, hidden_packed)
     )
     hidden_one, hidden_two = row_blocks(hidden_packed[0])
-    x_own = joined_halves(x_half, "token_join")
-    cot = joined_halves(cot_half, "cot_join")
-    x_own, first_blocks, hidden_one, hidden_two, cot = lax.optimization_barrier(
-        (x_own, first_blocks, hidden_one, hidden_two, cot)
-    )
+    x_got, hidden_one = lax.optimization_barrier((swap_cols(x_half), hidden_one))
+    x_own = joined_halves(x_half, x_got, "token_join")
+    cot = joined_halves(cot_half, swap_cols(cot_half), "cot_join")
+    x_own, first_blocks = lax.optimization_barrier((x_own, first_blocks))
     x_other = swap_pair(x_own)
     hidden_three = swap_rows(hidden_two, 1)
     copy_two = swap_copies(hidden_two)
@@ -1311,9 +1353,13 @@
         *arrived,
         scratch=[((2, WIDTH, SPAN), low)],
     )
+    copy_one = swap_copies(hidden_one)
+    branch_own, branch_other, copy_one = lax.optimization_barrier(
+        (branch_own, branch_other, copy_one)
+    )
     branch = column_parts(branch_own, branch_other, "branch_half")
-    copy_one, copy_three = swap_copies(hidden_one), swap_copies(hidden_three)
-    branch, copy_one, copy_three = lax.optimization_barrier((branch, copy_one, copy_three))
+    copy_three = swap_copies(hidden_three)
+    branch, copy_three = lax.optimization_barrier((branch, copy_three))
     hidden_mine = [hidden_packed[0], hidden_one, hidden_two, hidden_three]
     hidden_copy = [hidden_packed[1], copy_one, copy_two, copy_three]
     first, first_low, normed = local_call(
@@ -1397,18 +1443,7 @@
         pre_copy,
     )
     got_up = swap_copies(sent_up)
-    out_pieces = local_call(
-        out_pieces_body, low_outs(rows, half_feats, SPAN), "out_pieces", flags, result
-    )
-    out_wide = local_call(
-        out_place_body,
-        low_outs(2, half_feats, SPAN * rows // 2),
-        "out_place",
-        flags,
-        *passed_on(out_pieces),
-    )
-    first_sum, kept_up, out_wide = lax.optimization_barrier((first_sum, kept_up, out_wide))
-    output = cols_back(*out_wide, low, "out_join")
+    first_sum, kept_up = lax.optimization_barrier((first_sum, kept_up))
     grad_hidden, branch_grad, vec_sums = local_call(
         norm_back_body,
         [block_wide, block_low, ((D, 2 * SUM_LANES), low)],
@@ -1456,40 +1491,29 @@
         prior,
     )
     down_held, down_sent = local_call(
-        pair_pieces_body,
-        low_outs(2, 2 * feat_rows, part),
+        down_pieces_body,
+        low_outs(2, 2 * feat_rows, part + SPAN // 2),
         "down_pieces",
         flags,
         kept_down,
-        got_down,
+        after(got_down, later[0]),
+        result,
     )
     down_got = swap_rows(down_sent, 1)
-    later, got_up, down_got = lax.optimization_barrier((later, got_up, down_got))
-
-    def pair_sums(held, got, name):
-        shape = (feat_rows, held.shape[1])
-        mine, sent = local_call(pair_sums_body, [(shape, wide), (shape, low)], name, held, got)
-        return mine, swap_rows(sent, 2)
-
-    down_sums = pair_sums(down_held, down_got, "down_sums")
+
     up_held, up_sent = local_call(
         pair_pieces_body,
-        low_outs(2, 2 * feat_rows, part + WIDTH),
+        low_outs(2, 2 * feat_rows, part + WIDTH + SUM_LANES),
         "up_pieces",
         flags,
         kept_up,
-        got_up,
+        after(got_up, later[0]),
         grad_out,
-    )
-    up_sums = pair_sums(up_held, swap_rows(up_sent, 1), "up_sums")
-    (hidden_sum,) = local_call(
-        hidden_sums_body,
-        low_outs(1, feat_rows, 2 * part + WIDTH),
-        "hidden_sums",
-        *down_sums,
-        *up_sums,
-    )
-    half_rows = ((rows, feat_rows // 2, 3 * WIDTH + SUM_LANES), low)
+        vec_sums,
+    )
+    up_got = swap_rows(up_sent, 1)
+    later, up_held = lax.optimization_barrier((later, up_held))
+    half_rows = ((rows, half_feats, 3 * WIDTH), low)
     kept_w, sent_w, x_grad_own, x_grad_other = local_call(
         grad_project_body,
         [half_rows, half_rows, block_wide, block_low],
@@ -1502,14 +1526,12 @@
         x_own,
         x_other,
         weight,
-        vec_sums,
         flags,
         *later,
         scratch=[state_shape, ((2, 3 * WIDTH, SPAN), low)],
     )
     got_w = swap_copies(sent_w)
     got_x = swap_pair(x_grad_other)
-    x_grad_own, got_x, got_w = lax.optimization_barrier((x_grad_own, got_x, got_w))
     x_half_grad, x_half_sent = local_call(
         partial(input_halves_body, rows=rows),
         [((D // 2, SPAN), wide), ((D // 2, SPAN), low)],
@@ -1519,7 +1541,8 @@
         got_x,
         scratch=[block_wide],
     )
-    last_lanes = 3 * WIDTH + SUM_LANES
+    got_half = swap_cols(x_half_sent)
+    last_lanes = 3 * WIDTH
     last_held, last_sent = local_call(
         last_pieces_body,
         low_outs(2, 2 * half_feats, last_lanes + SPAN),
@@ -1528,9 +1551,23 @@
         kept_w,
         got_w,
         x_half_grad,
-        swap_cols(x_half_sent),
+        got_half,
         grad_hidden,
     )
+    def pair_sums(held, got, name):
+        shape = (feat_rows, held.shape[1])
+        mine, sent = local_call(pair_sums_body, [(shape, wide), (shape, low)], name, held, got)
+        return mine, swap_rows(sent, 2)
+
+    down_part, down_far = local_call(
+        down_pairs_body,
+        [((feat_rows, part), wide), ((feat_rows, part + SPAN), low)],
+        "down_pairs",
+        down_held,
+        down_got,
+    )
+    down_far = swap_rows(down_far, 2)
+    up_part, up_far = pair_sums(up_held, up_got, "up_sums")
     last_got = swap_rows(last_sent, 1)
     last_part, last_far = local_call(
         last_pairs_body,
@@ -1538,6 +1575,25 @@
         "last_pairs",
         last_held,
         last_got,
+    )
+    down_sum, *out_wide = local_call(
+        down_sums_body,
+        low_outs(1, feat_rows, part) + low_outs(2, half_feats, SPAN * rows // 2),
+        "down_sums",
+        flags,
+        down_part,
+        down_held,
+        down_got,
+        down_far,
+        scratch=[((4, half_feats, SPAN), low)],
+    )
+    (hidden_sum,) = local_call(
+        hidden_sums_body,
+        low_outs(1, feat_rows, 2 * part + WIDTH + SUM_LANES),
+        "hidden_sums",
+        down_sum,
+        up_part,
+        up_far,
     )
     last_sum, *input_wide = local_call(
         last_sums_body,
@@ -1549,20 +1605,22 @@
         last_got,
         swap_rows(last_far, 2),
     )
+    output = cols_back(*out_wide, low, "out_join")
     input_grad = cols_back(*input_wide, wide, "input_join")
-    down_t, up_grad, out_t = local_call(
+    down_t, up_grad, out_t, vec_total = local_call(
         place_hidden_body,
-        [((feat_rows, 4 * part), wide)] * 2 + [((feat_rows, 2 * WIDTH), wide)],
+        [((feat_rows, 4 * part), wide)] * 2
+        + [((feat_rows, 2 * WIDTH), wide), ((feat_rows, SUM_LANES), wide)],
         "place_hidden",
         flags,
-        *all_quarters(hidden_sum),
-    )
-    query_grad, key_grad, value_grad, vec_total = local_call(
+        *all_quarters(hidden_sum, True),
+    )
+    query_grad, key_grad, value_grad = local_call(
         place_last_body,
-        [((feat_rows, 2 * WIDTH), wide)] * 3 + [((feat_rows, SUM_LANES), wide)],
+        [((feat_rows, 2 * WIDTH), wide)] * 3,
         "place_last",
         flags,
-        *all_quarters(last_sum),
+        *all_quarters(last_sum, True),
     )
     return (
         output,

time: 213 us -> 198 us (0.930)
  waiting for transfers between devices: 109 us -> 96.4 us
    ppermute x11, waiting for transfers between devices: 38.8 us -> 7.31 us  [swap_copies(): lax.ppermute(operand, 'dp', [(i, i ^ 2) for i in range(lax.axis_size('dp'...]
    ppermute x9, waiting for transfers between devices: 13.3 us -> 24.5 us  [swap_cols(): return lax.ppermute(operand, 'col', [(0, 1), (1, 0)])]
    ppermute x12, waiting for transfers between devices: 35.8 us -> 44.9 us  [swap_rows(): return lax.ppermute(operand, 'row', [(i, i ^ mask) for i in range(4)])]
    ppermute x6 -> x3, starting transfers between devices: 12.9 us -> 5.51 us  [rotate_rows(): lax.ppermute(operand, 'row', [(i, (i + step) % count) for i in range(coun...]
    ppermute x9, starting transfers between devices: 11.7 us -> 15 us  [swap_cols(): return lax.ppermute(operand, 'col', [(0, 1), (1, 0)])]
    ppermute x12, starting transfers between devices: 14.8 us -> 11.5 us  [swap_rows(): return lax.ppermute(operand, 'row', [(i, i ^ mask) for i in range(4)])]
    ppermute x11, starting transfers between devices: 12 us -> 14.9 us  [swap_copies(): lax.ppermute(operand, 'dp', [(i, i ^ 2) for i in range(lax.axis_size('dp'...]
    ppermute x6 -> x3, waiting for transfers between devices: 6.04 us -> 3.28 us  [rotate_rows(): lax.ppermute(operand, 'row', [(i, (i + step) % count) for i in range(coun...]
  transfers between devices with their start and end apart: 56 -> 53, of which waited for: 30 -> 27; matrix products, arithmetic and copies ran while one was open for 0% -> 1% of each run, Pallas kernels for 10% -> 12%
where the time goes in v4:
time: 198 us
  waiting for transfers between devices  96.4 us (49%)
  starting transfers between devices  61.9 us (31%)
  Pallas kernels  35.3 us (18%)
    ppermute x12, waiting for transfers between devices, swap_rows(): return lax.ppermute(operand, 'row', [(i, i ^ mask) for i in range(4)])  44.9 us
    pallas_call x38, Pallas kernels, local_call(): pl.pallas_call(body, out_shape=shapes, in_specs=[pl.BlockSpec(memory_spac...  35.3 us
    ppermute x9, waiting for transfers between devices, swap_cols(): return lax.ppermute(operand, 'col', [(0, 1), (1, 0)])  24.5 us
    ppermute x9, starting transfers between devices, swap_cols(): return lax.ppermute(operand, 'col', [(0, 1), (1, 0)])  15 us
    ppermute x11, starting transfers between devices, swap_copies(): lax.ppermute(operand, 'dp', [(i, i ^ 2) for i in range(lax.axis_size('dp'...  14.9 us
    ppermute x6, starting transfers between devices, shift_rows(): return lax.ppermute(operand, 'row', pairs)  12.9 us
    ppermute x12, starting transfers between devices, swap_rows(): return lax.ppermute(operand, 'row', [(i, i ^ mask) for i in range(4)])  11.5 us
    ppermute x10, waiting for transfers between devices, swap_pair(): lax.ppermute(operand, 'dp', [(i, i ^ 1) for i in range(lax.axis_size('dp'...  8.47 us
  transfers between devices with their start and end apart: 53, of which 27 were waited for; matrix products, arithmetic and copies ran while one was open for 1% of the time, Pallas kernels for 12%

profile of v4, /device:TPU:0, one launch (start us, length us, event | category | flops | bytes accessed | tf_op | source)
XLA Modules:
  0.0 197.6 jit_solution(9766708588987779547)
XLA Ops:
  1.9 3.0 %collective-permute-start.1 = (bf16[192,512]{1,0:T(8,128)(2,1)S(1)}, bf16[192,512]{1,0:T(8,128)(2,1)S(1)}, u32[]{:S(2)}, u32[]{:S(2)}) collective-permute-start(bf16[192,512]{1,0:T(8,128)(2,1)S(1)} %pad_maximum_fusion.1), channel_id=1, source_target_pairs={{0,1},{1,0},{2,3},{3,2},{4,5},{5,4},{6,7},{7,6},{8,9},{9,8},{10,11... | collective-permute-start | bytes 589832 | tf_op jit(solution)/shard_map/ppermute | solution.py:441
  7.0 2.6 %collective-permute-start.5 = (bf16[192,384]{1,0:T(8,128)(2,1)S(1)}, bf16[192,384]{1,0:T(8,128)(2,1)S(1)}, u32[]{:S(2)}, u32[]{:S(2)}) collective-permute-start(bf16[192,384]{1,0:T(8,128)(2,1)S(1)} %maximum_select_fusion), channel_id=1, source_target_pairs={{0,4},{2,6},{4,0},{6,2},{1,5},{3,7},{5,1},{7,3},{8,12},{10,14},{12... | collective-permute-start | bytes 442376 | tf_op jit(solution)/shard_map/ppermute | solution.py:459
  9.7 3.4 %collective-permute-done.refs_0_ = bf16[192,384]{1,0:T(8,128)(2,1)S(1)} collective-permute-done((bf16[192,384]{1,0:T(8,128)(2,1)S(1)}, bf16[192,384]{1,0:T(8,128)(2,1)S(1)}, u32[]{:S(2)}, u32[]{:S(2)}) %collective-permute-start) | collective-permute-done | bytes 147488 | tf_op jit(solution)/shard_map/ppermute | solution.py:459
  19.2 2.9 %collective-permute-start.4 = (bf16[208,256]{1,0:T(8,128)(2,1)S(1)}, bf16[208,256]{1,0:T(8,128)(2,1)S(1)}, u32[]{:S(2)}, u32[]{:S(2)}) collective-permute-start(bf16[208,256]{1,0:T(8,128)(2,1)S(1)} %get-tuple-element.148), channel_id=1, source_target_pairs={{0,6},{2,0},{4,2},{6,4},{1,7},{3,1},{5,3},{7,5},{8,14},{10,8},{12,... | collective-permute-start | bytes 319496 | tf_op jit(solution)/shard_map/ppermute | solution.py:464
  29.5 2.4 %collective-permute-start.16 = (bf16[192,768]{1,0:T(8,128)(2,1)S(1)}, bf16[192,768]{1,0:T(8,128)(2,1)S(1)}, u32[]{:S(2)}, u32[]{:S(2)}) collective-permute-start(bf16[192,768]{1,0:T(8,128)(2,1)S(1)} %get-tuple-element.162.refs_0_), channel_id=1, source_target_pairs={{0,4},{2,6},{4,0},{6,2},{1,5},{3,7},{5,1},{7,3},{8,12},{10,14},{12... | collective-permute-start | bytes 884744 | tf_op jit(solution)/shard_map/ppermute | solution.py:459
  34.7 4.2 %collective-permute-done.9.refs_1_ = bf16[192,768]{1,0:T(8,128)(2,1)S(1)} collective-permute-done((bf16[192,768]{1,0:T(8,128)(2,1)S(1)}, bf16[192,768]{1,0:T(8,128)(2,1)S(1)}, u32[]{:S(2)}, u32[]{:S(2)}) %collective-permute-start.9) | collective-permute-done | bytes 294944 | tf_op jit(solution)/shard_map/ppermute | solution.py:459
  39.5 2.5 %collective-permute-done.16.refs_2_ = bf16[192,768]{1,0:T(8,128)(2,1)S(1)} collective-permute-done((bf16[192,768]{1,0:T(8,128)(2,1)S(1)}, bf16[192,768]{1,0:T(8,128)(2,1)S(1)}, u32[]{:S(2)}, u32[]{:S(2)}) %collective-permute-start.16) | collective-permute-done | bytes 294944 | tf_op jit(solution)/shard_map/ppermute | solution.py:459
  45.8 3.9 %collective-permute-start.13 = (bf16[400,128]{1,0:T(8,128)(2,1)S(1)}, bf16[400,128]{1,0:T(8,128)(2,1)S(1)}, u32[]{:S(2)}, u32[]{:S(2)}) collective-permute-start(bf16[400,128]{1,0:T(8,128)(2,1)S(1)} %get-tuple-element.179), channel_id=1, source_target_pairs={{0,2},{2,4},{4,6},{1,3},{3,5},{5,7},{8,10},{10,12},{12,14},{9,11},... | collective-permute-start | bytes 307208 | tf_op jit(solution)/shard_map/ppermute | solution.py:455
  49.8 2.7 %collective-permute-start.14 = (bf16[400,128]{1,0:T(8,128)(2,1)S(1)}, bf16[400,128]{1,0:T(8,128)(2,1)S(1)}, u32[]{:S(2)}, u32[]{:S(2)}) collective-permute-start(bf16[400,128]{1,0:T(8,128)(2,1)S(1)} %get-tuple-element.179), channel_id=1, source_target_pairs={{0,4},{2,6},{1,5},{3,7},{8,12},{10,14},{9,13},{11,15},{16,20},{18,... | collective-permute-start | bytes 307208 | tf_op jit(solution)/shard_map/ppermute | solution.py:455
  52.5 2.1 %collective-permute-start.15 = (bf16[400,128]{1,0:T(8,128)(2,1)S(1)}, bf16[400,128]{1,0:T(8,128)(2,1)S(1)}, u32[]{:S(2)}, u32[]{:S(2)}) collective-permute-start(bf16[400,128]{1,0:T(8,128)(2,1)S(1)} %get-tuple-element.179), channel_id=1, source_target_pairs={{0,6},{1,7},{8,14},{9,15},{16,22},{17,23},{24,30},{25,31}} | collective-permute-start | bytes 307208 | tf_op jit(solution)/shard_map/ppermute | solution.py:455
  57.4 1.7 collective-permute-done.20.recv_ref
  59.2 2.3 %collective-permute-start.21 = (bf16[768,256]{1,0:T(8,128)(2,1)S(1)}, bf16[768,256]{1,0:T(8,128)(2,1)S(1)}, u32[]{:S(2)}, u32[]{:S(2)}) collective-permute-start(bf16[768,256]{1,0:T(8,128)(2,1)S(1)} %branch_half.1.half_ref), channel_id=1, source_target_pairs={{0,1},{1,0},{2,3},{3,2},{4,5},{5,4},{6,7},{7,6},{8,9},{9,8},{10,11... | collective-permute-start | bytes 1179656 | tf_op jit(solution)/shard_map/ppermute | solution.py:441
  63.0 7.3 %collective-permute-done.22.refs_3_ = bf16[192,768]{1,0:T(8,128)(2,1)S(1)} collective-permute-done((bf16[192,768]{1,0:T(8,128)(2,1)S(1)}, bf16[192,768]{1,0:T(8,128)(2,1)S(1)}, u32[]{:S(2)}, u32[]{:S(2)}) %collective-permute-start.22) | collective-permute-done | bytes 294944 | tf_op jit(solution)/shard_map/ppermute | solution.py:449
  71.6 1.7 collective-permute-done.23.other_ref
  73.3 2.2 %hidden_mine.1 = (bf16[768,768]{1,0:T(8,128)(2,1)S(1)}, bf16[384,512]{1,0:T(8,128)(2,1)S(1)}, f32[384,512]{1,0:T(8,128)S(1)}, f32[768,256]{1,0:T(8,128)S(1)}, f32[768,256]{1,0:T(8,128)S(1)}) custom-call(s32[5]{0:T(128)S(1)} %stack.38.flags_ref, bf16[768,256]{1,0:T(8,128)(2,1)S(1)} %get-tuple-element.193.own_ref, ...), custom_call_target="tpu_custom_call" | custom-call | tf_op jit(solution)/shard_map/hidden_mine/pallas_call | solution.py:497
  75.6 2.2 %hidden_copy.1 = (bf16[768,768]{1,0:T(8,128)(2,1)S(1)}, bf16[384,512]{1,0:T(8,128)(2,1)S(1)}, f32[384,512]{1,0:T(8,128)S(1)}, f32[768,256]{1,0:T(8,128)S(1)}, bf16[768,256]{1,0:T(8,128)(2,1)S(1)}) custom-call(s32[5]{0:T(128)S(1)} %stack.38.flags_ref, bf16[768,256]{1,0:T(8,128)(2,1)S(1)} %get-tuple-element.193.own_ref, ...), custom_call_target="tpu_custom_call" | custom-call | tf_op jit(solution)/shard_map/hidden_copy/pallas_call | solution.py:497
  79.7 1.8 collective-permute-start.25
  81.7 13.3 %collective-permute-done.26.recv_ref = bf16[384,256]{1,0:T(8,128)(2,1)S(1)} collective-permute-done((bf16[384,256]{1,0:T(8,128)(2,1)S(1)}, bf16[384,256]{1,0:T(8,128)(2,1)S(1)}, u32[]{:S(2)}, u32[]{:S(2)}) %collective-permute-start.26) | collective-permute-done | bytes 196640 | tf_op jit(solution)/shard_map/ppermute | solution.py:441
  99.7 1.8 hidden_back.1
  103.4 1.8 collective-permute-start.30
  107.7 6.9 %collective-permute-done.30.recv_ref = bf16[768,256]{1,0:T(8,128)(2,1)S(1)} collective-permute-done((bf16[768,256]{1,0:T(8,128)(2,1)S(1)}, bf16[768,256]{1,0:T(8,128)(2,1)S(1)}, u32[]{:S(2)}, u32[]{:S(2)}) %collective-permute-start.30) | collective-permute-done | bytes 393248 | tf_op jit(solution)/shard_map/ppermute | solution.py:441
  122.7 2.3 %collective-permute-done.32.refs_0_ = bf16[400,128]{1,0:T(8,128)(2,1)S(1)} collective-permute-done((bf16[400,128]{1,0:T(8,128)(2,1)S(1)}, bf16[400,128]{1,0:T(8,128)(2,1)S(1)}, u32[]{:S(2)}, u32[]{:S(2)}) %collective-permute-start.32) | collective-permute-done | bytes 102432 | tf_op jit(solution)/shard_map/ppermute | solution.py:455
  127.4 3.5 %collective-permute-done.36.refs_1_ = bf16[400,128]{1,0:T(8,128)(2,1)S(1)} collective-permute-done((bf16[400,128]{1,0:T(8,128)(2,1)S(1)}, bf16[400,128]{1,0:T(8,128)(2,1)S(1)}, u32[]{:S(2)}, u32[]{:S(2)}) %collective-permute-start.36) | collective-permute-done | bytes 102432 | tf_op jit(solution)/shard_map/ppermute | solution.py:455
  132.2 2.3 %grad_project.1 = (bf16[4,96,576]{2,1,0:T(8,128)(2,1)S(1)}, bf16[4,96,576]{2,1,0:T(8,128)(2,1)S(1)}, f32[768,256]{1,0:T(8,128)S(1)}, bf16[768,256]{1,0:T(8,128)(2,1)S(1)}) custom-call(bf16[2,192,256]{2,1,0:T(8,128)(2,1)S(1)} %get-tuple-element.239.grad_query_ref, f32[6,64,256]{2,1,0:T(8,128)S(1)} %get-tuple-element.240.grad_key_ref, ...), custom_call_target="tpu_custom_call" | custom-call | tf_op jit(solution)/shard_map/grad_project/pallas_call | solution.py:497
  137.7 1.8 collective-permute-start.41
  139.5 9.7 %collective-permute-done.33.got_ref = bf16[384,512]{1,0:T(8,128)(2,1)S(1)} collective-permute-done((bf16[384,512]{1,0:T(8,128)(2,1)S(1)}, bf16[384,512]{1,0:T(8,128)(2,1)S(1)}, u32[]{:S(2)}, u32[]{:S(2)}) %collective-permute-start.33) | collective-permute-done | bytes 393248 | tf_op jit(solution)/shard_map/ppermute | solution.py:459
  153.3 13.5 %collective-permute-done.34.far_ref = bf16[192,640]{1,0:T(8,128)(2,1)S(1)} collective-permute-done((bf16[192,640]{1,0:T(8,128)(2,1)S(1)}, bf16[192,640]{1,0:T(8,128)(2,1)S(1)}, u32[]{:S(2)}, u32[]{:S(2)}) %collective-permute-start.34) | collective-permute-done | bytes 245792 | tf_op jit(solution)/shard_map/ppermute | solution.py:459
  167.5 4.5 %collective-permute-done.49.up_far_ref = bf16[192,640]{1,0:T(8,128)(2,1)S(1)} collective-permute-done((bf16[192,640]{1,0:T(8,128)(2,1)S(1)}, bf16[192,640]{1,0:T(8,128)(2,1)S(1)}, u32[]{:S(2)}, u32[]{:S(2)}) %collective-permute-start.49) | collective-permute-done | bytes 245792 | tf_op jit(solution)/shard_map/ppermute | solution.py:459
  174.4 1.8 collective-permute-start.35
  176.2 3.0 %collective-permute-done.35.recv_ref = bf16[96,512]{1,0:T(8,128)(2,1)S(1)} collective-permute-done((bf16[96,512]{1,0:T(8,128)(2,1)S(1)}, bf16[96,512]{1,0:T(8,128)(2,1)S(1)}, u32[]{:S(2)}, u32[]{:S(2)}) %collective-permute-start.35) | collective-permute-done | bytes 98336 | tf_op jit(solution)/shard_map/ppermute | solution.py:441
  180.4 6.1 %collective-permute-done.43.far_ref = bf16[96,1088]{1,0:T(8,128)(2,1)S(1)} collective-permute-done((bf16[96,1088]{1,0:T(8,128)(2,1)S(1)}, bf16[96,1088]{1,0:T(8,128)(2,1)S(1)}, u32[]{:S(2)}, u32[]{:S(2)}) %collective-permute-start.43) | collective-permute-done | bytes 208928 | tf_op jit(solution)/shard_map/ppermute | solution.py:459
  191.6 2.2 %place_hidden.1 = (f32[192,1536]{1,0:T(8,128)}, f32[192,1536]{1,0:T(8,128)}, f32[192,384]{1,0:T(8,128)}, f32[192,64]{1,0:T(8,128)S(1)}) custom-call(s32[5]{0:T(128)S(1)} %stack.38.flags_ref, bf16[192,1024]{1,0:T(8,128)(2,1)S(1)} %hidden_sums.1.refs_0_, bf16[192,1024]{1,0:T(8,128)(2,1)S(1)} %collective-permute-done.50.refs_1_, ...), custom_call_target="tpu_custom_call" | custom-call | tf_op jit(solution)/shard_map/place_hidden/pallas_call | solution.py:497
  (143 shorter events, 72.6 us)
Async XLA Ops:
  1.9 11.2 %collective-permute-start.1 = (bf16[192,512]{1,0:T(8,128)(2,1)S(1)}, bf16[192,512]{1,0:T(8,128)(2,1)S(1)}, u32[]{:S(2)}, u32[]{:S(2)}) collective-permute-start(bf16[192,512]{1,0:T(8,128)(2,1)S(1)} %pad_maximum_fusion.1), channel_id=1, source_target_pairs={{0,1},{1,0},{2,3},{3,2},{4,5},{5,4},{6,7},{7,6},{8,9},{9,8},{10,11... | collective-permute-start | bytes 589832 | tf_op jit(solution)/shard_map/ppermute | solution.py:441
  7.0 9.2 %collective-permute-start.5 = (bf16[192,384]{1,0:T(8,128)(2,1)S(1)}, bf16[192,384]{1,0:T(8,128)(2,1)S(1)}, u32[]{:S(2)}, u32[]{:S(2)}) collective-permute-start(bf16[192,384]{1,0:T(8,128)(2,1)S(1)} %maximum_select_fusion), channel_id=1, source_target_pairs={{0,4},{2,6},{4,0},{6,2},{1,5},{3,7},{5,1},{7,3},{8,12},{10,14},{12... | collective-permute-start | bytes 442376 | tf_op jit(solution)/shard_map/ppermute | solution.py:459
  13.8 13.3 %collective-permute-start.7 = (bf16[192,384]{1,0:T(8,128)(2,1)S(1)}, bf16[192,384]{1,0:T(8,128)(2,1)S(1)}, u32[]{:S(2)}, u32[]{:S(2)}) collective-permute-start(bf16[192,384]{1,0:T(8,128)(2,1)S(1)} %collective-permute-done.refs_0_), channel_id=1, source_target_pairs={{0,16},{8,24},{16,0},{24,8},{1,17},{9,25},{17,1},{25,9},{2,18},{10... | collective-permute-start | bytes 442376 | tf_op jit(solution)/shard_map/ppermute | solution.py:449
  16.3 10.8 %collective-permute-start.6 = (bf16[192,384]{1,0:T(8,128)(2,1)S(1)}, bf16[192,384]{1,0:T(8,128)(2,1)S(1)}, u32[]{:S(2)}, u32[]{:S(2)}) collective-permute-start(bf16[192,384]{1,0:T(8,128)(2,1)S(1)} %collective-permute-done.5.refs_1_), channel_id=1, source_target_pairs={{0,2},{2,0},{4,6},{6,4},{1,3},{3,1},{5,7},{7,5},{8,10},{10,8},{12,... | collective-permute-start | bytes 442376 | tf_op jit(solution)/shard_map/ppermute | solution.py:459
  16.6 8.9 %collective-permute-start.2 = (bf16[208,256]{1,0:T(8,128)(2,1)S(1)}, bf16[208,256]{1,0:T(8,128)(2,1)S(1)}, u32[]{:S(2)}, u32[]{:S(2)}) collective-permute-start(bf16[208,256]{1,0:T(8,128)(2,1)S(1)} %get-tuple-element.146), channel_id=1, source_target_pairs={{0,2},{2,4},{4,6},{6,0},{1,3},{3,5},{5,7},{7,1},{8,10},{10,12},{12... | collective-permute-start | bytes 319496 | tf_op jit(solution)/shard_map/ppermute | solution.py:464
  27.9 11.0 %collective-permute-start.9 = (bf16[192,768]{1,0:T(8,128)(2,1)S(1)}, bf16[192,768]{1,0:T(8,128)(2,1)S(1)}, u32[]{:S(2)}, u32[]{:S(2)}) collective-permute-start(bf16[192,768]{1,0:T(8,128)(2,1)S(1)} %get-tuple-element.162.refs_0_), channel_id=1, source_target_pairs={{0,2},{2,0},{4,6},{6,4},{1,3},{3,1},{5,7},{7,5},{8,10},{10,8},{12,... | collective-permute-start | bytes 884744 | tf_op jit(solution)/shard_map/ppermute | solution.py:459
  29.5 12.5 %collective-permute-start.16 = (bf16[192,768]{1,0:T(8,128)(2,1)S(1)}, bf16[192,768]{1,0:T(8,128)(2,1)S(1)}, u32[]{:S(2)}, u32[]{:S(2)}) collective-permute-start(bf16[192,768]{1,0:T(8,128)(2,1)S(1)} %get-tuple-element.162.refs_0_), channel_id=1, source_target_pairs={{0,4},{2,6},{4,0},{6,2},{1,5},{3,7},{5,1},{7,3},{8,12},{10,14},{12... | collective-permute-start | bytes 884744 | tf_op jit(solution)/shard_map/ppermute | solution.py:459
  42.0 10.5 %collective-permute-start.17 = (bf16[192,768]{1,0:T(8,128)(2,1)S(1)}, bf16[192,768]{1,0:T(8,128)(2,1)S(1)}, u32[]{:S(2)}, u32[]{:S(2)}) collective-permute-start(bf16[192,768]{1,0:T(8,128)(2,1)S(1)} %collective-permute-done.16.refs_2_), channel_id=1, source_target_pairs={{0,2},{2,0},{4,6},{6,4},{1,3},{3,1},{5,7},{7,5},{8,10},{10,8},{12,... | collective-permute-start | bytes 884744 | tf_op jit(solution)/shard_map/ppermute | solution.py:459
  42.0 14.0 %collective-permute-start.18 = (bf16[192,768]{1,0:T(8,128)(2,1)S(1)}, bf16[192,768]{1,0:T(8,128)(2,1)S(1)}, u32[]{:S(2)}, u32[]{:S(2)}) collective-permute-start(bf16[192,768]{1,0:T(8,128)(2,1)S(1)} %collective-permute-done.16.refs_2_), channel_id=1, source_target_pairs={{0,16},{8,24},{16,0},{24,8},{1,17},{9,25},{17,1},{25,9},{2,18},{10... | collective-permute-start | bytes 884744 | tf_op jit(solution)/shard_map/ppermute | solution.py:449
  43.5 13.8 %collective-permute-start.19 = (bf16[192,768]{1,0:T(8,128)(2,1)S(1)}, bf16[192,768]{1,0:T(8,128)(2,1)S(1)}, u32[]{:S(2)}, u32[]{:S(2)}) collective-permute-start(bf16[192,768]{1,0:T(8,128)(2,1)S(1)} %collective-permute-done.9.refs_1_), channel_id=1, source_target_pairs={{0,16},{8,24},{16,0},{24,8},{1,17},{9,25},{17,1},{25,9},{2,18},{10... | collective-permute-start | bytes 884744 | tf_op jit(solution)/shard_map/ppermute | solution.py:449
  45.8 10.2 %collective-permute-start.13 = (bf16[400,128]{1,0:T(8,128)(2,1)S(1)}, bf16[400,128]{1,0:T(8,128)(2,1)S(1)}, u32[]{:S(2)}, u32[]{:S(2)}) collective-permute-start(bf16[400,128]{1,0:T(8,128)(2,1)S(1)} %get-tuple-element.179), channel_id=1, source_target_pairs={{0,2},{2,4},{4,6},{1,3},{3,5},{5,7},{8,10},{10,12},{12,14},{9,11},... | collective-permute-start | bytes 307208 | tf_op jit(solution)/shard_map/ppermute | solution.py:455
  59.2 11.7 %collective-permute-start.21 = (bf16[768,256]{1,0:T(8,128)(2,1)S(1)}, bf16[768,256]{1,0:T(8,128)(2,1)S(1)}, u32[]{:S(2)}, u32[]{:S(2)}) collective-permute-start(bf16[768,256]{1,0:T(8,128)(2,1)S(1)} %branch_half.1.half_ref), channel_id=1, source_target_pairs={{0,1},{1,0},{2,3},{3,2},{4,5},{5,4},{6,7},{7,6},{8,9},{9,8},{10,11... | collective-permute-start | bytes 1179656 | tf_op jit(solution)/shard_map/ppermute | solution.py:441
  61.5 8.8 %collective-permute-start.22 = (bf16[192,768]{1,0:T(8,128)(2,1)S(1)}, bf16[192,768]{1,0:T(8,128)(2,1)S(1)}, u32[]{:S(2)}, u32[]{:S(2)}) collective-permute-start(bf16[192,768]{1,0:T(8,128)(2,1)S(1)} %collective-permute-done.17.refs_3_), channel_id=1, source_target_pairs={{0,16},{8,24},{16,0},{24,8},{1,17},{9,25},{17,1},{25,9},{2,18},{10... | collective-permute-start | bytes 884744 | tf_op jit(solution)/shard_map/ppermute | solution.py:449
  79.7 16.0 %collective-permute-start.25 = (bf16[768,256]{1,0:T(8,128)(2,1)S(1)}, bf16[768,256]{1,0:T(8,128)(2,1)S(1)}, u32[]{:S(2)}, u32[]{:S(2)}) collective-permute-start(bf16[768,256]{1,0:T(8,128)(2,1)S(1)} %ffn_half.1.half_ref), channel_id=1, source_target_pairs={{0,1},{1,0},{2,3},{3,2},{4,5},{5,4},{6,7},{7,6},{8,9},{9,8},{10,11... | collective-permute-start | bytes 1179656 | tf_op jit(solution)/shard_map/ppermute | solution.py:441
  81.5 13.6 %collective-permute-start.26 = (bf16[384,256]{1,0:T(8,128)(2,1)S(1)}, bf16[384,256]{1,0:T(8,128)(2,1)S(1)}, u32[]{:S(2)}, u32[]{:S(2)}) collective-permute-start(bf16[384,256]{1,0:T(8,128)(2,1)S(1)} %get-tuple-element.202.half_ref), channel_id=1, source_target_pairs={{0,1},{1,0},{2,3},{3,2},{4,5},{5,4},{6,7},{7,6},{8,9},{9,8},{10,11... | collective-permute-start | bytes 589832 | tf_op jit(solution)/shard_map/ppermute | solution.py:441
  103.4 11.2 %collective-permute-start.30 = (bf16[768,256]{1,0:T(8,128)(2,1)S(1)}, bf16[768,256]{1,0:T(8,128)(2,1)S(1)}, u32[]{:S(2)}, u32[]{:S(2)}) collective-permute-start(bf16[768,256]{1,0:T(8,128)(2,1)S(1)} %first_half.1.half_ref), channel_id=1, source_target_pairs={{0,1},{1,0},{2,3},{3,2},{4,5},{5,4},{6,7},{7,6},{8,9},{9,8},{10,11... | collective-permute-start | bytes 1179656 | tf_op jit(solution)/shard_map/ppermute | solution.py:441
  106.2 16.5 %collective-permute-start.38 = (bf16[768,384]{1,0:T(8,128)(2,1)S(1)}, bf16[768,384]{1,0:T(8,128)(2,1)S(1)}, u32[]{:S(2)}, u32[]{:S(2)}) collective-permute-start(bf16[768,384]{1,0:T(8,128)(2,1)S(1)} %get-tuple-element.243), channel_id=1, source_target_pairs={{0,16},{8,24},{16,0},{24,8},{1,17},{9,25},{17,1},{25,9},{2,18},{10... | collective-permute-start | bytes 1769480 | tf_op jit(solution)/shard_map/ppermute | solution.py:449
  115.5 19.1 %collective-permute-start.28 = (bf16[768,384]{1,0:T(8,128)(2,1)S(1)}, bf16[768,384]{1,0:T(8,128)(2,1)S(1)}, u32[]{:S(2)}, u32[]{:S(2)}) collective-permute-start(bf16[768,384]{1,0:T(8,128)(2,1)S(1)} %get-tuple-element.208), channel_id=1, source_target_pairs={{0,16},{8,24},{16,0},{24,8},{1,17},{9,25},{17,1},{25,9},{2,18},{10... | collective-permute-start | bytes 1769480 | tf_op jit(solution)/shard_map/ppermute | solution.py:449
  119.4 11.5 %collective-permute-start.36 = (bf16[400,128]{1,0:T(8,128)(2,1)S(1)}, bf16[400,128]{1,0:T(8,128)(2,1)S(1)}, u32[]{:S(2)}, u32[]{:S(2)}) collective-permute-start(bf16[400,128]{1,0:T(8,128)(2,1)S(1)} %get-tuple-element.226), channel_id=1, source_target_pairs={{4,0},{6,2},{5,1},{7,3},{12,8},{14,10},{13,9},{15,11},{20,16},{22,... | collective-permute-start | bytes 307208 | tf_op jit(solution)/shard_map/ppermute | solution.py:455
  120.7 11.5 %collective-permute-start.37 = (bf16[400,128]{1,0:T(8,128)(2,1)S(1)}, bf16[400,128]{1,0:T(8,128)(2,1)S(1)}, u32[]{:S(2)}, u32[]{:S(2)}) collective-permute-start(bf16[400,128]{1,0:T(8,128)(2,1)S(1)} %get-tuple-element.226), channel_id=1, source_target_pairs={{6,0},{7,1},{14,8},{15,9},{22,16},{23,17},{30,24},{31,25}} | collective-permute-start | bytes 307208 | tf_op jit(solution)/shard_map/ppermute | solution.py:455
  125.8 25.1 %collective-permute-start.48 = (bf16[384,640]{1,0:T(8,128)(2,1)S(1)}, bf16[384,640]{1,0:T(8,128)(2,1)S(1)}, u32[]{:S(2)}, u32[]{:S(2)}) collective-permute-start(bf16[384,640]{1,0:T(8,128)(2,1)S(1)} %get-tuple-element.269), channel_id=1, source_target_pairs={{0,2},{2,0},{4,6},{6,4},{1,3},{3,1},{5,7},{7,5},{8,10},{10,8},{12,... | collective-permute-start | bytes 1474568 | tf_op jit(solution)/shard_map/ppermute | solution.py:459
  135.3 13.8 %collective-permute-start.33 = (bf16[384,512]{1,0:T(8,128)(2,1)S(1)}, bf16[384,512]{1,0:T(8,128)(2,1)S(1)}, u32[]{:S(2)}, u32[]{:S(2)}) collective-permute-start(bf16[384,512]{1,0:T(8,128)(2,1)S(1)} %get-tuple-element.230), channel_id=1, source_target_pairs={{0,2},{2,0},{4,6},{6,4},{1,3},{3,1},{5,7},{7,5},{8,10},{10,8},{12,... | collective-permute-start | bytes 1179656 | tf_op jit(solution)/shard_map/ppermute | solution.py:459
  135.4 17.0 %collective-permute-start.39 = (bf16[4,96,576]{2,1,0:T(8,128)(2,1)S(1)}, bf16[4,96,576]{2,1,0:T(8,128)(2,1)S(1)}, u32[]{:S(2)}, u32[]{:S(2)}) collective-permute-start(bf16[4,96,576]{2,1,0:T(8,128)(2,1)S(1)} %get-tuple-element.251), channel_id=1, source_target_pairs={{0,16},{8,24},{16,0},{24,8},{1,17},{9,25},{17,1},{25,9},{2,18},{10... | collective-permute-start | bytes 1327112 | tf_op jit(solution)/shard_map/ppermute | solution.py:449
  137.7 14.8 %collective-permute-start.41 = (bf16[384,256]{1,0:T(8,128)(2,1)S(1)}, bf16[384,256]{1,0:T(8,128)(2,1)S(1)}, u32[]{:S(2)}, u32[]{:S(2)}) collective-permute-start(bf16[384,256]{1,0:T(8,128)(2,1)S(1)} %get-tuple-element.255), channel_id=1, source_target_pairs={{0,1},{1,0},{2,3},{3,2},{4,5},{5,4},{6,7},{7,6},{8,9},{9,8},{10,11... | collective-permute-start | bytes 589832 | tf_op jit(solution)/shard_map/ppermute | solution.py:441
  149.3 17.6 %collective-permute-start.34 = (bf16[192,640]{1,0:T(8,128)(2,1)S(1)}, bf16[192,640]{1,0:T(8,128)(2,1)S(1)}, u32[]{:S(2)}, u32[]{:S(2)}) collective-permute-start(bf16[192,640]{1,0:T(8,128)(2,1)S(1)} %get-tuple-element.232), channel_id=1, source_target_pairs={{0,4},{2,6},{4,0},{6,2},{1,5},{3,7},{5,1},{7,3},{8,12},{10,14},{12... | collective-permute-start | bytes 737288 | tf_op jit(solution)/shard_map/ppermute | solution.py:459
  151.0 21.0 %collective-permute-start.49 = (bf16[192,640]{1,0:T(8,128)(2,1)S(1)}, bf16[192,640]{1,0:T(8,128)(2,1)S(1)}, u32[]{:S(2)}, u32[]{:S(2)}) collective-permute-start(bf16[192,640]{1,0:T(8,128)(2,1)S(1)} %get-tuple-element.271), channel_id=1, source_target_pairs={{0,4},{2,6},{4,0},{6,2},{1,5},{3,7},{5,1},{7,3},{8,12},{10,14},{12... | collective-permute-start | bytes 737288 | tf_op jit(solution)/shard_map/ppermute | solution.py:459
  153.2 21.1 %collective-permute-start.42 = (bf16[192,832]{1,0:T(8,128)(2,1)S(1)}, bf16[192,832]{1,0:T(8,128)(2,1)S(1)}, u32[]{:S(2)}, u32[]{:S(2)}) collective-permute-start(bf16[192,832]{1,0:T(8,128)(2,1)S(1)} %get-tuple-element.258), channel_id=1, source_target_pairs={{0,2},{2,0},{4,6},{6,4},{1,3},{3,1},{5,7},{7,5},{8,10},{10,8},{12,... | collective-permute-start | bytes 958472 | tf_op jit(solution)/shard_map/ppermute | solution.py:459
  172.1 17.0 %collective-permute-start.50 = (bf16[192,1024]{1,0:T(8,128)(2,1)S(1)}, bf16[192,1024]{1,0:T(8,128)(2,1)S(1)}, u32[]{:S(2)}, u32[]{:S(2)}) collective-permute-start(bf16[192,1024]{1,0:T(8,128)(2,1)S(1)} %hidden_sums.1.refs_0_), channel_id=1, source_target_pairs={{0,16},{8,24},{16,0},{24,8},{1,17},{9,25},{17,1},{25,9},{2,18},{10... | collective-permute-start | bytes 1179656 | tf_op jit(solution)/shard_map/ppermute | solution.py:449
  173.6 16.1 %collective-permute-start.51 = (bf16[192,1024]{1,0:T(8,128)(2,1)S(1)}, bf16[192,1024]{1,0:T(8,128)(2,1)S(1)}, u32[]{:S(2)}, u32[]{:S(2)}) collective-permute-start(bf16[192,1024]{1,0:T(8,128)(2,1)S(1)} %hidden_sums.1.refs_0_), channel_id=1, source_target_pairs={{0,8},{8,0},{16,24},{24,16},{1,9},{9,1},{17,25},{25,17},{2,10},{10... | collective-permute-start | bytes 1179656 | tf_op jit(solution)/shard_map/ppermute | solution.py:445
  173.6 17.9 %collective-permute-start.52 = (bf16[192,1024]{1,0:T(8,128)(2,1)S(1)}, bf16[192,1024]{1,0:T(8,128)(2,1)S(1)}, u32[]{:S(2)}, u32[]{:S(2)}) collective-permute-start(bf16[192,1024]{1,0:T(8,128)(2,1)S(1)} %hidden_sums.1.refs_0_), channel_id=1, source_target_pairs={{0,24},{8,16},{16,8},{24,0},{1,25},{9,17},{17,9},{25,1},{2,26},{10... | collective-permute-start | bytes 1179656 | tf_op jit(solution)/shard_map/ppermute | solution.py:1174
  174.4 12.2 %collective-permute-start.43 = (bf16[96,1088]{1,0:T(8,128)(2,1)S(1)}, bf16[96,1088]{1,0:T(8,128)(2,1)S(1)}, u32[]{:S(2)}, u32[]{:S(2)}) collective-permute-start(bf16[96,1088]{1,0:T(8,128)(2,1)S(1)} %get-tuple-element.260), channel_id=1, source_target_pairs={{0,4},{2,6},{4,0},{6,2},{1,5},{3,7},{5,1},{7,3},{8,12},{10,14},{12... | collective-permute-start | bytes 626696 | tf_op jit(solution)/shard_map/ppermute | solution.py:459
  187.5 8.5 %collective-permute-start.45 = (bf16[96,576]{1,0:T(8,128)(2,1)S(1)}, bf16[96,576]{1,0:T(8,128)(2,1)S(1)}, u32[]{:S(2)}, u32[]{:S(2)}) collective-permute-start(bf16[96,576]{1,0:T(8,128)(2,1)S(1)} %get-tuple-element.263.refs_0_), channel_id=1, source_target_pairs={{0,16},{8,24},{16,0},{24,8},{1,17},{9,25},{17,1},{25,9},{2,18},{10... | collective-permute-start | bytes 331784 | tf_op jit(solution)/shard_map/ppermute | solution.py:449
  (32 other events, 212.4 us)

commit v5 on v4

--- a/solution.py
+++ b/solution.py
@@ -567,25 +567,29 @@
 
 
 def place_tokens_body(flags_ref, *refs, rows, part):
-    pieces, (half_ref, cot_ref, vec_ref) = refs[:rows], refs[rows:]
+    pieces, (half_ref, vec_ref) = refs[:rows], refs[rows:]
+    below = half_ref.shape[0] // 2
     for step, ref in enumerate(pieces):
         row = came_from(flags_ref, step, rows)
         half_ref[pl.ds(pl.multiple_of(row * part, 16), part), :] = ref[:part]
-        cot_ref[pl.ds(pl.multiple_of(row * part, 16), part), :] = ref[part : 2 * part]
+        half_ref[pl.ds(pl.multiple_of(below + row * part, 16), part), :] = ref[part : 2 * part]
         extra = ref[2 * part :].astype(wide)
         sums = [extra[2 * i : 2 * i + 1] + extra[2 * i + 1 : 2 * i + 2] for i in range(4)]
         columns = jnp.concatenate(sums + [jnp.zeros((4, SPAN), wide)], 0).T
         vec_ref[pl.ds(pl.multiple_of(row * 2 * part, 8), 2 * part), :] = columns[: 2 * part]
 
 
-def join_halves_body(flags_ref, half_ref, recv_ref, full_ref, *, rows):
-    part = half_ref.shape[0] // rows
+def join_halves_body(flags_ref, half_ref, recv_ref, x_ref, cot_ref, *, rows):
+    part = half_ref.shape[0] // (2 * rows)
     first_col = flags_ref[COL] == 0
-    for row in range(rows):
-        own = half_ref[row * part : (row + 1) * part]
-        other = recv_ref[row * part : (row + 1) * part]
-        full_ref[2 * row * part : (2 * row + 1) * part] = jnp.where(first_col, own, other)
-        full_ref[(2 * row + 1) * part : (2 * row + 2) * part] = jnp.where(first_col, other, own)
+    for place, full_ref in enumerate((x_ref, cot_ref)):
+        for row in range(rows):
+            source = (place * rows + row) * part
+            own = half_ref[source : source + part]
+            other = recv_ref[source : source + part]
+            start = 2 * row * part
+            full_ref[start : start + part] = jnp.where(first_col, own, other)
+            full_ref[start + part : start + 2 * part] = jnp.where(first_col, other, own)
 
 
 def add_body(own_ref, recv_ref, half_ref):
@@ -679,74 +683,112 @@
     place_back(flags_ref, pieces, rows, own_ref, other_ref)
 
 
-def pair_pieces_body(flags_ref, kept_ref, got_ref, *refs):
-    extras, (held_ref, sent_ref) = refs[:-2], refs[-2:]
-    rows = 4
-    feats, part = kept_ref.shape[0] // rows, kept_ref.shape[1]
-    for mask in range(rows):
-        ref = sent_ref if mask % 2 else held_ref
-        out = slice(mask // 2 * feats, (mask // 2 + 1) * feats)
-        place = partner(flags_ref[ROW], mask)
-        rows_in = pl.ds(pl.multiple_of(place * feats, 16), feats)
-        ref[out, :part] = (
-            kept_ref[rows_in, :].astype(wide) + got_ref[rows_in, :].astype(wide)
+def down_grad_body(
+    flags_ref, own_ref, other_ref, mine_ref, copy_ref, held_ref, sent_ref, grad_ref
+):
+    feats, part = held_ref.shape[0] // 2, mine_ref.shape[0]
+    for act_ref, cols in ((mine_ref, slice(0, part)), (copy_ref, slice(part, 2 * part))):
+        grad_ref[:, cols] = (
+            dot_nt(own_ref[...], act_ref[:, :SPAN]) + dot_nt(other_ref[...], act_ref[:, SPAN:])
         ).astype(low)
-        lane = part
-        for extra in extras:
-            width = min(extra.shape[1], ref.shape[1] - lane)
-            ref[out, lane : lane + width] = extra[rows_in, :width]
-            lane = lane + width
-
-
-def pair_sums_body(held_ref, got_ref, sum_ref, sent_ref):
-    feats = sum_ref.shape[0]
-    sum_ref[...] = held_ref[:feats].astype(wide) + got_ref[:feats].astype(wide)
-    sent_ref[...] = (held_ref[feats:].astype(wide) + got_ref[feats:].astype(wide)).astype(low)
-
-
-def hidden_sums_body(down_ref, up_ref, up_far_ref, sum_ref):
-    part = down_ref.shape[1]
-    sum_ref[:, :part] = down_ref[...]
-    sum_ref[:, part:] = (up_ref[...] + up_far_ref[...].astype(wide)).astype(low)
-
-
-def down_pieces_body(flags_ref, kept_ref, got_ref, result_ref, held_ref, sent_ref):
-    feats, part = kept_ref.shape[0] // 4, kept_ref.shape[1]
-    half = feats // 2
     for mask in range(4):
         ref = sent_ref if mask % 2 else held_ref
         start = mask // 2 * feats
         place = partner(flags_ref[ROW], mask)
         rows_in = pl.ds(pl.multiple_of(place * feats, 16), feats)
-        ref[start : start + feats, :part] = (
+        ref[start : start + feats, :] = grad_ref[rows_in, :]
+
+
+def down_pairs_body(held_ref, got_ref, kept_ref, sent_ref):
+    part = kept_ref.shape[1]
+    kept_ref[...] = held_ref[:, :part].astype(wide) + got_ref[:, :part].astype(wide)
+    sent_ref[...] = (held_ref[:, part:].astype(wide) + got_ref[:, part:].astype(wide)).astype(low)
+
+
+def mix_body(
+    flags_ref, own_ref, other_ref, attn_wide_ref, vec_ref, pair_ref, kept_ref, sent_ref, grad_ref
+):
+    grad_ref[:, :WIDTH] = (
+        dot_nt(own_ref[...], attn_wide_ref[:WIDTH, :].astype(low))
+        + dot_nt(other_ref[...], attn_wide_ref[WIDTH : 2 * WIDTH, :].astype(low))
+    ).astype(low)
+    grad_ref[:, WIDTH:] = vec_ref[:, :SUM_LANES]
+    first_copy = flags_ref[COPY] == 0
+    half = (WIDTH + SUM_LANES) // 2
+    kept_ref[...] = jnp.where(first_copy, grad_ref[:, :half], grad_ref[:, half:])
+    sent = jnp.where(first_copy, grad_ref[:, half:], grad_ref[:, :half])
+    lines, part = pair_ref.shape
+    sent_ref[:, :part] = pair_ref[...]
+    sent_ref[:, part : part + half] = sent[:lines]
+    sent_ref[:, part + half :] = sent[lines:]
+
+
+def down_far_body(kept_ref, got_ref, sum_ref, sent_ref):
+    feats, part = sum_ref.shape
+    sum_ref[...] = kept_ref[:feats] + got_ref[:feats, :part].astype(wide)
+    sent_ref[...] = (kept_ref[feats:] + got_ref[feats:, :part].astype(wide)).astype(low)
+
+
+def up_pieces_body(
+    flags_ref, result_ref, kept_ref, got_ref, mix_ref, mix_got_ref, held_ref, sent_ref, sum_ref
+):
+    feats, part = kept_ref.shape[0] // 4, kept_ref.shape[1]
+    half, lanes = feats // 2, SPAN // 2
+    lines, cols = mix_got_ref.shape[0], mix_ref.shape[1]
+    sum_ref[:lines] = (
+        mix_ref[:lines].astype(wide) + mix_got_ref[:, part : part + cols].astype(wide)
+    ).astype(low)
+    sum_ref[lines:] = (
+        mix_ref[lines:].astype(wide) + mix_got_ref[:, part + cols :].astype(wide)
+    ).astype(low)
+    for mask in range(4):
+        ref = sent_ref if mask % 2 else held_ref
+        start = mask // 2 * feats
+        out = slice(start, start + feats)
+        place = partner(flags_ref[ROW], mask)
+        rows_in = pl.ds(pl.multiple_of((place * 2 + flags_ref[COL]) * half, 16), half)
+        ref[start : start + half, :lanes] = result_ref[rows_in, :lanes]
+        ref[start + half : start + feats, :lanes] = result_ref[rows_in, lanes:]
+        rows_in = pl.ds(pl.multiple_of(place * feats, 16), feats)
+        ref[out, lanes : lanes + part] = (
             kept_ref[rows_in, :].astype(wide) + got_ref[rows_in, :].astype(wide)
         ).astype(low)
-        rows_in = pl.ds(pl.multiple_of((place * 2 + flags_ref[COL]) * half, 16), half)
-        ref[start : start + half, part:] = result_ref[rows_in, : SPAN // 2]
-        ref[start + half : start + feats, part:] = result_ref[rows_in, SPAN // 2 :]
-
-
-def down_pairs_body(held_ref, got_ref, sum_ref, sent_ref):
-    feats, part = sum_ref.shape
+        ref[out, lanes + part :] = sum_ref[rows_in, :]
+
+
+def up_pairs_body(held_ref, got_ref, sum_ref, sent_ref):
+    feats, total = held_ref.shape[0] // 2, held_ref.shape[1]
     lanes = SPAN // 2
-    sum_ref[...] = held_ref[:feats, :part].astype(wide) + got_ref[:feats, :part].astype(wide)
-    pair = held_ref[feats:, :part].astype(wide) + got_ref[feats:, :part].astype(wide)
-    sent_ref[:, :part] = pair.astype(low)
-    sent_ref[:, part : part + lanes] = held_ref[feats:, part:]
-    sent_ref[:, part + lanes :] = got_ref[feats:, part:]
-
-
-def down_sums_body(
-    flags_ref, part_ref, held_ref, got_ref, far_ref, sum_ref, own_ref, other_ref, piece_ref
+    sum_ref[...] = held_ref[:feats, lanes:].astype(wide) + got_ref[:feats, lanes:].astype(wide)
+    pair = held_ref[feats:, lanes:].astype(wide) + got_ref[feats:, lanes:].astype(wide)
+    sent_ref[:, :lanes] = held_ref[feats:, :lanes]
+    sent_ref[:, lanes:total] = pair.astype(low)
+    sent_ref[:, total:] = got_ref[feats:, :lanes]
+
+
+def hidden_sums_body(
+    flags_ref,
+    down_ref,
+    down_far_ref,
+    up_ref,
+    held_ref,
+    got_ref,
+    far_ref,
+    sum_ref,
+    own_ref,
+    other_ref,
+    piece_ref,
 ):
-    feats, part = part_ref.shape
+    feats, part = down_ref.shape
     lanes = SPAN // 2
-    sum_ref[...] = (part_ref[...] + far_ref[:, :part].astype(wide)).astype(low)
+    total = lanes + up_ref.shape[1]
+    sum_ref[:, :part] = (down_ref[...] + down_far_ref[...].astype(wide)).astype(low)
+    sum_ref[:, part:] = (up_ref[...] + far_ref[:, lanes:total].astype(wide)).astype(low)
     pieces = (
-        held_ref[:feats, part:],
-        got_ref[:feats, part:],
-        far_ref[:, part : part + lanes],
-        far_ref[:, part + lanes :],
+        held_ref[:feats, :lanes],
+        got_ref[:feats, :lanes],
+        far_ref[:, :lanes],
+        far_ref[:, total:],
     )
     for place, piece in enumerate(pieces):
         piece_ref[place, :, :lanes] = piece[: feats // 2]
@@ -1059,24 +1101,25 @@
     sum_ref[...] = (lane_sums((grad_in * normed, grad_in), 0) + grad_ref[:, SPAN:]).astype(low)
 
 
-def hidden_body(flags_ref, own_ref, other_ref, *refs):
-    weight_ref, act_ref, slope_ref, part_own_ref, part_other_ref = refs[-5:]
-    blocks, earlier = refs[:4], refs[4:-5]
-    part = act_ref.shape[0]
-    for mask, ref in enumerate(blocks):
-        weight_ref[row_block(flags_ref, mask, ref.shape[0]), :] = ref[...]
-    up = weight_ref[:, :part]
-    down = weight_ref[:, part:]
-    for seq, (x_ref, part_ref) in enumerate(
-        ((own_ref, part_own_ref), (other_ref, part_other_ref))
-    ):
+def hidden_weights_body(flags_ref, *refs):
+    blocks, outs = refs[:-2], refs[-2:]
+    for half, weight_ref in enumerate(outs):
+        for mask, ref in enumerate(blocks[4 * half : 4 * half + 4]):
+            weight_ref[row_block(flags_ref, mask, ref.shape[0]), :] = ref[...]
+
+
+def hidden_body(own_ref, other_ref, mine_ref, copy_ref, *refs):
+    acts, slopes, parts = refs[:2], refs[2:4], refs[4:]
+    part = acts[0].shape[0]
+    for seq, (x_ref, part_ref) in enumerate(zip((own_ref, other_ref), parts)):
         cols = slice(seq * SPAN, (seq + 1) * SPAN)
-        act, slope = gelu_and_slope(dot_tn(up, x_ref[...]))
-        act_ref[:, cols] = act
-        slope_ref[:, cols] = slope
-        total = dot_nn(down, act)
-        if earlier:
-            total = total + earlier[seq][...]
+        total = None
+        for weight_ref, act_ref, slope_ref in zip((mine_ref, copy_ref), acts, slopes):
+            act, slope = gelu_and_slope(dot_tn(weight_ref[:, :part], x_ref[...]))
+            act_ref[:, cols] = act
+            slope_ref[:, cols] = slope
+            term = dot_nn(weight_ref[:, part:], act)
+            total = term if total is None else total + term
         part_ref[...] = total.astype(part_ref.dtype)
 
 
@@ -1116,13 +1159,6 @@
         ).astype(low)
 
 
-def out_grad_body(own_ref, other_ref, attn_wide_ref, out_ref):
-    out_ref[...] = (
-        dot_nt(own_ref[...], attn_wide_ref[:WIDTH, :].astype(low))
-        + dot_nt(other_ref[...], attn_wide_ref[WIDTH : 2 * WIDTH, :].astype(low))
-    ).astype(low)
-
-
 def quarters(flags_ref, refs):
     core, copy = flags_ref[CORE], flags_ref[COPY]
     for ref, other_core, other_copy in zip(refs, (0, 0, 1, 1), (0, 1, 0, 1)):
@@ -1138,13 +1174,18 @@
         cols = pl.ds(pl.multiple_of(place * part, 128), part)
         down_ref[:, cols] = ref[:, :part].astype(wide)
         up_ref[:, cols] = ref[:, part : 2 * part].astype(wide)
-    sums = [ref[:, 2 * part :].astype(wide) for ref in refs[:4]]
-    own, other = sums[0] + sums[1], sums[2] + sums[3]
-    vec_ref[...] = own[:, WIDTH:] + other[:, WIDTH:]
-    own, other = own[:, :WIDTH], other[:, :WIDTH]
-    first_core = flags_ref[CORE] == 0
-    out_ref[:, :WIDTH] = jnp.where(first_core, own, other)
-    out_ref[:, WIDTH:] = jnp.where(first_core, other, own)
+    half = (WIDTH + SUM_LANES) // 2
+    first_core, first_copy = flags_ref[CORE] == 0, flags_ref[COPY] == 0
+    sums = []
+    for own_ref, copy_ref in (refs[:2], refs[2:4]):
+        own, copied = own_ref[:, 2 * part :].astype(wide), copy_ref[:, 2 * part :].astype(wide)
+        sums.append((jnp.where(first_copy, own, copied), jnp.where(first_copy, copied, own)))
+    first = [jnp.where(first_core, sums[0][i], sums[1][i]) for i in (0, 1)]
+    second = [jnp.where(first_core, sums[1][i], sums[0][i]) for i in (0, 1)]
+    for parts, start in ((first, 0), (second, WIDTH)):
+        out_ref[:, start : start + half] = parts[0]
+        out_ref[:, start + half : start + WIDTH] = parts[1][:, : WIDTH - half]
+    vec_ref[...] = first[1][:, WIDTH - half :] + second[1][:, WIDTH - half :]
 
 
 def place_last_body(flags_ref, *refs):
@@ -1211,11 +1252,6 @@
             rotate_rows(piece, step) for step, piece in enumerate(pieces) if step
         ]
 
-    def joined_halves(half, got, name):
-        return local_call(
-            partial(join_halves_body, rows=rows), [((D, SPAN), low)], name, flags, half, got
-        )[0]
-
     def cols_back(own, other, kind, name):
         return local_call(
             join_back_body,
@@ -1291,24 +1327,26 @@
         (token_pieces, first_three, first_copies[0])
     )
     first_blocks = [first_one, first_two, first_three, *first_copies]
-    x_half, cot_half, norm_vecs = local_call(
+    x_half, norm_vecs = local_call(
         partial(place_tokens_body, rows=rows, part=half_feats),
-        low_outs(2, D // 2, SPAN) + [((D, 8), wide)],
+        low_outs(1, D, SPAN) + [((D, 8), wide)],
         "token_place",
         flags,
         *token_pieces,
     )
-    x_half, trig, reweight, hidden_packed = lax.optimization_barrier(
-        (x_half, trig, reweight, hidden_packed)
-    )
+    x_half, trig, reweight = lax.optimization_barrier((x_half, trig, reweight))
     hidden_one, hidden_two = row_blocks(hidden_packed[0])
     x_got, hidden_one = lax.optimization_barrier((swap_cols(x_half), hidden_one))
-    x_own = joined_halves(x_half, x_got, "token_join")
-    cot = joined_halves(cot_half, swap_cols(cot_half), "cot_join")
+    x_own, cot = local_call(
+        partial(join_halves_body, rows=rows),
+        low_outs(2, D, SPAN),
+        "token_join",
+        flags,
+        x_half,
+        x_got,
+    )
     x_own, first_blocks = lax.optimization_barrier((x_own, first_blocks))
     x_other = swap_pair(x_own)
-    hidden_three = swap_rows(hidden_two, 1)
-    copy_two = swap_copies(hidden_two)
     state_shape = ((STATE_ROWS + SUM_ROWS, 2 * HD), low)
     sets = 2 * HEADS
     block_low = ((D, SPAN), low)
@@ -1324,6 +1362,8 @@
         first_packed,
         *first_blocks,
     )
+    hidden_three = swap_rows(hidden_two, 1)
+    copy_two = swap_copies(hidden_two)
     arrived = [shift_rows(state, step) for step in range(1, rows)]
     arrived, hidden_three, copy_two = lax.optimization_barrier(
         (arrived, hidden_three, copy_two)
@@ -1360,8 +1400,21 @@
     branch = column_parts(branch_own, branch_other, "branch_half")
     copy_three = swap_copies(hidden_three)
     branch, copy_three = lax.optimization_barrier((branch, copy_three))
-    hidden_mine = [hidden_packed[0], hidden_one, hidden_two, hidden_three]
-    hidden_copy = [hidden_packed[1], copy_one, copy_two, copy_three]
+    hidden_mine, hidden_copy = local_call(
+        hidden_weights_body,
+        low_outs(2, D, 2 * part),
+        "hidden_weights",
+        flags,
+        hidden_packed[0],
+        hidden_one,
+        hidden_two,
+        hidden_three,
+        hidden_packed[1],
+        copy_one,
+        copy_two,
+        copy_three,
+    )
+    branch, hidden_mine = lax.optimization_barrier((branch, hidden_mine))
     first, first_low, normed = local_call(
         norm_body,
         [block_wide, block_low, ((D + 8, SPAN), wide)],
@@ -1371,27 +1424,15 @@
         norm_vecs,
     )
     first_other = swap_pair(first_low)
-    half_hidden = [((part, 2 * SPAN), low), ((part, 2 * SPAN), wide)]
-    hidden_weight = [((D, 2 * part), low)]
-    hidden_mine, act_mine, slope_mine, ffn_own, ffn_other = local_call(
+    hidden_acts = [((part, 2 * SPAN), low)] * 2 + [((part, 2 * SPAN), wide)] * 2
+    act_mine, act_copy, slope_mine, slope_copy, ffn_own, ffn_other = local_call(
         hidden_body,
-        hidden_weight + half_hidden + [block_wide, block_wide],
-        "hidden_mine",
-        flags,
+        hidden_acts + [block_wide, block_low],
+        "hidden",
         first_low,
         first_other,
-        *hidden_mine,
-    )
-    hidden_copy, act_copy, slope_copy, ffn_own, ffn_other = local_call(
-        hidden_body,
-        hidden_weight + half_hidden + [block_wide, block_low],
-        "hidden_copy",
-        flags,
-        first_low,
-        first_other,
-        *hidden_copy,
-        ffn_own,
-        ffn_other,
+        hidden_mine,
+        hidden_copy,
     )
     ffn = column_parts(ffn_own, ffn_other, "ffn_half")
     result, grad_second, grad_ffn = local_call(
@@ -1406,18 +1447,20 @@
     )
     grad_ffn_other = swap_pair(grad_ffn)
     pair_low = ((D, part), low)
-    kept_down, sent_down = local_call(
-        half_grads_body,
-        [pair_low, pair_low],
+    down_held, down_sent = local_call(
+        down_grad_body,
+        low_outs(2, 2 * feat_rows, 2 * part),
         "down_grad",
+        flags,
         grad_ffn,
         grad_ffn_other,
         act_mine,
         act_copy,
-    )
-    got_down = swap_copies(sent_down)
-    grad_ffn, grad_ffn_other, kept_down = lax.optimization_barrier(
-        (grad_ffn, grad_ffn_other, kept_down)
+        scratch=[((D, 2 * part), low)],
+    )
+    down_got = swap_rows(down_sent, 1)
+    grad_ffn, grad_ffn_other, down_held = lax.optimization_barrier(
+        (grad_ffn, grad_ffn_other, down_held)
     )
     hidden_low = ((part, 2 * SPAN), low)
     pre_mine, pre_copy, first_own_part, first_other_part = local_call(
@@ -1443,7 +1486,14 @@
         pre_copy,
     )
     got_up = swap_copies(sent_up)
-    first_sum, kept_up = lax.optimization_barrier((first_sum, kept_up))
+    down_kept, down_pair = local_call(
+        down_pairs_body,
+        [((2 * feat_rows, part), wide), ((2 * feat_rows, part), low)],
+        "down_pairs",
+        down_held,
+        down_got,
+    )
+    first_sum, kept_up, down_kept = lax.optimization_barrier((first_sum, kept_up, down_kept))
     grad_hidden, branch_grad, vec_sums = local_call(
         norm_back_body,
         [block_wide, block_low, ((D, 2 * SUM_LANES), low)],
@@ -1454,14 +1504,6 @@
         norm_vecs,
     )
     branch_grad_other = swap_pair(branch_grad)
-    (grad_out,) = local_call(
-        out_grad_body,
-        [((D, WIDTH), low)],
-        "out_grad",
-        branch_grad,
-        branch_grad_other,
-        attn_wide,
-    )
     grad_num, grad_den, grad_state = local_call(
         grad_attend_body,
         [((sets, HD, SPAN), low), ((SUM_ROWS, SPAN), wide), state_shape],
@@ -1474,6 +1516,19 @@
         trig,
     )
     later = [shift_rows(grad_state, -step) for step in range(1, rows)]
+    half_lanes = (WIDTH + SUM_LANES) // 2
+    mix_kept, mix_sent = local_call(
+        mix_body,
+        [((D, half_lanes), low), ((2 * feat_rows, part + 2 * half_lanes), low)],
+        "mix",
+        flags,
+        branch_grad,
+        branch_grad_other,
+        attn_wide,
+        vec_sums,
+        after(down_pair, grad_num),
+        scratch=[((D, WIDTH + SUM_LANES), low)],
+    )
     grad_query, grad_key, grad_value = local_call(
         grad_block_body,
         [
@@ -1490,26 +1545,27 @@
         weights,
         prior,
     )
-    down_held, down_sent = local_call(
-        down_pieces_body,
-        low_outs(2, 2 * feat_rows, part + SPAN // 2),
-        "down_pieces",
-        flags,
-        kept_down,
-        after(got_down, later[0]),
-        result,
-    )
-    down_got = swap_rows(down_sent, 1)
-
+    mix_got = swap_copies(after(mix_sent, got_up))
+    up_lanes = SPAN // 2 + part + half_lanes
+    down_part, down_far = local_call(
+        down_far_body,
+        [((feat_rows, part), wide), ((feat_rows, part), low)],
+        "down_far",
+        down_kept,
+        mix_got,
+    )
+    down_far = swap_rows(down_far, 2)
     up_held, up_sent = local_call(
-        pair_pieces_body,
-        low_outs(2, 2 * feat_rows, part + WIDTH + SUM_LANES),
+        up_pieces_body,
+        low_outs(2, 2 * feat_rows, up_lanes),
         "up_pieces",
         flags,
+        result,
         kept_up,
-        after(got_up, later[0]),
-        grad_out,
-        vec_sums,
+        after(got_up, grad_query),
+        mix_kept,
+        mix_got,
+        scratch=[((D, half_lanes), low)],
     )
     up_got = swap_rows(up_sent, 1)
     later, up_held = lax.optimization_barrier((later, up_held))
@@ -1554,20 +1610,14 @@
         got_half,
         grad_hidden,
     )
-    def pair_sums(held, got, name):
-        shape = (feat_rows, held.shape[1])
-        mine, sent = local_call(pair_sums_body, [(shape, wide), (shape, low)], name, held, got)
-        return mine, swap_rows(sent, 2)
-
-    down_part, down_far = local_call(
-        down_pairs_body,
-        [((feat_rows, part), wide), ((feat_rows, part + SPAN), low)],
-        "down_pairs",
-        down_held,
-        down_got,
-    )
-    down_far = swap_rows(down_far, 2)
-    up_part, up_far = pair_sums(up_held, up_got, "up_sums")
+    up_part, up_far = local_call(
+        up_pairs_body,
+        [((feat_rows, up_lanes - SPAN // 2), wide), ((feat_rows, up_lanes + SPAN // 2), low)],
+        "up_pairs",
+        up_held,
+        up_got,
+    )
+    up_far = swap_rows(up_far, 2)
     last_got = swap_rows(last_sent, 1)
     last_part, last_far = local_call(
         last_pairs_body,
@@ -1576,24 +1626,19 @@
         last_held,
         last_got,
     )
-    down_sum, *out_wide = local_call(
-        down_sums_body,
-        low_outs(1, feat_rows, part) + low_outs(2, half_feats, SPAN * rows // 2),
-        "down_sums",
+    hidden_sum, *out_wide = local_call(
+        hidden_sums_body,
+        low_outs(1, feat_rows, 2 * part + half_lanes)
+        + low_outs(2, half_feats, SPAN * rows // 2),
+        "hidden_sums",
         flags,
         down_part,
-        down_held,
-        down_got,
         down_far,
+        up_part,
+        up_held,
+        up_got,
+        up_far,
         scratch=[((4, half_feats, SPAN), low)],
-    )
-    (hidden_sum,) = local_call(
-        hidden_sums_body,
-        low_outs(1, feat_rows, 2 * part + WIDTH + SUM_LANES),
-        "hidden_sums",
-        down_sum,
-        up_part,
-        up_far,
     )
     last_sum, *input_wide = local_call(
         last_sums_body,

time: 198 us -> 190 us (0.960)
  waiting for transfers between devices: 96.4 us -> 87.2 us
  starting transfers between devices: 61.9 us -> 65.2 us
    ppermute x9 -> x8, waiting for transfers between devices: 24.5 us -> 13.7 us  [swap_cols(): return lax.ppermute(operand, 'col', [(0, 1), (1, 0)])]
    ppermute x11, waiting for transfers between devices: 7.31 us -> 15.5 us  [swap_copies(): lax.ppermute(operand, 'dp', [(i, i ^ 2) for i in range(lax.axis_size('dp'...]
    ppermute x12, starting transfers between devices: 11.5 us -> 17.7 us  [swap_rows(): return lax.ppermute(operand, 'row', [(i, i ^ mask) for i in range(4)])]
    ppermute x6, waiting for transfers between devices: 7.69 us -> 2.04 us  [shift_rows(): return lax.ppermute(operand, 'row', pairs)]
    ppermute x12, waiting for transfers between devices: 44.9 us -> 41.4 us  [swap_rows(): return lax.ppermute(operand, 'row', [(i, i ^ mask) for i in range(4)])]
    ppermute x10, waiting for transfers between devices: 8.47 us -> 10.8 us  [swap_pair(): lax.ppermute(operand, 'dp', [(i, i ^ 1) for i in range(lax.axis_size('dp'...]
    ppermute x9 -> x8, starting transfers between devices: 15 us -> 13 us  [swap_cols(): return lax.ppermute(operand, 'col', [(0, 1), (1, 0)])]
    pallas_call x38 -> x36, Pallas kernels: 35.3 us -> 33.4 us  [local_call(): pl.pallas_call(body, out_shape=shapes, in_specs=[pl.BlockSpec(memory_spac...]
  transfers between devices with their start and end apart: 53 -> 52, of which waited for: 27 -> 27; matrix products, arithmetic and copies ran while one was open for 1% -> 1% of each run, Pallas kernels for 12% -> 12%
where the time goes in v5:
time: 190 us
  waiting for transfers between devices  87.2 us (46%)
  starting transfers between devices  65.2 us (34%)
  Pallas kernels  33.4 us (18%)
    ppermute x12, waiting for transfers between devices, swap_rows(): return lax.ppermute(operand, 'row', [(i, i ^ mask) for i in range(4)])  41.4 us
    pallas_call x36, Pallas kernels, local_call(): pl.pallas_call(body, out_shape=shapes, in_specs=[pl.BlockSpec(memory_spac...  33.4 us
    ppermute x12, starting transfers between devices, swap_rows(): return lax.ppermute(operand, 'row', [(i, i ^ mask) for i in range(4)])  17.7 us
    ppermute x11, waiting for transfers between devices, swap_copies(): lax.ppermute(operand, 'dp', [(i, i ^ 2) for i in range(lax.axis_size('dp'...  15.5 us
    ppermute x11, starting transfers between devices, swap_copies(): lax.ppermute(operand, 'dp', [(i, i ^ 2) for i in range(lax.axis_size('dp'...  13.7 us
    ppermute x8, waiting for transfers between devices, swap_cols(): return lax.ppermute(operand, 'col', [(0, 1), (1, 0)])  13.7 us
    ppermute x6, starting transfers between devices, shift_rows(): return lax.ppermute(operand, 'row', pairs)  13 us
    ppermute x8, starting transfers between devices, swap_cols(): return lax.ppermute(operand, 'col', [(0, 1), (1, 0)])  13 us
  transfers between devices with their start and end apart: 52, of which 27 were waited for; matrix products, arithmetic and copies ran while one was open for 1% of the time, Pallas kernels for 12%

profile of v5, /device:TPU:0, one launch (start us, length us, event | category | flops | bytes accessed | tf_op | source)
XLA Modules:
  0.0 189.7 jit_solution(12170139163108281933)
XLA Ops:
  1.9 3.0 %collective-permute-start.1 = (bf16[192,512]{1,0:T(8,128)(2,1)S(1)}, bf16[192,512]{1,0:T(8,128)(2,1)S(1)}, u32[]{:S(2)}, u32[]{:S(2)}) collective-permute-start(bf16[192,512]{1,0:T(8,128)(2,1)S(1)} %pad_maximum_fusion.1), channel_id=1, source_target_pairs={{0,1},{1,0},{2,3},{3,2},{4,5},{5,4},{6,7},{7,6},{8,9},{9,8},{10,11... | collective-permute-start | bytes 589832 | tf_op jit(solution)/shard_map/ppermute | solution.py:441
  7.0 2.6 %collective-permute-start.5 = (bf16[192,384]{1,0:T(8,128)(2,1)S(1)}, bf16[192,384]{1,0:T(8,128)(2,1)S(1)}, u32[]{:S(2)}, u32[]{:S(2)}) collective-permute-start(bf16[192,384]{1,0:T(8,128)(2,1)S(1)} %maximum_select_fusion), channel_id=1, source_target_pairs={{0,4},{2,6},{4,0},{6,2},{1,5},{3,7},{5,1},{7,3},{8,12},{10,14},{12... | collective-permute-start | bytes 442376 | tf_op jit(solution)/shard_map/ppermute | solution.py:459
  9.7 3.4 %collective-permute-done.refs_0_ = bf16[192,384]{1,0:T(8,128)(2,1)S(1)} collective-permute-done((bf16[192,384]{1,0:T(8,128)(2,1)S(1)}, bf16[192,384]{1,0:T(8,128)(2,1)S(1)}, u32[]{:S(2)}, u32[]{:S(2)}) %collective-permute-start) | collective-permute-done | bytes 147488 | tf_op jit(solution)/shard_map/ppermute | solution.py:459
  16.6 1.7 collective-permute-start.2
  19.2 2.9 %collective-permute-start.4 = (bf16[208,256]{1,0:T(8,128)(2,1)S(1)}, bf16[208,256]{1,0:T(8,128)(2,1)S(1)}, u32[]{:S(2)}, u32[]{:S(2)}) collective-permute-start(bf16[208,256]{1,0:T(8,128)(2,1)S(1)} %get-tuple-element.152), channel_id=1, source_target_pairs={{0,6},{2,0},{4,2},{6,4},{1,7},{3,1},{5,3},{7,5},{8,14},{10,8},{12,... | collective-permute-start | bytes 319496 | tf_op jit(solution)/shard_map/ppermute | solution.py:464
  23.1 2.4 %collective-permute-done.2.refs_1_ = bf16[208,256]{1,0:T(8,128)(2,1)S(1)} collective-permute-done((bf16[208,256]{1,0:T(8,128)(2,1)S(1)}, bf16[208,256]{1,0:T(8,128)(2,1)S(1)}, u32[]{:S(2)}, u32[]{:S(2)}) %collective-permute-start.2) | collective-permute-done | bytes 106528 | tf_op jit(solution)/shard_map/ppermute | solution.py:464
  30.2 2.3 %collective-permute-start.16 = (bf16[192,768]{1,0:T(8,128)(2,1)S(1)}, bf16[192,768]{1,0:T(8,128)(2,1)S(1)}, u32[]{:S(2)}, u32[]{:S(2)}) collective-permute-start(bf16[192,768]{1,0:T(8,128)(2,1)S(1)} %get-tuple-element.164.refs_0_), channel_id=1, source_target_pairs={{0,4},{2,6},{4,0},{6,2},{1,5},{3,7},{5,1},{7,3},{8,12},{10,14},{12... | collective-permute-start | bytes 884744 | tf_op jit(solution)/shard_map/ppermute | solution.py:459
  34.6 5.0 %collective-permute-done.9.refs_1_ = bf16[192,768]{1,0:T(8,128)(2,1)S(1)} collective-permute-done((bf16[192,768]{1,0:T(8,128)(2,1)S(1)}, bf16[192,768]{1,0:T(8,128)(2,1)S(1)}, u32[]{:S(2)}, u32[]{:S(2)}) %collective-permute-start.9) | collective-permute-done | bytes 294944 | tf_op jit(solution)/shard_map/ppermute | solution.py:459
  40.3 2.5 %collective-permute-done.16.refs_2_ = bf16[192,768]{1,0:T(8,128)(2,1)S(1)} collective-permute-done((bf16[192,768]{1,0:T(8,128)(2,1)S(1)}, bf16[192,768]{1,0:T(8,128)(2,1)S(1)}, u32[]{:S(2)}, u32[]{:S(2)}) %collective-permute-start.16) | collective-permute-done | bytes 294944 | tf_op jit(solution)/shard_map/ppermute | solution.py:459
  46.7 3.8 %collective-permute-start.13 = (bf16[400,128]{1,0:T(8,128)(2,1)S(1)}, bf16[400,128]{1,0:T(8,128)(2,1)S(1)}, u32[]{:S(2)}, u32[]{:S(2)}) collective-permute-start(bf16[400,128]{1,0:T(8,128)(2,1)S(1)} %get-tuple-element.182), channel_id=1, source_target_pairs={{0,2},{2,4},{4,6},{1,3},{3,5},{5,7},{8,10},{10,12},{12,14},{9,11},... | collective-permute-start | bytes 307208 | tf_op jit(solution)/shard_map/ppermute | solution.py:455
  50.5 2.7 %collective-permute-start.14 = (bf16[400,128]{1,0:T(8,128)(2,1)S(1)}, bf16[400,128]{1,0:T(8,128)(2,1)S(1)}, u32[]{:S(2)}, u32[]{:S(2)}) collective-permute-start(bf16[400,128]{1,0:T(8,128)(2,1)S(1)} %get-tuple-element.182), channel_id=1, source_target_pairs={{0,4},{2,6},{1,5},{3,7},{8,12},{10,14},{9,13},{11,15},{16,20},{18,... | collective-permute-start | bytes 307208 | tf_op jit(solution)/shard_map/ppermute | solution.py:455
  53.3 2.4 %collective-permute-start.15 = (bf16[400,128]{1,0:T(8,128)(2,1)S(1)}, bf16[400,128]{1,0:T(8,128)(2,1)S(1)}, u32[]{:S(2)}, u32[]{:S(2)}) collective-permute-start(bf16[400,128]{1,0:T(8,128)(2,1)S(1)} %get-tuple-element.182), channel_id=1, source_target_pairs={{0,6},{1,7},{8,14},{9,15},{16,22},{17,23},{24,30},{25,31}} | collective-permute-start | bytes 307208 | tf_op jit(solution)/shard_map/ppermute | solution.py:455
  58.4 1.7 collective-permute-done.20.recv_ref
  63.3 7.3 %collective-permute-done.22.refs_7_ = bf16[192,768]{1,0:T(8,128)(2,1)S(1)} collective-permute-done((bf16[192,768]{1,0:T(8,128)(2,1)S(1)}, bf16[192,768]{1,0:T(8,128)(2,1)S(1)}, u32[]{:S(2)}, u32[]{:S(2)}) %collective-permute-start.22) | collective-permute-done | bytes 294944 | tf_op jit(solution)/shard_map/ppermute | solution.py:449
  72.9 1.7 collective-permute-done.23.other_ref
  74.6 1.8 hidden.1
  79.9 9.6 %collective-permute-done.25.recv_ref = bf16[768,256]{1,0:T(8,128)(2,1)S(1)} collective-permute-done((bf16[768,256]{1,0:T(8,128)(2,1)S(1)}, bf16[768,256]{1,0:T(8,128)(2,1)S(1)}, u32[]{:S(2)}, u32[]{:S(2)}) %collective-permute-start.25) | collective-permute-done | bytes 393248 | tf_op jit(solution)/shard_map/ppermute | solution.py:441
  90.8 1.7 collective-permute-done.26.other_ref
  94.1 1.8 hidden_back.1
  101.9 9.8 %collective-permute-done.29.got_ref = bf16[384,768]{1,0:T(8,128)(2,1)S(1)} collective-permute-done((bf16[384,768]{1,0:T(8,128)(2,1)S(1)}, bf16[384,768]{1,0:T(8,128)(2,1)S(1)}, u32[]{:S(2)}, u32[]{:S(2)}) %collective-permute-start.29) | collective-permute-done | bytes 589856 | tf_op jit(solution)/shard_map/ppermute | solution.py:459
  112.7 1.7 collective-permute-done.30.other_ref
  123.6 6.1 %collective-permute-done.32.got_ref.mix_got_ref = bf16[384,640]{1,0:T(8,128)(2,1)S(1)} collective-permute-done((bf16[384,640]{1,0:T(8,128)(2,1)S(1)}, bf16[384,640]{1,0:T(8,128)(2,1)S(1)}, u32[]{:S(2)}, u32[]{:S(2)}) %collective-permute-start.32) | collective-permute-done | bytes 491552 | tf_op jit(solution)/shard_map/ppermute | solution.py:449
  132.3 2.3 %grad_project.1 = (bf16[4,96,576]{2,1,0:T(8,128)(2,1)S(1)}, bf16[4,96,576]{2,1,0:T(8,128)(2,1)S(1)}, f32[768,256]{1,0:T(8,128)S(1)}, bf16[768,256]{1,0:T(8,128)(2,1)S(1)}) custom-call(bf16[2,192,256]{2,1,0:T(8,128)(2,1)S(1)} %get-tuple-element.247.grad_query_ref, f32[6,64,256]{2,1,0:T(8,128)S(1)} %get-tuple-element.257.grad_key_ref, ...), custom_call_target="tpu_custom_call" | custom-call | tf_op jit(solution)/shard_map/grad_project/pallas_call | solution.py:497
  138.7 4.3 %collective-permute-done.37.got_ref = bf16[384,640]{1,0:T(8,128)(2,1)S(1)} collective-permute-done((bf16[384,640]{1,0:T(8,128)(2,1)S(1)}, bf16[384,640]{1,0:T(8,128)(2,1)S(1)}, u32[]{:S(2)}, u32[]{:S(2)}) %collective-permute-start.37) | collective-permute-done | bytes 491552 | tf_op jit(solution)/shard_map/ppermute | solution.py:459
  143.2 3.1 %collective-permute-start.38 = (bf16[192,768]{1,0:T(8,128)(2,1)S(1)}, bf16[192,768]{1,0:T(8,128)(2,1)S(1)}, u32[]{:S(2)}, u32[]{:S(2)}) collective-permute-start(bf16[192,768]{1,0:T(8,128)(2,1)S(1)} %get-tuple-element.254), channel_id=1, source_target_pairs={{0,4},{2,6},{4,0},{6,2},{1,5},{3,7},{5,1},{7,3},{8,12},{10,14},{12... | collective-permute-start | bytes 884744 | tf_op jit(solution)/shard_map/ppermute | solution.py:459
  146.3 2.1 %collective-permute-done.40.got_ref = bf16[4,96,576]{2,1,0:T(8,128)(2,1)S(1)} collective-permute-done((bf16[4,96,576]{2,1,0:T(8,128)(2,1)S(1)}, bf16[4,96,576]{2,1,0:T(8,128)(2,1)S(1)}, u32[]{:S(2)}, u32[]{:S(2)}) %collective-permute-start.40) | collective-permute-done | bytes 442400 | tf_op jit(solution)/shard_map/ppermute | solution.py:449
  149.6 3.1 %collective-permute-start.33 = (bf16[192,384]{1,0:T(8,128)(2,1)S(1)}, bf16[192,384]{1,0:T(8,128)(2,1)S(1)}, u32[]{:S(2)}, u32[]{:S(2)}) collective-permute-start(bf16[192,384]{1,0:T(8,128)(2,1)S(1)} %get-tuple-element.240), channel_id=1, source_target_pairs={{0,4},{2,6},{4,0},{6,2},{1,5},{3,7},{5,1},{7,3},{8,12},{10,14},{12... | collective-permute-start | bytes 442376 | tf_op jit(solution)/shard_map/ppermute | solution.py:459
  152.8 9.9 %collective-permute-done.33.down_far_ref = bf16[192,384]{1,0:T(8,128)(2,1)S(1)} collective-permute-done((bf16[192,384]{1,0:T(8,128)(2,1)S(1)}, bf16[192,384]{1,0:T(8,128)(2,1)S(1)}, u32[]{:S(2)}, u32[]{:S(2)}) %collective-permute-start.33) | collective-permute-done | bytes 147488 | tf_op jit(solution)/shard_map/ppermute | solution.py:459
  167.1 1.9 %collective-permute-start.44 = (bf16[96,1088]{1,0:T(8,128)(2,1)S(1)}, bf16[96,1088]{1,0:T(8,128)(2,1)S(1)}, u32[]{:S(2)}, u32[]{:S(2)}) collective-permute-start(bf16[96,1088]{1,0:T(8,128)(2,1)S(1)} %get-tuple-element.272), channel_id=1, source_target_pairs={{0,4},{2,6},{4,0},{6,2},{1,5},{3,7},{5,1},{7,3},{8,12},{10,14},{12... | collective-permute-start | bytes 626696 | tf_op jit(solution)/shard_map/ppermute | solution.py:459
  170.5 3.1 %collective-permute-done.39.recv_ref = bf16[96,512]{1,0:T(8,128)(2,1)S(1)} collective-permute-done((bf16[96,512]{1,0:T(8,128)(2,1)S(1)}, bf16[96,512]{1,0:T(8,128)(2,1)S(1)}, u32[]{:S(2)}, u32[]{:S(2)}) %collective-permute-start.39) | collective-permute-done | bytes 98336 | tf_op jit(solution)/shard_map/ppermute | solution.py:441
  174.9 4.0 %collective-permute-done.44.far_ref = bf16[96,1088]{1,0:T(8,128)(2,1)S(1)} collective-permute-done((bf16[96,1088]{1,0:T(8,128)(2,1)S(1)}, bf16[96,1088]{1,0:T(8,128)(2,1)S(1)}, u32[]{:S(2)}, u32[]{:S(2)}) %collective-permute-start.44) | collective-permute-done | bytes 208928 | tf_op jit(solution)/shard_map/ppermute | solution.py:459
  183.6 2.2 %place_hidden.1 = (f32[192,1536]{1,0:T(8,128)}, f32[192,1536]{1,0:T(8,128)}, f32[192,384]{1,0:T(8,128)}, f32[192,64]{1,0:T(8,128)S(1)}) custom-call(s32[5]{0:T(128)S(1)} %stack.38.flags_ref, bf16[192,896]{1,0:T(8,128)(2,1)S(1)} %get-tuple-element.279.refs_0_, bf16[192,896]{1,0:T(8,128)(2,1)S(1)} %collective-permute-done.49.refs_1_, ...), custom_call_target="tpu_custom_call" | custom-call | tf_op jit(solution)/shard_map/place_hidden/pallas_call | solution.py:497
  (139 shorter events, 74.3 us)
Async XLA Ops:
  1.9 11.2 %collective-permute-start.1 = (bf16[192,512]{1,0:T(8,128)(2,1)S(1)}, bf16[192,512]{1,0:T(8,128)(2,1)S(1)}, u32[]{:S(2)}, u32[]{:S(2)}) collective-permute-start(bf16[192,512]{1,0:T(8,128)(2,1)S(1)} %pad_maximum_fusion.1), channel_id=1, source_target_pairs={{0,1},{1,0},{2,3},{3,2},{4,5},{5,4},{6,7},{7,6},{8,9},{9,8},{10,11... | collective-permute-start | bytes 589832 | tf_op jit(solution)/shard_map/ppermute | solution.py:441
  7.0 9.2 %collective-permute-start.5 = (bf16[192,384]{1,0:T(8,128)(2,1)S(1)}, bf16[192,384]{1,0:T(8,128)(2,1)S(1)}, u32[]{:S(2)}, u32[]{:S(2)}) collective-permute-start(bf16[192,384]{1,0:T(8,128)(2,1)S(1)} %maximum_select_fusion), channel_id=1, source_target_pairs={{0,4},{2,6},{4,0},{6,2},{1,5},{3,7},{5,1},{7,3},{8,12},{10,14},{12... | collective-permute-start | bytes 442376 | tf_op jit(solution)/shard_map/ppermute | solution.py:459
  13.8 13.1 %collective-permute-start.7 = (bf16[192,384]{1,0:T(8,128)(2,1)S(1)}, bf16[192,384]{1,0:T(8,128)(2,1)S(1)}, u32[]{:S(2)}, u32[]{:S(2)}) collective-permute-start(bf16[192,384]{1,0:T(8,128)(2,1)S(1)} %collective-permute-done.refs_0_), channel_id=1, source_target_pairs={{0,16},{8,24},{16,0},{24,8},{1,17},{9,25},{17,1},{25,9},{2,18},{10... | collective-permute-start | bytes 442376 | tf_op jit(solution)/shard_map/ppermute | solution.py:449
  16.3 10.6 %collective-permute-start.6 = (bf16[192,384]{1,0:T(8,128)(2,1)S(1)}, bf16[192,384]{1,0:T(8,128)(2,1)S(1)}, u32[]{:S(2)}, u32[]{:S(2)}) collective-permute-start(bf16[192,384]{1,0:T(8,128)(2,1)S(1)} %collective-permute-done.5.refs_1_), channel_id=1, source_target_pairs={{0,2},{2,0},{4,6},{6,4},{1,3},{3,1},{5,7},{7,5},{8,10},{10,8},{12,... | collective-permute-start | bytes 442376 | tf_op jit(solution)/shard_map/ppermute | solution.py:459
  16.6 8.9 %collective-permute-start.2 = (bf16[208,256]{1,0:T(8,128)(2,1)S(1)}, bf16[208,256]{1,0:T(8,128)(2,1)S(1)}, u32[]{:S(2)}, u32[]{:S(2)}) collective-permute-start(bf16[208,256]{1,0:T(8,128)(2,1)S(1)} %get-tuple-element.150), channel_id=1, source_target_pairs={{0,2},{2,4},{4,6},{6,0},{1,3},{3,5},{5,7},{7,1},{8,10},{10,12},{12... | collective-permute-start | bytes 319496 | tf_op jit(solution)/shard_map/ppermute | solution.py:464
  27.6 12.1 %collective-permute-start.8 = (bf16[768,256]{1,0:T(8,128)(2,1)S(1)}, bf16[768,256]{1,0:T(8,128)(2,1)S(1)}, u32[]{:S(2)}, u32[]{:S(2)}) collective-permute-start(bf16[768,256]{1,0:T(8,128)(2,1)S(1)} %get-tuple-element.163.half_ref), channel_id=1, source_target_pairs={{0,1},{1,0},{2,3},{3,2},{4,5},{5,4},{6,7},{7,6},{8,9},{9,8},{10,11... | collective-permute-start | bytes 1179656 | tf_op jit(solution)/shard_map/ppermute | solution.py:441
  28.8 10.8 %collective-permute-start.9 = (bf16[192,768]{1,0:T(8,128)(2,1)S(1)}, bf16[192,768]{1,0:T(8,128)(2,1)S(1)}, u32[]{:S(2)}, u32[]{:S(2)}) collective-permute-start(bf16[192,768]{1,0:T(8,128)(2,1)S(1)} %get-tuple-element.164.refs_0_), channel_id=1, source_target_pairs={{0,2},{2,0},{4,6},{6,4},{1,3},{3,1},{5,7},{7,5},{8,10},{10,8},{12,... | collective-permute-start | bytes 884744 | tf_op jit(solution)/shard_map/ppermute | solution.py:459
  30.2 12.6 %collective-permute-start.16 = (bf16[192,768]{1,0:T(8,128)(2,1)S(1)}, bf16[192,768]{1,0:T(8,128)(2,1)S(1)}, u32[]{:S(2)}, u32[]{:S(2)}) collective-permute-start(bf16[192,768]{1,0:T(8,128)(2,1)S(1)} %get-tuple-element.164.refs_0_), channel_id=1, source_target_pairs={{0,4},{2,6},{4,0},{6,2},{1,5},{3,7},{5,1},{7,3},{8,12},{10,14},{12... | collective-permute-start | bytes 884744 | tf_op jit(solution)/shard_map/ppermute | solution.py:459
  42.8 10.4 %collective-permute-start.17 = (bf16[192,768]{1,0:T(8,128)(2,1)S(1)}, bf16[192,768]{1,0:T(8,128)(2,1)S(1)}, u32[]{:S(2)}, u32[]{:S(2)}) collective-permute-start(bf16[192,768]{1,0:T(8,128)(2,1)S(1)} %collective-permute-done.16.refs_2_), channel_id=1, source_target_pairs={{0,2},{2,0},{4,6},{6,4},{1,3},{3,1},{5,7},{7,5},{8,10},{10,8},{12,... | collective-permute-start | bytes 884744 | tf_op jit(solution)/shard_map/ppermute | solution.py:459
  42.9 14.1 %collective-permute-start.18 = (bf16[192,768]{1,0:T(8,128)(2,1)S(1)}, bf16[192,768]{1,0:T(8,128)(2,1)S(1)}, u32[]{:S(2)}, u32[]{:S(2)}) collective-permute-start(bf16[192,768]{1,0:T(8,128)(2,1)S(1)} %collective-permute-done.16.refs_2_), channel_id=1, source_target_pairs={{0,16},{8,24},{16,0},{24,8},{1,17},{9,25},{17,1},{25,9},{2,18},{10... | collective-permute-start | bytes 884744 | tf_op jit(solution)/shard_map/ppermute | solution.py:449
  44.4 13.9 %collective-permute-start.19 = (bf16[192,768]{1,0:T(8,128)(2,1)S(1)}, bf16[192,768]{1,0:T(8,128)(2,1)S(1)}, u32[]{:S(2)}, u32[]{:S(2)}) collective-permute-start(bf16[192,768]{1,0:T(8,128)(2,1)S(1)} %collective-permute-done.9.refs_1_), channel_id=1, source_target_pairs={{0,16},{8,24},{16,0},{24,8},{1,17},{9,25},{17,1},{25,9},{2,18},{10... | collective-permute-start | bytes 884744 | tf_op jit(solution)/shard_map/ppermute | solution.py:449
  46.7 10.4 %collective-permute-start.13 = (bf16[400,128]{1,0:T(8,128)(2,1)S(1)}, bf16[400,128]{1,0:T(8,128)(2,1)S(1)}, u32[]{:S(2)}, u32[]{:S(2)}) collective-permute-start(bf16[400,128]{1,0:T(8,128)(2,1)S(1)} %get-tuple-element.182), channel_id=1, source_target_pairs={{0,2},{2,4},{4,6},{1,3},{3,5},{5,7},{8,10},{10,12},{12,14},{9,11},... | collective-permute-start | bytes 307208 | tf_op jit(solution)/shard_map/ppermute | solution.py:455
  60.2 11.2 %collective-permute-start.21 = (bf16[768,256]{1,0:T(8,128)(2,1)S(1)}, bf16[768,256]{1,0:T(8,128)(2,1)S(1)}, u32[]{:S(2)}, u32[]{:S(2)}) collective-permute-start(bf16[768,256]{1,0:T(8,128)(2,1)S(1)} %branch_half.1.half_ref), channel_id=1, source_target_pairs={{0,1},{1,0},{2,3},{3,2},{4,5},{5,4},{6,7},{7,6},{8,9},{9,8},{10,11... | collective-permute-start | bytes 1179656 | tf_op jit(solution)/shard_map/ppermute | solution.py:441
  61.8 8.8 %collective-permute-start.22 = (bf16[192,768]{1,0:T(8,128)(2,1)S(1)}, bf16[192,768]{1,0:T(8,128)(2,1)S(1)}, u32[]{:S(2)}, u32[]{:S(2)}) collective-permute-start(bf16[192,768]{1,0:T(8,128)(2,1)S(1)} %collective-permute-done.17.refs_3_), channel_id=1, source_target_pairs={{0,16},{8,24},{16,0},{24,8},{1,17},{9,25},{17,1},{25,9},{2,18},{10... | collective-permute-start | bytes 884744 | tf_op jit(solution)/shard_map/ppermute | solution.py:449
  78.3 11.2 %collective-permute-start.25 = (bf16[768,256]{1,0:T(8,128)(2,1)S(1)}, bf16[768,256]{1,0:T(8,128)(2,1)S(1)}, u32[]{:S(2)}, u32[]{:S(2)}) collective-permute-start(bf16[768,256]{1,0:T(8,128)(2,1)S(1)} %ffn_half.1.half_ref), channel_id=1, source_target_pairs={{0,1},{1,0},{2,3},{3,2},{4,5},{5,4},{6,7},{7,6},{8,9},{9,8},{10,11... | collective-permute-start | bytes 1179656 | tf_op jit(solution)/shard_map/ppermute | solution.py:441
  96.1 15.6 %collective-permute-start.29 = (bf16[384,768]{1,0:T(8,128)(2,1)S(1)}, bf16[384,768]{1,0:T(8,128)(2,1)S(1)}, u32[]{:S(2)}, u32[]{:S(2)}) collective-permute-start(bf16[384,768]{1,0:T(8,128)(2,1)S(1)} %get-tuple-element.223), channel_id=1, source_target_pairs={{0,2},{2,0},{4,6},{6,4},{1,3},{3,1},{5,7},{7,5},{8,10},{10,8},{12,... | collective-permute-start | bytes 1769480 | tf_op jit(solution)/shard_map/ppermute | solution.py:459
  97.8 14.1 %collective-permute-start.28 = (bf16[768,256]{1,0:T(8,128)(2,1)S(1)}, bf16[768,256]{1,0:T(8,128)(2,1)S(1)}, u32[]{:S(2)}, u32[]{:S(2)}) collective-permute-start(bf16[768,256]{1,0:T(8,128)(2,1)S(1)} %first_half.1.half_ref), channel_id=1, source_target_pairs={{0,1},{1,0},{2,3},{3,2},{4,5},{5,4},{6,7},{7,6},{8,9},{9,8},{10,11... | collective-permute-start | bytes 1179656 | tf_op jit(solution)/shard_map/ppermute | solution.py:441
  100.4 16.0 %collective-permute-start.31 = (bf16[768,384]{1,0:T(8,128)(2,1)S(1)}, bf16[768,384]{1,0:T(8,128)(2,1)S(1)}, u32[]{:S(2)}, u32[]{:S(2)}) collective-permute-start(bf16[768,384]{1,0:T(8,128)(2,1)S(1)} %get-tuple-element.237), channel_id=1, source_target_pairs={{0,16},{8,24},{16,0},{24,8},{1,17},{9,25},{17,1},{25,9},{2,18},{10... | collective-permute-start | bytes 1769480 | tf_op jit(solution)/shard_map/ppermute | solution.py:449
  116.4 13.3 %collective-permute-start.32 = (bf16[384,640]{1,0:T(8,128)(2,1)S(1)}, bf16[384,640]{1,0:T(8,128)(2,1)S(1)}, u32[]{:S(2)}, u32[]{:S(2)}) collective-permute-start(bf16[384,640]{1,0:T(8,128)(2,1)S(1)} %get-tuple-element.238), channel_id=1, source_target_pairs={{0,16},{8,24},{16,0},{24,8},{1,17},{9,25},{17,1},{25,9},{2,18},{10... | collective-permute-start | bytes 1474568 | tf_op jit(solution)/shard_map/ppermute | solution.py:449
  117.9 13.0 %collective-permute-start.34 = (bf16[400,128]{1,0:T(8,128)(2,1)S(1)}, bf16[400,128]{1,0:T(8,128)(2,1)S(1)}, u32[]{:S(2)}, u32[]{:S(2)}) collective-permute-start(bf16[400,128]{1,0:T(8,128)(2,1)S(1)} %get-tuple-element.241), channel_id=1, source_target_pairs={{2,0},{4,2},{6,4},{3,1},{5,3},{7,5},{10,8},{12,10},{14,12},{11,9},... | collective-permute-start | bytes 307208 | tf_op jit(solution)/shard_map/ppermute | solution.py:455
  119.2 13.1 %collective-permute-start.35 = (bf16[400,128]{1,0:T(8,128)(2,1)S(1)}, bf16[400,128]{1,0:T(8,128)(2,1)S(1)}, u32[]{:S(2)}, u32[]{:S(2)}) collective-permute-start(bf16[400,128]{1,0:T(8,128)(2,1)S(1)} %get-tuple-element.241), channel_id=1, source_target_pairs={{4,0},{6,2},{5,1},{7,3},{12,8},{14,10},{13,9},{15,11},{20,16},{22,... | collective-permute-start | bytes 307208 | tf_op jit(solution)/shard_map/ppermute | solution.py:455
  120.5 11.8 %collective-permute-start.36 = (bf16[400,128]{1,0:T(8,128)(2,1)S(1)}, bf16[400,128]{1,0:T(8,128)(2,1)S(1)}, u32[]{:S(2)}, u32[]{:S(2)}) collective-permute-start(bf16[400,128]{1,0:T(8,128)(2,1)S(1)} %get-tuple-element.241), channel_id=1, source_target_pairs={{6,0},{7,1},{14,8},{15,9},{22,16},{23,17},{30,24},{31,25}} | collective-permute-start | bytes 307208 | tf_op jit(solution)/shard_map/ppermute | solution.py:455
  130.6 12.5 %collective-permute-start.37 = (bf16[384,640]{1,0:T(8,128)(2,1)S(1)}, bf16[384,640]{1,0:T(8,128)(2,1)S(1)}, u32[]{:S(2)}, u32[]{:S(2)}) collective-permute-start(bf16[384,640]{1,0:T(8,128)(2,1)S(1)} %get-tuple-element.252), channel_id=1, source_target_pairs={{0,2},{2,0},{4,6},{6,4},{1,3},{3,1},{5,7},{7,5},{8,10},{10,8},{12,... | collective-permute-start | bytes 1474568 | tf_op jit(solution)/shard_map/ppermute | solution.py:459
  134.7 13.6 %collective-permute-start.40 = (bf16[4,96,576]{2,1,0:T(8,128)(2,1)S(1)}, bf16[4,96,576]{2,1,0:T(8,128)(2,1)S(1)}, u32[]{:S(2)}, u32[]{:S(2)}) collective-permute-start(bf16[4,96,576]{2,1,0:T(8,128)(2,1)S(1)} %get-tuple-element.263), channel_id=1, source_target_pairs={{0,16},{8,24},{16,0},{24,8},{1,17},{9,25},{17,1},{25,9},{2,18},{10... | collective-permute-start | bytes 1327112 | tf_op jit(solution)/shard_map/ppermute | solution.py:449
  137.1 11.2 %collective-permute-start.42 = (bf16[384,256]{1,0:T(8,128)(2,1)S(1)}, bf16[384,256]{1,0:T(8,128)(2,1)S(1)}, u32[]{:S(2)}, u32[]{:S(2)}) collective-permute-start(bf16[384,256]{1,0:T(8,128)(2,1)S(1)} %get-tuple-element.267), channel_id=1, source_target_pairs={{0,1},{1,0},{2,3},{3,2},{4,5},{5,4},{6,7},{7,6},{8,9},{9,8},{10,11... | collective-permute-start | bytes 589832 | tf_op jit(solution)/shard_map/ppermute | solution.py:441
  143.2 19.5 %collective-permute-start.38 = (bf16[192,768]{1,0:T(8,128)(2,1)S(1)}, bf16[192,768]{1,0:T(8,128)(2,1)S(1)}, u32[]{:S(2)}, u32[]{:S(2)}) collective-permute-start(bf16[192,768]{1,0:T(8,128)(2,1)S(1)} %get-tuple-element.254), channel_id=1, source_target_pairs={{0,4},{2,6},{4,0},{6,2},{1,5},{3,7},{5,1},{7,3},{8,12},{10,14},{12... | collective-permute-start | bytes 884744 | tf_op jit(solution)/shard_map/ppermute | solution.py:459
  149.2 17.9 %collective-permute-start.43 = (bf16[192,832]{1,0:T(8,128)(2,1)S(1)}, bf16[192,832]{1,0:T(8,128)(2,1)S(1)}, u32[]{:S(2)}, u32[]{:S(2)}) collective-permute-start(bf16[192,832]{1,0:T(8,128)(2,1)S(1)} %get-tuple-element.270), channel_id=1, source_target_pairs={{0,2},{2,0},{4,6},{6,4},{1,3},{3,1},{5,7},{7,5},{8,10},{10,8},{12,... | collective-permute-start | bytes 958472 | tf_op jit(solution)/shard_map/ppermute | solution.py:459
  149.6 13.0 %collective-permute-start.33 = (bf16[192,384]{1,0:T(8,128)(2,1)S(1)}, bf16[192,384]{1,0:T(8,128)(2,1)S(1)}, u32[]{:S(2)}, u32[]{:S(2)}) collective-permute-start(bf16[192,384]{1,0:T(8,128)(2,1)S(1)} %get-tuple-element.240), channel_id=1, source_target_pairs={{0,4},{2,6},{4,0},{6,2},{1,5},{3,7},{5,1},{7,3},{8,12},{10,14},{12... | collective-permute-start | bytes 442376 | tf_op jit(solution)/shard_map/ppermute | solution.py:459
  163.3 17.9 %collective-permute-start.49 = (bf16[192,896]{1,0:T(8,128)(2,1)S(1)}, bf16[192,896]{1,0:T(8,128)(2,1)S(1)}, u32[]{:S(2)}, u32[]{:S(2)}) collective-permute-start(bf16[192,896]{1,0:T(8,128)(2,1)S(1)} %get-tuple-element.279.refs_0_), channel_id=1, source_target_pairs={{0,16},{8,24},{16,0},{24,8},{1,17},{9,25},{17,1},{25,9},{2,18},{10... | collective-permute-start | bytes 1032200 | tf_op jit(solution)/shard_map/ppermute | solution.py:449
  164.8 17.2 %collective-permute-start.50 = (bf16[192,896]{1,0:T(8,128)(2,1)S(1)}, bf16[192,896]{1,0:T(8,128)(2,1)S(1)}, u32[]{:S(2)}, u32[]{:S(2)}) collective-permute-start(bf16[192,896]{1,0:T(8,128)(2,1)S(1)} %get-tuple-element.279.refs_0_), channel_id=1, source_target_pairs={{0,8},{8,0},{16,24},{24,16},{1,9},{9,1},{17,25},{25,17},{2,10},{10... | collective-permute-start | bytes 1032200 | tf_op jit(solution)/shard_map/ppermute | solution.py:445
  164.8 18.8 %collective-permute-start.51 = (bf16[192,896]{1,0:T(8,128)(2,1)S(1)}, bf16[192,896]{1,0:T(8,128)(2,1)S(1)}, u32[]{:S(2)}, u32[]{:S(2)}) collective-permute-start(bf16[192,896]{1,0:T(8,128)(2,1)S(1)} %get-tuple-element.279.refs_0_), channel_id=1, source_target_pairs={{0,24},{8,16},{16,8},{24,0},{1,25},{9,17},{17,9},{25,1},{2,26},{10... | collective-permute-start | bytes 1032200 | tf_op jit(solution)/shard_map/ppermute | solution.py:1215
  167.1 11.8 %collective-permute-start.44 = (bf16[96,1088]{1,0:T(8,128)(2,1)S(1)}, bf16[96,1088]{1,0:T(8,128)(2,1)S(1)}, u32[]{:S(2)}, u32[]{:S(2)}) collective-permute-start(bf16[96,1088]{1,0:T(8,128)(2,1)S(1)} %get-tuple-element.272), channel_id=1, source_target_pairs={{0,4},{2,6},{4,0},{6,2},{1,5},{3,7},{5,1},{7,3},{8,12},{10,14},{12... | collective-permute-start | bytes 626696 | tf_op jit(solution)/shard_map/ppermute | solution.py:459
  (31 other events, 211.5 us)

commit v6 on v5

--- a/solution.py
+++ b/solution.py
@@ -1189,7 +1189,8 @@
 
 
 def place_last_body(flags_ref, *refs):
-    outs = refs[4:]
+    join_back_body(flags_ref, refs[4], refs[5], refs[6])
+    outs = refs[7:]
     first_core = flags_ref[CORE] == 0
     part = refs[0].shape[0]
     for own_ref, other_ref, other_copy in ((refs[0], refs[2], 0), (refs[1], refs[3], 1)):
@@ -1545,7 +1546,7 @@
         weights,
         prior,
     )
-    mix_got = swap_copies(after(mix_sent, got_up))
+    mix_got = swap_copies(after(mix_sent, got_up, grad_den))
     up_lanes = SPAN // 2 + part + half_lanes
     down_part, down_far = local_call(
         down_far_body,
@@ -1587,6 +1588,7 @@
         scratch=[state_shape, ((2, 3 * WIDTH, SPAN), low)],
     )
     got_w = swap_copies(sent_w)
+    got_w = after(got_w, down_part)
     got_x = swap_pair(x_grad_other)
     x_half_grad, x_half_sent = local_call(
         partial(input_halves_body, rows=rows),
@@ -1651,7 +1653,6 @@
         swap_rows(last_far, 2),
     )
     output = cols_back(*out_wide, low, "out_join")
-    input_grad = cols_back(*input_wide, wide, "input_join")
     down_t, up_grad, out_t, vec_total = local_call(
         place_hidden_body,
         [((feat_rows, 4 * part), wide)] * 2
@@ -1660,12 +1661,16 @@
         flags,
         *all_quarters(hidden_sum, True),
     )
-    query_grad, key_grad, value_grad = local_call(
+    last_parts = all_quarters(last_sum, True)
+    last_parts = (after(last_parts[0], up_grad), *last_parts[1:])
+    input_grad, query_grad, key_grad, value_grad = local_call(
         place_last_body,
-        [((feat_rows, 2 * WIDTH), wide)] * 3,
+        [((feat_rows, SPAN * rows // 2), wide)] + [((feat_rows, 2 * WIDTH), wide)] * 3,
         "place_last",
         flags,
-        *all_quarters(last_sum, True),
+        *last_parts,
+        input_wide[0],
+        swap_cols(input_wide[1]),
     )
     return (
         output,

time: 190 us -> 189 us (level)
    pallas_call x36 -> x35, Pallas kernels: 33.4 us -> 32.2 us  [local_call(): pl.pallas_call(body, out_shape=shapes, in_specs=[pl.BlockSpec(memory_spac...]
  transfers between devices with their start and end apart: 52 -> 52, of which waited for: 27 -> 28; matrix products, arithmetic and copies ran while one was open for 1% -> 1% of each run, Pallas kernels for 12% -> 12%
where the time goes in v6:
time: 189 us
  waiting for transfers between devices  87.4 us (46%)
  starting transfers between devices  65.1 us (34%)
  Pallas kernels  32.2 us (17%)
    ppermute x12, waiting for transfers between devices, swap_rows(): return lax.ppermute(operand, 'row', [(i, i ^ mask) for i in range(4)])  41.6 us
    pallas_call x35, Pallas kernels, local_call(): pl.pallas_call(body, out_shape=shapes, in_specs=[pl.BlockSpec(memory_spac...  32.2 us
    ppermute x12, starting transfers between devices, swap_rows(): return lax.ppermute(operand, 'row', [(i, i ^ mask) for i in range(4)])  17.5 us
    ppermute x11, waiting for transfers between devices, swap_copies(): lax.ppermute(operand, 'dp', [(i, i ^ 2) for i in range(lax.axis_size('dp'...  15.5 us
    ppermute x11, starting transfers between devices, swap_copies(): lax.ppermute(operand, 'dp', [(i, i ^ 2) for i in range(lax.axis_size('dp'...  13.7 us
    ppermute x8, waiting for transfers between devices, swap_cols(): return lax.ppermute(operand, 'col', [(0, 1), (1, 0)])  13.7 us
    ppermute x6, starting transfers between devices, shift_rows(): return lax.ppermute(operand, 'row', pairs)  13 us
    ppermute x8, starting transfers between devices, swap_cols(): return lax.ppermute(operand, 'col', [(0, 1), (1, 0)])  13 us
  transfers between devices with their start and end apart: 52, of which 28 were waited for; matrix products, arithmetic and copies ran while one was open for 1% of the time, Pallas kernels for 12%

profile of v6, /device:TPU:0, one launch (start us, length us, event | category | flops | bytes accessed | tf_op | source)
XLA Modules:
  0.0 188.6 jit_solution(18213437688245085383)
XLA Ops:
  1.9 3.0 %collective-permute-start.1 = (bf16[192,512]{1,0:T(8,128)(2,1)S(1)}, bf16[192,512]{1,0:T(8,128)(2,1)S(1)}, u32[]{:S(2)}, u32[]{:S(2)}) collective-permute-start(bf16[192,512]{1,0:T(8,128)(2,1)S(1)} %pad_maximum_fusion.1), channel_id=1, source_target_pairs={{0,1},{1,0},{2,3},{3,2},{4,5},{5,4},{6,7},{7,6},{8,9},{9,8},{10,11... | collective-permute-start | bytes 589832 | tf_op jit(solution)/shard_map/ppermute | solution.py:441
  7.0 2.6 %collective-permute-start.5 = (bf16[192,384]{1,0:T(8,128)(2,1)S(1)}, bf16[192,384]{1,0:T(8,128)(2,1)S(1)}, u32[]{:S(2)}, u32[]{:S(2)}) collective-permute-start(bf16[192,384]{1,0:T(8,128)(2,1)S(1)} %maximum_select_fusion), channel_id=1, source_target_pairs={{0,4},{2,6},{4,0},{6,2},{1,5},{3,7},{5,1},{7,3},{8,12},{10,14},{12... | collective-permute-start | bytes 442376 | tf_op jit(solution)/shard_map/ppermute | solution.py:459
  9.7 3.4 %collective-permute-done.refs_0_ = bf16[192,384]{1,0:T(8,128)(2,1)S(1)} collective-permute-done((bf16[192,384]{1,0:T(8,128)(2,1)S(1)}, bf16[192,384]{1,0:T(8,128)(2,1)S(1)}, u32[]{:S(2)}, u32[]{:S(2)}) %collective-permute-start) | collective-permute-done | bytes 147488 | tf_op jit(solution)/shard_map/ppermute | solution.py:459
  19.2 2.9 %collective-permute-start.4 = (bf16[208,256]{1,0:T(8,128)(2,1)S(1)}, bf16[208,256]{1,0:T(8,128)(2,1)S(1)}, u32[]{:S(2)}, u32[]{:S(2)}) collective-permute-start(bf16[208,256]{1,0:T(8,128)(2,1)S(1)} %get-tuple-element.155), channel_id=1, source_target_pairs={{0,6},{2,0},{4,2},{6,4},{1,7},{3,1},{5,3},{7,5},{8,14},{10,8},{12,... | collective-permute-start | bytes 319496 | tf_op jit(solution)/shard_map/ppermute | solution.py:464
  23.1 2.4 %collective-permute-done.2.refs_1_ = bf16[208,256]{1,0:T(8,128)(2,1)S(1)} collective-permute-done((bf16[208,256]{1,0:T(8,128)(2,1)S(1)}, bf16[208,256]{1,0:T(8,128)(2,1)S(1)}, u32[]{:S(2)}, u32[]{:S(2)}) %collective-permute-start.2) | collective-permute-done | bytes 106528 | tf_op jit(solution)/shard_map/ppermute | solution.py:464
  30.2 2.3 %collective-permute-start.16 = (bf16[192,768]{1,0:T(8,128)(2,1)S(1)}, bf16[192,768]{1,0:T(8,128)(2,1)S(1)}, u32[]{:S(2)}, u32[]{:S(2)}) collective-permute-start(bf16[192,768]{1,0:T(8,128)(2,1)S(1)} %get-tuple-element.167.refs_0_), channel_id=1, source_target_pairs={{0,4},{2,6},{4,0},{6,2},{1,5},{3,7},{5,1},{7,3},{8,12},{10,14},{12... | collective-permute-start | bytes 884744 | tf_op jit(solution)/shard_map/ppermute | solution.py:459
  34.6 5.0 %collective-permute-done.9.refs_1_ = bf16[192,768]{1,0:T(8,128)(2,1)S(1)} collective-permute-done((bf16[192,768]{1,0:T(8,128)(2,1)S(1)}, bf16[192,768]{1,0:T(8,128)(2,1)S(1)}, u32[]{:S(2)}, u32[]{:S(2)}) %collective-permute-start.9) | collective-permute-done | bytes 294944 | tf_op jit(solution)/shard_map/ppermute | solution.py:459
  40.3 2.5 %collective-permute-done.16.refs_2_ = bf16[192,768]{1,0:T(8,128)(2,1)S(1)} collective-permute-done((bf16[192,768]{1,0:T(8,128)(2,1)S(1)}, bf16[192,768]{1,0:T(8,128)(2,1)S(1)}, u32[]{:S(2)}, u32[]{:S(2)}) %collective-permute-start.16) | collective-permute-done | bytes 294944 | tf_op jit(solution)/shard_map/ppermute | solution.py:459
  46.7 3.8 %collective-permute-start.13 = (bf16[400,128]{1,0:T(8,128)(2,1)S(1)}, bf16[400,128]{1,0:T(8,128)(2,1)S(1)}, u32[]{:S(2)}, u32[]{:S(2)}) collective-permute-start(bf16[400,128]{1,0:T(8,128)(2,1)S(1)} %get-tuple-element.185), channel_id=1, source_target_pairs={{0,2},{2,4},{4,6},{1,3},{3,5},{5,7},{8,10},{10,12},{12,14},{9,11},... | collective-permute-start | bytes 307208 | tf_op jit(solution)/shard_map/ppermute | solution.py:455
  50.5 2.7 %collective-permute-start.14 = (bf16[400,128]{1,0:T(8,128)(2,1)S(1)}, bf16[400,128]{1,0:T(8,128)(2,1)S(1)}, u32[]{:S(2)}, u32[]{:S(2)}) collective-permute-start(bf16[400,128]{1,0:T(8,128)(2,1)S(1)} %get-tuple-element.185), channel_id=1, source_target_pairs={{0,4},{2,6},{1,5},{3,7},{8,12},{10,14},{9,13},{11,15},{16,20},{18,... | collective-permute-start | bytes 307208 | tf_op jit(solution)/shard_map/ppermute | solution.py:455
  53.3 2.4 %collective-permute-start.15 = (bf16[400,128]{1,0:T(8,128)(2,1)S(1)}, bf16[400,128]{1,0:T(8,128)(2,1)S(1)}, u32[]{:S(2)}, u32[]{:S(2)}) collective-permute-start(bf16[400,128]{1,0:T(8,128)(2,1)S(1)} %get-tuple-element.185), channel_id=1, source_target_pairs={{0,6},{1,7},{8,14},{9,15},{16,22},{17,23},{24,30},{25,31}} | collective-permute-start | bytes 307208 | tf_op jit(solution)/shard_map/ppermute | solution.py:455
  58.4 1.7 collective-permute-done.20.recv_ref
  63.3 7.3 %collective-permute-done.22.refs_7_ = bf16[192,768]{1,0:T(8,128)(2,1)S(1)} collective-permute-done((bf16[192,768]{1,0:T(8,128)(2,1)S(1)}, bf16[192,768]{1,0:T(8,128)(2,1)S(1)}, u32[]{:S(2)}, u32[]{:S(2)}) %collective-permute-start.22) | collective-permute-done | bytes 294944 | tf_op jit(solution)/shard_map/ppermute | solution.py:449
  72.9 1.7 collective-permute-done.23.other_ref
  74.6 1.8 hidden.1
  79.9 9.6 %collective-permute-done.25.recv_ref = bf16[768,256]{1,0:T(8,128)(2,1)S(1)} collective-permute-done((bf16[768,256]{1,0:T(8,128)(2,1)S(1)}, bf16[768,256]{1,0:T(8,128)(2,1)S(1)}, u32[]{:S(2)}, u32[]{:S(2)}) %collective-permute-start.25) | collective-permute-done | bytes 393248 | tf_op jit(solution)/shard_map/ppermute | solution.py:441
  90.8 1.7 collective-permute-done.26.other_ref
  94.1 1.8 hidden_back.1
  101.9 9.8 %collective-permute-done.29.got_ref = bf16[384,768]{1,0:T(8,128)(2,1)S(1)} collective-permute-done((bf16[384,768]{1,0:T(8,128)(2,1)S(1)}, bf16[384,768]{1,0:T(8,128)(2,1)S(1)}, u32[]{:S(2)}, u32[]{:S(2)}) %collective-permute-start.29) | collective-permute-done | bytes 589856 | tf_op jit(solution)/shard_map/ppermute | solution.py:459
  112.7 1.7 collective-permute-done.30.other_ref
  123.6 6.1 %collective-permute-done.32.got_ref.mix_got_ref = bf16[384,640]{1,0:T(8,128)(2,1)S(1)} collective-permute-done((bf16[384,640]{1,0:T(8,128)(2,1)S(1)}, bf16[384,640]{1,0:T(8,128)(2,1)S(1)}, u32[]{:S(2)}, u32[]{:S(2)}) %collective-permute-start.32) | collective-permute-done | bytes 491552 | tf_op jit(solution)/shard_map/ppermute | solution.py:449
  132.3 2.3 %grad_project.1 = (bf16[4,96,576]{2,1,0:T(8,128)(2,1)S(1)}, bf16[4,96,576]{2,1,0:T(8,128)(2,1)S(1)}, f32[768,256]{1,0:T(8,128)S(1)}, bf16[768,256]{1,0:T(8,128)(2,1)S(1)}) custom-call(bf16[2,192,256]{2,1,0:T(8,128)(2,1)S(1)} %get-tuple-element.250.grad_query_ref, f32[6,64,256]{2,1,0:T(8,128)S(1)} %get-tuple-element.260.grad_key_ref, ...), custom_call_target="tpu_custom_call" | custom-call | tf_op jit(solution)/shard_map/grad_project/pallas_call | solution.py:497
  138.7 4.4 %collective-permute-done.37.got_ref = bf16[384,640]{1,0:T(8,128)(2,1)S(1)} collective-permute-done((bf16[384,640]{1,0:T(8,128)(2,1)S(1)}, bf16[384,640]{1,0:T(8,128)(2,1)S(1)}, u32[]{:S(2)}, u32[]{:S(2)}) %collective-permute-start.37) | collective-permute-done | bytes 491552 | tf_op jit(solution)/shard_map/ppermute | solution.py:459
  143.2 3.1 %collective-permute-start.38 = (bf16[192,768]{1,0:T(8,128)(2,1)S(1)}, bf16[192,768]{1,0:T(8,128)(2,1)S(1)}, u32[]{:S(2)}, u32[]{:S(2)}) collective-permute-start(bf16[192,768]{1,0:T(8,128)(2,1)S(1)} %get-tuple-element.257), channel_id=1, source_target_pairs={{0,4},{2,6},{4,0},{6,2},{1,5},{3,7},{5,1},{7,3},{8,12},{10,14},{12... | collective-permute-start | bytes 884744 | tf_op jit(solution)/shard_map/ppermute | solution.py:459
  146.3 2.0 %collective-permute-done.40.got_ref = bf16[4,96,576]{2,1,0:T(8,128)(2,1)S(1)} collective-permute-done((bf16[4,96,576]{2,1,0:T(8,128)(2,1)S(1)}, bf16[4,96,576]{2,1,0:T(8,128)(2,1)S(1)}, u32[]{:S(2)}, u32[]{:S(2)}) %collective-permute-start.40) | collective-permute-done | bytes 442400 | tf_op jit(solution)/shard_map/ppermute | solution.py:449
  149.6 3.0 %collective-permute-start.33 = (bf16[192,384]{1,0:T(8,128)(2,1)S(1)}, bf16[192,384]{1,0:T(8,128)(2,1)S(1)}, u32[]{:S(2)}, u32[]{:S(2)}) collective-permute-start(bf16[192,384]{1,0:T(8,128)(2,1)S(1)} %get-tuple-element.244), channel_id=1, source_target_pairs={{0,4},{2,6},{4,0},{6,2},{1,5},{3,7},{5,1},{7,3},{8,12},{10,14},{12... | collective-permute-start | bytes 442376 | tf_op jit(solution)/shard_map/ppermute | solution.py:459
  152.6 10.0 %collective-permute-done.33.down_far_ref = bf16[192,384]{1,0:T(8,128)(2,1)S(1)} collective-permute-done((bf16[192,384]{1,0:T(8,128)(2,1)S(1)}, bf16[192,384]{1,0:T(8,128)(2,1)S(1)}, u32[]{:S(2)}, u32[]{:S(2)}) %collective-permute-start.33) | collective-permute-done | bytes 147488 | tf_op jit(solution)/shard_map/ppermute | solution.py:459
  167.1 1.9 %collective-permute-start.44 = (bf16[96,1088]{1,0:T(8,128)(2,1)S(1)}, bf16[96,1088]{1,0:T(8,128)(2,1)S(1)}, u32[]{:S(2)}, u32[]{:S(2)}) collective-permute-start(bf16[96,1088]{1,0:T(8,128)(2,1)S(1)} %get-tuple-element.276), channel_id=1, source_target_pairs={{0,4},{2,6},{4,0},{6,2},{1,5},{3,7},{5,1},{7,3},{8,12},{10,14},{12... | collective-permute-start | bytes 626696 | tf_op jit(solution)/shard_map/ppermute | solution.py:459
  170.5 3.1 %collective-permute-done.39.recv_ref = bf16[96,512]{1,0:T(8,128)(2,1)S(1)} collective-permute-done((bf16[96,512]{1,0:T(8,128)(2,1)S(1)}, bf16[96,512]{1,0:T(8,128)(2,1)S(1)}, u32[]{:S(2)}, u32[]{:S(2)}) %collective-permute-start.39) | collective-permute-done | bytes 98336 | tf_op jit(solution)/shard_map/ppermute | solution.py:441
  174.9 4.0 %collective-permute-done.44.far_ref = bf16[96,1088]{1,0:T(8,128)(2,1)S(1)} collective-permute-done((bf16[96,1088]{1,0:T(8,128)(2,1)S(1)}, bf16[96,1088]{1,0:T(8,128)(2,1)S(1)}, u32[]{:S(2)}, u32[]{:S(2)}) %collective-permute-start.44) | collective-permute-done | bytes 208928 | tf_op jit(solution)/shard_map/ppermute | solution.py:459
  183.6 2.2 %place_hidden.1 = (f32[192,1536]{1,0:T(8,128)}, f32[192,1536]{1,0:T(8,128)}, f32[192,384]{1,0:T(8,128)}, f32[192,64]{1,0:T(8,128)S(1)}) custom-call(s32[5]{0:T(128)S(1)} %stack.38.flags_ref, bf16[192,896]{1,0:T(8,128)(2,1)S(1)} %get-tuple-element.278.refs_0_, bf16[192,896]{1,0:T(8,128)(2,1)S(1)} %collective-permute-done.45.refs_1_, ...), custom_call_target="tpu_custom_call" | custom-call | tf_op jit(solution)/shard_map/place_hidden/pallas_call | solution.py:497
  186.8 1.7 place_last.1
  (138 shorter events, 73.2 us)
Async XLA Ops:
  1.9 11.2 %collective-permute-start.1 = (bf16[192,512]{1,0:T(8,128)(2,1)S(1)}, bf16[192,512]{1,0:T(8,128)(2,1)S(1)}, u32[]{:S(2)}, u32[]{:S(2)}) collective-permute-start(bf16[192,512]{1,0:T(8,128)(2,1)S(1)} %pad_maximum_fusion.1), channel_id=1, source_target_pairs={{0,1},{1,0},{2,3},{3,2},{4,5},{5,4},{6,7},{7,6},{8,9},{9,8},{10,11... | collective-permute-start | bytes 589832 | tf_op jit(solution)/shard_map/ppermute | solution.py:441
  7.0 9.2 %collective-permute-start.5 = (bf16[192,384]{1,0:T(8,128)(2,1)S(1)}, bf16[192,384]{1,0:T(8,128)(2,1)S(1)}, u32[]{:S(2)}, u32[]{:S(2)}) collective-permute-start(bf16[192,384]{1,0:T(8,128)(2,1)S(1)} %maximum_select_fusion), channel_id=1, source_target_pairs={{0,4},{2,6},{4,0},{6,2},{1,5},{3,7},{5,1},{7,3},{8,12},{10,14},{12... | collective-permute-start | bytes 442376 | tf_op jit(solution)/shard_map/ppermute | solution.py:459
  13.8 13.1 %collective-permute-start.7 = (bf16[192,384]{1,0:T(8,128)(2,1)S(1)}, bf16[192,384]{1,0:T(8,128)(2,1)S(1)}, u32[]{:S(2)}, u32[]{:S(2)}) collective-permute-start(bf16[192,384]{1,0:T(8,128)(2,1)S(1)} %collective-permute-done.refs_0_), channel_id=1, source_target_pairs={{0,16},{8,24},{16,0},{24,8},{1,17},{9,25},{17,1},{25,9},{2,18},{10... | collective-permute-start | bytes 442376 | tf_op jit(solution)/shard_map/ppermute | solution.py:449
  16.3 10.6 %collective-permute-start.6 = (bf16[192,384]{1,0:T(8,128)(2,1)S(1)}, bf16[192,384]{1,0:T(8,128)(2,1)S(1)}, u32[]{:S(2)}, u32[]{:S(2)}) collective-permute-start(bf16[192,384]{1,0:T(8,128)(2,1)S(1)} %collective-permute-done.5.refs_1_), channel_id=1, source_target_pairs={{0,2},{2,0},{4,6},{6,4},{1,3},{3,1},{5,7},{7,5},{8,10},{10,8},{12,... | collective-permute-start | bytes 442376 | tf_op jit(solution)/shard_map/ppermute | solution.py:459
  16.6 8.9 %collective-permute-start.2 = (bf16[208,256]{1,0:T(8,128)(2,1)S(1)}, bf16[208,256]{1,0:T(8,128)(2,1)S(1)}, u32[]{:S(2)}, u32[]{:S(2)}) collective-permute-start(bf16[208,256]{1,0:T(8,128)(2,1)S(1)} %get-tuple-element.153), channel_id=1, source_target_pairs={{0,2},{2,4},{4,6},{6,0},{1,3},{3,5},{5,7},{7,1},{8,10},{10,12},{12... | collective-permute-start | bytes 319496 | tf_op jit(solution)/shard_map/ppermute | solution.py:464
  27.6 12.1 %collective-permute-start.8 = (bf16[768,256]{1,0:T(8,128)(2,1)S(1)}, bf16[768,256]{1,0:T(8,128)(2,1)S(1)}, u32[]{:S(2)}, u32[]{:S(2)}) collective-permute-start(bf16[768,256]{1,0:T(8,128)(2,1)S(1)} %get-tuple-element.166.half_ref), channel_id=1, source_target_pairs={{0,1},{1,0},{2,3},{3,2},{4,5},{5,4},{6,7},{7,6},{8,9},{9,8},{10,11... | collective-permute-start | bytes 1179656 | tf_op jit(solution)/shard_map/ppermute | solution.py:441
  28.8 10.8 %collective-permute-start.9 = (bf16[192,768]{1,0:T(8,128)(2,1)S(1)}, bf16[192,768]{1,0:T(8,128)(2,1)S(1)}, u32[]{:S(2)}, u32[]{:S(2)}) collective-permute-start(bf16[192,768]{1,0:T(8,128)(2,1)S(1)} %get-tuple-element.167.refs_0_), channel_id=1, source_target_pairs={{0,2},{2,0},{4,6},{6,4},{1,3},{3,1},{5,7},{7,5},{8,10},{10,8},{12,... | collective-permute-start | bytes 884744 | tf_op jit(solution)/shard_map/ppermute | solution.py:459
  30.2 12.6 %collective-permute-start.16 = (bf16[192,768]{1,0:T(8,128)(2,1)S(1)}, bf16[192,768]{1,0:T(8,128)(2,1)S(1)}, u32[]{:S(2)}, u32[]{:S(2)}) collective-permute-start(bf16[192,768]{1,0:T(8,128)(2,1)S(1)} %get-tuple-element.167.refs_0_), channel_id=1, source_target_pairs={{0,4},{2,6},{4,0},{6,2},{1,5},{3,7},{5,1},{7,3},{8,12},{10,14},{12... | collective-permute-start | bytes 884744 | tf_op jit(solution)/shard_map/ppermute | solution.py:459
  42.8 10.5 %collective-permute-start.17 = (bf16[192,768]{1,0:T(8,128)(2,1)S(1)}, bf16[192,768]{1,0:T(8,128)(2,1)S(1)}, u32[]{:S(2)}, u32[]{:S(2)}) collective-permute-start(bf16[192,768]{1,0:T(8,128)(2,1)S(1)} %collective-permute-done.16.refs_2_), channel_id=1, source_target_pairs={{0,2},{2,0},{4,6},{6,4},{1,3},{3,1},{5,7},{7,5},{8,10},{10,8},{12,... | collective-permute-start | bytes 884744 | tf_op jit(solution)/shard_map/ppermute | solution.py:459
  42.9 14.1 %collective-permute-start.18 = (bf16[192,768]{1,0:T(8,128)(2,1)S(1)}, bf16[192,768]{1,0:T(8,128)(2,1)S(1)}, u32[]{:S(2)}, u32[]{:S(2)}) collective-permute-start(bf16[192,768]{1,0:T(8,128)(2,1)S(1)} %collective-permute-done.16.refs_2_), channel_id=1, source_target_pairs={{0,16},{8,24},{16,0},{24,8},{1,17},{9,25},{17,1},{25,9},{2,18},{10... | collective-permute-start | bytes 884744 | tf_op jit(solution)/shard_map/ppermute | solution.py:449
  44.4 13.9 %collective-permute-start.19 = (bf16[192,768]{1,0:T(8,128)(2,1)S(1)}, bf16[192,768]{1,0:T(8,128)(2,1)S(1)}, u32[]{:S(2)}, u32[]{:S(2)}) collective-permute-start(bf16[192,768]{1,0:T(8,128)(2,1)S(1)} %collective-permute-done.9.refs_1_), channel_id=1, source_target_pairs={{0,16},{8,24},{16,0},{24,8},{1,17},{9,25},{17,1},{25,9},{2,18},{10... | collective-permute-start | bytes 884744 | tf_op jit(solution)/shard_map/ppermute | solution.py:449
  46.7 10.4 %collective-permute-start.13 = (bf16[400,128]{1,0:T(8,128)(2,1)S(1)}, bf16[400,128]{1,0:T(8,128)(2,1)S(1)}, u32[]{:S(2)}, u32[]{:S(2)}) collective-permute-start(bf16[400,128]{1,0:T(8,128)(2,1)S(1)} %get-tuple-element.185), channel_id=1, source_target_pairs={{0,2},{2,4},{4,6},{1,3},{3,5},{5,7},{8,10},{10,12},{12,14},{9,11},... | collective-permute-start | bytes 307208 | tf_op jit(solution)/shard_map/ppermute | solution.py:455
  60.2 11.2 %collective-permute-start.21 = (bf16[768,256]{1,0:T(8,128)(2,1)S(1)}, bf16[768,256]{1,0:T(8,128)(2,1)S(1)}, u32[]{:S(2)}, u32[]{:S(2)}) collective-permute-start(bf16[768,256]{1,0:T(8,128)(2,1)S(1)} %branch_half.1.half_ref), channel_id=1, source_target_pairs={{0,1},{1,0},{2,3},{3,2},{4,5},{5,4},{6,7},{7,6},{8,9},{9,8},{10,11... | collective-permute-start | bytes 1179656 | tf_op jit(solution)/shard_map/ppermute | solution.py:441
  61.8 8.8 %collective-permute-start.22 = (bf16[192,768]{1,0:T(8,128)(2,1)S(1)}, bf16[192,768]{1,0:T(8,128)(2,1)S(1)}, u32[]{:S(2)}, u32[]{:S(2)}) collective-permute-start(bf16[192,768]{1,0:T(8,128)(2,1)S(1)} %collective-permute-done.17.refs_3_), channel_id=1, source_target_pairs={{0,16},{8,24},{16,0},{24,8},{1,17},{9,25},{17,1},{25,9},{2,18},{10... | collective-permute-start | bytes 884744 | tf_op jit(solution)/shard_map/ppermute | solution.py:449
  78.3 11.2 %collective-permute-start.25 = (bf16[768,256]{1,0:T(8,128)(2,1)S(1)}, bf16[768,256]{1,0:T(8,128)(2,1)S(1)}, u32[]{:S(2)}, u32[]{:S(2)}) collective-permute-start(bf16[768,256]{1,0:T(8,128)(2,1)S(1)} %ffn_half.1.half_ref), channel_id=1, source_target_pairs={{0,1},{1,0},{2,3},{3,2},{4,5},{5,4},{6,7},{7,6},{8,9},{9,8},{10,11... | collective-permute-start | bytes 1179656 | tf_op jit(solution)/shard_map/ppermute | solution.py:441
  96.1 15.6 %collective-permute-start.29 = (bf16[384,768]{1,0:T(8,128)(2,1)S(1)}, bf16[384,768]{1,0:T(8,128)(2,1)S(1)}, u32[]{:S(2)}, u32[]{:S(2)}) collective-permute-start(bf16[384,768]{1,0:T(8,128)(2,1)S(1)} %get-tuple-element.226), channel_id=1, source_target_pairs={{0,2},{2,0},{4,6},{6,4},{1,3},{3,1},{5,7},{7,5},{8,10},{10,8},{12,... | collective-permute-start | bytes 1769480 | tf_op jit(solution)/shard_map/ppermute | solution.py:459
  97.8 14.1 %collective-permute-start.28 = (bf16[768,256]{1,0:T(8,128)(2,1)S(1)}, bf16[768,256]{1,0:T(8,128)(2,1)S(1)}, u32[]{:S(2)}, u32[]{:S(2)}) collective-permute-start(bf16[768,256]{1,0:T(8,128)(2,1)S(1)} %first_half.1.half_ref), channel_id=1, source_target_pairs={{0,1},{1,0},{2,3},{3,2},{4,5},{5,4},{6,7},{7,6},{8,9},{9,8},{10,11... | collective-permute-start | bytes 1179656 | tf_op jit(solution)/shard_map/ppermute | solution.py:441
  100.4 16.0 %collective-permute-start.31 = (bf16[768,384]{1,0:T(8,128)(2,1)S(1)}, bf16[768,384]{1,0:T(8,128)(2,1)S(1)}, u32[]{:S(2)}, u32[]{:S(2)}) collective-permute-start(bf16[768,384]{1,0:T(8,128)(2,1)S(1)} %get-tuple-element.240), channel_id=1, source_target_pairs={{0,16},{8,24},{16,0},{24,8},{1,17},{9,25},{17,1},{25,9},{2,18},{10... | collective-permute-start | bytes 1769480 | tf_op jit(solution)/shard_map/ppermute | solution.py:449
  116.4 13.3 %collective-permute-start.32 = (bf16[384,640]{1,0:T(8,128)(2,1)S(1)}, bf16[384,640]{1,0:T(8,128)(2,1)S(1)}, u32[]{:S(2)}, u32[]{:S(2)}) collective-permute-start(bf16[384,640]{1,0:T(8,128)(2,1)S(1)} %get-tuple-element.242), channel_id=1, source_target_pairs={{0,16},{8,24},{16,0},{24,8},{1,17},{9,25},{17,1},{25,9},{2,18},{10... | collective-permute-start | bytes 1474568 | tf_op jit(solution)/shard_map/ppermute | solution.py:449
  117.9 13.0 %collective-permute-start.34 = (bf16[400,128]{1,0:T(8,128)(2,1)S(1)}, bf16[400,128]{1,0:T(8,128)(2,1)S(1)}, u32[]{:S(2)}, u32[]{:S(2)}) collective-permute-start(bf16[400,128]{1,0:T(8,128)(2,1)S(1)} %get-tuple-element.245), channel_id=1, source_target_pairs={{2,0},{4,2},{6,4},{3,1},{5,3},{7,5},{10,8},{12,10},{14,12},{11,9},... | collective-permute-start | bytes 307208 | tf_op jit(solution)/shard_map/ppermute | solution.py:455
  119.2 13.1 %collective-permute-start.35 = (bf16[400,128]{1,0:T(8,128)(2,1)S(1)}, bf16[400,128]{1,0:T(8,128)(2,1)S(1)}, u32[]{:S(2)}, u32[]{:S(2)}) collective-permute-start(bf16[400,128]{1,0:T(8,128)(2,1)S(1)} %get-tuple-element.245), channel_id=1, source_target_pairs={{4,0},{6,2},{5,1},{7,3},{12,8},{14,10},{13,9},{15,11},{20,16},{22,... | collective-permute-start | bytes 307208 | tf_op jit(solution)/shard_map/ppermute | solution.py:455
  120.5 11.8 %collective-permute-start.36 = (bf16[400,128]{1,0:T(8,128)(2,1)S(1)}, bf16[400,128]{1,0:T(8,128)(2,1)S(1)}, u32[]{:S(2)}, u32[]{:S(2)}) collective-permute-start(bf16[400,128]{1,0:T(8,128)(2,1)S(1)} %get-tuple-element.245), channel_id=1, source_target_pairs={{6,0},{7,1},{14,8},{15,9},{22,16},{23,17},{30,24},{31,25}} | collective-permute-start | bytes 307208 | tf_op jit(solution)/shard_map/ppermute | solution.py:455
  130.6 12.5 %collective-permute-start.37 = (bf16[384,640]{1,0:T(8,128)(2,1)S(1)}, bf16[384,640]{1,0:T(8,128)(2,1)S(1)}, u32[]{:S(2)}, u32[]{:S(2)}) collective-permute-start(bf16[384,640]{1,0:T(8,128)(2,1)S(1)} %get-tuple-element.255), channel_id=1, source_target_pairs={{0,2},{2,0},{4,6},{6,4},{1,3},{3,1},{5,7},{7,5},{8,10},{10,8},{12,... | collective-permute-start | bytes 1474568 | tf_op jit(solution)/shard_map/ppermute | solution.py:459
  134.7 13.6 %collective-permute-start.40 = (bf16[4,96,576]{2,1,0:T(8,128)(2,1)S(1)}, bf16[4,96,576]{2,1,0:T(8,128)(2,1)S(1)}, u32[]{:S(2)}, u32[]{:S(2)}) collective-permute-start(bf16[4,96,576]{2,1,0:T(8,128)(2,1)S(1)} %get-tuple-element.266), channel_id=1, source_target_pairs={{0,16},{8,24},{16,0},{24,8},{1,17},{9,25},{17,1},{25,9},{2,18},{10... | collective-permute-start | bytes 1327112 | tf_op jit(solution)/shard_map/ppermute | solution.py:449
  137.1 11.2 %collective-permute-start.42 = (bf16[384,256]{1,0:T(8,128)(2,1)S(1)}, bf16[384,256]{1,0:T(8,128)(2,1)S(1)}, u32[]{:S(2)}, u32[]{:S(2)}) collective-permute-start(bf16[384,256]{1,0:T(8,128)(2,1)S(1)} %get-tuple-element.271), channel_id=1, source_target_pairs={{0,1},{1,0},{2,3},{3,2},{4,5},{5,4},{6,7},{7,6},{8,9},{9,8},{10,11... | collective-permute-start | bytes 589832 | tf_op jit(solution)/shard_map/ppermute | solution.py:441
  143.2 19.5 %collective-permute-start.38 = (bf16[192,768]{1,0:T(8,128)(2,1)S(1)}, bf16[192,768]{1,0:T(8,128)(2,1)S(1)}, u32[]{:S(2)}, u32[]{:S(2)}) collective-permute-start(bf16[192,768]{1,0:T(8,128)(2,1)S(1)} %get-tuple-element.257), channel_id=1, source_target_pairs={{0,4},{2,6},{4,0},{6,2},{1,5},{3,7},{5,1},{7,3},{8,12},{10,14},{12... | collective-permute-start | bytes 884744 | tf_op jit(solution)/shard_map/ppermute | solution.py:459
  149.2 17.9 %collective-permute-start.43 = (bf16[192,832]{1,0:T(8,128)(2,1)S(1)}, bf16[192,832]{1,0:T(8,128)(2,1)S(1)}, u32[]{:S(2)}, u32[]{:S(2)}) collective-permute-start(bf16[192,832]{1,0:T(8,128)(2,1)S(1)} %get-tuple-element.274), channel_id=1, source_target_pairs={{0,2},{2,0},{4,6},{6,4},{1,3},{3,1},{5,7},{7,5},{8,10},{10,8},{12,... | collective-permute-start | bytes 958472 | tf_op jit(solution)/shard_map/ppermute | solution.py:459
  149.6 13.1 %collective-permute-start.33 = (bf16[192,384]{1,0:T(8,128)(2,1)S(1)}, bf16[192,384]{1,0:T(8,128)(2,1)S(1)}, u32[]{:S(2)}, u32[]{:S(2)}) collective-permute-start(bf16[192,384]{1,0:T(8,128)(2,1)S(1)} %get-tuple-element.244), channel_id=1, source_target_pairs={{0,4},{2,6},{4,0},{6,2},{1,5},{3,7},{5,1},{7,3},{8,12},{10,14},{12... | collective-permute-start | bytes 442376 | tf_op jit(solution)/shard_map/ppermute | solution.py:459
  163.3 17.9 %collective-permute-start.45 = (bf16[192,896]{1,0:T(8,128)(2,1)S(1)}, bf16[192,896]{1,0:T(8,128)(2,1)S(1)}, u32[]{:S(2)}, u32[]{:S(2)}) collective-permute-start(bf16[192,896]{1,0:T(8,128)(2,1)S(1)} %get-tuple-element.278.refs_0_), channel_id=1, source_target_pairs={{0,16},{8,24},{16,0},{24,8},{1,17},{9,25},{17,1},{25,9},{2,18},{10... | collective-permute-start | bytes 1032200 | tf_op jit(solution)/shard_map/ppermute | solution.py:449
  164.9 17.2 %collective-permute-start.46 = (bf16[192,896]{1,0:T(8,128)(2,1)S(1)}, bf16[192,896]{1,0:T(8,128)(2,1)S(1)}, u32[]{:S(2)}, u32[]{:S(2)}) collective-permute-start(bf16[192,896]{1,0:T(8,128)(2,1)S(1)} %get-tuple-element.278.refs_0_), channel_id=1, source_target_pairs={{0,8},{8,0},{16,24},{24,16},{1,9},{9,1},{17,25},{25,17},{2,10},{10... | collective-permute-start | bytes 1032200 | tf_op jit(solution)/shard_map/ppermute | solution.py:445
  164.9 18.7 %collective-permute-start.47 = (bf16[192,896]{1,0:T(8,128)(2,1)S(1)}, bf16[192,896]{1,0:T(8,128)(2,1)S(1)}, u32[]{:S(2)}, u32[]{:S(2)}) collective-permute-start(bf16[192,896]{1,0:T(8,128)(2,1)S(1)} %get-tuple-element.278.refs_0_), channel_id=1, source_target_pairs={{0,24},{8,16},{16,8},{24,0},{1,25},{9,17},{17,9},{25,1},{2,26},{10... | collective-permute-start | bytes 1032200 | tf_op jit(solution)/shard_map/ppermute | solution.py:1216
  167.1 11.8 %collective-permute-start.44 = (bf16[96,1088]{1,0:T(8,128)(2,1)S(1)}, bf16[96,1088]{1,0:T(8,128)(2,1)S(1)}, u32[]{:S(2)}, u32[]{:S(2)}) collective-permute-start(bf16[96,1088]{1,0:T(8,128)(2,1)S(1)} %get-tuple-element.276), channel_id=1, source_target_pairs={{0,4},{2,6},{4,0},{6,2},{1,5},{3,7},{5,1},{7,3},{8,12},{10,14},{12... | collective-permute-start | bytes 626696 | tf_op jit(solution)/shard_map/ppermute | solution.py:459
  (31 other events, 207.6 us)

commit v7 on v6

--- a/solution.py
+++ b/solution.py
@@ -1117,7 +1117,7 @@
         for weight_ref, act_ref, slope_ref in zip((mine_ref, copy_ref), acts, slopes):
             act, slope = gelu_and_slope(dot_tn(weight_ref[:, :part], x_ref[...]))
             act_ref[:, cols] = act
-            slope_ref[:, cols] = slope
+            slope_ref[:, cols] = slope.astype(low)
             term = dot_nn(weight_ref[:, part:], act)
             total = term if total is None else total + term
         part_ref[...] = total.astype(part_ref.dtype)
@@ -1145,7 +1145,7 @@
             (mine_ref, slope_mine_ref, pre_mine_ref),
             (copy_ref, slope_copy_ref, pre_copy_ref),
         ):
-            grad_pre = (dot_tn(weight_ref[:, part:], x_ref[...]) * slope_ref[:, cols]).astype(low)
+            grad_pre = (dot_tn(weight_ref[:, part:], x_ref[...]) * slope_ref[:, cols].astype(wide)).astype(low)
             pre_ref[:, cols] = grad_pre
             term = dot_nn(weight_ref[:, :part], grad_pre)
             total = term if total is None else total + term
@@ -1168,7 +1168,7 @@
 
 
 def place_hidden_body(flags_ref, *refs):
-    down_ref, up_ref, out_ref, vec_ref = refs[4:]
+    down_ref, up_ref, out_ref = refs[4:7]
     part = up_ref.shape[1] // 4
     for place, ref in quarters(flags_ref, refs[:4]):
         cols = pl.ds(pl.multiple_of(place * part, 128), part)
@@ -1185,7 +1185,18 @@
     for parts, start in ((first, 0), (second, WIDTH)):
         out_ref[:, start : start + half] = parts[0]
         out_ref[:, start + half : start + WIDTH] = parts[1][:, : WIDTH - half]
-    vec_ref[...] = first[1][:, WIDTH - half :] + second[1][:, WIDTH - half :]
+    vecs = first[1][:, WIDTH - half :] + second[1][:, WIDTH - half :]
+    lines = lax.broadcasted_iota(jnp.int32, (8, SUM_LANES), 0)
+    lanes = lax.broadcasted_iota(jnp.int32, (8, SUM_LANES), 1)
+    picked = lax.dot_general(
+        (lines == lanes).astype(wide),
+        vecs,
+        (((1,), (1,)), ((), ())),
+        precision=highest,
+        preferred_element_type=wide,
+    )
+    for line, ref in enumerate(refs[7:]):
+        ref[...] = picked[line : line + 1]
 
 
 def place_last_body(flags_ref, *refs):
@@ -1425,7 +1436,7 @@
         norm_vecs,
     )
     first_other = swap_pair(first_low)
-    hidden_acts = [((part, 2 * SPAN), low)] * 2 + [((part, 2 * SPAN), wide)] * 2
+    hidden_acts = [((part, 2 * SPAN), low)] * 4
     act_mine, act_copy, slope_mine, slope_copy, ffn_own, ffn_other = local_call(
         hidden_body,
         hidden_acts + [block_wide, block_low],
@@ -1653,10 +1664,11 @@
         swap_rows(last_far, 2),
     )
     output = cols_back(*out_wide, low, "out_join")
-    down_t, up_grad, out_t, vec_total = local_call(
+    down_t, up_grad, out_t, *vec_sums_all = local_call(
         place_hidden_body,
         [((feat_rows, 4 * part), wide)] * 2
-        + [((feat_rows, 2 * WIDTH), wide), ((feat_rows, SUM_LANES), wide)],
+        + [((feat_rows, 2 * WIDTH), wide)]
+        + [((1, feat_rows), wide)] * 4,
         "place_hidden",
         flags,
         *all_quarters(hidden_sum, True),
@@ -1679,12 +1691,12 @@
         key_grad,
         value_grad,
         out_t.T,
-        vec_total[:, 0],
-        vec_total[:, 1],
+        vec_sums_all[0].reshape(feat_rows),
+        vec_sums_all[1].reshape(feat_rows),
         up_grad,
         down_t.T,
-        vec_total[:, 2],
-        vec_total[:, 3],
+        vec_sums_all[2].reshape(feat_rows),
+        vec_sums_all[3].reshape(feat_rows),
     )
 
 

time: 189 us -> 189 us (level)
    ppermute x12, waiting for transfers between devices: 41.6 us -> 45.9 us  [swap_rows(): return lax.ppermute(operand, 'row', [(i, i ^ mask) for i in range(4)])]
    ppermute x8, waiting for transfers between devices: 13.7 us -> 10.5 us  [swap_cols(): return lax.ppermute(operand, 'col', [(0, 1), (1, 0)])]
  transfers between devices with their start and end apart: 52 -> 52, of which waited for: 28 -> 25; matrix products, arithmetic and copies ran while one was open for 1% -> 0% of each run, Pallas kernels for 12% -> 12%
where the time goes in v7:
time: 189 us
  waiting for transfers between devices  88.5 us (47%)
  starting transfers between devices  65.1 us (34%)
  Pallas kernels  32.5 us (17%)
    ppermute x12, waiting for transfers between devices, swap_rows(): return lax.ppermute(operand, 'row', [(i, i ^ mask) for i in range(4)])  45.9 us
    pallas_call x35, Pallas kernels, local_call(): pl.pallas_call(body, out_shape=shapes, in_specs=[pl.BlockSpec(memory_spac...  32.5 us
    ppermute x12, starting transfers between devices, swap_rows(): return lax.ppermute(operand, 'row', [(i, i ^ mask) for i in range(4)])  17.5 us
    ppermute x11, waiting for transfers between devices, swap_copies(): lax.ppermute(operand, 'dp', [(i, i ^ 2) for i in range(lax.axis_size('dp'...  15.5 us
    ppermute x11, starting transfers between devices, swap_copies(): lax.ppermute(operand, 'dp', [(i, i ^ 2) for i in range(lax.axis_size('dp'...  13.7 us
    ppermute x6, starting transfers between devices, shift_rows(): return lax.ppermute(operand, 'row', pairs)  13 us
    ppermute x8, starting transfers between devices, swap_cols(): return lax.ppermute(operand, 'col', [(0, 1), (1, 0)])  13 us
    ppermute x10, waiting for transfers between devices, swap_pair(): lax.ppermute(operand, 'dp', [(i, i ^ 1) for i in range(lax.axis_size('dp'...  10.8 us
  transfers between devices with their start and end apart: 52, of which 25 were waited for; matrix products, arithmetic and copies ran while one was open for 0% of the time, Pallas kernels for 12%

profile of v7, /device:TPU:0, one launch (start us, length us, event | category | flops | bytes accessed | tf_op | source)
XLA Modules:
  0.0 189.1 jit_solution(18071797571121292270)
XLA Ops:
  1.9 3.0 %collective-permute-start.1 = (bf16[192,512]{1,0:T(8,128)(2,1)S(1)}, bf16[192,512]{1,0:T(8,128)(2,1)S(1)}, u32[]{:S(2)}, u32[]{:S(2)}) collective-permute-start(bf16[192,512]{1,0:T(8,128)(2,1)S(1)} %pad_maximum_fusion.1), channel_id=1, source_target_pairs={{0,1},{1,0},{2,3},{3,2},{4,5},{5,4},{6,7},{7,6},{8,9},{9,8},{10,11... | collective-permute-start | bytes 589832 | tf_op jit(solution)/shard_map/ppermute | solution.py:441
  7.0 2.6 %collective-permute-start.5 = (bf16[192,384]{1,0:T(8,128)(2,1)S(1)}, bf16[192,384]{1,0:T(8,128)(2,1)S(1)}, u32[]{:S(2)}, u32[]{:S(2)}) collective-permute-start(bf16[192,384]{1,0:T(8,128)(2,1)S(1)} %maximum_select_fusion), channel_id=1, source_target_pairs={{0,4},{2,6},{4,0},{6,2},{1,5},{3,7},{5,1},{7,3},{8,12},{10,14},{12... | collective-permute-start | bytes 442376 | tf_op jit(solution)/shard_map/ppermute | solution.py:459
  9.7 3.4 %collective-permute-done.refs_0_ = bf16[192,384]{1,0:T(8,128)(2,1)S(1)} collective-permute-done((bf16[192,384]{1,0:T(8,128)(2,1)S(1)}, bf16[192,384]{1,0:T(8,128)(2,1)S(1)}, u32[]{:S(2)}, u32[]{:S(2)}) %collective-permute-start) | collective-permute-done | bytes 147488 | tf_op jit(solution)/shard_map/ppermute | solution.py:459
  16.6 1.7 collective-permute-start.2
  19.2 2.9 %collective-permute-start.4 = (bf16[208,256]{1,0:T(8,128)(2,1)S(1)}, bf16[208,256]{1,0:T(8,128)(2,1)S(1)}, u32[]{:S(2)}, u32[]{:S(2)}) collective-permute-start(bf16[208,256]{1,0:T(8,128)(2,1)S(1)} %get-tuple-element.158), channel_id=1, source_target_pairs={{0,6},{2,0},{4,2},{6,4},{1,7},{3,1},{5,3},{7,5},{8,14},{10,8},{12,... | collective-permute-start | bytes 319496 | tf_op jit(solution)/shard_map/ppermute | solution.py:464
  23.1 2.4 %collective-permute-done.2.refs_1_ = bf16[208,256]{1,0:T(8,128)(2,1)S(1)} collective-permute-done((bf16[208,256]{1,0:T(8,128)(2,1)S(1)}, bf16[208,256]{1,0:T(8,128)(2,1)S(1)}, u32[]{:S(2)}, u32[]{:S(2)}) %collective-permute-start.2) | collective-permute-done | bytes 106528 | tf_op jit(solution)/shard_map/ppermute | solution.py:464
  30.2 2.3 %collective-permute-start.16 = (bf16[192,768]{1,0:T(8,128)(2,1)S(1)}, bf16[192,768]{1,0:T(8,128)(2,1)S(1)}, u32[]{:S(2)}, u32[]{:S(2)}) collective-permute-start(bf16[192,768]{1,0:T(8,128)(2,1)S(1)} %get-tuple-element.170.refs_0_), channel_id=1, source_target_pairs={{0,4},{2,6},{4,0},{6,2},{1,5},{3,7},{5,1},{7,3},{8,12},{10,14},{12... | collective-permute-start | bytes 884744 | tf_op jit(solution)/shard_map/ppermute | solution.py:459
  34.6 5.0 %collective-permute-done.9.refs_1_ = bf16[192,768]{1,0:T(8,128)(2,1)S(1)} collective-permute-done((bf16[192,768]{1,0:T(8,128)(2,1)S(1)}, bf16[192,768]{1,0:T(8,128)(2,1)S(1)}, u32[]{:S(2)}, u32[]{:S(2)}) %collective-permute-start.9) | collective-permute-done | bytes 294944 | tf_op jit(solution)/shard_map/ppermute | solution.py:459
  40.3 2.5 %collective-permute-done.16.refs_2_ = bf16[192,768]{1,0:T(8,128)(2,1)S(1)} collective-permute-done((bf16[192,768]{1,0:T(8,128)(2,1)S(1)}, bf16[192,768]{1,0:T(8,128)(2,1)S(1)}, u32[]{:S(2)}, u32[]{:S(2)}) %collective-permute-start.16) | collective-permute-done | bytes 294944 | tf_op jit(solution)/shard_map/ppermute | solution.py:459
  46.7 3.8 %collective-permute-start.13 = (bf16[400,128]{1,0:T(8,128)(2,1)S(1)}, bf16[400,128]{1,0:T(8,128)(2,1)S(1)}, u32[]{:S(2)}, u32[]{:S(2)}) collective-permute-start(bf16[400,128]{1,0:T(8,128)(2,1)S(1)} %get-tuple-element.188), channel_id=1, source_target_pairs={{0,2},{2,4},{4,6},{1,3},{3,5},{5,7},{8,10},{10,12},{12,14},{9,11},... | collective-permute-start | bytes 307208 | tf_op jit(solution)/shard_map/ppermute | solution.py:455
  50.5 2.7 %collective-permute-start.14 = (bf16[400,128]{1,0:T(8,128)(2,1)S(1)}, bf16[400,128]{1,0:T(8,128)(2,1)S(1)}, u32[]{:S(2)}, u32[]{:S(2)}) collective-permute-start(bf16[400,128]{1,0:T(8,128)(2,1)S(1)} %get-tuple-element.188), channel_id=1, source_target_pairs={{0,4},{2,6},{1,5},{3,7},{8,12},{10,14},{9,13},{11,15},{16,20},{18,... | collective-permute-start | bytes 307208 | tf_op jit(solution)/shard_map/ppermute | solution.py:455
  53.3 2.4 %collective-permute-start.15 = (bf16[400,128]{1,0:T(8,128)(2,1)S(1)}, bf16[400,128]{1,0:T(8,128)(2,1)S(1)}, u32[]{:S(2)}, u32[]{:S(2)}) collective-permute-start(bf16[400,128]{1,0:T(8,128)(2,1)S(1)} %get-tuple-element.188), channel_id=1, source_target_pairs={{0,6},{1,7},{8,14},{9,15},{16,22},{17,23},{24,30},{25,31}} | collective-permute-start | bytes 307208 | tf_op jit(solution)/shard_map/ppermute | solution.py:455
  58.4 1.7 collective-permute-done.20.recv_ref
  63.3 7.3 %collective-permute-done.22.refs_7_ = bf16[192,768]{1,0:T(8,128)(2,1)S(1)} collective-permute-done((bf16[192,768]{1,0:T(8,128)(2,1)S(1)}, bf16[192,768]{1,0:T(8,128)(2,1)S(1)}, u32[]{:S(2)}, u32[]{:S(2)}) %collective-permute-start.22) | collective-permute-done | bytes 294944 | tf_op jit(solution)/shard_map/ppermute | solution.py:449
  72.9 1.7 collective-permute-done.23.other_ref
  74.6 1.8 hidden.1
  79.9 9.6 %collective-permute-done.25.recv_ref = bf16[768,256]{1,0:T(8,128)(2,1)S(1)} collective-permute-done((bf16[768,256]{1,0:T(8,128)(2,1)S(1)}, bf16[768,256]{1,0:T(8,128)(2,1)S(1)}, u32[]{:S(2)}, u32[]{:S(2)}) %collective-permute-start.25) | collective-permute-done | bytes 393248 | tf_op jit(solution)/shard_map/ppermute | solution.py:441
  90.8 1.7 collective-permute-done.26.other_ref
  94.1 1.8 hidden_back.1
  101.9 9.8 %collective-permute-done.29.got_ref = bf16[384,768]{1,0:T(8,128)(2,1)S(1)} collective-permute-done((bf16[384,768]{1,0:T(8,128)(2,1)S(1)}, bf16[384,768]{1,0:T(8,128)(2,1)S(1)}, u32[]{:S(2)}, u32[]{:S(2)}) %collective-permute-start.29) | collective-permute-done | bytes 589856 | tf_op jit(solution)/shard_map/ppermute | solution.py:459
  112.8 1.7 collective-permute-done.30.other_ref
  123.6 6.1 %collective-permute-done.32.got_ref.mix_got_ref = bf16[384,640]{1,0:T(8,128)(2,1)S(1)} collective-permute-done((bf16[384,640]{1,0:T(8,128)(2,1)S(1)}, bf16[384,640]{1,0:T(8,128)(2,1)S(1)}, u32[]{:S(2)}, u32[]{:S(2)}) %collective-permute-start.32) | collective-permute-done | bytes 491552 | tf_op jit(solution)/shard_map/ppermute | solution.py:449
  132.4 2.3 %grad_project.1 = (bf16[4,96,576]{2,1,0:T(8,128)(2,1)S(1)}, bf16[4,96,576]{2,1,0:T(8,128)(2,1)S(1)}, f32[768,256]{1,0:T(8,128)S(1)}, bf16[768,256]{1,0:T(8,128)(2,1)S(1)}) custom-call(bf16[2,192,256]{2,1,0:T(8,128)(2,1)S(1)} %get-tuple-element.253.grad_query_ref, f32[6,64,256]{2,1,0:T(8,128)S(1)} %get-tuple-element.263.grad_key_ref, ...), custom_call_target="tpu_custom_call" | custom-call | tf_op jit(solution)/shard_map/grad_project/pallas_call | solution.py:497
  138.8 4.3 %collective-permute-done.37.got_ref = bf16[384,640]{1,0:T(8,128)(2,1)S(1)} collective-permute-done((bf16[384,640]{1,0:T(8,128)(2,1)S(1)}, bf16[384,640]{1,0:T(8,128)(2,1)S(1)}, u32[]{:S(2)}, u32[]{:S(2)}) %collective-permute-start.37) | collective-permute-done | bytes 491552 | tf_op jit(solution)/shard_map/ppermute | solution.py:459
  143.2 3.1 %collective-permute-start.38 = (bf16[192,768]{1,0:T(8,128)(2,1)S(1)}, bf16[192,768]{1,0:T(8,128)(2,1)S(1)}, u32[]{:S(2)}, u32[]{:S(2)}) collective-permute-start(bf16[192,768]{1,0:T(8,128)(2,1)S(1)} %get-tuple-element.260), channel_id=1, source_target_pairs={{0,4},{2,6},{4,0},{6,2},{1,5},{3,7},{5,1},{7,3},{8,12},{10,14},{12... | collective-permute-start | bytes 884744 | tf_op jit(solution)/shard_map/ppermute | solution.py:459
  146.4 2.1 %collective-permute-done.40.got_ref = bf16[4,96,576]{2,1,0:T(8,128)(2,1)S(1)} collective-permute-done((bf16[4,96,576]{2,1,0:T(8,128)(2,1)S(1)}, bf16[4,96,576]{2,1,0:T(8,128)(2,1)S(1)}, u32[]{:S(2)}, u32[]{:S(2)}) %collective-permute-start.40) | collective-permute-done | bytes 442400 | tf_op jit(solution)/shard_map/ppermute | solution.py:449
  149.7 3.0 %collective-permute-start.33 = (bf16[192,384]{1,0:T(8,128)(2,1)S(1)}, bf16[192,384]{1,0:T(8,128)(2,1)S(1)}, u32[]{:S(2)}, u32[]{:S(2)}) collective-permute-start(bf16[192,384]{1,0:T(8,128)(2,1)S(1)} %get-tuple-element.247), channel_id=1, source_target_pairs={{0,4},{2,6},{4,0},{6,2},{1,5},{3,7},{5,1},{7,3},{8,12},{10,14},{12... | collective-permute-start | bytes 442376 | tf_op jit(solution)/shard_map/ppermute | solution.py:459
  152.7 10.0 %collective-permute-done.33.down_far_ref = bf16[192,384]{1,0:T(8,128)(2,1)S(1)} collective-permute-done((bf16[192,384]{1,0:T(8,128)(2,1)S(1)}, bf16[192,384]{1,0:T(8,128)(2,1)S(1)}, u32[]{:S(2)}, u32[]{:S(2)}) %collective-permute-start.33) | collective-permute-done | bytes 147488 | tf_op jit(solution)/shard_map/ppermute | solution.py:459
  167.2 1.9 %collective-permute-start.44 = (bf16[96,1088]{1,0:T(8,128)(2,1)S(1)}, bf16[96,1088]{1,0:T(8,128)(2,1)S(1)}, u32[]{:S(2)}, u32[]{:S(2)}) collective-permute-start(bf16[96,1088]{1,0:T(8,128)(2,1)S(1)} %get-tuple-element.279), channel_id=1, source_target_pairs={{0,4},{2,6},{4,0},{6,2},{1,5},{3,7},{5,1},{7,3},{8,12},{10,14},{12... | collective-permute-start | bytes 626696 | tf_op jit(solution)/shard_map/ppermute | solution.py:459
  170.6 8.4 %collective-permute-done.44.far_ref = bf16[96,1088]{1,0:T(8,128)(2,1)S(1)} collective-permute-done((bf16[96,1088]{1,0:T(8,128)(2,1)S(1)}, bf16[96,1088]{1,0:T(8,128)(2,1)S(1)}, u32[]{:S(2)}, u32[]{:S(2)}) %collective-permute-start.44) | collective-permute-done | bytes 208928 | tf_op jit(solution)/shard_map/ppermute | solution.py:459
  184.9 2.4 %place_hidden.1 = (f32[192,1536]{1,0:T(8,128)}, f32[192,1536]{1,0:T(8,128)}, f32[192,384]{1,0:T(8,128)}, f32[1,192]{1,0:T(1,128)}, f32[1,192]{1,0:T(1,128)}, /*index=5*/f32[1,192]{1,0:T(1,128)}, f32[1,192]{1,0:T(1,128)}) custom-call(s32[5]{0:T(128)S(1)} %stack.38.flags_ref, bf16[192,896]{1,0:T(8,128)(2,1)S(1)} %get-tuple-element.281.refs_0_, ...), custom_call_target="tpu_custom_call" | custom-call | tf_op jit(solution)/shard_map/place_hidden/pallas_call | solution.py:497
  187.4 1.7 place_last.1
  (137 shorter events, 70.6 us)
Async XLA Ops:
  1.9 11.2 %collective-permute-start.1 = (bf16[192,512]{1,0:T(8,128)(2,1)S(1)}, bf16[192,512]{1,0:T(8,128)(2,1)S(1)}, u32[]{:S(2)}, u32[]{:S(2)}) collective-permute-start(bf16[192,512]{1,0:T(8,128)(2,1)S(1)} %pad_maximum_fusion.1), channel_id=1, source_target_pairs={{0,1},{1,0},{2,3},{3,2},{4,5},{5,4},{6,7},{7,6},{8,9},{9,8},{10,11... | collective-permute-start | bytes 589832 | tf_op jit(solution)/shard_map/ppermute | solution.py:441
  7.0 9.2 %collective-permute-start.5 = (bf16[192,384]{1,0:T(8,128)(2,1)S(1)}, bf16[192,384]{1,0:T(8,128)(2,1)S(1)}, u32[]{:S(2)}, u32[]{:S(2)}) collective-permute-start(bf16[192,384]{1,0:T(8,128)(2,1)S(1)} %maximum_select_fusion), channel_id=1, source_target_pairs={{0,4},{2,6},{4,0},{6,2},{1,5},{3,7},{5,1},{7,3},{8,12},{10,14},{12... | collective-permute-start | bytes 442376 | tf_op jit(solution)/shard_map/ppermute | solution.py:459
  13.8 13.1 %collective-permute-start.7 = (bf16[192,384]{1,0:T(8,128)(2,1)S(1)}, bf16[192,384]{1,0:T(8,128)(2,1)S(1)}, u32[]{:S(2)}, u32[]{:S(2)}) collective-permute-start(bf16[192,384]{1,0:T(8,128)(2,1)S(1)} %collective-permute-done.refs_0_), channel_id=1, source_target_pairs={{0,16},{8,24},{16,0},{24,8},{1,17},{9,25},{17,1},{25,9},{2,18},{10... | collective-permute-start | bytes 442376 | tf_op jit(solution)/shard_map/ppermute | solution.py:449
  16.3 10.6 %collective-permute-start.6 = (bf16[192,384]{1,0:T(8,128)(2,1)S(1)}, bf16[192,384]{1,0:T(8,128)(2,1)S(1)}, u32[]{:S(2)}, u32[]{:S(2)}) collective-permute-start(bf16[192,384]{1,0:T(8,128)(2,1)S(1)} %collective-permute-done.5.refs_1_), channel_id=1, source_target_pairs={{0,2},{2,0},{4,6},{6,4},{1,3},{3,1},{5,7},{7,5},{8,10},{10,8},{12,... | collective-permute-start | bytes 442376 | tf_op jit(solution)/shard_map/ppermute | solution.py:459
  16.6 8.9 %collective-permute-start.2 = (bf16[208,256]{1,0:T(8,128)(2,1)S(1)}, bf16[208,256]{1,0:T(8,128)(2,1)S(1)}, u32[]{:S(2)}, u32[]{:S(2)}) collective-permute-start(bf16[208,256]{1,0:T(8,128)(2,1)S(1)} %get-tuple-element.156), channel_id=1, source_target_pairs={{0,2},{2,4},{4,6},{6,0},{1,3},{3,5},{5,7},{7,1},{8,10},{10,12},{12... | collective-permute-start | bytes 319496 | tf_op jit(solution)/shard_map/ppermute | solution.py:464
  27.6 12.1 %collective-permute-start.8 = (bf16[768,256]{1,0:T(8,128)(2,1)S(1)}, bf16[768,256]{1,0:T(8,128)(2,1)S(1)}, u32[]{:S(2)}, u32[]{:S(2)}) collective-permute-start(bf16[768,256]{1,0:T(8,128)(2,1)S(1)} %get-tuple-element.169.half_ref), channel_id=1, source_target_pairs={{0,1},{1,0},{2,3},{3,2},{4,5},{5,4},{6,7},{7,6},{8,9},{9,8},{10,11... | collective-permute-start | bytes 1179656 | tf_op jit(solution)/shard_map/ppermute | solution.py:441
  28.8 10.8 %collective-permute-start.9 = (bf16[192,768]{1,0:T(8,128)(2,1)S(1)}, bf16[192,768]{1,0:T(8,128)(2,1)S(1)}, u32[]{:S(2)}, u32[]{:S(2)}) collective-permute-start(bf16[192,768]{1,0:T(8,128)(2,1)S(1)} %get-tuple-element.170.refs_0_), channel_id=1, source_target_pairs={{0,2},{2,0},{4,6},{6,4},{1,3},{3,1},{5,7},{7,5},{8,10},{10,8},{12,... | collective-permute-start | bytes 884744 | tf_op jit(solution)/shard_map/ppermute | solution.py:459
  30.2 12.6 %collective-permute-start.16 = (bf16[192,768]{1,0:T(8,128)(2,1)S(1)}, bf16[192,768]{1,0:T(8,128)(2,1)S(1)}, u32[]{:S(2)}, u32[]{:S(2)}) collective-permute-start(bf16[192,768]{1,0:T(8,128)(2,1)S(1)} %get-tuple-element.170.refs_0_), channel_id=1, source_target_pairs={{0,4},{2,6},{4,0},{6,2},{1,5},{3,7},{5,1},{7,3},{8,12},{10,14},{12... | collective-permute-start | bytes 884744 | tf_op jit(solution)/shard_map/ppermute | solution.py:459
  42.8 10.4 %collective-permute-start.17 = (bf16[192,768]{1,0:T(8,128)(2,1)S(1)}, bf16[192,768]{1,0:T(8,128)(2,1)S(1)}, u32[]{:S(2)}, u32[]{:S(2)}) collective-permute-start(bf16[192,768]{1,0:T(8,128)(2,1)S(1)} %collective-permute-done.16.refs_2_), channel_id=1, source_target_pairs={{0,2},{2,0},{4,6},{6,4},{1,3},{3,1},{5,7},{7,5},{8,10},{10,8},{12,... | collective-permute-start | bytes 884744 | tf_op jit(solution)/shard_map/ppermute | solution.py:459
  42.9 14.1 %collective-permute-start.18 = (bf16[192,768]{1,0:T(8,128)(2,1)S(1)}, bf16[192,768]{1,0:T(8,128)(2,1)S(1)}, u32[]{:S(2)}, u32[]{:S(2)}) collective-permute-start(bf16[192,768]{1,0:T(8,128)(2,1)S(1)} %collective-permute-done.16.refs_2_), channel_id=1, source_target_pairs={{0,16},{8,24},{16,0},{24,8},{1,17},{9,25},{17,1},{25,9},{2,18},{10... | collective-permute-start | bytes 884744 | tf_op jit(solution)/shard_map/ppermute | solution.py:449
  44.4 13.9 %collective-permute-start.19 = (bf16[192,768]{1,0:T(8,128)(2,1)S(1)}, bf16[192,768]{1,0:T(8,128)(2,1)S(1)}, u32[]{:S(2)}, u32[]{:S(2)}) collective-permute-start(bf16[192,768]{1,0:T(8,128)(2,1)S(1)} %collective-permute-done.9.refs_1_), channel_id=1, source_target_pairs={{0,16},{8,24},{16,0},{24,8},{1,17},{9,25},{17,1},{25,9},{2,18},{10... | collective-permute-start | bytes 884744 | tf_op jit(solution)/shard_map/ppermute | solution.py:449
  46.7 10.4 %collective-permute-start.13 = (bf16[400,128]{1,0:T(8,128)(2,1)S(1)}, bf16[400,128]{1,0:T(8,128)(2,1)S(1)}, u32[]{:S(2)}, u32[]{:S(2)}) collective-permute-start(bf16[400,128]{1,0:T(8,128)(2,1)S(1)} %get-tuple-element.188), channel_id=1, source_target_pairs={{0,2},{2,4},{4,6},{1,3},{3,5},{5,7},{8,10},{10,12},{12,14},{9,11},... | collective-permute-start | bytes 307208 | tf_op jit(solution)/shard_map/ppermute | solution.py:455
  60.2 11.2 %collective-permute-start.21 = (bf16[768,256]{1,0:T(8,128)(2,1)S(1)}, bf16[768,256]{1,0:T(8,128)(2,1)S(1)}, u32[]{:S(2)}, u32[]{:S(2)}) collective-permute-start(bf16[768,256]{1,0:T(8,128)(2,1)S(1)} %branch_half.1.half_ref), channel_id=1, source_target_pairs={{0,1},{1,0},{2,3},{3,2},{4,5},{5,4},{6,7},{7,6},{8,9},{9,8},{10,11... | collective-permute-start | bytes 1179656 | tf_op jit(solution)/shard_map/ppermute | solution.py:441
  78.3 11.2 %collective-permute-start.25 = (bf16[768,256]{1,0:T(8,128)(2,1)S(1)}, bf16[768,256]{1,0:T(8,128)(2,1)S(1)}, u32[]{:S(2)}, u32[]{:S(2)}) collective-permute-start(bf16[768,256]{1,0:T(8,128)(2,1)S(1)} %ffn_half.1.half_ref), channel_id=1, source_target_pairs={{0,1},{1,0},{2,3},{3,2},{4,5},{5,4},{6,7},{7,6},{8,9},{9,8},{10,11... | collective-permute-start | bytes 1179656 | tf_op jit(solution)/shard_map/ppermute | solution.py:441
  96.1 15.6 %collective-permute-start.29 = (bf16[384,768]{1,0:T(8,128)(2,1)S(1)}, bf16[384,768]{1,0:T(8,128)(2,1)S(1)}, u32[]{:S(2)}, u32[]{:S(2)}) collective-permute-start(bf16[384,768]{1,0:T(8,128)(2,1)S(1)} %get-tuple-element.229), channel_id=1, source_target_pairs={{0,2},{2,0},{4,6},{6,4},{1,3},{3,1},{5,7},{7,5},{8,10},{10,8},{12,... | collective-permute-start | bytes 1769480 | tf_op jit(solution)/shard_map/ppermute | solution.py:459
  97.8 14.1 %collective-permute-start.28 = (bf16[768,256]{1,0:T(8,128)(2,1)S(1)}, bf16[768,256]{1,0:T(8,128)(2,1)S(1)}, u32[]{:S(2)}, u32[]{:S(2)}) collective-permute-start(bf16[768,256]{1,0:T(8,128)(2,1)S(1)} %first_half.1.half_ref), channel_id=1, source_target_pairs={{0,1},{1,0},{2,3},{3,2},{4,5},{5,4},{6,7},{7,6},{8,9},{9,8},{10,11... | collective-permute-start | bytes 1179656 | tf_op jit(solution)/shard_map/ppermute | solution.py:441
  100.4 16.0 %collective-permute-start.31 = (bf16[768,384]{1,0:T(8,128)(2,1)S(1)}, bf16[768,384]{1,0:T(8,128)(2,1)S(1)}, u32[]{:S(2)}, u32[]{:S(2)}) collective-permute-start(bf16[768,384]{1,0:T(8,128)(2,1)S(1)} %get-tuple-element.243), channel_id=1, source_target_pairs={{0,16},{8,24},{16,0},{24,8},{1,17},{9,25},{17,1},{25,9},{2,18},{10... | collective-permute-start | bytes 1769480 | tf_op jit(solution)/shard_map/ppermute | solution.py:449
  116.4 13.3 %collective-permute-start.32 = (bf16[384,640]{1,0:T(8,128)(2,1)S(1)}, bf16[384,640]{1,0:T(8,128)(2,1)S(1)}, u32[]{:S(2)}, u32[]{:S(2)}) collective-permute-start(bf16[384,640]{1,0:T(8,128)(2,1)S(1)} %get-tuple-element.245), channel_id=1, source_target_pairs={{0,16},{8,24},{16,0},{24,8},{1,17},{9,25},{17,1},{25,9},{2,18},{10... | collective-permute-start | bytes 1474568 | tf_op jit(solution)/shard_map/ppermute | solution.py:449
  118.0 13.0 %collective-permute-start.34 = (bf16[400,128]{1,0:T(8,128)(2,1)S(1)}, bf16[400,128]{1,0:T(8,128)(2,1)S(1)}, u32[]{:S(2)}, u32[]{:S(2)}) collective-permute-start(bf16[400,128]{1,0:T(8,128)(2,1)S(1)} %get-tuple-element.248), channel_id=1, source_target_pairs={{2,0},{4,2},{6,4},{3,1},{5,3},{7,5},{10,8},{12,10},{14,12},{11,9},... | collective-permute-start | bytes 307208 | tf_op jit(solution)/shard_map/ppermute | solution.py:455
  119.2 13.1 %collective-permute-start.35 = (bf16[400,128]{1,0:T(8,128)(2,1)S(1)}, bf16[400,128]{1,0:T(8,128)(2,1)S(1)}, u32[]{:S(2)}, u32[]{:S(2)}) collective-permute-start(bf16[400,128]{1,0:T(8,128)(2,1)S(1)} %get-tuple-element.248), channel_id=1, source_target_pairs={{4,0},{6,2},{5,1},{7,3},{12,8},{14,10},{13,9},{15,11},{20,16},{22,... | collective-permute-start | bytes 307208 | tf_op jit(solution)/shard_map/ppermute | solution.py:455
  120.5 11.8 %collective-permute-start.36 = (bf16[400,128]{1,0:T(8,128)(2,1)S(1)}, bf16[400,128]{1,0:T(8,128)(2,1)S(1)}, u32[]{:S(2)}, u32[]{:S(2)}) collective-permute-start(bf16[400,128]{1,0:T(8,128)(2,1)S(1)} %get-tuple-element.248), channel_id=1, source_target_pairs={{6,0},{7,1},{14,8},{15,9},{22,16},{23,17},{30,24},{31,25}} | collective-permute-start | bytes 307208 | tf_op jit(solution)/shard_map/ppermute | solution.py:455
  130.6 12.5 %collective-permute-start.37 = (bf16[384,640]{1,0:T(8,128)(2,1)S(1)}, bf16[384,640]{1,0:T(8,128)(2,1)S(1)}, u32[]{:S(2)}, u32[]{:S(2)}) collective-permute-start(bf16[384,640]{1,0:T(8,128)(2,1)S(1)} %get-tuple-element.258), channel_id=1, source_target_pairs={{0,2},{2,0},{4,6},{6,4},{1,3},{3,1},{5,7},{7,5},{8,10},{10,8},{12,... | collective-permute-start | bytes 1474568 | tf_op jit(solution)/shard_map/ppermute | solution.py:459
  134.8 13.6 %collective-permute-start.40 = (bf16[4,96,576]{2,1,0:T(8,128)(2,1)S(1)}, bf16[4,96,576]{2,1,0:T(8,128)(2,1)S(1)}, u32[]{:S(2)}, u32[]{:S(2)}) collective-permute-start(bf16[4,96,576]{2,1,0:T(8,128)(2,1)S(1)} %get-tuple-element.269), channel_id=1, source_target_pairs={{0,16},{8,24},{16,0},{24,8},{1,17},{9,25},{17,1},{25,9},{2,18},{10... | collective-permute-start | bytes 1327112 | tf_op jit(solution)/shard_map/ppermute | solution.py:449
  137.2 11.2 %collective-permute-start.42 = (bf16[384,256]{1,0:T(8,128)(2,1)S(1)}, bf16[384,256]{1,0:T(8,128)(2,1)S(1)}, u32[]{:S(2)}, u32[]{:S(2)}) collective-permute-start(bf16[384,256]{1,0:T(8,128)(2,1)S(1)} %get-tuple-element.274), channel_id=1, source_target_pairs={{0,1},{1,0},{2,3},{3,2},{4,5},{5,4},{6,7},{7,6},{8,9},{9,8},{10,11... | collective-permute-start | bytes 589832 | tf_op jit(solution)/shard_map/ppermute | solution.py:441
  143.2 19.4 %collective-permute-start.38 = (bf16[192,768]{1,0:T(8,128)(2,1)S(1)}, bf16[192,768]{1,0:T(8,128)(2,1)S(1)}, u32[]{:S(2)}, u32[]{:S(2)}) collective-permute-start(bf16[192,768]{1,0:T(8,128)(2,1)S(1)} %get-tuple-element.260), channel_id=1, source_target_pairs={{0,4},{2,6},{4,0},{6,2},{1,5},{3,7},{5,1},{7,3},{8,12},{10,14},{12... | collective-permute-start | bytes 884744 | tf_op jit(solution)/shard_map/ppermute | solution.py:459
  149.2 17.9 %collective-permute-start.43 = (bf16[192,832]{1,0:T(8,128)(2,1)S(1)}, bf16[192,832]{1,0:T(8,128)(2,1)S(1)}, u32[]{:S(2)}, u32[]{:S(2)}) collective-permute-start(bf16[192,832]{1,0:T(8,128)(2,1)S(1)} %get-tuple-element.277), channel_id=1, source_target_pairs={{0,2},{2,0},{4,6},{6,4},{1,3},{3,1},{5,7},{7,5},{8,10},{10,8},{12,... | collective-permute-start | bytes 958472 | tf_op jit(solution)/shard_map/ppermute | solution.py:459
  149.7 13.0 %collective-permute-start.33 = (bf16[192,384]{1,0:T(8,128)(2,1)S(1)}, bf16[192,384]{1,0:T(8,128)(2,1)S(1)}, u32[]{:S(2)}, u32[]{:S(2)}) collective-permute-start(bf16[192,384]{1,0:T(8,128)(2,1)S(1)} %get-tuple-element.247), channel_id=1, source_target_pairs={{0,4},{2,6},{4,0},{6,2},{1,5},{3,7},{5,1},{7,3},{8,12},{10,14},{12... | collective-permute-start | bytes 442376 | tf_op jit(solution)/shard_map/ppermute | solution.py:459
  163.3 18.0 %collective-permute-start.45 = (bf16[192,896]{1,0:T(8,128)(2,1)S(1)}, bf16[192,896]{1,0:T(8,128)(2,1)S(1)}, u32[]{:S(2)}, u32[]{:S(2)}) collective-permute-start(bf16[192,896]{1,0:T(8,128)(2,1)S(1)} %get-tuple-element.281.refs_0_), channel_id=1, source_target_pairs={{0,16},{8,24},{16,0},{24,8},{1,17},{9,25},{17,1},{25,9},{2,18},{10... | collective-permute-start | bytes 1032200 | tf_op jit(solution)/shard_map/ppermute | solution.py:449
  164.9 17.3 %collective-permute-start.46 = (bf16[192,896]{1,0:T(8,128)(2,1)S(1)}, bf16[192,896]{1,0:T(8,128)(2,1)S(1)}, u32[]{:S(2)}, u32[]{:S(2)}) collective-permute-start(bf16[192,896]{1,0:T(8,128)(2,1)S(1)} %get-tuple-element.281.refs_0_), channel_id=1, source_target_pairs={{0,8},{8,0},{16,24},{24,16},{1,9},{9,1},{17,25},{25,17},{2,10},{10... | collective-permute-start | bytes 1032200 | tf_op jit(solution)/shard_map/ppermute | solution.py:445
  164.9 20.0 %collective-permute-start.47 = (bf16[192,896]{1,0:T(8,128)(2,1)S(1)}, bf16[192,896]{1,0:T(8,128)(2,1)S(1)}, u32[]{:S(2)}, u32[]{:S(2)}) collective-permute-start(bf16[192,896]{1,0:T(8,128)(2,1)S(1)} %get-tuple-element.281.refs_0_), channel_id=1, source_target_pairs={{0,24},{8,16},{16,8},{24,0},{1,25},{9,17},{17,9},{25,1},{2,26},{10... | collective-permute-start | bytes 1032200 | tf_op jit(solution)/shard_map/ppermute | solution.py:1227
  167.2 11.8 %collective-permute-start.44 = (bf16[96,1088]{1,0:T(8,128)(2,1)S(1)}, bf16[96,1088]{1,0:T(8,128)(2,1)S(1)}, u32[]{:S(2)}, u32[]{:S(2)}) collective-permute-start(bf16[96,1088]{1,0:T(8,128)(2,1)S(1)} %get-tuple-element.279), channel_id=1, source_target_pairs={{0,4},{2,6},{4,0},{6,2},{1,5},{3,7},{5,1},{7,3},{8,12},{10,14},{12... | collective-permute-start | bytes 626696 | tf_op jit(solution)/shard_map/ppermute | solution.py:459
  169.1 12.2 %collective-permute-start.39 = (bf16[96,512]{1,0:T(8,128)(2,1)S(1)}, bf16[96,512]{1,0:T(8,128)(2,1)S(1)}, u32[]{:S(2)}, u32[]{:S(2)}) collective-permute-start(bf16[96,512]{1,0:T(8,128)(2,1)S(1)} %get-tuple-element.262), channel_id=1, source_target_pairs={{0,1},{1,0},{2,3},{3,2},{4,5},{5,4},{6,7},{7,6},{8,9},{9,8},{10,11... | collective-permute-start | bytes 294920 | tf_op jit(solution)/shard_map/ppermute | solution.py:441
  (31 other events, 213.5 us)

commit v8 on v6

--- a/solution.py
+++ b/solution.py
@@ -1335,7 +1335,9 @@
         flags,
         *token_pieces,
     )
-    x_half, trig, reweight = lax.optimization_barrier((x_half, trig, reweight))
+    x_half, trig, reweight, hidden_packed = lax.optimization_barrier(
+        (x_half, trig, reweight, hidden_packed)
+    )
     hidden_one, hidden_two = row_blocks(hidden_packed[0])
     x_got, hidden_one = lax.optimization_barrier((swap_cols(x_half), hidden_one))
     x_own, cot = local_call(
@@ -1588,7 +1590,6 @@
         scratch=[state_shape, ((2, 3 * WIDTH, SPAN), low)],
     )
     got_w = swap_copies(sent_w)
-    got_w = after(got_w, down_part)
     got_x = swap_pair(x_grad_other)
     x_half_grad, x_half_sent = local_call(
         partial(input_halves_body, rows=rows),
@@ -1617,7 +1618,7 @@
         [((feat_rows, up_lanes - SPAN // 2), wide), ((feat_rows, up_lanes + SPAN // 2), low)],
         "up_pairs",
         up_held,
-        up_got,
+        after(up_got, kept_w),
     )
     up_far = swap_rows(up_far, 2)
     last_got = swap_rows(last_sent, 1)

time: 189 us -> 188 us (level)
  transfers between devices with their start and end apart: 52 -> 52, of which waited for: 28 -> 27; matrix products, arithmetic and copies ran while one was open for 1% -> 1% of each run, Pallas kernels for 12% -> 12%
where the time goes in v8:
time: 188 us
  waiting for transfers between devices  86.6 us (46%)
  starting transfers between devices  64.9 us (35%)
  Pallas kernels  32.2 us (17%)
    ppermute x12, waiting for transfers between devices, swap_rows(): return lax.ppermute(operand, 'row', [(i, i ^ mask) for i in range(4)])  41.4 us
    pallas_call x35, Pallas kernels, local_call(): pl.pallas_call(body, out_shape=shapes, in_specs=[pl.BlockSpec(memory_spac...  32.2 us
    ppermute x12, starting transfers between devices, swap_rows(): return lax.ppermute(operand, 'row', [(i, i ^ mask) for i in range(4)])  17.6 us
    ppermute x11, waiting for transfers between devices, swap_copies(): lax.ppermute(operand, 'dp', [(i, i ^ 2) for i in range(lax.axis_size('dp'...  15.6 us
    ppermute x11, starting transfers between devices, swap_copies(): lax.ppermute(operand, 'dp', [(i, i ^ 2) for i in range(lax.axis_size('dp'...  13.7 us
    ppermute x8, waiting for transfers between devices, swap_cols(): return lax.ppermute(operand, 'col', [(0, 1), (1, 0)])  13.7 us
    ppermute x8, starting transfers between devices, swap_cols(): return lax.ppermute(operand, 'col', [(0, 1), (1, 0)])  12.9 us
    ppermute x6, starting transfers between devices, shift_rows(): return lax.ppermute(operand, 'row', pairs)  12.9 us
  transfers between devices with their start and end apart: 52, of which 27 were waited for; matrix products, arithmetic and copies ran while one was open for 1% of the time, Pallas kernels for 12%

profile of v8, /device:TPU:0, one launch (start us, length us, event | category | flops | bytes accessed | tf_op | source)
XLA Modules:
  0.0 187.7 jit_solution(4144055229569616431)
XLA Ops:
  1.9 3.0 %collective-permute-start.1 = (bf16[192,512]{1,0:T(8,128)(2,1)S(1)}, bf16[192,512]{1,0:T(8,128)(2,1)S(1)}, u32[]{:S(2)}, u32[]{:S(2)}) collective-permute-start(bf16[192,512]{1,0:T(8,128)(2,1)S(1)} %pad_maximum_fusion.1), channel_id=1, source_target_pairs={{0,1},{1,0},{2,3},{3,2},{4,5},{5,4},{6,7},{7,6},{8,9},{9,8},{10,11... | collective-permute-start | bytes 589832 | tf_op jit(solution)/shard_map/ppermute | solution.py:441
  7.0 2.6 %collective-permute-start.5 = (bf16[192,384]{1,0:T(8,128)(2,1)S(1)}, bf16[192,384]{1,0:T(8,128)(2,1)S(1)}, u32[]{:S(2)}, u32[]{:S(2)}) collective-permute-start(bf16[192,384]{1,0:T(8,128)(2,1)S(1)} %maximum_select_fusion), channel_id=1, source_target_pairs={{0,4},{2,6},{4,0},{6,2},{1,5},{3,7},{5,1},{7,3},{8,12},{10,14},{12... | collective-permute-start | bytes 442376 | tf_op jit(solution)/shard_map/ppermute | solution.py:459
  9.7 3.4 %collective-permute-done.refs_0_ = bf16[192,384]{1,0:T(8,128)(2,1)S(1)} collective-permute-done((bf16[192,384]{1,0:T(8,128)(2,1)S(1)}, bf16[192,384]{1,0:T(8,128)(2,1)S(1)}, u32[]{:S(2)}, u32[]{:S(2)}) %collective-permute-start) | collective-permute-done | bytes 147488 | tf_op jit(solution)/shard_map/ppermute | solution.py:459
  19.2 2.9 %collective-permute-start.4 = (bf16[208,256]{1,0:T(8,128)(2,1)S(1)}, bf16[208,256]{1,0:T(8,128)(2,1)S(1)}, u32[]{:S(2)}, u32[]{:S(2)}) collective-permute-start(bf16[208,256]{1,0:T(8,128)(2,1)S(1)} %get-tuple-element.157), channel_id=1, source_target_pairs={{0,6},{2,0},{4,2},{6,4},{1,7},{3,1},{5,3},{7,5},{8,14},{10,8},{12,... | collective-permute-start | bytes 319496 | tf_op jit(solution)/shard_map/ppermute | solution.py:464
  23.8 1.7 collective-permute-done.2.refs_1_
  29.5 2.3 %collective-permute-start.16 = (bf16[192,768]{1,0:T(8,128)(2,1)S(1)}, bf16[192,768]{1,0:T(8,128)(2,1)S(1)}, u32[]{:S(2)}, u32[]{:S(2)}) collective-permute-start(bf16[192,768]{1,0:T(8,128)(2,1)S(1)} %get-tuple-element.171.refs_0_), channel_id=1, source_target_pairs={{0,4},{2,6},{4,0},{6,2},{1,5},{3,7},{5,1},{7,3},{8,12},{10,14},{12... | collective-permute-start | bytes 884744 | tf_op jit(solution)/shard_map/ppermute | solution.py:459
  33.9 5.1 %collective-permute-done.9.refs_1_ = bf16[192,768]{1,0:T(8,128)(2,1)S(1)} collective-permute-done((bf16[192,768]{1,0:T(8,128)(2,1)S(1)}, bf16[192,768]{1,0:T(8,128)(2,1)S(1)}, u32[]{:S(2)}, u32[]{:S(2)}) %collective-permute-start.9) | collective-permute-done | bytes 294944 | tf_op jit(solution)/shard_map/ppermute | solution.py:459
  39.8 2.3 %collective-permute-done.16.refs_2_ = bf16[192,768]{1,0:T(8,128)(2,1)S(1)} collective-permute-done((bf16[192,768]{1,0:T(8,128)(2,1)S(1)}, bf16[192,768]{1,0:T(8,128)(2,1)S(1)}, u32[]{:S(2)}, u32[]{:S(2)}) %collective-permute-start.16) | collective-permute-done | bytes 294944 | tf_op jit(solution)/shard_map/ppermute | solution.py:459
  46.0 3.8 %collective-permute-start.13 = (bf16[400,128]{1,0:T(8,128)(2,1)S(1)}, bf16[400,128]{1,0:T(8,128)(2,1)S(1)}, u32[]{:S(2)}, u32[]{:S(2)}) collective-permute-start(bf16[400,128]{1,0:T(8,128)(2,1)S(1)} %get-tuple-element.189), channel_id=1, source_target_pairs={{0,2},{2,4},{4,6},{1,3},{3,5},{5,7},{8,10},{10,12},{12,14},{9,11},... | collective-permute-start | bytes 307208 | tf_op jit(solution)/shard_map/ppermute | solution.py:455
  49.8 2.7 %collective-permute-start.14 = (bf16[400,128]{1,0:T(8,128)(2,1)S(1)}, bf16[400,128]{1,0:T(8,128)(2,1)S(1)}, u32[]{:S(2)}, u32[]{:S(2)}) collective-permute-start(bf16[400,128]{1,0:T(8,128)(2,1)S(1)} %get-tuple-element.189), channel_id=1, source_target_pairs={{0,4},{2,6},{1,5},{3,7},{8,12},{10,14},{9,13},{11,15},{16,20},{18,... | collective-permute-start | bytes 307208 | tf_op jit(solution)/shard_map/ppermute | solution.py:455
  52.5 2.4 %collective-permute-start.15 = (bf16[400,128]{1,0:T(8,128)(2,1)S(1)}, bf16[400,128]{1,0:T(8,128)(2,1)S(1)}, u32[]{:S(2)}, u32[]{:S(2)}) collective-permute-start(bf16[400,128]{1,0:T(8,128)(2,1)S(1)} %get-tuple-element.189), channel_id=1, source_target_pairs={{0,6},{1,7},{8,14},{9,15},{16,22},{17,23},{24,30},{25,31}} | collective-permute-start | bytes 307208 | tf_op jit(solution)/shard_map/ppermute | solution.py:455
  57.6 1.7 collective-permute-done.20.recv_ref
  62.4 7.3 %collective-permute-done.22.refs_7_ = bf16[192,768]{1,0:T(8,128)(2,1)S(1)} collective-permute-done((bf16[192,768]{1,0:T(8,128)(2,1)S(1)}, bf16[192,768]{1,0:T(8,128)(2,1)S(1)}, u32[]{:S(2)}, u32[]{:S(2)}) %collective-permute-start.22) | collective-permute-done | bytes 294944 | tf_op jit(solution)/shard_map/ppermute | solution.py:449
  72.0 1.7 collective-permute-done.23.other_ref
  73.7 1.8 hidden.1
  79.0 9.6 %collective-permute-done.25.recv_ref = bf16[768,256]{1,0:T(8,128)(2,1)S(1)} collective-permute-done((bf16[768,256]{1,0:T(8,128)(2,1)S(1)}, bf16[768,256]{1,0:T(8,128)(2,1)S(1)}, u32[]{:S(2)}, u32[]{:S(2)}) %collective-permute-start.25) | collective-permute-done | bytes 393248 | tf_op jit(solution)/shard_map/ppermute | solution.py:441
  90.0 1.7 collective-permute-done.26.other_ref
  93.3 1.8 hidden_back.1
  101.1 9.8 %collective-permute-done.29.got_ref = bf16[384,768]{1,0:T(8,128)(2,1)S(1)} collective-permute-done((bf16[384,768]{1,0:T(8,128)(2,1)S(1)}, bf16[384,768]{1,0:T(8,128)(2,1)S(1)}, u32[]{:S(2)}, u32[]{:S(2)}) %collective-permute-start.29) | collective-permute-done | bytes 589856 | tf_op jit(solution)/shard_map/ppermute | solution.py:459
  111.9 1.7 collective-permute-done.30.other_ref
  122.7 6.1 %collective-permute-done.32.got_ref.mix_got_ref = bf16[384,640]{1,0:T(8,128)(2,1)S(1)} collective-permute-done((bf16[384,640]{1,0:T(8,128)(2,1)S(1)}, bf16[384,640]{1,0:T(8,128)(2,1)S(1)}, u32[]{:S(2)}, u32[]{:S(2)}) %collective-permute-start.32) | collective-permute-done | bytes 491552 | tf_op jit(solution)/shard_map/ppermute | solution.py:449
  131.5 2.3 %grad_project.1 = (bf16[4,96,576]{2,1,0:T(8,128)(2,1)S(1)}, bf16[4,96,576]{2,1,0:T(8,128)(2,1)S(1)}, f32[768,256]{1,0:T(8,128)S(1)}, bf16[768,256]{1,0:T(8,128)(2,1)S(1)}) custom-call(bf16[2,192,256]{2,1,0:T(8,128)(2,1)S(1)} %get-tuple-element.254.grad_query_ref, f32[6,64,256]{2,1,0:T(8,128)S(1)} %get-tuple-element.260.grad_key_ref, ...), custom_call_target="tpu_custom_call" | custom-call | tf_op jit(solution)/shard_map/grad_project/pallas_call | solution.py:497
  137.9 4.3 %collective-permute-done.37.got_ref = bf16[384,640]{1,0:T(8,128)(2,1)S(1)} collective-permute-done((bf16[384,640]{1,0:T(8,128)(2,1)S(1)}, bf16[384,640]{1,0:T(8,128)(2,1)S(1)}, u32[]{:S(2)}, u32[]{:S(2)}) %collective-permute-start.37) | collective-permute-done | bytes 491552 | tf_op jit(solution)/shard_map/ppermute | solution.py:459
  142.3 3.1 %collective-permute-start.38 = (bf16[192,768]{1,0:T(8,128)(2,1)S(1)}, bf16[192,768]{1,0:T(8,128)(2,1)S(1)}, u32[]{:S(2)}, u32[]{:S(2)}) collective-permute-start(bf16[192,768]{1,0:T(8,128)(2,1)S(1)} %get-tuple-element.268), channel_id=1, source_target_pairs={{0,4},{2,6},{4,0},{6,2},{1,5},{3,7},{5,1},{7,3},{8,12},{10,14},{12... | collective-permute-start | bytes 884744 | tf_op jit(solution)/shard_map/ppermute | solution.py:459
  145.4 2.1 %collective-permute-done.40.got_ref = bf16[4,96,576]{2,1,0:T(8,128)(2,1)S(1)} collective-permute-done((bf16[4,96,576]{2,1,0:T(8,128)(2,1)S(1)}, bf16[4,96,576]{2,1,0:T(8,128)(2,1)S(1)}, u32[]{:S(2)}, u32[]{:S(2)}) %collective-permute-start.40) | collective-permute-done | bytes 442400 | tf_op jit(solution)/shard_map/ppermute | solution.py:449
  148.8 3.1 %collective-permute-start.33 = (bf16[192,384]{1,0:T(8,128)(2,1)S(1)}, bf16[192,384]{1,0:T(8,128)(2,1)S(1)}, u32[]{:S(2)}, u32[]{:S(2)}) collective-permute-start(bf16[192,384]{1,0:T(8,128)(2,1)S(1)} %get-tuple-element.248), channel_id=1, source_target_pairs={{0,4},{2,6},{4,0},{6,2},{1,5},{3,7},{5,1},{7,3},{8,12},{10,14},{12... | collective-permute-start | bytes 442376 | tf_op jit(solution)/shard_map/ppermute | solution.py:459
  151.9 9.9 %collective-permute-done.33.down_far_ref = bf16[192,384]{1,0:T(8,128)(2,1)S(1)} collective-permute-done((bf16[192,384]{1,0:T(8,128)(2,1)S(1)}, bf16[192,384]{1,0:T(8,128)(2,1)S(1)}, u32[]{:S(2)}, u32[]{:S(2)}) %collective-permute-start.33) | collective-permute-done | bytes 147488 | tf_op jit(solution)/shard_map/ppermute | solution.py:459
  166.3 1.9 %collective-permute-start.44 = (bf16[96,1088]{1,0:T(8,128)(2,1)S(1)}, bf16[96,1088]{1,0:T(8,128)(2,1)S(1)}, u32[]{:S(2)}, u32[]{:S(2)}) collective-permute-start(bf16[96,1088]{1,0:T(8,128)(2,1)S(1)} %get-tuple-element.280), channel_id=1, source_target_pairs={{0,4},{2,6},{4,0},{6,2},{1,5},{3,7},{5,1},{7,3},{8,12},{10,14},{12... | collective-permute-start | bytes 626696 | tf_op jit(solution)/shard_map/ppermute | solution.py:459
  169.7 3.1 %collective-permute-done.39.recv_ref = bf16[96,512]{1,0:T(8,128)(2,1)S(1)} collective-permute-done((bf16[96,512]{1,0:T(8,128)(2,1)S(1)}, bf16[96,512]{1,0:T(8,128)(2,1)S(1)}, u32[]{:S(2)}, u32[]{:S(2)}) %collective-permute-start.39) | collective-permute-done | bytes 98336 | tf_op jit(solution)/shard_map/ppermute | solution.py:441
  174.0 4.0 %collective-permute-done.44.far_ref = bf16[96,1088]{1,0:T(8,128)(2,1)S(1)} collective-permute-done((bf16[96,1088]{1,0:T(8,128)(2,1)S(1)}, bf16[96,1088]{1,0:T(8,128)(2,1)S(1)}, u32[]{:S(2)}, u32[]{:S(2)}) %collective-permute-start.44) | collective-permute-done | bytes 208928 | tf_op jit(solution)/shard_map/ppermute | solution.py:459
  182.8 2.2 %place_hidden.1 = (f32[192,1536]{1,0:T(8,128)}, f32[192,1536]{1,0:T(8,128)}, f32[192,384]{1,0:T(8,128)}, f32[192,64]{1,0:T(8,128)S(1)}) custom-call(s32[5]{0:T(128)S(1)} %stack.38.flags_ref, bf16[192,896]{1,0:T(8,128)(2,1)S(1)} %get-tuple-element.282.refs_0_, bf16[192,896]{1,0:T(8,128)(2,1)S(1)} %collective-permute-done.45.refs_1_, ...), custom_call_target="tpu_custom_call" | custom-call | tf_op jit(solution)/shard_map/place_hidden/pallas_call | solution.py:497
  186.0 1.7 place_last.1
  (138 shorter events, 73.1 us)
Async XLA Ops:
  1.9 11.2 %collective-permute-start.1 = (bf16[192,512]{1,0:T(8,128)(2,1)S(1)}, bf16[192,512]{1,0:T(8,128)(2,1)S(1)}, u32[]{:S(2)}, u32[]{:S(2)}) collective-permute-start(bf16[192,512]{1,0:T(8,128)(2,1)S(1)} %pad_maximum_fusion.1), channel_id=1, source_target_pairs={{0,1},{1,0},{2,3},{3,2},{4,5},{5,4},{6,7},{7,6},{8,9},{9,8},{10,11... | collective-permute-start | bytes 589832 | tf_op jit(solution)/shard_map/ppermute | solution.py:441
  7.0 9.2 %collective-permute-start.5 = (bf16[192,384]{1,0:T(8,128)(2,1)S(1)}, bf16[192,384]{1,0:T(8,128)(2,1)S(1)}, u32[]{:S(2)}, u32[]{:S(2)}) collective-permute-start(bf16[192,384]{1,0:T(8,128)(2,1)S(1)} %maximum_select_fusion), channel_id=1, source_target_pairs={{0,4},{2,6},{4,0},{6,2},{1,5},{3,7},{5,1},{7,3},{8,12},{10,14},{12... | collective-permute-start | bytes 442376 | tf_op jit(solution)/shard_map/ppermute | solution.py:459
  13.8 13.1 %collective-permute-start.7 = (bf16[192,384]{1,0:T(8,128)(2,1)S(1)}, bf16[192,384]{1,0:T(8,128)(2,1)S(1)}, u32[]{:S(2)}, u32[]{:S(2)}) collective-permute-start(bf16[192,384]{1,0:T(8,128)(2,1)S(1)} %collective-permute-done.refs_0_), channel_id=1, source_target_pairs={{0,16},{8,24},{16,0},{24,8},{1,17},{9,25},{17,1},{25,9},{2,18},{10... | collective-permute-start | bytes 442376 | tf_op jit(solution)/shard_map/ppermute | solution.py:449
  16.3 10.6 %collective-permute-start.6 = (bf16[192,384]{1,0:T(8,128)(2,1)S(1)}, bf16[192,384]{1,0:T(8,128)(2,1)S(1)}, u32[]{:S(2)}, u32[]{:S(2)}) collective-permute-start(bf16[192,384]{1,0:T(8,128)(2,1)S(1)} %collective-permute-done.5.refs_1_), channel_id=1, source_target_pairs={{0,2},{2,0},{4,6},{6,4},{1,3},{3,1},{5,7},{7,5},{8,10},{10,8},{12,... | collective-permute-start | bytes 442376 | tf_op jit(solution)/shard_map/ppermute | solution.py:459
  16.6 8.9 %collective-permute-start.2 = (bf16[208,256]{1,0:T(8,128)(2,1)S(1)}, bf16[208,256]{1,0:T(8,128)(2,1)S(1)}, u32[]{:S(2)}, u32[]{:S(2)}) collective-permute-start(bf16[208,256]{1,0:T(8,128)(2,1)S(1)} %get-tuple-element.155), channel_id=1, source_target_pairs={{0,2},{2,4},{4,6},{6,0},{1,3},{3,5},{5,7},{7,1},{8,10},{10,12},{12... | collective-permute-start | bytes 319496 | tf_op jit(solution)/shard_map/ppermute | solution.py:464
  27.6 11.4 %collective-permute-start.8 = (bf16[768,256]{1,0:T(8,128)(2,1)S(1)}, bf16[768,256]{1,0:T(8,128)(2,1)S(1)}, u32[]{:S(2)}, u32[]{:S(2)}) collective-permute-start(bf16[768,256]{1,0:T(8,128)(2,1)S(1)} %get-tuple-element.170.half_ref), channel_id=1, source_target_pairs={{0,1},{1,0},{2,3},{3,2},{4,5},{5,4},{6,7},{7,6},{8,9},{9,8},{10,11... | collective-permute-start | bytes 1179656 | tf_op jit(solution)/shard_map/ppermute | solution.py:441
  28.1 10.9 %collective-permute-start.9 = (bf16[192,768]{1,0:T(8,128)(2,1)S(1)}, bf16[192,768]{1,0:T(8,128)(2,1)S(1)}, u32[]{:S(2)}, u32[]{:S(2)}) collective-permute-start(bf16[192,768]{1,0:T(8,128)(2,1)S(1)} %get-tuple-element.171.refs_0_), channel_id=1, source_target_pairs={{0,2},{2,0},{4,6},{6,4},{1,3},{3,1},{5,7},{7,5},{8,10},{10,8},{12,... | collective-permute-start | bytes 884744 | tf_op jit(solution)/shard_map/ppermute | solution.py:459
  29.5 12.6 %collective-permute-start.16 = (bf16[192,768]{1,0:T(8,128)(2,1)S(1)}, bf16[192,768]{1,0:T(8,128)(2,1)S(1)}, u32[]{:S(2)}, u32[]{:S(2)}) collective-permute-start(bf16[192,768]{1,0:T(8,128)(2,1)S(1)} %get-tuple-element.171.refs_0_), channel_id=1, source_target_pairs={{0,4},{2,6},{4,0},{6,2},{1,5},{3,7},{5,1},{7,3},{8,12},{10,14},{12... | collective-permute-start | bytes 884744 | tf_op jit(solution)/shard_map/ppermute | solution.py:459
  42.1 10.4 %collective-permute-start.17 = (bf16[192,768]{1,0:T(8,128)(2,1)S(1)}, bf16[192,768]{1,0:T(8,128)(2,1)S(1)}, u32[]{:S(2)}, u32[]{:S(2)}) collective-permute-start(bf16[192,768]{1,0:T(8,128)(2,1)S(1)} %collective-permute-done.16.refs_2_), channel_id=1, source_target_pairs={{0,2},{2,0},{4,6},{6,4},{1,3},{3,1},{5,7},{7,5},{8,10},{10,8},{12,... | collective-permute-start | bytes 884744 | tf_op jit(solution)/shard_map/ppermute | solution.py:459
  42.2 14.0 %collective-permute-start.18 = (bf16[192,768]{1,0:T(8,128)(2,1)S(1)}, bf16[192,768]{1,0:T(8,128)(2,1)S(1)}, u32[]{:S(2)}, u32[]{:S(2)}) collective-permute-start(bf16[192,768]{1,0:T(8,128)(2,1)S(1)} %collective-permute-done.16.refs_2_), channel_id=1, source_target_pairs={{0,16},{8,24},{16,0},{24,8},{1,17},{9,25},{17,1},{25,9},{2,18},{10... | collective-permute-start | bytes 884744 | tf_op jit(solution)/shard_map/ppermute | solution.py:449
  43.7 13.8 %collective-permute-start.19 = (bf16[192,768]{1,0:T(8,128)(2,1)S(1)}, bf16[192,768]{1,0:T(8,128)(2,1)S(1)}, u32[]{:S(2)}, u32[]{:S(2)}) collective-permute-start(bf16[192,768]{1,0:T(8,128)(2,1)S(1)} %collective-permute-done.9.refs_1_), channel_id=1, source_target_pairs={{0,16},{8,24},{16,0},{24,8},{1,17},{9,25},{17,1},{25,9},{2,18},{10... | collective-permute-start | bytes 884744 | tf_op jit(solution)/shard_map/ppermute | solution.py:449
  46.0 10.2 %collective-permute-start.13 = (bf16[400,128]{1,0:T(8,128)(2,1)S(1)}, bf16[400,128]{1,0:T(8,128)(2,1)S(1)}, u32[]{:S(2)}, u32[]{:S(2)}) collective-permute-start(bf16[400,128]{1,0:T(8,128)(2,1)S(1)} %get-tuple-element.189), channel_id=1, source_target_pairs={{0,2},{2,4},{4,6},{1,3},{3,5},{5,7},{8,10},{10,12},{12,14},{9,11},... | collective-permute-start | bytes 307208 | tf_op jit(solution)/shard_map/ppermute | solution.py:455
  59.4 11.2 %collective-permute-start.21 = (bf16[768,256]{1,0:T(8,128)(2,1)S(1)}, bf16[768,256]{1,0:T(8,128)(2,1)S(1)}, u32[]{:S(2)}, u32[]{:S(2)}) collective-permute-start(bf16[768,256]{1,0:T(8,128)(2,1)S(1)} %branch_half.1.half_ref), channel_id=1, source_target_pairs={{0,1},{1,0},{2,3},{3,2},{4,5},{5,4},{6,7},{7,6},{8,9},{9,8},{10,11... | collective-permute-start | bytes 1179656 | tf_op jit(solution)/shard_map/ppermute | solution.py:441
  61.0 8.8 %collective-permute-start.22 = (bf16[192,768]{1,0:T(8,128)(2,1)S(1)}, bf16[192,768]{1,0:T(8,128)(2,1)S(1)}, u32[]{:S(2)}, u32[]{:S(2)}) collective-permute-start(bf16[192,768]{1,0:T(8,128)(2,1)S(1)} %collective-permute-done.17.refs_3_), channel_id=1, source_target_pairs={{0,16},{8,24},{16,0},{24,8},{1,17},{9,25},{17,1},{25,9},{2,18},{10... | collective-permute-start | bytes 884744 | tf_op jit(solution)/shard_map/ppermute | solution.py:449
  77.4 11.2 %collective-permute-start.25 = (bf16[768,256]{1,0:T(8,128)(2,1)S(1)}, bf16[768,256]{1,0:T(8,128)(2,1)S(1)}, u32[]{:S(2)}, u32[]{:S(2)}) collective-permute-start(bf16[768,256]{1,0:T(8,128)(2,1)S(1)} %ffn_half.1.half_ref), channel_id=1, source_target_pairs={{0,1},{1,0},{2,3},{3,2},{4,5},{5,4},{6,7},{7,6},{8,9},{9,8},{10,11... | collective-permute-start | bytes 1179656 | tf_op jit(solution)/shard_map/ppermute | solution.py:441
  95.3 15.6 %collective-permute-start.29 = (bf16[384,768]{1,0:T(8,128)(2,1)S(1)}, bf16[384,768]{1,0:T(8,128)(2,1)S(1)}, u32[]{:S(2)}, u32[]{:S(2)}) collective-permute-start(bf16[384,768]{1,0:T(8,128)(2,1)S(1)} %get-tuple-element.230), channel_id=1, source_target_pairs={{0,2},{2,0},{4,6},{6,4},{1,3},{3,1},{5,7},{7,5},{8,10},{10,8},{12,... | collective-permute-start | bytes 1769480 | tf_op jit(solution)/shard_map/ppermute | solution.py:459
  97.0 14.1 %collective-permute-start.28 = (bf16[768,256]{1,0:T(8,128)(2,1)S(1)}, bf16[768,256]{1,0:T(8,128)(2,1)S(1)}, u32[]{:S(2)}, u32[]{:S(2)}) collective-permute-start(bf16[768,256]{1,0:T(8,128)(2,1)S(1)} %first_half.1.half_ref), channel_id=1, source_target_pairs={{0,1},{1,0},{2,3},{3,2},{4,5},{5,4},{6,7},{7,6},{8,9},{9,8},{10,11... | collective-permute-start | bytes 1179656 | tf_op jit(solution)/shard_map/ppermute | solution.py:441
  99.5 16.0 %collective-permute-start.31 = (bf16[768,384]{1,0:T(8,128)(2,1)S(1)}, bf16[768,384]{1,0:T(8,128)(2,1)S(1)}, u32[]{:S(2)}, u32[]{:S(2)}) collective-permute-start(bf16[768,384]{1,0:T(8,128)(2,1)S(1)} %get-tuple-element.244), channel_id=1, source_target_pairs={{0,16},{8,24},{16,0},{24,8},{1,17},{9,25},{17,1},{25,9},{2,18},{10... | collective-permute-start | bytes 1769480 | tf_op jit(solution)/shard_map/ppermute | solution.py:449
  115.5 13.3 %collective-permute-start.32 = (bf16[384,640]{1,0:T(8,128)(2,1)S(1)}, bf16[384,640]{1,0:T(8,128)(2,1)S(1)}, u32[]{:S(2)}, u32[]{:S(2)}) collective-permute-start(bf16[384,640]{1,0:T(8,128)(2,1)S(1)} %get-tuple-element.246), channel_id=1, source_target_pairs={{0,16},{8,24},{16,0},{24,8},{1,17},{9,25},{17,1},{25,9},{2,18},{10... | collective-permute-start | bytes 1474568 | tf_op jit(solution)/shard_map/ppermute | solution.py:449
  117.1 13.0 %collective-permute-start.34 = (bf16[400,128]{1,0:T(8,128)(2,1)S(1)}, bf16[400,128]{1,0:T(8,128)(2,1)S(1)}, u32[]{:S(2)}, u32[]{:S(2)}) collective-permute-start(bf16[400,128]{1,0:T(8,128)(2,1)S(1)} %get-tuple-element.249), channel_id=1, source_target_pairs={{2,0},{4,2},{6,4},{3,1},{5,3},{7,5},{10,8},{12,10},{14,12},{11,9},... | collective-permute-start | bytes 307208 | tf_op jit(solution)/shard_map/ppermute | solution.py:455
  118.4 13.1 %collective-permute-start.35 = (bf16[400,128]{1,0:T(8,128)(2,1)S(1)}, bf16[400,128]{1,0:T(8,128)(2,1)S(1)}, u32[]{:S(2)}, u32[]{:S(2)}) collective-permute-start(bf16[400,128]{1,0:T(8,128)(2,1)S(1)} %get-tuple-element.249), channel_id=1, source_target_pairs={{4,0},{6,2},{5,1},{7,3},{12,8},{14,10},{13,9},{15,11},{20,16},{22,... | collective-permute-start | bytes 307208 | tf_op jit(solution)/shard_map/ppermute | solution.py:455
  119.7 11.8 %collective-permute-start.36 = (bf16[400,128]{1,0:T(8,128)(2,1)S(1)}, bf16[400,128]{1,0:T(8,128)(2,1)S(1)}, u32[]{:S(2)}, u32[]{:S(2)}) collective-permute-start(bf16[400,128]{1,0:T(8,128)(2,1)S(1)} %get-tuple-element.249), channel_id=1, source_target_pairs={{6,0},{7,1},{14,8},{15,9},{22,16},{23,17},{30,24},{31,25}} | collective-permute-start | bytes 307208 | tf_op jit(solution)/shard_map/ppermute | solution.py:455
  129.7 12.5 %collective-permute-start.37 = (bf16[384,640]{1,0:T(8,128)(2,1)S(1)}, bf16[384,640]{1,0:T(8,128)(2,1)S(1)}, u32[]{:S(2)}, u32[]{:S(2)}) collective-permute-start(bf16[384,640]{1,0:T(8,128)(2,1)S(1)} %get-tuple-element.259), channel_id=1, source_target_pairs={{0,2},{2,0},{4,6},{6,4},{1,3},{3,1},{5,7},{7,5},{8,10},{10,8},{12,... | collective-permute-start | bytes 1474568 | tf_op jit(solution)/shard_map/ppermute | solution.py:459
  133.9 13.6 %collective-permute-start.40 = (bf16[4,96,576]{2,1,0:T(8,128)(2,1)S(1)}, bf16[4,96,576]{2,1,0:T(8,128)(2,1)S(1)}, u32[]{:S(2)}, u32[]{:S(2)}) collective-permute-start(bf16[4,96,576]{2,1,0:T(8,128)(2,1)S(1)} %get-tuple-element.271), channel_id=1, source_target_pairs={{0,16},{8,24},{16,0},{24,8},{1,17},{9,25},{17,1},{25,9},{2,18},{10... | collective-permute-start | bytes 1327112 | tf_op jit(solution)/shard_map/ppermute | solution.py:449
  136.3 11.2 %collective-permute-start.42 = (bf16[384,256]{1,0:T(8,128)(2,1)S(1)}, bf16[384,256]{1,0:T(8,128)(2,1)S(1)}, u32[]{:S(2)}, u32[]{:S(2)}) collective-permute-start(bf16[384,256]{1,0:T(8,128)(2,1)S(1)} %get-tuple-element.275), channel_id=1, source_target_pairs={{0,1},{1,0},{2,3},{3,2},{4,5},{5,4},{6,7},{7,6},{8,9},{9,8},{10,11... | collective-permute-start | bytes 589832 | tf_op jit(solution)/shard_map/ppermute | solution.py:441
  142.3 19.5 %collective-permute-start.38 = (bf16[192,768]{1,0:T(8,128)(2,1)S(1)}, bf16[192,768]{1,0:T(8,128)(2,1)S(1)}, u32[]{:S(2)}, u32[]{:S(2)}) collective-permute-start(bf16[192,768]{1,0:T(8,128)(2,1)S(1)} %get-tuple-element.268), channel_id=1, source_target_pairs={{0,4},{2,6},{4,0},{6,2},{1,5},{3,7},{5,1},{7,3},{8,12},{10,14},{12... | collective-permute-start | bytes 884744 | tf_op jit(solution)/shard_map/ppermute | solution.py:459
  148.3 17.9 %collective-permute-start.43 = (bf16[192,832]{1,0:T(8,128)(2,1)S(1)}, bf16[192,832]{1,0:T(8,128)(2,1)S(1)}, u32[]{:S(2)}, u32[]{:S(2)}) collective-permute-start(bf16[192,832]{1,0:T(8,128)(2,1)S(1)} %get-tuple-element.278), channel_id=1, source_target_pairs={{0,2},{2,0},{4,6},{6,4},{1,3},{3,1},{5,7},{7,5},{8,10},{10,8},{12,... | collective-permute-start | bytes 958472 | tf_op jit(solution)/shard_map/ppermute | solution.py:459
  148.8 13.0 %collective-permute-start.33 = (bf16[192,384]{1,0:T(8,128)(2,1)S(1)}, bf16[192,384]{1,0:T(8,128)(2,1)S(1)}, u32[]{:S(2)}, u32[]{:S(2)}) collective-permute-start(bf16[192,384]{1,0:T(8,128)(2,1)S(1)} %get-tuple-element.248), channel_id=1, source_target_pairs={{0,4},{2,6},{4,0},{6,2},{1,5},{3,7},{5,1},{7,3},{8,12},{10,14},{12... | collective-permute-start | bytes 442376 | tf_op jit(solution)/shard_map/ppermute | solution.py:459
  162.5 17.9 %collective-permute-start.45 = (bf16[192,896]{1,0:T(8,128)(2,1)S(1)}, bf16[192,896]{1,0:T(8,128)(2,1)S(1)}, u32[]{:S(2)}, u32[]{:S(2)}) collective-permute-start(bf16[192,896]{1,0:T(8,128)(2,1)S(1)} %get-tuple-element.282.refs_0_), channel_id=1, source_target_pairs={{0,16},{8,24},{16,0},{24,8},{1,17},{9,25},{17,1},{25,9},{2,18},{10... | collective-permute-start | bytes 1032200 | tf_op jit(solution)/shard_map/ppermute | solution.py:449
  164.0 17.2 %collective-permute-start.46 = (bf16[192,896]{1,0:T(8,128)(2,1)S(1)}, bf16[192,896]{1,0:T(8,128)(2,1)S(1)}, u32[]{:S(2)}, u32[]{:S(2)}) collective-permute-start(bf16[192,896]{1,0:T(8,128)(2,1)S(1)} %get-tuple-element.282.refs_0_), channel_id=1, source_target_pairs={{0,8},{8,0},{16,24},{24,16},{1,9},{9,1},{17,25},{25,17},{2,10},{10... | collective-permute-start | bytes 1032200 | tf_op jit(solution)/shard_map/ppermute | solution.py:445
  164.0 18.8 %collective-permute-start.47 = (bf16[192,896]{1,0:T(8,128)(2,1)S(1)}, bf16[192,896]{1,0:T(8,128)(2,1)S(1)}, u32[]{:S(2)}, u32[]{:S(2)}) collective-permute-start(bf16[192,896]{1,0:T(8,128)(2,1)S(1)} %get-tuple-element.282.refs_0_), channel_id=1, source_target_pairs={{0,24},{8,16},{16,8},{24,0},{1,25},{9,17},{17,9},{25,1},{2,26},{10... | collective-permute-start | bytes 1032200 | tf_op jit(solution)/shard_map/ppermute | solution.py:1216
  166.3 11.8 %collective-permute-start.44 = (bf16[96,1088]{1,0:T(8,128)(2,1)S(1)}, bf16[96,1088]{1,0:T(8,128)(2,1)S(1)}, u32[]{:S(2)}, u32[]{:S(2)}) collective-permute-start(bf16[96,1088]{1,0:T(8,128)(2,1)S(1)} %get-tuple-element.280), channel_id=1, source_target_pairs={{0,4},{2,6},{4,0},{6,2},{1,5},{3,7},{5,1},{7,3},{8,12},{10,14},{12... | collective-permute-start | bytes 626696 | tf_op jit(solution)/shard_map/ppermute | solution.py:459
  (31 other events, 203.9 us)
